TPU v7x, 32 devices: a whole 2x2x4 slice. The times are simulated.
32 devices in a mesh: ctx: 8 (over y, x, core), head: 4 (over z).
Axes of the slice: x: 2, y: 2, z: 4, core: 2. Of those that a mesh axis runs over, the one named last changes fastest.
Arguments:
- query_states: bfloat16 [2048, 2048], P('ctx', 'head'), may hold values from -28 to 28
- key_states: bfloat16 [2048, 2048], P('ctx', 'head'), may hold values from -4 to 4
- value_states: bfloat16 [2048, 2048], P('ctx', 'head'), may hold values from -6 to 6
- out_weight: bfloat16 [2048, 2048], P('head'), may hold values from -0.125 to 0.125
- grad_mixed: bfloat16 [2048, 2048], P(('ctx', 'head')), may hold values from -6 to 6
- key_blocks: int32 [16, 4], P('ctx'), may hold values from 0 to 15, as said below
- host_ids: int32 [16], replicated, may hold values from 0 to 3
- host_bias: float32 [16], P('head'), may hold values from 0.5 to 3
Outputs:
- mixed_out: bfloat16 [2048, 2048], P(('ctx', 'head'))
- grad_query: bfloat16 [2048, 2048], P('ctx', 'head')
- grad_key: bfloat16 [2048, 2048], P('ctx', 'head')
- grad_value: bfloat16 [2048, 2048], P('ctx', 'head')
Inputs may be any that keep to these rules, and one draw needn't show every extreme that they name: `key_blocks`: row i lists 4 different blocks, the first being block i itself; every listed block lies among the 2 blocks of a ctx index at most 2 places from that of block i on the closed loop of ctx indices.
All inputs are finite; a program needn't handle non-finite values.
Results may differ from a plain program's by a relative error of at most 0.022.
Values may be sent and summed in bfloat16 or wider, within the bound.
No kernel may reach another device: no remote copies, remote signals or barrier semaphores. Data moves between devices by JAX's collectives and lax.ppermute only.
A program may use at most 64 MiB of HBM per device.

v0:
```python
import jax
import jax.numpy as jnp
from jax import lax
from jax.sharding import PartitionSpec as P

HDIM = 128
BLK = 128
HOPS = 2


def from_behind(shard, axis, by):
    devices = lax.axis_size(axis)
    return lax.ppermute(shard, axis, [(i, (i + by) % devices) for i in range(devices)])


def per_device(
    query_states, key_states, value_states, out_weight, grad_mixed, key_blocks, host_ids, host_bias
):
    logit_scale = HDIM ** (-0.5)
    blocks_dev = key_blocks.shape[0]
    neighbours = key_blocks.shape[1]
    heads_dev = host_bias.shape[0]
    row_count = query_states.shape[0]
    columns = query_states.shape[1]
    loop_size = lax.axis_size("ctx")
    position = lax.axis_index("ctx")
    span = 2 * HOPS + 1
    key_value = jnp.stack([key_states, value_states])
    nearby = {0: key_value}
    for offset in range(-HOPS, HOPS + 1):
        if offset != 0:
            nearby[offset] = from_behind(key_value, "ctx", -offset)
    window = jnp.concatenate([nearby[offset] for offset in range(-HOPS, HOPS + 1)], axis=1)
    window = window.reshape(2, span * blocks_dev, BLK, heads_dev, HDIM)
    owner_dev = key_blocks // blocks_dev
    distance = jnp.mod(owner_dev - position, loop_size)
    distance = jnp.where(distance > loop_size // 2, distance - loop_size, distance)
    slot_list = ((distance + HOPS) * blocks_dev + key_blocks % blocks_dev).reshape(-1)
    chosen = jnp.take(window, slot_list, axis=1).reshape(
        2, blocks_dev, neighbours, BLK, heads_dev, HDIM
    )
    selected_keys = chosen[0]
    selected_values = chosen[1]
    own_hosts = lax.dynamic_slice_in_dim(host_ids, position * blocks_dev, blocks_dev)
    matches = (
        key_blocks[:, :, None] == jnp.arange(host_ids.shape[0], dtype=jnp.int32)[None, None, :]
    )
    far_hosts = jnp.sum(jnp.where(matches, host_ids[None, None, :], 0), axis=2)
    same_host = (own_hosts[:, None] == far_hosts).astype(jnp.float32)
    queries = query_states.reshape(blocks_dev, BLK, heads_dev, HDIM)
    attention_logits = (
        jnp.einsum("bqhd,bnkhd->bhqnk", queries, selected_keys, preferred_element_type=jnp.float32)
        * logit_scale
    )
    attention_logits = (
        attention_logits + host_bias[None, :, None, None, None] * same_host[:, None, None, :, None]
    )
    highest = jnp.max(attention_logits, axis=(3, 4), keepdims=True)
    weights = jnp.exp(attention_logits - highest)
    probs = weights / jnp.sum(weights, axis=(3, 4), keepdims=True)
    batch_probabilities = probs.astype(jnp.bfloat16)
    attended = jnp.einsum(
        "bhqnk,bnkhd->bqhd",
        batch_probabilities,
        selected_values,
        preferred_element_type=jnp.float32,
    )
    attended = attended.astype(jnp.bfloat16).reshape(row_count, columns)
    mixed_out = lax.psum_scatter(
        jnp.dot(attended, out_weight, preferred_element_type=jnp.float32).astype(jnp.bfloat16),
        "head",
        scatter_dimension=0,
        tiled=True,
    )
    upstream = lax.dot_general(
        lax.all_gather(grad_mixed, "head", axis=0, tiled=True),
        out_weight,
        (((1,), (1,)), ((), ())),
        preferred_element_type=jnp.float32,
    ).astype(jnp.bfloat16)
    upstream_blocks = upstream.reshape(blocks_dev, BLK, heads_dev, HDIM)
    selected_value_gradient = jnp.einsum(
        "bhqnk,bqhd->bnkhd",
        batch_probabilities,
        upstream_blocks,
        preferred_element_type=jnp.float32,
    )
    probability_gradient = jnp.einsum(
        "bqhd,bnkhd->bhqnk", upstream_blocks, selected_values, preferred_element_type=jnp.float32
    )
    row_term = jnp.sum(probs * probability_gradient, axis=(3, 4), keepdims=True)
    logit_gradient = (probs * (probability_gradient - row_term) * logit_scale).astype(jnp.bfloat16)
    grad_query = jnp.einsum(
        "bhqnk,bnkhd->bqhd", logit_gradient, selected_keys, preferred_element_type=jnp.float32
    )
    grad_query = grad_query.astype(jnp.bfloat16).reshape(row_count, columns)
    selected_key_gradient = jnp.einsum(
        "bhqnk,bqhd->bnkhd", logit_gradient, queries, preferred_element_type=jnp.float32
    )
    stacked = jnp.stack([selected_key_gradient, selected_value_gradient]).reshape(
        2, blocks_dev * neighbours, BLK, heads_dev, HDIM
    )
    window_grad = (
        jnp.zeros((2, span * blocks_dev, BLK, heads_dev, HDIM), jnp.float32)
        .at[:, slot_list]
        .add(stacked)
    )
    window_grad = window_grad.reshape(2, span, row_count, columns)
    totals = window_grad[:, HOPS]
    for offset in range(-HOPS, HOPS + 1):
        if offset != 0:
            totals = totals + from_behind(
                window_grad[:, offset + HOPS].astype(jnp.bfloat16), "ctx", offset
            ).astype(jnp.float32)
    grad_key = totals[0].astype(jnp.bfloat16)
    grad_value = totals[1].astype(jnp.bfloat16)
    return (mixed_out, grad_query, grad_key, grad_value)


def solution(mesh):
    in_specs = (
        P("ctx", "head"),
        P("ctx", "head"),
        P("ctx", "head"),
        P("head", None),
        P(("ctx", "head"), None),
        P("ctx", None),
        P(),
        P("head"),
    )
    out_specs = (P(("ctx", "head"), None), P("ctx", "head"), P("ctx", "head"), P("ctx", "head"))
    return jax.shard_map(
        per_device, mesh=mesh, in_specs=in_specs, out_specs=out_specs, check_vma=False
    )
```

profile of v0, /device:TPU:0, one launch (start us, length us, event | category | flops | bytes accessed | tf_op | source)
XLA Modules:
  0.0 174.8 jit_solution(889628082627599199)
XLA Ops:
  7.2 2.0 %pad_maximum_fusion = bf16[2,256,512]{2,1,0:T(8,128)(2,1)} fusion(bf16[1,256,512]{2,1,0:T(8,128)(2,1)} %bitcast.120, bf16[1,256,512]{2,1,0:T(8,128)(2,1)} %bitcast.122), kind=kLoop, calls=%fused_computation.35 | loop fusion | flops 262144 | bytes 1048576 | tf_op jit(solution)/shard_map/stack | solution.py:28
  9.3 3.9 %collective-permute-start.3 = (bf16[2,256,512]{2,1,0:T(8,128)(2,1)}, bf16[2,256,512]{2,1,0:T(8,128)(2,1)S(1)}, u32[]{:S(2)}, u32[]{:S(2)}) collective-permute-start(bf16[2,256,512]{2,1,0:T(8,128)(2,1)} %pad_maximum_fusion), channel_id=1, source_target_pairs={{0,24},{4,28},{8,0},{12,4},{16,8},{20,12},{24,16},{28,20},{1,25},{... | collective-permute-start | bytes 1572872 | tf_op jit(solution)/shard_map/ppermute | solution.py:13
  13.2 0.5 collective-permute-start.1
  13.7 0.7 collective-permute-start
  14.5 0.7 fusion.24
  15.2 0.9 select_reduce_fusion
  16.1 0.7 dynamic_slice.3
  17.0 0.7 broadcast_multiply_fusion
  17.8 1.0 reshape.114
  18.8 29.3 %collective-permute-done = bf16[2,256,512]{2,1,0:T(8,128)(2,1)} collective-permute-done((bf16[2,256,512]{2,1,0:T(8,128)(2,1)}, bf16[2,256,512]{2,1,0:T(8,128)(2,1)}, u32[]{:S(2)}, u32[]{:S(2)}) %collective-permute-start) | collective-permute-done | bytes 524320 | tf_op jit(solution)/shard_map/ppermute | solution.py:13
  48.1 1.9 %constant_dynamic-update-slice_fusion.4 = bf16[2,1280,512]{2,1,0:T(8,128)(2,1)} fusion(bf16[2,256,512]{2,1,0:T(8,128)(2,1)} %collective-permute-done), kind=kLoop, calls=%fused_computation.52 | loop fusion | bytes 1048576
  50.0 1.9 %constant_dynamic-update-slice_fusion.3 = bf16[2,1280,512]{2,1,0:T(8,128)(2,1)} fusion(bf16[2,1280,512]{2,1,0:T(8,128)(2,1)} %constant_dynamic-update-slice_fusion.4, bf16[2,256,512]{2,1,0:T(8,128)(2,1)} %collective-permute-done.1), kind=kLoop, calls=%fused_computation.51 | loop fusion | bytes 1048576
  51.9 0.8 constant_dynamic-update-slice_fusion.2
  52.7 1.9 %constant_dynamic-update-slice_fusion.1 = bf16[2,1280,512]{2,1,0:T(8,128)(2,1)} fusion(bf16[2,1280,512]{2,1,0:T(8,128)(2,1)} %constant_dynamic-update-slice_fusion.2, bf16[2,256,512]{2,1,0:T(8,128)(2,1)} %collective-permute-done.2), kind=kLoop, calls=%fused_computation.49 | loop fusion | bytes 1048576
  54.6 0.8 constant_dynamic-update-slice_fusion
  55.5 4.9 %reshape.112 = bf16[2,10,128,4,128]{4,3,2,1,0:T(4,128)(2,1)} reshape(bf16[2,1280,512]{2,1,0:T(8,128)(2,1)} %constant_dynamic-update-slice_fusion) | data formatting | bytes 5242880 | tf_op jit(solution)/shard_map/reshape | solution.py:34
  60.4 4.0 %copy.85 = bf16[2,10,128,4,128]{4,2,3,1,0:T(8,128)(2,1)} copy(bf16[2,10,128,4,128]{4,3,2,1,0:T(4,128)(2,1)} %reshape.112) | data formatting | bytes 5242880 | tf_op jit(solution)/shard_map/reshape | solution.py:34
  64.3 3.9 %gather_fusion = bf16[8,2,128,4,128]{4,2,3,1,0:T(8,128)(2,1)} fusion(bf16[2,10,128,4,128]{4,2,3,1,0:T(8,128)(2,1)} %copy.85, s32[1024]{0:T(1024)S(1)} %pad_clamp_fusion), kind=kCustom, calls=%fused_computation | custom fusion | bytes 4194336 | tf_op jit(solution)/shard_map/jit(_take)/gather | solution.py:39
  68.2 1.9 %select_bitcast_fusion = bf16[2,8,128,4,128]{4,2,3,0,1:T(8,128)(2,1)S(1)} fusion(bf16[8,2,128,4,128]{4,2,3,1,0:T(8,128)(2,1)} %gather_fusion, pred[8]{0:T(512)(128)(4,1)S(1)} %compare_and_fusion), kind=kLoop, calls=%fused_computation.7 | loop fusion | flops 1048576 | bytes 4194312 | tf_op jit(solution)/shard_map/jit(_take)/select_n | solution.py:39
  70.4 0.5 bitcast_reduce_fusion
  71.3 0.5 fusion.2
  71.8 0.8 copy-done.2
  72.6 1.6 fusion.6
  74.2 1.8 %copy.90 = bf16[2,128,4,128]{3,2,1,0:T(4,128)(2,1)} copy(bf16[2,128,4,128]{1,3,2,0:T(8,128)(2,1)} %fusion.6) | data formatting | bytes 524288 | tf_op jit(solution)/shard_map/convert_element_type | solution.py:68
  76.0 2.6 %convolution_convert_fusion = bf16[256,2048]{1,0:T(8,128)(2,1)} fusion(bf16[512,2048]{1,0:T(8,128)(2,1)S(1)} %copy-done, bf16[32,8,4,128]{3,2,1,0:T(4,128)(2,1)} %bitcast.124), kind=kOutput, calls=%fused_computation.3 | convolution fusion | flops 537395200 | bytes 3407872 | tf_op jit(solution)/shard_map/dot_general | solution.py:70
  78.7 2.7 %convolution_convert_fusion.1 = bf16[256,512]{1,0:T(8,128)(2,1)} fusion(bf16[256,2048]{1,0:T(8,128)(2,1)} %all-gather.2.cloned.1.call-done, bf16[512,2048]{1,0:T(8,128)(2,1)S(1)} %copy-done), kind=kOutput, calls=%fused_computation.19 | convolution fusion | flops 537001984 | bytes 3407872 | tf_op jit(solution)/shard_map/dot_general | solution.py:75
  81.4 1.7 reshape.116
  83.1 2.5 %multiply_reduce_fusion = (f32[2,4,128]{2,1,0:T(4,128)S(1)}, f32[2,4,128,512]{2,3,1,0:S(1)}) fusion(f32[2,4,128]{2,1,0:T(4,128)S(1)} %fusion.2, f32[2,4,128]{2,1,0:T(4,128)S(1)} %get-tuple-element.12, f32[2,4,4]{2,1,0:T(4,128)S(1)} %broadcast_multiply_fusion, f32[2,4,4,128,128]{4,3,2,1,0:T(8,128)} %copy-done.2, bf16[2,4,128,512]{2,3,1,0:T(8,128)(2,1)S(1)} %bitcast.114, ...), kind=kOutput, calls=%fused_computation.9 | convolution fusion | flops 137362432 | bytes 5517440
  85.7 0.8 multiply_convert_fusion
  86.6 2.1 %convolution_bitcast_fusion = f32[2,4,128,4,128]{2,4,1,3,0:T(8,128)} fusion(bf16[2,128,4,128,1]{3,2,1,0,4:T(4,128)(2,1)S(1)} %bitcast.125, f32[2,4,4,128,128]{4,3,2,1,0:T(8,128)S(1)} %copy-done.3, f32[2,4,128]{2,1,0:T(4,128)S(1)} %fusion.2, f32[2,4,128]{2,1,0:T(4,128)S(1)} %get-tuple-element.12, f32[2,4,4]{2,1,0:T(4,128)S(1)} %broadcast_multiply_fusion), kind=kOutput, calls=%fused_computation.11 | convolution fusion | flops 136839168 | bytes 4464768 | tf_op jit(solution)/shard_map/bhqnk,bqhd->bnkhd/dot_general | solution.py:82
  88.7 2.9 %copy.100 = f32[2,4,128,4,128]{4,2,3,1,0:T(8,128)} copy(f32[2,4,128,4,128]{2,4,1,3,0:T(8,128)} %convolution_bitcast_fusion) | data formatting | bytes 4194304 | tf_op jit(solution)/shard_map/bhqnk,bqhd->bnkhd/transpose | solution.py:82
  92.2 1.5 copy-done.6
  93.7 0.5 maximum_bitcast_fusion
  94.2 2.3 %copy.101 = f32[8,2,128,4,128]{4,2,3,1,0:T(8,128)} copy(f32[8,2,128,4,128]{4,2,3,0,1:T(8,128)S(1)} %maximum_bitcast_fusion) | data formatting | bytes 8388608 | tf_op jit(solution)/shard_map/stack | solution.py:100
  96.5 2.9 %broadcast_in_dim.39 = f32[2,10,128,4,128]{4,2,3,1,0:T(8,128)} broadcast(f32[]{:T(128)} %constant.75.clone.1), dimensions={} | broadcast | bytes 5242884 | tf_op jit(solution)/shard_map/broadcast_in_dim | solution.py:104
  99.4 9.5 %scatter_fusion = f32[2,10,128,4,128]{4,2,3,1,0:T(8,128)} fusion(f32[2,10,128,4,128]{4,2,3,1,0:T(8,128)} %broadcast_in_dim.39, s32[8]{0:T(128)S(1)} %fusion.28, f32[8,2,128,4,128]{4,2,3,1,0:T(8,128)} %copy.101), kind=kCustom, calls=%fused_computation.1 | custom fusion | flops 1048576 | bytes 12582944 | tf_op jit(solution)/shard_map/scatter-add | solution.py:106
  108.9 8.7 %copy.102 = f32[2,10,128,4,128]{4,3,2,1,0:T(4,128)} copy(f32[2,10,128,4,128]{4,2,3,1,0:T(8,128)} %scatter_fusion) | data formatting | bytes 10485760 | tf_op jit(solution)/shard_map/scatter-add | solution.py:106
  117.6 7.4 %reshape.118 = f32[2,5,256,512]{3,2,1,0:T(8,128)} reshape(f32[2,10,128,4,128]{4,3,2,1,0:T(4,128)} %copy.102) | data formatting | bytes 10485760 | tf_op jit(solution)/shard_map/reshape | solution.py:108
  125.0 2.8 %convert.10 = bf16[2,5,256,512]{3,2,1,0:T(8,128)(2,1)S(1)} convert(f32[2,5,256,512]{3,2,1,0:T(8,128)} %reshape.118) | non-fusion elementwise | flops 1310720 | bytes 7864320 | tf_op jit(solution)/shard_map/convert.5
  127.9 1.4 slice_bitcast_fusion.4
  129.3 1.6 collective-permute-start.4
  131.5 0.5 fusion.5
  132.2 0.7 copy.156
  133.0 11.5 %collective-permute-done.4 = bf16[2,256,512]{2,1,0:T(8,128)(2,1)} collective-permute-done((bf16[2,256,512]{2,1,0:T(8,128)(2,1)}, bf16[2,256,512]{2,1,0:T(8,128)(2,1)}, u32[]{:S(2)}, u32[]{:S(2)}) %collective-permute-start.4) | collective-permute-done | bytes 524320 | tf_op jit(solution)/shard_map/ppermute | solution.py:13
  144.5 10.4 %collective-permute-done.5 = bf16[2,256,512]{2,1,0:T(8,128)(2,1)} collective-permute-done((bf16[2,256,512]{2,1,0:T(8,128)(2,1)}, bf16[2,256,512]{2,1,0:T(8,128)(2,1)}, u32[]{:S(2)}, u32[]{:S(2)}) %collective-permute-start.5) | collective-permute-done | bytes 524320 | tf_op jit(solution)/shard_map/ppermute | solution.py:13
  154.8 10.1 %collective-permute-done.7 = bf16[2,256,512]{2,1,0:T(8,128)(2,1)} collective-permute-done((bf16[2,256,512]{2,1,0:T(8,128)(2,1)}, bf16[2,256,512]{2,1,0:T(8,128)(2,1)}, u32[]{:S(2)}, u32[]{:S(2)}) %collective-permute-start.7) | collective-permute-done | bytes 524320 | tf_op jit(solution)/shard_map/ppermute | solution.py:13
  164.9 2.2 %fusion.11 = bf16[2,256,512]{2,1,0:T(8,128)(2,1)S(1)} fusion(f32[2,5,256,512]{3,2,1,0:T(8,128)} %reshape.118, bf16[2,256,512]{2,1,0:T(8,128)(2,1)} %collective-permute-done.7, bf16[2,256,512]{2,1,0:T(8,128)(2,1)} %collective-permute-done.6, bf16[2,256,512]{2,1,0:T(8,128)(2,1)} %collective-permute-done.5, bf16[2,256,512]{2,1,0:T(8,128)(2,1)} %collective-permute-done.4), kind=kLoop, calls=%fused_computation.27 | loop fusion | flops 2359296 | bytes 3670016 | tf_op jit(solution)/shard_map/convert.1
  167.1 0.8 slice_bitcast_fusion.5
  (43 shorter events, 2.7 us)
Async XLA Ops:
  7.2 68.9 %copy-start = (bf16[512,2048]{1,0:T(8,128)(2,1)S(1)}, bf16[512,2048]{1,0:T(8,128)(2,1)}, u32[]{:S(2)}) copy-start(bf16[512,2048]{1,0:T(8,128)(2,1)} %param.11) | copy-start | bytes 6291460
  7.2 44.7 %copy-start.7 = (bf16[256,512]{1,0:T(8,128)(2,1)S(1)}, bf16[256,512]{1,0:T(8,128)(2,1)}, u32[]{:S(2)}) copy-start(bf16[256,512]{1,0:T(8,128)(2,1)} %param.10) | copy-start | bytes 786436
  7.2 44.7 %copy-start.8 = (bf16[256,512]{1,0:T(8,128)(2,1)S(1)}, bf16[256,512]{1,0:T(8,128)(2,1)}, u32[]{:S(2)}) copy-start(bf16[256,512]{1,0:T(8,128)(2,1)} %param.9) | copy-start | bytes 786436
  7.2 71.5 %all-gather.2.cloned.1.call-start = ((), (), s32[]{:S(2)}) async-start(), calls=%async_computation.2 | async-start | bytes 1310720 | tf_op jit(solution)/shard_map/all_gather | solution.py:76
  9.3 45.3 %collective-permute-start.3 = (bf16[2,256,512]{2,1,0:T(8,128)(2,1)}, bf16[2,256,512]{2,1,0:T(8,128)(2,1)S(1)}, u32[]{:S(2)}, u32[]{:S(2)}) collective-permute-start(bf16[2,256,512]{2,1,0:T(8,128)(2,1)} %pad_maximum_fusion), channel_id=1, source_target_pairs={{0,24},{4,28},{8,0},{12,4},{16,8},{20,12},{24,16},{28,20},{1,25},{... | collective-permute-start | bytes 1572872 | tf_op jit(solution)/shard_map/ppermute | solution.py:13
  13.2 39.5 %collective-permute-start.2 = (bf16[2,256,512]{2,1,0:T(8,128)(2,1)}, bf16[2,256,512]{2,1,0:T(8,128)(2,1)}, u32[]{:S(2)}, u32[]{:S(2)}) collective-permute-start(bf16[2,256,512]{2,1,0:T(8,128)(2,1)} %pad_maximum_fusion), channel_id=1, source_target_pairs={{0,28},{4,0},{8,4},{12,8},{16,12},{20,16},{24,20},{28,24},{1,29},{... | collective-permute-start | bytes 1572872 | tf_op jit(solution)/shard_map/ppermute | solution.py:13
  13.2 36.8 %collective-permute-start.1 = (bf16[2,256,512]{2,1,0:T(8,128)(2,1)}, bf16[2,256,512]{2,1,0:T(8,128)(2,1)}, u32[]{:S(2)}, u32[]{:S(2)}) collective-permute-start(bf16[2,256,512]{2,1,0:T(8,128)(2,1)} %pad_maximum_fusion), channel_id=1, source_target_pairs={{0,4},{4,8},{8,12},{12,16},{16,20},{20,24},{24,28},{28,0},{1,5},{5... | collective-permute-start | bytes 1572872 | tf_op jit(solution)/shard_map/ppermute | solution.py:13
  13.7 34.4 %collective-permute-start = (bf16[2,256,512]{2,1,0:T(8,128)(2,1)}, bf16[2,256,512]{2,1,0:T(8,128)(2,1)}, u32[]{:S(2)}, u32[]{:S(2)}) collective-permute-start(bf16[2,256,512]{2,1,0:T(8,128)(2,1)} %pad_maximum_fusion), channel_id=1, source_target_pairs={{0,8},{4,12},{8,16},{12,20},{16,24},{20,28},{24,0},{28,4},{1,9},{5... | collective-permute-start | bytes 1572872 | tf_op jit(solution)/shard_map/ppermute | solution.py:13
  14.4 153.5 %reduce-scatter.2.cloned.1.call-start = ((), (), s32[]{:S(2)}) async-start(), calls=%async_computation.1 | async-start | bytes 1310720 | tf_op jit(solution)/shard_map/reduce_scatter | solution.py:69
  70.3 1.0 copy-start.4
  71.3 1.3 copy-start.2
  83.1 2.5 %copy-start.3 = (f32[2,4,4,128,128]{4,3,2,1,0:T(8,128)S(1)}, f32[2,4,4,128,128]{4,3,2,1,0:T(8,128)}, u32[]{:S(2)}) copy-start(f32[2,4,4,128,128]{4,3,2,1,0:T(8,128)} %copy-done.2) | copy-start | bytes 6291460
  85.7 1.0 copy-start.9
  92.1 1.6 copy-start.6
  127.9 3.7 %copy-start.5 = (bf16[1,8,128,4,128]{4,2,3,0,1:T(8,128)(2,1)S(1)}, bf16[1,8,128,4,128]{4,2,3,0,1:T(8,128)(2,1)}, u32[]{:S(2)}) copy-start(bf16[1,8,128,4,128]{4,2,3,0,1:T(8,128)(2,1)} %copy-done.4) | copy-start | bytes 3145732
  129.3 15.2 %collective-permute-start.4 = (bf16[2,256,512]{2,1,0:T(8,128)(2,1)}, bf16[2,256,512]{2,1,0:T(8,128)(2,1)}, u32[]{:S(2)}, u32[]{:S(2)}) collective-permute-start(bf16[2,256,512]{2,1,0:T(8,128)(2,1)} %get-tuple-element.4), channel_id=1, source_target_pairs={{0,24},{4,28},{8,0},{12,4},{16,8},{20,12},{24,16},{28,20},{1,25},{... | collective-permute-start | bytes 1572872 | tf_op jit(solution)/shard_map/ppermute | solution.py:13
  130.9 23.9 %collective-permute-start.5 = (bf16[2,256,512]{2,1,0:T(8,128)(2,1)}, bf16[2,256,512]{2,1,0:T(8,128)(2,1)}, u32[]{:S(2)}, u32[]{:S(2)}) collective-permute-start(bf16[2,256,512]{2,1,0:T(8,128)(2,1)} %get-tuple-element.5), channel_id=1, source_target_pairs={{0,28},{4,0},{8,4},{12,8},{16,12},{20,16},{24,20},{28,24},{1,29},{... | collective-permute-start | bytes 1572872 | tf_op jit(solution)/shard_map/ppermute | solution.py:13
  130.9 34.0 %collective-permute-start.7 = (bf16[2,256,512]{2,1,0:T(8,128)(2,1)}, bf16[2,256,512]{2,1,0:T(8,128)(2,1)}, u32[]{:S(2)}, u32[]{:S(2)}) collective-permute-start(bf16[2,256,512]{2,1,0:T(8,128)(2,1)} %get-tuple-element.6), channel_id=1, source_target_pairs={{0,8},{4,12},{8,16},{12,20},{16,24},{20,28},{24,0},{28,4},{1,9},{5... | collective-permute-start | bytes 1572872 | tf_op jit(solution)/shard_map/ppermute | solution.py:13
  131.3 33.6 %collective-permute-start.6 = (bf16[2,256,512]{2,1,0:T(8,128)(2,1)}, bf16[2,256,512]{2,1,0:T(8,128)(2,1)}, u32[]{:S(2)}, u32[]{:S(2)}) collective-permute-start(bf16[2,256,512]{2,1,0:T(8,128)(2,1)} %get-tuple-element.7), channel_id=1, source_target_pairs={{0,4},{4,8},{8,12},{12,16},{16,20},{20,24},{24,28},{28,0},{1,5},{5... | collective-permute-start | bytes 1572872 | tf_op jit(solution)/shard_map/ppermute | solution.py:13
  132.2 35.7 %copy-start.1 = (bf16[512,2048]{1,0:T(8,128)(2,1)S(1)}, bf16[512,2048]{1,0:T(8,128)(2,1)}, u32[]{:S(2)}) copy-start(bf16[512,2048]{1,0:T(8,128)(2,1)} %param.11) | copy-start | bytes 6291460
Sparse Core Ops, SparseCore 0:
  14.5 29.0 all-gather.1
  78.8 27.4 reduce-scatter.1
where the time goes:
time: 176 us; the launch traced here: 175 us
  waiting for transfers between devices  61.3 us (35%)
  local copies, waits for them, and re-layouts  55.4 us (31%)
  other arithmetic  23.5 us (13%)
  between operations  14.2 us (8%)
  matrix products  12.9 us (7%)
  starting transfers between devices  7.45 us (4%)
    ppermute x8, waiting for transfers between devices, from_behind(): lax.ppermute(shard, axis, [(i, (i + by) % devices) for i in range(devices)])  61.3 us
    scatter-add x1, other arithmetic, per_device(): window_grad = jnp.zeros((2, span * blocks_dev, BLK, heads_dev, HDIM), jnp...  9.46 us
    unnamed x24, local copies, waits for them, and re-layouts  9.23 us
    reshape x2, local copies, waits for them, and re-layouts, per_device(): window = window.reshape(2, span * blocks_dev, BLK, heads_dev, HDIM)  8.85 us
    scatter-add x1, local copies, waits for them, and re-layouts, per_device(): window_grad = jnp.zeros((2, span * blocks_dev, BLK, heads_dev, HDIM), jnp...  8.72 us
    reshape x1, local copies, waits for them, and re-layouts, per_device(): window_grad = window_grad.reshape(2, span, row_count, columns)  7.43 us
    ppermute x8, starting transfers between devices, from_behind(): lax.ppermute(shard, axis, [(i, (i + by) % devices) for i in range(devices)])  7.37 us
    another operation x2, other arithmetic  5.02 us
  transfers between devices with their start and end apart: 10, of which 4 were waited for; matrix products, arithmetic and copies ran while one was open for 50% of the time, Pallas kernels for 0%

commit v1 on v0

v1 whole, which is shorter than its diff:
```python
import functools

import jax
import jax.numpy as jnp
from jax import lax
from jax.experimental import pallas as pl
from jax.experimental.pallas import tpu as pltpu
from jax.sharding import PartitionSpec as P

HDIM = 128
BLK = 128
HOPS = 2
SCALE = HDIM ** (-0.5)
CUBE = (0, 1, 2, 3, 6, 7)
NT = (((1,), (1,)), ((), ()))
VMEM = pl.BlockSpec(memory_space=pltpu.VMEM)
SMEM = pl.BlockSpec(memory_space=pltpu.SMEM)
ANY = pl.BlockSpec(memory_space=pl.ANY)
PARAMS = pltpu.CompilerParams(vmem_limit_bytes=48 * 1024 * 1024)


def ndot(a, b):
    return lax.dot_general(a, b, (((1,), (0,)), ((), ())), preferred_element_type=jnp.float32)


def tdot(a, b):
    return lax.dot_general(a, b, NT, preferred_element_type=jnp.float32)


def stat_rows(pairs):
    return -(-2 * pairs // 16) * 16


def window_tags(size):
    return CUBE if size == 8 else tuple([0] + [o for o in range(-HOPS, HOPS + 1) if o != 0])


def tag_owner(position, tag, size):
    return position ^ tag if size == 8 else lax.rem(position + tag + size, size)


def find_shard(position, owner, size):
    shard = 0
    for index, tag in enumerate(window_tags(size)):
        shard = shard + jnp.where(tag_owner(position, tag, size) == owner, index, 0)
    return shard


def exchange(x, size):
    def move(v, pairs):
        return lax.ppermute(v, "ctx", pairs)

    if size == 8:
        flip = lambda mask: [(i, i ^ mask) for i in range(size)]
        near = move(x, flip(2))
        mate = move(x, flip(1))
        far = move(near, flip(4))
        return [x, mate, near, move(near, flip(1)), far, move(far, flip(1))]
    return [x] + [
        move(x, [(i, (i - tag) % size) for i in range(size)]) for tag in window_tags(size)[1:]
    ]


def load_windows(groups, sem):
    waits = []
    count = 0
    for refs, window in groups:
        rows = refs[0].shape[0]
        copies = []
        for index, ref in enumerate(refs):
            copy = pltpu.make_async_copy(ref, window.at[pl.ds(index * rows, rows)], sem.at[count])
            copy.start()
            copies.append(copy)
            count += 1
        waits.append(copies)
    return waits


def neighbour_rows(size, blocks_dev, rows, keys_ref, hosts_ref):
    position = lax.axis_index("ctx")
    table = []
    for b in range(blocks_dev):
        host = hosts_ref[position * blocks_dev + b]
        line = []
        for n in range(keys_ref.shape[1]):
            j = keys_ref[b, n]
            owner = lax.div(j, blocks_dev)
            shard = find_shard(position, owner, size)
            row = pl.multiple_of(shard * rows + lax.rem(j, blocks_dev) * BLK, BLK)
            line.append((row, jnp.where(hosts_ref[j] == host, 1.0, 0.0).astype(jnp.float32)))
        table.append(line)
    return table


def attend_kernel(size, groups, nsh, *refs):
    keys_ref, hosts_ref, bias_ref, q_ref, w_ref = refs[:5]
    k_refs = refs[5:5 + nsh]
    v_refs = refs[5 + nsh:5 + 2 * nsh]
    rest = refs[5 + 2 * nsh:]
    part_refs = rest[:groups]
    o32_ref, lse_ref = rest[groups:groups + 2]
    kwin, vwin, att, sem = rest[groups + 2:]
    rows, columns = q_ref.shape
    blocks_dev = rows // BLK
    heads_dev = columns // HDIM
    waits = load_windows([(k_refs, kwin), (v_refs, vwin)], sem)
    table = neighbour_rows(size, blocks_dev, rows, keys_ref, hosts_ref)
    for copies in waits:
        for copy in copies:
            copy.wait()
    lane = lax.broadcasted_iota(jnp.int32, (BLK, BLK), 1)
    lse_all = jnp.zeros((BLK, BLK), jnp.float32)
    for b in range(blocks_dev):
        for h in range(heads_dev):
            cols = slice(h * HDIM, (h + 1) * HDIM)
            q = q_ref[b * BLK:(b + 1) * BLK, cols]
            scores = [
                tdot(q, kwin[pl.ds(row, BLK), cols]) * SCALE + bias_ref[h] * same
                for row, same in table[b]
            ]
            top = jnp.max(functools.reduce(jnp.maximum, scores), axis=1, keepdims=True)
            weights = [jnp.exp(s - top) for s in scores]
            total = jnp.sum(functools.reduce(jnp.add, weights), axis=1, keepdims=True)
            inv = 1.0 / total
            out = jnp.zeros((BLK, HDIM), jnp.float32)
            for (row, _), w in zip(table[b], weights):
                out = out + ndot((w * inv).astype(jnp.bfloat16), vwin[pl.ds(row, BLK), cols])
            o32_ref[b * BLK:(b + 1) * BLK, cols] = out
            att[b * BLK:(b + 1) * BLK, cols] = out.astype(jnp.bfloat16)
            lse_all = jnp.where(lane == b * heads_dev + h, top + jnp.log(total), lse_all)
    lse_ref[...] = lse_all
    me = lax.axis_index("head")
    part = rows // groups
    for step in range(groups):
        owner = lax.rem(me + step, groups)
        chunk = att[pl.ds(pl.multiple_of(owner * part, part), part), :]
        part_refs[step][...] = ndot(chunk, w_ref[...]).astype(jnp.bfloat16)


def upstream_kernel(groups, *refs):
    w_ref, o32_ref, lse_ref = refs[:3]
    piece_refs = refs[3:3 + groups]
    up_ref, stats_ref = refs[3 + groups:]
    rows, columns = o32_ref.shape
    blocks_dev = rows // BLK
    heads_dev = columns // HDIM
    me = lax.axis_index("head")
    part = rows // groups
    for step in range(groups):
        owner = lax.rem(me - step + groups, groups)
        up_ref[pl.ds(pl.multiple_of(owner * part, part), part), :] = tdot(
            piece_refs[step][...], w_ref[...]
        ).astype(jnp.bfloat16)
    pairs = blocks_dev * heads_dev
    lane = lax.broadcasted_iota(jnp.int32, (BLK, BLK), 1)
    stats = lse_ref[...]
    for b in range(blocks_dev):
        for h in range(heads_dev):
            cols = slice(h * HDIM, (h + 1) * HDIM)
            up = up_ref[b * BLK:(b + 1) * BLK, cols].astype(jnp.float32)
            term = jnp.sum(up * o32_ref[b * BLK:(b + 1) * BLK, cols], axis=1, keepdims=True)
            stats = jnp.where(lane == pairs + b * heads_dev + h, term, stats)
    stats_ref[...] = stats
    high = stat_rows(pairs)
    turned = jnp.transpose(stats)[:high, :]
    up_ref[rows:, :] = jnp.zeros((up_ref.shape[0] - rows, columns), jnp.bfloat16)
    for index in range(3):
        piece = turned.astype(jnp.bfloat16)
        turned = turned - piece.astype(jnp.float32)
        row = rows + high * (index * BLK // columns)
        col = index * BLK % columns
        up_ref[row:row + high, col:col + BLK] = piece


def query_kernel(size, nsh, *refs):
    keys_ref, hosts_ref, bias_ref, q_ref, up_ref, stats_ref = refs[:6]
    k_refs = refs[6:6 + nsh]
    v_refs = refs[6 + nsh:6 + 2 * nsh]
    dq_ref, kwin, vwin, sem = refs[6 + 2 * nsh:]
    rows, columns = q_ref.shape
    blocks_dev = rows // BLK
    heads_dev = columns // HDIM
    pairs = blocks_dev * heads_dev
    waits = load_windows([(k_refs, kwin), (v_refs, vwin)], sem)
    table = neighbour_rows(size, blocks_dev, rows, keys_ref, hosts_ref)
    for copies in waits:
        for copy in copies:
            copy.wait()
    for b in range(blocks_dev):
        for h in range(heads_dev):
            cols = slice(h * HDIM, (h + 1) * HDIM)
            pair = b * heads_dev + h
            q = q_ref[b * BLK:(b + 1) * BLK, cols]
            up = up_ref[b * BLK:(b + 1) * BLK, cols]
            lse = stats_ref[:, pair:pair + 1]
            term = stats_ref[:, pairs + pair:pairs + pair + 1]
            total = jnp.zeros((BLK, HDIM), jnp.float32)
            for row, same in table[b]:
                k = kwin[pl.ds(row, BLK), cols]
                p = jnp.exp(tdot(q, k) * SCALE + bias_ref[h] * same - lse)
                dp = tdot(up, vwin[pl.ds(row, BLK), cols])
                ds = (p * (dp - term) * SCALE).astype(jnp.bfloat16)
                total = total + ndot(ds, k)
            dq_ref[b * BLK:(b + 1) * BLK, cols] = total.astype(jnp.bfloat16)


def key_kernel(size, nsh, *refs):
    keys_ref, hosts_ref, bias_ref, k_ref, v_ref = refs[:5]
    q_refs = refs[5:5 + nsh]
    up_refs = refs[5 + nsh:5 + 2 * nsh]
    dk_ref, dv_ref, qwin, upwin, stats, dk_acc, dv_acc, sem = refs[5 + 2 * nsh:]
    rows, columns = k_ref.shape
    long_rows = up_refs[0].shape[0]
    blocks_dev = rows // BLK
    heads_dev = columns // HDIM
    pairs = blocks_dev * heads_dev
    position = lax.axis_index("ctx")
    waits = load_windows([(q_refs, qwin), (up_refs, upwin)], sem)
    dk_acc[...] = jnp.zeros_like(dk_acc)
    dv_acc[...] = jnp.zeros_like(dv_acc)
    for copies in waits:
        for copy in copies:
            copy.wait()
    high = stat_rows(pairs)
    for index in range(nsh):
        total = jnp.zeros((high, BLK), jnp.float32)
        for piece in reversed(range(3)):
            row = index * long_rows + rows + high * (piece * BLK // columns)
            col = piece * BLK % columns
            total = total + upwin[row:row + high, col:col + BLK].astype(jnp.float32)
        stats[index] = total

    tags = window_tags(size)

    def visit(step, carry):
        own = lax.rem(step, blocks_dev)
        mine = position * blocks_dev + own
        inner = lax.rem(lax.div(step, blocks_dev), blocks_dev)
        shard = lax.div(step, blocks_dev * blocks_dev)
        owner = 0
        for index, tag in enumerate(tags):
            owner = owner + jnp.where(shard == index, tag_owner(position, tag, size), 0)
        block = owner * blocks_dev + inner
        hit = keys_ref[block, 0] == mine
        for n in range(1, keys_ref.shape[1]):
            hit = hit | (keys_ref[block, n] == mine)

        @pl.when(hit)
        def _():
            same = jnp.where(hosts_ref[block] == hosts_ref[mine], 1.0, 0.0).astype(jnp.float32)
            krow = pl.ds(pl.multiple_of(own * BLK, BLK), BLK)
            qrow = pl.ds(pl.multiple_of(shard * rows + inner * BLK, BLK), BLK)
            urow = pl.ds(pl.multiple_of(shard * long_rows + inner * BLK, 16), BLK)
            for h in range(heads_dev):
                cols = slice(h * HDIM, (h + 1) * HDIM)
                k = k_ref[krow, cols]
                v = v_ref[krow, cols]
                q = qwin[qrow, cols]
                up = upwin[urow, cols]
                lse = stats[shard, pl.ds(inner * heads_dev + h, 1), :]
                term = stats[shard, pl.ds(pairs + inner * heads_dev + h, 1), :]
                p = jnp.exp(tdot(k, q) * SCALE + bias_ref[h] * same - lse)
                dp = tdot(v, up)
                ds = (p * (dp - term) * SCALE).astype(jnp.bfloat16)
                dk_acc[krow, cols] += ndot(ds, q)
                dv_acc[krow, cols] += ndot(p.astype(jnp.bfloat16), up)

        return carry

    lax.fori_loop(0, nsh * blocks_dev * blocks_dev, visit, 0)
    dk_ref[...] = dk_acc[...].astype(jnp.bfloat16)
    dv_ref[...] = dv_acc[...].astype(jnp.bfloat16)


def cost(flops, nbytes):
    return pl.CostEstimate(flops=flops, bytes_accessed=nbytes, transcendentals=0)


def per_device(
    query_states, key_states, value_states, out_weight, grad_mixed, key_blocks, host_ids, host_bias
):
    size = lax.axis_size("ctx")
    groups = lax.axis_size("head")
    rows, columns = query_states.shape
    width = out_weight.shape[1]
    part = rows // groups
    blocks_dev = rows // BLK
    pairs = blocks_dev * (columns // HDIM)
    nsh = len(window_tags(size))
    bf16, f32 = jnp.bfloat16, jnp.float32
    high = stat_rows(pairs)
    extra = high * (-(-3 * BLK // columns))
    long_rows = rows + extra

    def ring(x, step):
        return lax.ppermute(x, "head", [(i, (i + step) % groups) for i in range(groups)])

    all_keys = lax.all_gather(key_blocks, "ctx", axis=0, tiled=True)
    pieces = [grad_mixed] + [ring(grad_mixed, step) for step in range(1, groups)]
    k_win = exchange(key_states, size)
    v_win = exchange(value_states, size)
    q_win = exchange(query_states, size)

    parts_o32_lse = pl.pallas_call(
        functools.partial(attend_kernel, size, groups, nsh),
        out_shape=[jax.ShapeDtypeStruct((part, width), bf16)] * groups
        + [jax.ShapeDtypeStruct((rows, columns), f32), jax.ShapeDtypeStruct((BLK, BLK), f32)],
        in_specs=[SMEM] * 3 + [VMEM] * 2 + [ANY] * (2 * nsh),
        out_specs=[VMEM] * (groups + 2),
        scratch_shapes=[
            pltpu.VMEM((nsh * rows, columns), bf16),
            pltpu.VMEM((nsh * rows, columns), bf16),
            pltpu.VMEM((rows, columns), bf16),
            pltpu.SemaphoreType.DMA((2 * nsh,)),
        ],
        compiler_params=PARAMS,
        cost_estimate=cost(10**9, 8 * 10**6),
        name="attend",
    )(key_blocks, host_ids, host_bias, query_states, out_weight, *k_win, *v_win)
    parts = parts_o32_lse[:groups]
    o32, lse = parts_o32_lse[groups:]
    mixed = parts[0].astype(f32)
    arrived = [ring(parts[step], step) for step in range(1, groups)]

    up, stats = pl.pallas_call(
        functools.partial(upstream_kernel, groups),
        out_shape=[
            jax.ShapeDtypeStruct((long_rows, columns), bf16),
            jax.ShapeDtypeStruct((BLK, BLK), f32),
        ],
        in_specs=[VMEM] * (3 + groups),
        out_specs=[VMEM] * 2,
        compiler_params=PARAMS,
        cost_estimate=cost(6 * 10**8, 4 * 10**6),
        name="upstream",
    )(out_weight, o32, lse, *pieces)
    up_win = exchange(up, size)

    grad_query = pl.pallas_call(
        functools.partial(query_kernel, size, nsh),
        out_shape=jax.ShapeDtypeStruct((rows, columns), bf16),
        in_specs=[SMEM] * 3 + [VMEM] * 3 + [ANY] * (2 * nsh),
        out_specs=VMEM,
        scratch_shapes=[
            pltpu.VMEM((nsh * rows, columns), bf16),
            pltpu.VMEM((nsh * rows, columns), bf16),
            pltpu.SemaphoreType.DMA((2 * nsh,)),
        ],
        compiler_params=PARAMS,
        cost_estimate=cost(10**9, 8 * 10**6),
        name="query_grad",
    )(key_blocks, host_ids, host_bias, query_states, up, stats, *k_win, *v_win)

    grad_key, grad_value = pl.pallas_call(
        functools.partial(key_kernel, size, nsh),
        out_shape=[jax.ShapeDtypeStruct((rows, columns), bf16)] * 2,
        in_specs=[SMEM] * 3 + [VMEM] * 2 + [ANY] * (2 * nsh),
        out_specs=[VMEM] * 2,
        scratch_shapes=[
            pltpu.VMEM((nsh * rows, columns), bf16),
            pltpu.VMEM((nsh * long_rows, columns), bf16),
            pltpu.VMEM((nsh, high, BLK), f32),
            pltpu.VMEM((rows, columns), f32),
            pltpu.VMEM((rows, columns), f32),
            pltpu.SemaphoreType.DMA((2 * nsh,)),
        ],
        compiler_params=PARAMS,
        cost_estimate=cost(10**9, 8 * 10**6),
        name="key_grad",
    )(all_keys, host_ids, host_bias, key_states, value_states, *q_win, *up_win)

    for piece in arrived:
        mixed = mixed + piece.astype(f32)
    return (mixed.astype(bf16), grad_query, grad_key, grad_value)


def solution(mesh):
    in_specs = (
        P("ctx", "head"),
        P("ctx", "head"),
        P("ctx", "head"),
        P("head", None),
        P(("ctx", "head"), None),
        P("ctx", None),
        P(),
        P("head"),
    )
    out_specs = (P(("ctx", "head"), None), P("ctx", "head"), P("ctx", "head"), P("ctx", "head"))
    return jax.shard_map(
        per_device, mesh=mesh, in_specs=in_specs, out_specs=out_specs, check_vma=False
    )
```

time: 176 us -> 106 us (0.60)
  local copies, waits for them, and re-layouts: 55.4 us -> 4.86 us
  Pallas kernels: 0 us -> 23.6 us
  waiting for transfers between devices: 61.3 us -> 38.3 us
  other arithmetic: 23.5 us -> 0.84 us
  starting transfers between devices: 7.45 us -> 27.7 us
  between operations: 14.2 us -> 0.73 us
  matrix products: 12.9 us -> 0 us
  blocking collectives: 0 us -> 8.85 us
    pallas_call x0 -> x4, Pallas kernels: none -> 23.6 us  [the longest x1 8.52 us: per_device(): pl.pallas_call(functools.partial(key_kernel, size, nsh), out_shape=[jax.S...]
    ppermute x8 -> x26, waiting for transfers between devices: 61.3 us -> 38.3 us  [the longest x20 26.2 us: move(): return lax.ppermute(v, 'ctx', pairs)]
    ppermute x8 -> x26, starting transfers between devices: 7.37 us -> 27.7 us  [the longest x20 14.2 us: move(): return lax.ppermute(v, 'ctx', pairs)]
    reshape x7 -> x0, local copies, waits for them, and re-layouts: 19.2 us -> none  [the longest x2 8.85 us: per_device(): window = window.reshape(2, span * blocks_dev, BLK, heads_dev, HDIM)]
    dot_general x7 -> x0, matrix products: 10.4 us -> none  [the longest x1 2.68 us: per_device(): lax.dot_general(lax.all_gather(grad_mixed, 'head', axis=0, tiled=True), o...]
    scatter-add x1 -> x0, other arithmetic: 9.46 us -> none  [per_device(): window_grad = jnp.zeros((2, span * blocks_dev, BLK, heads_dev, HDIM), jnp...]
    all_gather x0 -> x1, blocking collectives: none -> 8.85 us  [per_device(): all_keys = lax.all_gather(key_blocks, 'ctx', axis=0, tiled=True)]
    scatter-add x1 -> x0, local copies, waits for them, and re-layouts: 8.72 us -> none  [per_device(): window_grad = jnp.zeros((2, span * blocks_dev, BLK, heads_dev, HDIM), jnp...]
  transfers between devices with their start and end apart: 10 -> 26, of which waited for: 4 -> 10; matrix products, arithmetic and copies ran while one was open for 50% -> 1% of each run, Pallas kernels for 0% -> 12%
where the time goes in v1:
time: 106 us; the launch traced here: 105 us
  waiting for transfers between devices  38.3 us (36%)
  starting transfers between devices  27.7 us (26%)
  Pallas kernels  23.6 us (22%)
  blocking collectives  8.85 us (8%)
  local copies, waits for them, and re-layouts  4.86 us (5%)
    ppermute x20, waiting for transfers between devices, move(): return lax.ppermute(v, 'ctx', pairs)  26.2 us
    ppermute x20, starting transfers between devices, move(): return lax.ppermute(v, 'ctx', pairs)  14.2 us
    ppermute x6, starting transfers between devices, ring(): lax.ppermute(x, 'head', [(i, (i + step) % groups) for i in range(groups)])  13.4 us
    ppermute x6, waiting for transfers between devices, ring(): lax.ppermute(x, 'head', [(i, (i + step) % groups) for i in range(groups)])  12.1 us
    all_gather x1, blocking collectives, per_device(): all_keys = lax.all_gather(key_blocks, 'ctx', axis=0, tiled=True)  8.85 us
    pallas_call x1, Pallas kernels, per_device(): pl.pallas_call(functools.partial(key_kernel, size, nsh), out_shape=[jax.S...  8.52 us
    pallas_call x1, Pallas kernels, per_device(): pl.pallas_call(functools.partial(attend_kernel, size, groups, nsh), out_s...  7 us
    pallas_call x1, Pallas kernels, per_device(): pl.pallas_call(functools.partial(query_kernel, size, nsh), out_shape=jax....  5.13 us
  transfers between devices with their start and end apart: 26, of which 10 were waited for; matrix products, arithmetic and copies ran while one was open for 1% of the time, Pallas kernels for 12%

profile of v1, /device:TPU:0, one launch (start us, length us, event | category | flops | bytes accessed | tf_op | source)
XLA Modules:
  0.0 104.8 jit_solution(18323427651327513313)
XLA Ops:
  0.6 3.0 %collective-permute-start.1 = (bf16[256,512]{1,0:T(8,128)(2,1)}, bf16[256,512]{1,0:T(8,128)(2,1)S(1)}, u32[]{:S(2)}, u32[]{:S(2)}) collective-permute-start(bf16[256,512]{1,0:T(8,128)(2,1)} %refs_3_.7), channel_id=1, source_target_pairs={{0,8},{4,12},{8,0},{12,4},{16,24},{20,28},{24,16},{28,20},{1,9},{5... | collective-permute-start | bytes 786440 | tf_op jit(solution)/shard_map/ppermute | solution.py:51
  3.6 0.1 collective-permute-start.6
  3.7 0.0 collective-permute-start
  3.7 7.3 %collective-permute-done.1.refs_7_.refs_8_ = bf16[256,512]{1,0:T(8,128)(2,1)S(1)} collective-permute-done((bf16[256,512]{1,0:T(8,128)(2,1)}, bf16[256,512]{1,0:T(8,128)(2,1)S(1)}, u32[]{:S(2)}, u32[]{:S(2)}) %collective-permute-start.1) | collective-permute-done | bytes 262176 | tf_op jit(solution)/shard_map/ppermute | solution.py:51
  11.0 2.1 %collective-permute-start.3 = (bf16[256,512]{1,0:T(8,128)(2,1)S(1)}, bf16[256,512]{1,0:T(8,128)(2,1)S(1)}, u32[]{:S(2)}, u32[]{:S(2)}) collective-permute-start(bf16[256,512]{1,0:T(8,128)(2,1)S(1)} %collective-permute-done.1.refs_7_.refs_8_), channel_id=1, source_target_pairs={{0,16},{4,20},{8,24},{12,28},{16,0},{20,4},{24,8},{28,12},{1,17},{... | collective-permute-start | bytes 786440 | tf_op jit(solution)/shard_map/ppermute | solution.py:51
  13.1 2.7 %collective-permute-done.6.refs_13_.refs_14_ = bf16[256,512]{1,0:T(8,128)(2,1)S(1)} collective-permute-done((bf16[256,512]{1,0:T(8,128)(2,1)}, bf16[256,512]{1,0:T(8,128)(2,1)S(1)}, u32[]{:S(2)}, u32[]{:S(2)}) %collective-permute-start.6) | collective-permute-done | bytes 262176 | tf_op jit(solution)/shard_map/ppermute | solution.py:51
  15.8 1.8 %collective-permute-start.8 = (bf16[256,512]{1,0:T(8,128)(2,1)S(1)}, bf16[256,512]{1,0:T(8,128)(2,1)S(1)}, u32[]{:S(2)}, u32[]{:S(2)}) collective-permute-start(bf16[256,512]{1,0:T(8,128)(2,1)S(1)} %collective-permute-done.6.refs_13_.refs_14_), channel_id=1, source_target_pairs={{0,16},{4,20},{8,24},{12,28},{16,0},{20,4},{24,8},{28,12},{1,17},{... | collective-permute-start | bytes 786440 | tf_op jit(solution)/shard_map/ppermute | solution.py:51
  17.5 0.0 collective-permute-start.5
  17.6 0.5 collective-permute-start.2
  18.1 0.0 collective-permute-start.7
  18.1 0.0 collective-permute-done.3.refs_9_.refs_10_
  18.1 0.5 collective-permute-start.4
  18.6 4.7 %collective-permute-done.8.refs_15_.refs_16_ = bf16[256,512]{1,0:T(8,128)(2,1)S(1)} collective-permute-done((bf16[256,512]{1,0:T(8,128)(2,1)S(1)}, bf16[256,512]{1,0:T(8,128)(2,1)S(1)}, u32[]{:S(2)}, u32[]{:S(2)}) %collective-permute-start.8) | collective-permute-done | bytes 262176 | tf_op jit(solution)/shard_map/ppermute | solution.py:51
  23.3 0.0 collective-permute-start.9
  23.3 0.0 collective-permute-done.5.refs_12_.refs_13_
  23.3 1.9 %collective-permute-start.13 = (bf16[64,2048]{1,0:T(8,128)(2,1)}, bf16[64,2048]{1,0:T(8,128)(2,1)S(1)}, u32[]{:S(2)}, u32[]{:S(2)}) collective-permute-start(bf16[64,2048]{1,0:T(8,128)(2,1)} %refs_3_.5), channel_id=1, source_target_pairs={{0,1},{1,2},{2,3},{3,0},{4,5},{5,6},{6,7},{7,4},{8,9},{9,10},{10,1... | collective-permute-start | bytes 786440 | tf_op jit(solution)/shard_map/ppermute | solution.py:296
  25.1 2.6 %collective-permute-start.14 = (bf16[64,2048]{1,0:T(8,128)(2,1)}, bf16[64,2048]{1,0:T(8,128)(2,1)S(1)}, u32[]{:S(2)}, u32[]{:S(2)}) collective-permute-start(bf16[64,2048]{1,0:T(8,128)(2,1)} %refs_3_.5), channel_id=1, source_target_pairs={{0,2},{1,3},{2,0},{3,1},{4,6},{5,7},{6,4},{7,5},{8,10},{9,11},{10,... | collective-permute-start | bytes 786440 | tf_op jit(solution)/shard_map/ppermute | solution.py:296
  27.7 1.3 %collective-permute-start.15 = (bf16[64,2048]{1,0:T(8,128)(2,1)}, bf16[64,2048]{1,0:T(8,128)(2,1)S(1)}, u32[]{:S(2)}, u32[]{:S(2)}) collective-permute-start(bf16[64,2048]{1,0:T(8,128)(2,1)} %refs_3_.5), channel_id=1, source_target_pairs={{0,3},{1,0},{2,1},{3,2},{4,7},{5,4},{6,5},{7,6},{8,11},{9,8},{10,9... | collective-permute-start | bytes 786440 | tf_op jit(solution)/shard_map/ppermute | solution.py:296
  29.1 0.9 copy-done.1
  30.0 0.9 copy-done.3
  31.0 0.9 copy-done.5
  31.9 0.7 copy-done.8
  32.6 0.7 copy-done.9
  33.3 0.7 copy-done.11
  33.9 7.0 %attend.1 = (bf16[64,2048]{1,0:T(8,128)(2,1)S(1)}, bf16[64,2048]{1,0:T(8,128)(2,1)S(1)}, bf16[64,2048]{1,0:T(8,128)(2,1)S(1)}, bf16[64,2048]{1,0:T(8,128)(2,1)S(...) custom-call(s32[2,4]{1,0:T(2,128)S(1)} %copy-done.8, s32[16]{0:T(128)S(1)} %copy-done.9, f32[4]{0:T(128)S(1)} %copy-done.11, ...), custom_call_target="tpu_custom_call" | custom-call | flops 1000000000 | bytes 8000000 | tf_op jit(solution)/shard_map/attend/pallas_call | solution.py:304
  40.9 0.0 copy-start.6
  41.0 4.7 %collective-permute-done.14.refs_5_ = bf16[64,2048]{1,0:T(8,128)(2,1)S(1)} collective-permute-done((bf16[64,2048]{1,0:T(8,128)(2,1)}, bf16[64,2048]{1,0:T(8,128)(2,1)S(1)}, u32[]{:S(2)}, u32[]{:S(2)}) %collective-permute-start.14) | collective-permute-done | bytes 262176 | tf_op jit(solution)/shard_map/ppermute | solution.py:296
  45.7 2.9 %upstream.1 = (bf16[272,512]{1,0:T(8,128)(2,1)S(1)}, f32[128,128]{1,0:T(8,128)S(1)}) custom-call(bf16[512,2048]{1,0:T(8,128)(2,1)S(1)} %copy-done, f32[256,512]{1,0:T(8,128)S(1)} %get-tuple-element.18.refs_1_, f32[128,128]{1,0:T(8,128)S(1)} %get-tuple-element.19.refs_2_, bf16[64,2048]{1,0:T(8,128)(2,1)S(1)} %copy-done.7, ...), custom_call_target="tpu_custom_call" | custom-call | flops 600000000 | bytes 4000000 | tf_op jit(solution)/shard_map/upstream/pallas_call | solution.py:325
  48.6 1.5 %collective-permute-start.22 = (bf16[272,512]{1,0:T(8,128)(2,1)S(1)}, bf16[272,512]{1,0:T(8,128)(2,1)S(1)}, u32[]{:S(2)}, u32[]{:S(2)}) collective-permute-start(bf16[272,512]{1,0:T(8,128)(2,1)S(1)} %get-tuple-element.20.refs_4_.refs_11_), channel_id=1, source_target_pairs={{0,8},{4,12},{8,0},{12,4},{16,24},{20,28},{24,16},{28,20},{1,9},{5... | collective-permute-start | bytes 835592 | tf_op jit(solution)/shard_map/ppermute | solution.py:51
  50.1 0.5 collective-permute-start.17
  50.7 7.5 %collective-permute-done.22.refs_13_ = bf16[272,512]{1,0:T(8,128)(2,1)S(1)} collective-permute-done((bf16[272,512]{1,0:T(8,128)(2,1)S(1)}, bf16[272,512]{1,0:T(8,128)(2,1)S(1)}, u32[]{:S(2)}, u32[]{:S(2)}) %collective-permute-start.22) | collective-permute-done | bytes 278560 | tf_op jit(solution)/shard_map/ppermute | solution.py:51
  58.2 1.5 %collective-permute-start.24 = (bf16[272,512]{1,0:T(8,128)(2,1)S(1)}, bf16[272,512]{1,0:T(8,128)(2,1)S(1)}, u32[]{:S(2)}, u32[]{:S(2)}) collective-permute-start(bf16[272,512]{1,0:T(8,128)(2,1)S(1)} %collective-permute-done.22.refs_13_), channel_id=1, source_target_pairs={{0,16},{4,20},{8,24},{12,28},{16,0},{20,4},{24,8},{28,12},{1,17},{... | collective-permute-start | bytes 835592 | tf_op jit(solution)/shard_map/ppermute | solution.py:51
  59.7 3.1 %collective-permute-done.17.refs_7_ = bf16[256,512]{1,0:T(8,128)(2,1)S(1)} collective-permute-done((bf16[256,512]{1,0:T(8,128)(2,1)S(1)}, bf16[256,512]{1,0:T(8,128)(2,1)S(1)}, u32[]{:S(2)}, u32[]{:S(2)}) %collective-permute-start.17) | collective-permute-done | bytes 262176 | tf_op jit(solution)/shard_map/ppermute | solution.py:51
  62.8 1.5 %collective-permute-start.19 = (bf16[256,512]{1,0:T(8,128)(2,1)S(1)}, bf16[256,512]{1,0:T(8,128)(2,1)S(1)}, u32[]{:S(2)}, u32[]{:S(2)}) collective-permute-start(bf16[256,512]{1,0:T(8,128)(2,1)S(1)} %collective-permute-done.17.refs_7_), channel_id=1, source_target_pairs={{0,16},{4,20},{8,24},{12,28},{16,0},{20,4},{24,8},{28,12},{1,17},{... | collective-permute-start | bytes 786440 | tf_op jit(solution)/shard_map/ppermute | solution.py:51
  64.3 6.9 %collective-permute-start.12 = (bf16[64,2048]{1,0:T(8,128)(2,1)S(1)}, bf16[64,2048]{1,0:T(8,128)(2,1)S(1)}, u32[]{:S(2)}, u32[]{:S(2)}) collective-permute-start(bf16[64,2048]{1,0:T(8,128)(2,1)S(1)} %get-tuple-element.17), channel_id=1, source_target_pairs={{0,3},{1,0},{2,1},{3,2},{4,7},{5,4},{6,5},{7,6},{8,11},{9,8},{10,9... | collective-permute-start | bytes 786440 | tf_op jit(solution)/shard_map/ppermute | solution.py:296
  71.2 0.7 collective-permute-start.11
  72.0 8.9 %all-gather = s32[8,2,4]{2,1,0:T(2,128)S(1)} all-gather(s32[1,2,4]{2,1,0:T(2,128)S(1)} %bitcast.3), channel_id=1, replica_groups=mesh['ctx'=8,'head'=4] {'ctx'}, dimensions={0}, use_global_device_ids=true | all-gather | bytes 288 | tf_op jit(solution)/shard_map/all_gather | solution.py:298
  80.8 5.1 %query_grad.1 = bf16[256,512]{1,0:T(8,128)(2,1)} custom-call(s32[2,4]{1,0:T(2,128)S(1)} %copy-done.8, s32[16]{0:T(128)S(1)} %copy-done.9, f32[4]{0:T(128)S(1)} %copy-done.11, bf16[256,512]{1,0:T(8,128)(2,1)S(1)} %copy-done.1, bf16[272,512]{1,0:T(8,128)(2,1)S(1)} %get-tuple-element.20.refs_4_.refs_11_, f32[128,128]{1,0:T(8,128)S(1)} %get-tuple-element.21.refs_5_, ...), custom_call_target="tpu_custom_call" | custom-call | flops 1000000000 | bytes 8000000 | tf_op jit(solution)/shard_map/query_grad/pallas_call | solution.py:339
  86.0 0.4 collective-permute-start.18
  86.4 0.2 collective-permute-start.20
  86.6 7.4 %collective-permute-done.11 = bf16[64,2048]{1,0:T(8,128)(2,1)S(1)} collective-permute-done((bf16[64,2048]{1,0:T(8,128)(2,1)S(1)}, bf16[64,2048]{1,0:T(8,128)(2,1)S(1)}, u32[]{:S(2)}, u32[]{:S(2)}) %collective-permute-start.11) | collective-permute-done | bytes 262176 | tf_op jit(solution)/shard_map/ppermute | solution.py:296
  93.9 0.5 collective-permute-start.23
  94.4 0.1 collective-permute-start.25
  94.5 0.8 add_convert_fusion
  95.4 0.1 collective-permute-done.21.refs_12_
  95.5 0.4 collective-permute-done.23.refs_14_
  95.9 0.4 collective-permute-done.25.refs_16_
  96.3 8.5 %key_grad.1 = (bf16[256,512]{1,0:T(8,128)(2,1)}, bf16[256,512]{1,0:T(8,128)(2,1)}) custom-call(s32[16,4]{1,0:T(8,128)S(1)} %bitcast.2, s32[16]{0:T(128)S(1)} %copy-done.10, f32[4]{0:T(128)S(1)} %copy-done.11, bf16[256,512]{1,0:T(8,128)(2,1)S(1)} %copy-done.4, bf16[256,512]{1,0:T(8,128)(2,1)S(1)} %copy-done.6, bf16[256,512]{1,0:T(8,128)(2,1)S(1)} %copy-done.2, ...), custom_call_target="tpu_custom_call" | custom-call | flops 1000000000 | bytes 8000000 | tf_op jit(solution)/shard_map/key_grad/pallas_call | solution.py:354
  (34 shorter events, 0.1 us)
Async XLA Ops:
  0.6 45.1 %copy-start = (bf16[512,2048]{1,0:T(8,128)(2,1)S(1)}, bf16[512,2048]{1,0:T(8,128)(2,1)}, u32[]{:S(2)}) copy-start(bf16[512,2048]{1,0:T(8,128)(2,1)} %refs_0_.4) | copy-start | bytes 6291460
  0.6 10.4 %collective-permute-start.1 = (bf16[256,512]{1,0:T(8,128)(2,1)}, bf16[256,512]{1,0:T(8,128)(2,1)S(1)}, u32[]{:S(2)}, u32[]{:S(2)}) collective-permute-start(bf16[256,512]{1,0:T(8,128)(2,1)} %refs_3_.7), channel_id=1, source_target_pairs={{0,8},{4,12},{8,0},{12,4},{16,24},{20,28},{24,16},{28,20},{1,9},{5... | collective-permute-start | bytes 786440 | tf_op jit(solution)/shard_map/ppermute | solution.py:51
  3.6 12.1 %collective-permute-start.6 = (bf16[256,512]{1,0:T(8,128)(2,1)}, bf16[256,512]{1,0:T(8,128)(2,1)S(1)}, u32[]{:S(2)}, u32[]{:S(2)}) collective-permute-start(bf16[256,512]{1,0:T(8,128)(2,1)} %refs_4_.3), channel_id=1, source_target_pairs={{0,8},{4,12},{8,0},{12,4},{16,24},{20,28},{24,16},{28,20},{1,9},{5... | collective-permute-start | bytes 786440 | tf_op jit(solution)/shard_map/ppermute | solution.py:51
  3.7 14.3 %collective-permute-start = (bf16[256,512]{1,0:T(8,128)(2,1)}, bf16[256,512]{1,0:T(8,128)(2,1)S(1)}, u32[]{:S(2)}, u32[]{:S(2)}) collective-permute-start(bf16[256,512]{1,0:T(8,128)(2,1)} %refs_3_.7), channel_id=1, source_target_pairs={{0,4},{4,0},{8,12},{12,8},{16,20},{20,16},{24,28},{28,24},{1,5},{5... | collective-permute-start | bytes 786440 | tf_op jit(solution)/shard_map/ppermute | solution.py:51
  11.0 7.1 %collective-permute-start.3 = (bf16[256,512]{1,0:T(8,128)(2,1)S(1)}, bf16[256,512]{1,0:T(8,128)(2,1)S(1)}, u32[]{:S(2)}, u32[]{:S(2)}) collective-permute-start(bf16[256,512]{1,0:T(8,128)(2,1)S(1)} %collective-permute-done.1.refs_7_.refs_8_), channel_id=1, source_target_pairs={{0,16},{4,20},{8,24},{12,28},{16,0},{20,4},{24,8},{28,12},{1,17},{... | collective-permute-start | bytes 786440 | tf_op jit(solution)/shard_map/ppermute | solution.py:51
  15.8 7.5 %collective-permute-start.8 = (bf16[256,512]{1,0:T(8,128)(2,1)S(1)}, bf16[256,512]{1,0:T(8,128)(2,1)S(1)}, u32[]{:S(2)}, u32[]{:S(2)}) collective-permute-start(bf16[256,512]{1,0:T(8,128)(2,1)S(1)} %collective-permute-done.6.refs_13_.refs_14_), channel_id=1, source_target_pairs={{0,16},{4,20},{8,24},{12,28},{16,0},{20,4},{24,8},{28,12},{1,17},{... | collective-permute-start | bytes 786440 | tf_op jit(solution)/shard_map/ppermute | solution.py:51
  17.5 5.7 %collective-permute-start.5 = (bf16[256,512]{1,0:T(8,128)(2,1)}, bf16[256,512]{1,0:T(8,128)(2,1)S(1)}, u32[]{:S(2)}, u32[]{:S(2)}) collective-permute-start(bf16[256,512]{1,0:T(8,128)(2,1)} %refs_4_.3), channel_id=1, source_target_pairs={{0,4},{4,0},{8,12},{12,8},{16,20},{20,16},{24,28},{28,24},{1,5},{5... | collective-permute-start | bytes 786440 | tf_op jit(solution)/shard_map/ppermute | solution.py:51
  17.6 7.6 %collective-permute-start.2 = (bf16[256,512]{1,0:T(8,128)(2,1)S(1)}, bf16[256,512]{1,0:T(8,128)(2,1)S(1)}, u32[]{:S(2)}, u32[]{:S(2)}) collective-permute-start(bf16[256,512]{1,0:T(8,128)(2,1)S(1)} %collective-permute-done.1.refs_7_.refs_8_), channel_id=1, source_target_pairs={{0,4},{4,0},{8,12},{12,8},{16,20},{20,16},{24,28},{28,24},{1,5},{5... | collective-permute-start | bytes 786440 | tf_op jit(solution)/shard_map/ppermute | solution.py:51
  18.1 9.7 %collective-permute-start.7 = (bf16[256,512]{1,0:T(8,128)(2,1)S(1)}, bf16[256,512]{1,0:T(8,128)(2,1)S(1)}, u32[]{:S(2)}, u32[]{:S(2)}) collective-permute-start(bf16[256,512]{1,0:T(8,128)(2,1)S(1)} %collective-permute-done.6.refs_13_.refs_14_), channel_id=1, source_target_pairs={{0,4},{4,0},{8,12},{12,8},{16,20},{20,16},{24,28},{28,24},{1,5},{5... | collective-permute-start | bytes 786440 | tf_op jit(solution)/shard_map/ppermute | solution.py:51
  18.1 11.0 %collective-permute-start.4 = (bf16[256,512]{1,0:T(8,128)(2,1)S(1)}, bf16[256,512]{1,0:T(8,128)(2,1)S(1)}, u32[]{:S(2)}, u32[]{:S(2)}) collective-permute-start(bf16[256,512]{1,0:T(8,128)(2,1)S(1)} %collective-permute-done.3.refs_9_.refs_10_), channel_id=1, source_target_pairs={{0,4},{4,0},{8,12},{12,8},{16,20},{20,16},{24,28},{28,24},{1,5},{5... | collective-permute-start | bytes 786440 | tf_op jit(solution)/shard_map/ppermute | solution.py:51
  23.3 5.8 %collective-permute-start.9 = (bf16[256,512]{1,0:T(8,128)(2,1)S(1)}, bf16[256,512]{1,0:T(8,128)(2,1)S(1)}, u32[]{:S(2)}, u32[]{:S(2)}) collective-permute-start(bf16[256,512]{1,0:T(8,128)(2,1)S(1)} %collective-permute-done.8.refs_15_.refs_16_), channel_id=1, source_target_pairs={{0,4},{4,0},{8,12},{12,8},{16,20},{20,16},{24,28},{28,24},{1,5},{5... | collective-permute-start | bytes 786440 | tf_op jit(solution)/shard_map/ppermute | solution.py:51
  23.3 17.7 %collective-permute-start.13 = (bf16[64,2048]{1,0:T(8,128)(2,1)}, bf16[64,2048]{1,0:T(8,128)(2,1)S(1)}, u32[]{:S(2)}, u32[]{:S(2)}) collective-permute-start(bf16[64,2048]{1,0:T(8,128)(2,1)} %refs_3_.5), channel_id=1, source_target_pairs={{0,1},{1,2},{2,3},{3,0},{4,5},{5,6},{6,7},{7,4},{8,9},{9,10},{10,1... | collective-permute-start | bytes 786440 | tf_op jit(solution)/shard_map/ppermute | solution.py:296
  25.1 20.6 %collective-permute-start.14 = (bf16[64,2048]{1,0:T(8,128)(2,1)}, bf16[64,2048]{1,0:T(8,128)(2,1)S(1)}, u32[]{:S(2)}, u32[]{:S(2)}) collective-permute-start(bf16[64,2048]{1,0:T(8,128)(2,1)} %refs_3_.5), channel_id=1, source_target_pairs={{0,2},{1,3},{2,0},{3,1},{4,6},{5,7},{6,4},{7,5},{8,10},{9,11},{10,... | collective-permute-start | bytes 786440 | tf_op jit(solution)/shard_map/ppermute | solution.py:296
  27.7 18.0 %collective-permute-start.15 = (bf16[64,2048]{1,0:T(8,128)(2,1)}, bf16[64,2048]{1,0:T(8,128)(2,1)S(1)}, u32[]{:S(2)}, u32[]{:S(2)}) collective-permute-start(bf16[64,2048]{1,0:T(8,128)(2,1)} %refs_3_.5), channel_id=1, source_target_pairs={{0,3},{1,0},{2,1},{3,2},{4,7},{5,4},{6,5},{7,6},{8,11},{9,8},{10,9... | collective-permute-start | bytes 786440 | tf_op jit(solution)/shard_map/ppermute | solution.py:296
  29.1 1.0 copy-start.1
  30.0 0.9 copy-start.3
  31.0 0.9 copy-start.5
  31.9 0.7 copy-start.8
  32.6 0.7 copy-start.9
  33.3 0.7 copy-start.11
  33.9 11.8 %copy-start.7 = (bf16[64,2048]{1,0:T(8,128)(2,1)S(1)}, bf16[64,2048]{1,0:T(8,128)(2,1)}, u32[]{:S(2)}) copy-start(bf16[64,2048]{1,0:T(8,128)(2,1)} %refs_3_.5) | copy-start | bytes 786436
  40.9 39.9 %copy-start.6 = (bf16[256,512]{1,0:T(8,128)(2,1)S(1)}, bf16[256,512]{1,0:T(8,128)(2,1)}, u32[]{:S(2)}) copy-start(bf16[256,512]{1,0:T(8,128)(2,1)} %refs_4_.3) | copy-start | bytes 786436
  48.6 9.6 %collective-permute-start.22 = (bf16[272,512]{1,0:T(8,128)(2,1)S(1)}, bf16[272,512]{1,0:T(8,128)(2,1)S(1)}, u32[]{:S(2)}, u32[]{:S(2)}) collective-permute-start(bf16[272,512]{1,0:T(8,128)(2,1)S(1)} %get-tuple-element.20.refs_4_.refs_11_), channel_id=1, source_target_pairs={{0,8},{4,12},{8,0},{12,4},{16,24},{20,28},{24,16},{28,20},{1,9},{5... | collective-permute-start | bytes 835592 | tf_op jit(solution)/shard_map/ppermute | solution.py:51
  50.1 12.7 %collective-permute-start.17 = (bf16[256,512]{1,0:T(8,128)(2,1)S(1)}, bf16[256,512]{1,0:T(8,128)(2,1)S(1)}, u32[]{:S(2)}, u32[]{:S(2)}) collective-permute-start(bf16[256,512]{1,0:T(8,128)(2,1)S(1)} %copy-done.1), channel_id=1, source_target_pairs={{0,8},{4,12},{8,0},{12,4},{16,24},{20,28},{24,16},{28,20},{1,9},{5... | collective-permute-start | bytes 786440 | tf_op jit(solution)/shard_map/ppermute | solution.py:51
  50.7 21.3 %collective-permute-start.16 = (bf16[256,512]{1,0:T(8,128)(2,1)S(1)}, bf16[256,512]{1,0:T(8,128)(2,1)S(1)}, u32[]{:S(2)}, u32[]{:S(2)}) collective-permute-start(bf16[256,512]{1,0:T(8,128)(2,1)S(1)} %copy-done.1), channel_id=1, source_target_pairs={{0,4},{4,0},{8,12},{12,8},{16,20},{20,16},{24,28},{28,24},{1,5},{5... | collective-permute-start | bytes 786440 | tf_op jit(solution)/shard_map/ppermute | solution.py:51
  58.2 36.3 %collective-permute-start.24 = (bf16[272,512]{1,0:T(8,128)(2,1)S(1)}, bf16[272,512]{1,0:T(8,128)(2,1)S(1)}, u32[]{:S(2)}, u32[]{:S(2)}) collective-permute-start(bf16[272,512]{1,0:T(8,128)(2,1)S(1)} %collective-permute-done.22.refs_13_), channel_id=1, source_target_pairs={{0,16},{4,20},{8,24},{12,28},{16,0},{20,4},{24,8},{28,12},{1,17},{... | collective-permute-start | bytes 835592 | tf_op jit(solution)/shard_map/ppermute | solution.py:51
  62.8 23.2 %collective-permute-start.19 = (bf16[256,512]{1,0:T(8,128)(2,1)S(1)}, bf16[256,512]{1,0:T(8,128)(2,1)S(1)}, u32[]{:S(2)}, u32[]{:S(2)}) collective-permute-start(bf16[256,512]{1,0:T(8,128)(2,1)S(1)} %collective-permute-done.17.refs_7_), channel_id=1, source_target_pairs={{0,16},{4,20},{8,24},{12,28},{16,0},{20,4},{24,8},{28,12},{1,17},{... | collective-permute-start | bytes 786440 | tf_op jit(solution)/shard_map/ppermute | solution.py:51
  64.3 22.1 %collective-permute-start.12 = (bf16[64,2048]{1,0:T(8,128)(2,1)S(1)}, bf16[64,2048]{1,0:T(8,128)(2,1)S(1)}, u32[]{:S(2)}, u32[]{:S(2)}) collective-permute-start(bf16[64,2048]{1,0:T(8,128)(2,1)S(1)} %get-tuple-element.17), channel_id=1, source_target_pairs={{0,3},{1,0},{2,1},{3,2},{4,7},{5,4},{6,5},{7,6},{8,11},{9,8},{10,9... | collective-permute-start | bytes 786440 | tf_op jit(solution)/shard_map/ppermute | solution.py:296
  71.2 22.7 %collective-permute-start.11 = (bf16[64,2048]{1,0:T(8,128)(2,1)S(1)}, bf16[64,2048]{1,0:T(8,128)(2,1)S(1)}, u32[]{:S(2)}, u32[]{:S(2)}) collective-permute-start(bf16[64,2048]{1,0:T(8,128)(2,1)S(1)} %get-tuple-element.16), channel_id=1, source_target_pairs={{0,2},{1,3},{2,0},{3,1},{4,6},{5,7},{6,4},{7,5},{8,10},{9,11},{10,... | collective-permute-start | bytes 786440 | tf_op jit(solution)/shard_map/ppermute | solution.py:296
  72.0 22.0 %collective-permute-start.10 = (bf16[64,2048]{1,0:T(8,128)(2,1)S(1)}, bf16[64,2048]{1,0:T(8,128)(2,1)S(1)}, u32[]{:S(2)}, u32[]{:S(2)}) collective-permute-start(bf16[64,2048]{1,0:T(8,128)(2,1)S(1)} %get-tuple-element.15), channel_id=1, source_target_pairs={{0,1},{1,2},{2,3},{3,0},{4,5},{5,6},{6,7},{7,4},{8,9},{9,10},{10,1... | collective-permute-start | bytes 786440 | tf_op jit(solution)/shard_map/ppermute | solution.py:296
  80.8 15.4 %copy-start.2 = (bf16[256,512]{1,0:T(8,128)(2,1)S(1)}, bf16[256,512]{1,0:T(8,128)(2,1)}, u32[]{:S(2)}) copy-start(bf16[256,512]{1,0:T(8,128)(2,1)} %refs_5_.3) | copy-start | bytes 786436
  80.8 15.4 %copy-start.4 = (bf16[256,512]{1,0:T(8,128)(2,1)S(1)}, bf16[256,512]{1,0:T(8,128)(2,1)}, u32[]{:S(2)}) copy-start(bf16[256,512]{1,0:T(8,128)(2,1)} %refs_3_.7) | copy-start | bytes 786436
  80.8 15.4 %copy-start.10 = (s32[16]{0:T(128)S(1)}, s32[16]{0:T(128)}, u32[]{:S(2)}) copy-start(s32[16]{0:T(128)} %refs_1_.5) | copy-start | bytes 196
  86.0 9.4 %collective-permute-start.18 = (bf16[256,512]{1,0:T(8,128)(2,1)S(1)}, bf16[256,512]{1,0:T(8,128)(2,1)S(1)}, u32[]{:S(2)}, u32[]{:S(2)}) collective-permute-start(bf16[256,512]{1,0:T(8,128)(2,1)S(1)} %collective-permute-done.17.refs_7_), channel_id=1, source_target_pairs={{0,4},{4,0},{8,12},{12,8},{16,20},{20,16},{24,28},{28,24},{1,5},{5... | collective-permute-start | bytes 786440 | tf_op jit(solution)/shard_map/ppermute | solution.py:51
  86.4 9.0 %collective-permute-start.20 = (bf16[256,512]{1,0:T(8,128)(2,1)S(1)}, bf16[256,512]{1,0:T(8,128)(2,1)S(1)}, u32[]{:S(2)}, u32[]{:S(2)}) collective-permute-start(bf16[256,512]{1,0:T(8,128)(2,1)S(1)} %collective-permute-done.19.refs_9_), channel_id=1, source_target_pairs={{0,4},{4,0},{8,12},{12,8},{16,20},{20,16},{24,28},{28,24},{1,5},{5... | collective-permute-start | bytes 786440 | tf_op jit(solution)/shard_map/ppermute | solution.py:51
  93.9 1.6 %collective-permute-start.21 = (bf16[272,512]{1,0:T(8,128)(2,1)S(1)}, bf16[272,512]{1,0:T(8,128)(2,1)S(1)}, u32[]{:S(2)}, u32[]{:S(2)}) collective-permute-start(bf16[272,512]{1,0:T(8,128)(2,1)S(1)} %get-tuple-element.20.refs_4_.refs_11_), channel_id=1, source_target_pairs={{0,4},{4,0},{8,12},{12,8},{16,20},{20,16},{24,28},{28,24},{1,5},{5... | collective-permute-start | bytes 835592 | tf_op jit(solution)/shard_map/ppermute | solution.py:51
  93.9 2.0 %collective-permute-start.23 = (bf16[272,512]{1,0:T(8,128)(2,1)S(1)}, bf16[272,512]{1,0:T(8,128)(2,1)S(1)}, u32[]{:S(2)}, u32[]{:S(2)}) collective-permute-start(bf16[272,512]{1,0:T(8,128)(2,1)S(1)} %collective-permute-done.22.refs_13_), channel_id=1, source_target_pairs={{0,4},{4,0},{8,12},{12,8},{16,20},{20,16},{24,28},{28,24},{1,5},{5... | collective-permute-start | bytes 835592 | tf_op jit(solution)/shard_map/ppermute | solution.py:51
  94.4 1.8 %collective-permute-start.25 = (bf16[272,512]{1,0:T(8,128)(2,1)S(1)}, bf16[272,512]{1,0:T(8,128)(2,1)S(1)}, u32[]{:S(2)}, u32[]{:S(2)}) collective-permute-start(bf16[272,512]{1,0:T(8,128)(2,1)S(1)} %collective-permute-done.24.refs_15_), channel_id=1, source_target_pairs={{0,4},{4,0},{8,12},{12,8},{16,20},{20,16},{24,28},{28,24},{1,5},{5... | collective-permute-start | bytes 835592 | tf_op jit(solution)/shard_map/ppermute | solution.py:51

commit v2 on v1

v2 whole, which is shorter than its diff:
```python
import functools

import jax
import jax.numpy as jnp
from jax import lax
from jax.experimental import pallas as pl
from jax.experimental.pallas import tpu as pltpu
from jax.sharding import PartitionSpec as P

HDIM = 128
BLK = 128
HOPS = 2
SCALE = HDIM ** (-0.5)
CUBE = (0, 1, 2, 3, 6, 7)
NT = (((1,), (1,)), ((), ()))
VMEM = pl.BlockSpec(memory_space=pltpu.VMEM)
SMEM = pl.BlockSpec(memory_space=pltpu.SMEM)
ANY = pl.BlockSpec(memory_space=pl.ANY)
HBM = pl.BlockSpec(memory_space=pltpu.HBM)
NEVER = 1e30
PARAMS = pltpu.CompilerParams(vmem_limit_bytes=60 * 1024 * 1024)


def ndot(a, b):
    return lax.dot_general(a, b, (((1,), (0,)), ((), ())), preferred_element_type=jnp.float32)


def tdot(a, b):
    return lax.dot_general(a, b, NT, preferred_element_type=jnp.float32)


def stat_rows(pairs):
    return -(-2 * pairs // 16) * 16


def window_tags(size):
    return CUBE if size == 8 else tuple([0] + [o for o in range(-HOPS, HOPS + 1) if o != 0])


def tag_owner(position, tag, size):
    return position ^ tag if size == 8 else lax.rem(position + tag + size, size)


def find_shard(position, owner, size):
    shard = 0
    for index, tag in enumerate(window_tags(size)):
        shard = shard + jnp.where(tag_owner(position, tag, size) == owner, index, 0)
    return shard


def exchange(x, size, forward=False):
    def move(v, pairs):
        return lax.ppermute(v, "ctx", pairs)

    if size == 8:
        flip = lambda mask: [(i, i ^ mask) for i in range(size)]
        near = move(x, flip(2))
        far = move(near, flip(4)) if forward else move(x, flip(6))
        mate = move(x, flip(1))
        return [x, mate, near, move(near, flip(1)), far, move(far, flip(1))]
    return [x] + [
        move(x, [(i, (i - tag) % size) for i in range(size)]) for tag in window_tags(size)[1:]
    ]


def start_all(pairs, sem, first=0):
    copies = []
    for index, (source, target) in enumerate(pairs):
        copy = pltpu.make_async_copy(source, target, sem.at[first + index])
        copy.start()
        copies.append(copy)
    return copies


def wait_all(copies):
    for copy in copies:
        copy.wait()


def gather_blocks(size, keys, refs, target, sem, first, blocks_dev, neigh):
    position = lax.axis_index("ctx")
    waits = []
    for b in range(blocks_dev):
        for n in range(neigh):
            j = keys[b, n]
            shard = find_shard(position, lax.div(j, blocks_dev), size)
            row = pl.multiple_of(lax.rem(j, blocks_dev) * BLK, BLK)
            place = b * neigh + n
            for index, ref in enumerate(refs):

                @pl.when(shard == index)
                def _(ref=ref, place=place, row=row):
                    pltpu.make_async_copy(
                        ref.at[pl.ds(row, BLK)], target.at[pl.ds(place * BLK, BLK)], sem.at[first + place]
                    ).start()

            waits.append(
                pltpu.make_async_copy(
                    refs[0].at[pl.ds(0, BLK)], target.at[pl.ds(place * BLK, BLK)], sem.at[first + place]
                )
            )
    return waits


def shift_rows(keys, hosts, bias, b, h, blocks_dev, neigh):
    position = lax.axis_index("ctx")
    slot = lax.broadcasted_iota(jnp.int32, (1, neigh * BLK), 1) // BLK
    shift = jnp.zeros((1, neigh * BLK), jnp.float32)
    host = hosts[position * blocks_dev + b]
    for n in range(neigh):
        value = jnp.where(hosts[keys[b, n]] == host, bias[h], 0.0)
        shift = jnp.where(slot == n, value, shift)
    return shift


def attend_kernel(size, nsh, *refs):
    keys_hbm, hosts_hbm, bias_hbm, q_hbm, w_hbm = refs[:5]
    k_refs = refs[5:5 + nsh]
    v_refs = refs[5 + nsh:5 + 2 * nsh]
    rest = refs[5 + 2 * nsh:]
    mixed_ref, o32_ref, lse_ref = rest[:3]
    keys, hosts, bias, q_ref, w_ref, kcat, vcat, score, att, sem = rest[3:]
    rows, columns = q_ref.shape
    blocks_dev, neigh = keys.shape
    heads_dev = columns // HDIM
    small = start_all([(keys_hbm, keys), (hosts_hbm, hosts), (bias_hbm, bias)], sem)
    large = start_all([(q_hbm, q_ref), (w_hbm, w_ref)], sem, 3)
    wait_all(small)
    places = blocks_dev * neigh
    k_waits = gather_blocks(size, keys, k_refs, kcat, sem, 5, blocks_dev, neigh)
    v_waits = gather_blocks(size, keys, v_refs, vcat, sem, 5 + places, blocks_dev, neigh)
    large[0].wait()
    wait_all(k_waits)
    span = neigh * BLK
    units = [(b, h) for b in range(blocks_dev) for h in range(heads_dev)]
    for b, h in units:
        cols = slice(h * HDIM, (h + 1) * HDIM)
        s = tdot(q_ref[b * BLK:(b + 1) * BLK, cols], kcat[b * span:(b + 1) * span, cols])
        score[b * heads_dev + h] = s * SCALE + shift_rows(keys, hosts, bias, b, h, blocks_dev, neigh)
    wait_all(v_waits)
    lane = lax.broadcasted_iota(jnp.int32, (BLK, BLK), 1)
    lse_all = jnp.zeros((BLK, BLK), jnp.float32)
    for b, h in units:
        cols = slice(h * HDIM, (h + 1) * HDIM)
        s = score[b * heads_dev + h]
        top = jnp.max(s, axis=1, keepdims=True)
        weights = jnp.exp(s - top)
        total = jnp.sum(weights, axis=1, keepdims=True)
        probs = (weights * (1.0 / total)).astype(jnp.bfloat16)
        out = ndot(probs, vcat[b * span:(b + 1) * span, cols])
        o32_ref[b * BLK:(b + 1) * BLK, cols] = out
        att[b * BLK:(b + 1) * BLK, cols] = out.astype(jnp.bfloat16)
        lse_all = jnp.where(lane == b * heads_dev + h, top + jnp.log(total), lse_all)
    lse_ref[...] = lse_all
    large[1].wait()
    mixed_ref[...] = ndot(att[...], w_ref[...]).astype(jnp.bfloat16)


def upstream_kernel(*refs):
    keys_hbm, w_hbm, grads_any, o32_ref, lse_ref, up_ref, stats_ref, keys, w_ref, grads, sem = refs
    rows, columns = o32_ref.shape
    blocks_dev, neigh = keys.shape
    heads_dev = columns // HDIM
    wait_all(start_all([(w_hbm, w_ref), (keys_hbm, keys), (grads_any, grads)], sem))
    up_ref[0:rows, :] = tdot(grads[...], w_ref[...]).astype(jnp.bfloat16)
    pairs = blocks_dev * heads_dev
    lane = lax.broadcasted_iota(jnp.int32, (BLK, BLK), 1)
    stats = lse_ref[...]
    for b in range(blocks_dev):
        for h in range(heads_dev):
            cols = slice(h * HDIM, (h + 1) * HDIM)
            up = up_ref[b * BLK:(b + 1) * BLK, cols].astype(jnp.float32)
            term = jnp.sum(up * o32_ref[b * BLK:(b + 1) * BLK, cols], axis=1, keepdims=True)
            stats = jnp.where(lane == pairs + b * heads_dev + h, term, stats)
    stats_ref[...] = stats
    high = stat_rows(pairs)
    turned = jnp.transpose(stats)[:high, :]
    up_ref[rows:, :] = jnp.zeros((up_ref.shape[0] - rows, columns), jnp.bfloat16)
    pieces = []
    for index in range(3):
        piece = turned.astype(jnp.bfloat16)
        turned = turned - piece.astype(jnp.float32)
        pieces.append(piece)
    spot = lax.broadcasted_iota(jnp.int32, (high, BLK), 1)
    line = lax.broadcasted_iota(jnp.int32, (high, BLK), 0)
    listed = jnp.zeros((high, BLK), jnp.int32)
    for b in range(blocks_dev):
        for n in range(neigh):
            listed = jnp.where(spot == b * neigh + n, keys[b, n], listed)
    listed = jnp.where(line == 0, listed >> 7, listed & 127)
    pieces.append(listed.astype(jnp.float32).astype(jnp.bfloat16))
    for index, piece in enumerate(pieces):
        row = rows + high * (index * BLK // columns)
        col = index * BLK % columns
        up_ref[row:row + high, col:col + BLK] = piece


def query_kernel(size, nsh, *refs):
    keys_hbm, hosts_hbm, bias_hbm, q_hbm, up_ref, stats_ref = refs[:6]
    k_refs = refs[6:6 + nsh]
    v_refs = refs[6 + nsh:6 + 2 * nsh]
    dq_ref, keys, hosts, bias, q_ref, kcat, vcat, sem = refs[6 + 2 * nsh:]
    rows, columns = q_ref.shape
    blocks_dev, neigh = keys.shape
    heads_dev = columns // HDIM
    pairs = blocks_dev * heads_dev
    small = start_all([(keys_hbm, keys), (hosts_hbm, hosts), (bias_hbm, bias)], sem)
    large = start_all([(q_hbm, q_ref)], sem, 3)
    wait_all(small)
    places = blocks_dev * neigh
    waits = gather_blocks(size, keys, k_refs, kcat, sem, 4, blocks_dev, neigh)
    waits += gather_blocks(size, keys, v_refs, vcat, sem, 4 + places, blocks_dev, neigh)
    wait_all(large)
    wait_all(waits)
    span = neigh * BLK
    for b in range(blocks_dev):
        for h in range(heads_dev):
            cols = slice(h * HDIM, (h + 1) * HDIM)
            pair = b * heads_dev + h
            q = q_ref[b * BLK:(b + 1) * BLK, cols]
            up = up_ref[b * BLK:(b + 1) * BLK, cols]
            k = kcat[b * span:(b + 1) * span, cols]
            lse = stats_ref[:, pair:pair + 1]
            term = stats_ref[:, pairs + pair:pairs + pair + 1]
            shift = shift_rows(keys, hosts, bias, b, h, blocks_dev, neigh)
            p = jnp.exp(tdot(q, k) * SCALE + shift - lse)
            dp = tdot(up, vcat[b * span:(b + 1) * span, cols])
            ds = (p * (dp - term) * SCALE).astype(jnp.bfloat16)
            dq_ref[b * BLK:(b + 1) * BLK, cols] = ndot(ds, k).astype(jnp.bfloat16)


def key_kernel(size, nsh, neigh, *refs):
    hosts_hbm, bias_hbm, k_hbm, v_hbm = refs[:4]
    q_refs = refs[4:4 + nsh]
    up_refs = refs[4 + nsh:4 + 2 * nsh]
    dk_ref, dv_ref = refs[4 + 2 * nsh:6 + 2 * nsh]
    (hosts, bias, k_ref, v_ref, qwin, upwin, stats, lists, keys, hits, dk_acc, dv_acc, sem) = refs[
        6 + 2 * nsh:
    ]
    rows, columns = k_ref.shape
    long_rows = up_refs[0].shape[0]
    blocks_dev = rows // BLK
    heads_dev = columns // HDIM
    pairs = blocks_dev * heads_dev
    high = stat_rows(pairs)
    position = lax.axis_index("ctx")
    tail = [
        (ref.at[pl.ds(rows, long_rows - rows)], upwin.at[pl.ds(i * long_rows + rows, long_rows - rows)])
        for i, ref in enumerate(up_refs)
    ]
    first = start_all(tail, sem)
    body = [(ref.at[pl.ds(0, rows)], upwin.at[pl.ds(i * long_rows, rows)]) for i, ref in enumerate(up_refs)]
    body += [(ref, qwin.at[pl.ds(i * rows, rows)]) for i, ref in enumerate(q_refs)]
    body += [(hosts_hbm, hosts), (bias_hbm, bias), (k_hbm, k_ref), (v_hbm, v_ref)]
    later = start_all(body, sem, nsh)
    dk_acc[...] = jnp.zeros_like(dk_acc)
    dv_acc[...] = jnp.zeros_like(dv_acc)
    wait_all(first)

    def part_of(index, piece):
        row = index * long_rows + rows + high * (piece * BLK // columns)
        col = piece * BLK % columns
        return upwin[row:row + high, col:col + BLK].astype(jnp.float32)

    for index in range(nsh):
        stats[index] = (part_of(index, 2) + part_of(index, 1)) + part_of(index, 0)
        listed = part_of(index, 3).astype(jnp.int32)
        lists[index:index + 1, :] = listed[0:1, :] * 128 + listed[1:2, :]
    stats[nsh] = jnp.full((high, BLK), NEVER, jnp.float32)
    copy = pltpu.make_async_copy(lists, keys, sem.at[3 * nsh + 4])
    copy.start()
    copy.wait()

    counts = []
    for own in range(blocks_dev):
        mine = position * blocks_dev + own
        count = 0
        for index in range(nsh):
            for inner in range(blocks_dev):
                hit = keys[index, inner * neigh] == mine
                for n in range(1, neigh):
                    hit = hit | (keys[index, inner * neigh + n] == mine)
                hits[own, count] = index * blocks_dev + inner
                count = count + jnp.where(hit, 1, 0)
        hits[own, count] = -1
        counts.append(count)
    wait_all(later)

    for own in range(blocks_dev):
        mine = position * blocks_dev + own
        krow = slice(own * BLK, (own + 1) * BLK)

        def visit(step, carry, own=own, mine=mine, krow=krow):
            qs, ups, sames, lses, terms = [], [], [], [], []
            for turn in range(2):
                entry = hits[own, 2 * step + turn]
                spare = entry < 0
                entry = jnp.where(spare, 0, entry)
                shard = lax.div(entry, blocks_dev)
                inner = lax.rem(entry, blocks_dev)
                owner = 0
                for index, tag in enumerate(window_tags(size)):
                    owner = owner + jnp.where(shard == index, tag_owner(position, tag, size), 0)
                sames.append(hosts[owner * blocks_dev + inner] == hosts[mine])
                qs.append(pl.ds(pl.multiple_of(shard * rows + inner * BLK, BLK), BLK))
                ups.append(pl.ds(pl.multiple_of(shard * long_rows + inner * BLK, 16), BLK))
                lses.append((jnp.where(spare, nsh, shard), inner))
                terms.append((shard, inner))
            for h in range(heads_dev):
                cols = slice(h * HDIM, (h + 1) * HDIM)
                k = k_ref[krow, cols]
                v = v_ref[krow, cols]
                q = jnp.concatenate([qwin[r, cols] for r in qs], axis=0)
                up = jnp.concatenate([upwin[r, cols] for r in ups], axis=0)
                less = jnp.concatenate(
                    [
                        stats[shard, pl.ds(inner * heads_dev + h, 1), :] - jnp.where(same, bias[h], 0.0)
                        for (shard, inner), same in zip(lses, sames)
                    ],
                    axis=1,
                )
                term = jnp.concatenate(
                    [stats[shard, pl.ds(pairs + inner * heads_dev + h, 1), :] for shard, inner in terms],
                    axis=1,
                )
                p = jnp.exp(tdot(k, q) * SCALE - less)
                ds = (p * (tdot(v, up) - term) * SCALE).astype(jnp.bfloat16)
                dk_acc[krow, cols] += ndot(ds, q)
                dv_acc[krow, cols] += ndot(p.astype(jnp.bfloat16), up)
            return carry

        lax.fori_loop(0, lax.div(counts[own] + 1, 2), visit, 0)
    dk_ref[...] = dk_acc[...].astype(jnp.bfloat16)
    dv_ref[...] = dv_acc[...].astype(jnp.bfloat16)


def cost(flops, nbytes):
    return pl.CostEstimate(flops=flops, bytes_accessed=nbytes, transcendentals=0)


def per_device(
    query_states, key_states, value_states, out_weight, grad_mixed, key_blocks, host_ids, host_bias
):
    size = lax.axis_size("ctx")
    rows, columns = query_states.shape
    width = out_weight.shape[1]
    blocks_dev, neigh = key_blocks.shape
    heads_dev = columns // HDIM
    pairs = blocks_dev * heads_dev
    places = blocks_dev * neigh
    nsh = len(window_tags(size))
    bf16, f32, i32 = jnp.bfloat16, jnp.float32, jnp.int32
    high = stat_rows(pairs)
    extra = high * (-(-4 * BLK // columns))
    long_rows = rows + extra

    all_grads = lax.all_gather(grad_mixed, "head", axis=0, tiled=True)
    v_win = exchange(value_states, size, forward=True)
    k_win = exchange(key_states, size)
    late_query, _ = lax.optimization_barrier((query_states, v_win[2]))
    q_win = exchange(late_query, size)
    scalars = [
        pltpu.SMEM(key_blocks.shape, i32),
        pltpu.SMEM(host_ids.shape, i32),
        pltpu.SMEM(host_bias.shape, f32),
    ]

    share, o32, lse = pl.pallas_call(
        functools.partial(attend_kernel, size, nsh),
        out_shape=[
            jax.ShapeDtypeStruct((rows, width), bf16),
            jax.ShapeDtypeStruct((rows, columns), f32),
            jax.ShapeDtypeStruct((BLK, BLK), f32),
        ],
        in_specs=[HBM] * 5 + ([HBM] + [ANY] * (nsh - 1)) * 2,
        out_specs=[VMEM] * 3,
        scratch_shapes=scalars
        + [
            pltpu.VMEM((rows, columns), bf16),
            pltpu.VMEM((columns, width), bf16),
            pltpu.VMEM((places * BLK, columns), bf16),
            pltpu.VMEM((places * BLK, columns), bf16),
            pltpu.VMEM((pairs, BLK, neigh * BLK), f32),
            pltpu.VMEM((rows, columns), bf16),
            pltpu.SemaphoreType.DMA((5 + 2 * places,)),
        ],
        compiler_params=PARAMS,
        cost_estimate=cost(1000, 1000),
        name="attend",
    )(key_blocks, host_ids, host_bias, query_states, out_weight, *k_win, *v_win)
    mixed_out = lax.psum_scatter(share, "head", scatter_dimension=0, tiled=True)

    up, stats = pl.pallas_call(
        upstream_kernel,
        out_shape=[
            jax.ShapeDtypeStruct((long_rows, columns), bf16),
            jax.ShapeDtypeStruct((BLK, BLK), f32),
        ],
        in_specs=[HBM] * 2 + [ANY] + [VMEM] * 2,
        out_specs=[VMEM] * 2,
        scratch_shapes=[
            pltpu.SMEM(key_blocks.shape, i32),
            pltpu.VMEM((columns, width), bf16),
            pltpu.VMEM((rows, width), bf16),
            pltpu.SemaphoreType.DMA((3,)),
        ],
        compiler_params=PARAMS,
        cost_estimate=cost(1000, 1000),
        name="upstream",
    )(key_blocks, out_weight, all_grads, o32, lse)
    up_win = exchange(up, size)

    grad_query = pl.pallas_call(
        functools.partial(query_kernel, size, nsh),
        out_shape=jax.ShapeDtypeStruct((rows, columns), bf16),
        in_specs=[HBM] * 4 + [VMEM] * 2 + ([HBM] + [ANY] * (nsh - 1)) * 2,
        out_specs=VMEM,
        scratch_shapes=scalars
        + [
            pltpu.VMEM((rows, columns), bf16),
            pltpu.VMEM((places * BLK, columns), bf16),
            pltpu.VMEM((places * BLK, columns), bf16),
            pltpu.SemaphoreType.DMA((4 + 2 * places,)),
        ],
        compiler_params=PARAMS,
        cost_estimate=cost(1000, 1000),
        name="query_grad",
    )(key_blocks, host_ids, host_bias, query_states, up, stats, *k_win, *v_win)

    grad_key, grad_value = pl.pallas_call(
        functools.partial(key_kernel, size, nsh, neigh),
        out_shape=[jax.ShapeDtypeStruct((rows, columns), bf16)] * 2,
        in_specs=[HBM] * 5 + [ANY] * (2 * nsh - 1),
        out_specs=[VMEM] * 2,
        scratch_shapes=[
            pltpu.SMEM(host_ids.shape, i32),
            pltpu.SMEM(host_bias.shape, f32),
            pltpu.VMEM((rows, columns), bf16),
            pltpu.VMEM((rows, columns), bf16),
            pltpu.VMEM((nsh * rows, columns), bf16),
            pltpu.VMEM((nsh * long_rows, columns), bf16),
            pltpu.VMEM((nsh + 1, high, BLK), f32),
            pltpu.VMEM((8, BLK), i32),
            pltpu.SMEM((8, BLK), i32),
            pltpu.SMEM((blocks_dev, nsh * blocks_dev + 2), i32),
            pltpu.VMEM((rows, columns), f32),
            pltpu.VMEM((rows, columns), f32),
            pltpu.SemaphoreType.DMA((3 * nsh + 5,)),
        ],
        compiler_params=PARAMS,
        cost_estimate=cost(1000, 1000),
        name="key_grad",
    )(host_ids, host_bias, key_states, value_states, query_states, *q_win[1:], *up_win)

    return (mixed_out, grad_query, grad_key, grad_value)


def solution(mesh):
    in_specs = (
        P("ctx", "head"),
        P("ctx", "head"),
        P("ctx", "head"),
        P("head", None),
        P(("ctx", "head"), None),
        P("ctx", None),
        P(),
        P("head"),
    )
    out_specs = (P(("ctx", "head"), None), P("ctx", "head"), P("ctx", "head"), P("ctx", "head"))
    return jax.shard_map(
        per_device, mesh=mesh, in_specs=in_specs, out_specs=out_specs, check_vma=False
    )
```

time: 106 us -> 94.1 us (0.89)
  starting transfers between devices: 27.7 us -> 13.7 us
  between operations: 0.73 us -> 14.3 us
  blocking collectives: 8.85 us -> 0 us
  local copies, waits for them, and re-layouts: 4.86 us -> 2.5 us
  waiting for transfers between devices: 38.3 us -> 39.6 us
    ppermute x6 -> x0, starting transfers between devices: 13.4 us -> none  [ring(): lax.ppermute(x, 'head', [(i, (i + step) % groups) for i in range(groups)])]
    ppermute x6 -> x0, waiting for transfers between devices: 12.1 us -> none  [ring(): lax.ppermute(x, 'head', [(i, (i + step) % groups) for i in range(groups)])]
    ppermute x20, waiting for transfers between devices: 26.2 us -> 37.1 us  [move(): return lax.ppermute(v, 'ctx', pairs)]
    all_gather x1 -> x0, blocking collectives: 8.85 us -> none  [per_device(): all_keys = lax.all_gather(key_blocks, 'ctx', axis=0, tiled=True)]
    unnamed x24 -> x42, local copies, waits for them, and re-layouts: 4.86 us -> 2.5 us
    all_gather x0 -> x1, waiting for transfers between devices: none -> 1.77 us  [per_device(): all_grads = lax.all_gather(grad_mixed, 'head', axis=0, tiled=True)]
    pallas_call x1, Pallas kernels: 5.13 us -> 6.2 us  [per_device(): pl.pallas_call(functools.partial(query_kernel, size, nsh), out_shape=jax....]
  transfers between devices with their start and end apart: 26 -> 22, of which waited for: 10 -> 11; matrix products, arithmetic and copies ran while one was open for 1% -> 0% of each run, Pallas kernels for 12% -> 25%
where the time goes in v2:
time: 94.1 us; the launch traced here: 93.8 us
  waiting for transfers between devices  39.6 us (42%)
  Pallas kernels  23.7 us (25%)
  between operations  14.3 us (15%)
  starting transfers between devices  13.7 us (15%)
  local copies, waits for them, and re-layouts  2.5 us (3%)
    ppermute x20, waiting for transfers between devices, move(): return lax.ppermute(v, 'ctx', pairs)  37.1 us
    ppermute x20, starting transfers between devices, move(): return lax.ppermute(v, 'ctx', pairs)  13.6 us
    pallas_call x1, Pallas kernels, per_device(): pl.pallas_call(functools.partial(key_kernel, size, nsh, neigh), out_shape...  7.52 us
    pallas_call x1, Pallas kernels, per_device(): pl.pallas_call(functools.partial(query_kernel, size, nsh), out_shape=jax....  6.2 us
    pallas_call x1, Pallas kernels, per_device(): pl.pallas_call(functools.partial(attend_kernel, size, nsh), out_shape=[ja...  5.35 us
    pallas_call x1, Pallas kernels, per_device(): pl.pallas_call(upstream_kernel, out_shape=[jax.ShapeDtypeStruct((long_row...  4.58 us
    unnamed x42, local copies, waits for them, and re-layouts  2.5 us
  transfers between devices with their start and end apart: 22, of which 11 were waited for; matrix products, arithmetic and copies ran while one was open for 0% of the time, Pallas kernels for 25%

profile of v2, /device:TPU:0, one launch (start us, length us, event | category | flops | bytes accessed | tf_op | source)
XLA Modules:
  0.0 93.8 jit_solution(6311876245443555401)
XLA Ops:
  7.2 0.0 all-gather.2.cloned.1.call-start
  7.2 0.7 all-gather.2.cloned.1.call-update
  7.9 0.0 reduce-scatter.2.cloned.1.call-start
  7.9 3.0 %collective-permute-start.6 = (bf16[256,512]{1,0:T(8,128)(2,1)}, bf16[256,512]{1,0:T(8,128)(2,1)S(1)}, u32[]{:S(2)}, u32[]{:S(2)}) collective-permute-start(bf16[256,512]{1,0:T(8,128)(2,1)} %refs_3_.5), channel_id=1, source_target_pairs={{0,8},{4,12},{8,0},{12,4},{16,24},{20,28},{24,16},{28,20},{1,9},{5... | collective-permute-start | bytes 786440 | tf_op jit(solution)/shard_map/ppermute | solution.py:53
  10.9 0.0 collective-permute-start
  11.0 0.2 collective-permute-start.1
  11.1 2.8 %collective-permute-start.3 = (bf16[256,512]{1,0:T(8,128)(2,1)}, bf16[256,512]{1,0:T(8,128)(2,1)S(1)}, u32[]{:S(2)}, u32[]{:S(2)}) collective-permute-start(bf16[256,512]{1,0:T(8,128)(2,1)} %refs_2_.5), channel_id=1, source_target_pairs={{0,24},{4,28},{8,16},{12,20},{16,8},{20,12},{24,0},{28,4},{1,25},{... | collective-permute-start | bytes 786440 | tf_op jit(solution)/shard_map/ppermute | solution.py:53
  13.9 4.4 %collective-permute-done.6.refs_13_.refs_14_ = bf16[256,512]{1,0:T(8,128)(2,1)S(1)} collective-permute-done((bf16[256,512]{1,0:T(8,128)(2,1)}, bf16[256,512]{1,0:T(8,128)(2,1)S(1)}, u32[]{:S(2)}, u32[]{:S(2)}) %collective-permute-start.6) | collective-permute-done | bytes 262176 | tf_op jit(solution)/shard_map/ppermute | solution.py:53
  18.3 2.1 %collective-permute-start.8 = (bf16[256,512]{1,0:T(8,128)(2,1)S(1)}, bf16[256,512]{1,0:T(8,128)(2,1)S(1)}, u32[]{:S(2)}, u32[]{:S(2)}) collective-permute-start(bf16[256,512]{1,0:T(8,128)(2,1)S(1)} %collective-permute-done.6.refs_13_.refs_14_), channel_id=1, source_target_pairs={{0,16},{4,20},{8,24},{12,28},{16,0},{20,4},{24,8},{28,12},{1,17},{... | collective-permute-start | bytes 786440 | tf_op jit(solution)/shard_map/ppermute | solution.py:53
  20.4 0.5 collective-permute-start.7
  20.9 3.0 %collective-permute-done.1.refs_7_.refs_8_ = bf16[256,512]{1,0:T(8,128)(2,1)S(1)} collective-permute-done((bf16[256,512]{1,0:T(8,128)(2,1)}, bf16[256,512]{1,0:T(8,128)(2,1)S(1)}, u32[]{:S(2)}, u32[]{:S(2)}) %collective-permute-start.1) | collective-permute-done | bytes 262176 | tf_op jit(solution)/shard_map/ppermute | solution.py:53
  23.9 0.0 collective-permute-start.2
  23.9 6.1 %collective-permute-done.3.refs_9_.refs_10_ = bf16[256,512]{1,0:T(8,128)(2,1)S(1)} collective-permute-done((bf16[256,512]{1,0:T(8,128)(2,1)}, bf16[256,512]{1,0:T(8,128)(2,1)S(1)}, u32[]{:S(2)}, u32[]{:S(2)}) %collective-permute-start.3) | collective-permute-done | bytes 262176 | tf_op jit(solution)/shard_map/ppermute | solution.py:53
  30.0 0.0 collective-permute-start.4
  30.0 0.6 collective-permute-done.8.refs_15_.refs_16_
  30.6 0.0 collective-permute-start.9
  30.6 0.0 collective-permute-done.5.refs_12_.refs_13_
  30.6 0.9 collective-permute-done.4.refs_10_.refs_11_
  31.6 0.0 collective-permute-done.7.refs_14_.refs_15_
  31.6 0.6 collective-permute-done.9.refs_16_.refs_17_
  32.2 0.1 copy-done.9
  32.3 0.1 copy-done.7
  32.4 0.7 copy-done.10
  33.1 5.4 %attend.1 = (bf16[256,2048]{1,0:T(8,128)(2,1)}, f32[256,512]{1,0:T(8,128)}, f32[128,128]{1,0:T(8,128)}) custom-call(s32[2,4]{1,0:T(2,128)} %refs_0_.6, s32[16]{0:T(128)} %refs_0_.7, f32[4]{0:T(128)} %refs_1_.7, bf16[256,512]{1,0:T(8,128)(2,1)} %refs_4_.3, bf16[512,2048]{1,0:T(8,128)(2,1)} %refs_1_.5, bf16[256,512]{1,0:T(8,128)(2,1)} %refs_2_.5, ...), custom_call_target="tpu_custom_call" | custom-call | flops 1000 | bytes 1000 | tf_op jit(solution)/shard_map/attend/pallas_call | solution.py:368
  38.4 0.0 reduce-scatter.2.cloned.1.call-update
  38.4 0.0 copy-start
  38.5 1.8 %all-gather.2.cloned.1.call-done.refs_2_ = bf16[256,2048]{1,0:T(8,128)(2,1)} async-done(((bf16[64,2048]{1,0:T(8,128)(2,1)}), bf16[256,2048]{1,0:T(8,128)(2,1)}) %all-gather.2.cloned.1.call-update) | async-done | bytes 1048592 | tf_op jit(solution)/shard_map/all_gather | solution.py:357
  40.2 4.6 %upstream.1 = (bf16[272,512]{1,0:T(8,128)(2,1)}, f32[128,128]{1,0:T(8,128)}) custom-call(s32[2,4]{1,0:T(2,128)} %refs_0_.6, bf16[512,2048]{1,0:T(8,128)(2,1)} %refs_1_.5, bf16[256,2048]{1,0:T(8,128)(2,1)} %all-gather.2.cloned.1.call-done.refs_2_, f32[256,512]{1,0:T(8,128)} %get-tuple-element.13.refs_3_, f32[128,128]{1,0:T(8,128)} %get-tuple-element.14.refs_4_), custom_call_target="tpu_custom_call" | custom-call | flops 1000 | bytes 1000 | tf_op jit(solution)/shard_map/upstream/pallas_call | solution.py:393
  44.8 1.5 %collective-permute-start.16 = (bf16[272,512]{1,0:T(8,128)(2,1)}, bf16[272,512]{1,0:T(8,128)(2,1)S(1)}, u32[]{:S(2)}, u32[]{:S(2)}) collective-permute-start(bf16[272,512]{1,0:T(8,128)(2,1)} %get-tuple-element.15.refs_4_.refs_10_), channel_id=1, source_target_pairs={{0,8},{4,12},{8,0},{12,4},{16,24},{20,28},{24,16},{28,20},{1,9},{5... | collective-permute-start | bytes 835592 | tf_op jit(solution)/shard_map/ppermute | solution.py:53
  46.4 1.5 %collective-permute-start.18 = (bf16[272,512]{1,0:T(8,128)(2,1)}, bf16[272,512]{1,0:T(8,128)(2,1)S(1)}, u32[]{:S(2)}, u32[]{:S(2)}) collective-permute-start(bf16[272,512]{1,0:T(8,128)(2,1)} %get-tuple-element.15.refs_4_.refs_10_), channel_id=1, source_target_pairs={{0,24},{4,28},{8,16},{12,20},{16,8},{20,12},{24,0},{28,4},{1,25},{... | collective-permute-start | bytes 835592 | tf_op jit(solution)/shard_map/ppermute | solution.py:53
  47.8 1.5 %collective-permute-start.11 = (bf16[256,512]{1,0:T(8,128)(2,1)S(1)}, bf16[256,512]{1,0:T(8,128)(2,1)S(1)}, u32[]{:S(2)}, u32[]{:S(2)}) collective-permute-start(bf16[256,512]{1,0:T(8,128)(2,1)S(1)} %copy-done), channel_id=1, source_target_pairs={{0,8},{4,12},{8,0},{12,4},{16,24},{20,28},{24,16},{28,20},{1,9},{5... | collective-permute-start | bytes 786440 | tf_op jit(solution)/shard_map/ppermute | solution.py:53
  49.3 0.5 collective-permute-start.13
  49.8 0.0 collective-permute-done.10.refs_5_
  49.8 0.0 collective-permute-start.15
  49.9 4.8 %collective-permute-done.16.refs_12_ = bf16[272,512]{1,0:T(8,128)(2,1)S(1)} collective-permute-done((bf16[272,512]{1,0:T(8,128)(2,1)}, bf16[272,512]{1,0:T(8,128)(2,1)S(1)}, u32[]{:S(2)}, u32[]{:S(2)}) %collective-permute-start.16) | collective-permute-done | bytes 278560 | tf_op jit(solution)/shard_map/ppermute | solution.py:53
  54.7 0.0 collective-permute-start.17
  54.7 6.9 %collective-permute-done.18.refs_14_ = bf16[272,512]{1,0:T(8,128)(2,1)S(1)} collective-permute-done((bf16[272,512]{1,0:T(8,128)(2,1)}, bf16[272,512]{1,0:T(8,128)(2,1)S(1)}, u32[]{:S(2)}, u32[]{:S(2)}) %collective-permute-start.18) | collective-permute-done | bytes 278560 | tf_op jit(solution)/shard_map/ppermute | solution.py:53
  61.5 0.0 collective-permute-start.19
  61.5 4.7 %collective-permute-done.11.refs_6_ = bf16[256,512]{1,0:T(8,128)(2,1)S(1)} collective-permute-done((bf16[256,512]{1,0:T(8,128)(2,1)S(1)}, bf16[256,512]{1,0:T(8,128)(2,1)S(1)}, u32[]{:S(2)}, u32[]{:S(2)}) %collective-permute-start.11) | collective-permute-done | bytes 262176 | tf_op jit(solution)/shard_map/ppermute | solution.py:53
  66.3 5.2 %collective-permute-done.13.refs_8_ = bf16[256,512]{1,0:T(8,128)(2,1)S(1)} collective-permute-done((bf16[256,512]{1,0:T(8,128)(2,1)S(1)}, bf16[256,512]{1,0:T(8,128)(2,1)S(1)}, u32[]{:S(2)}, u32[]{:S(2)}) %collective-permute-start.13) | collective-permute-done | bytes 262176 | tf_op jit(solution)/shard_map/ppermute | solution.py:53
  71.5 6.2 %query_grad.1 = bf16[256,512]{1,0:T(8,128)(2,1)} custom-call(s32[2,4]{1,0:T(2,128)} %refs_0_.6, s32[16]{0:T(128)} %refs_0_.7, f32[4]{0:T(128)} %refs_1_.7, bf16[256,512]{1,0:T(8,128)(2,1)} %refs_4_.3, bf16[272,512]{1,0:T(8,128)(2,1)} %get-tuple-element.15.refs_4_.refs_10_, f32[128,128]{1,0:T(8,128)} %get-tuple-element.16.refs_5_, bf16[256,512]{1,0:T(8,128)(2,1)} %refs_2_.5, ...), custom_call_target="tpu_custom_call" | custom-call | flops 1000 | bytes 1000 | tf_op jit(solution)/shard_map/query_grad/pallas_call | solution.py:413
  77.8 0.6 copy-done.19
  78.4 0.1 copy-done.20
  78.5 0.1 copy-done.13
  78.6 0.1 copy-done.14
  78.7 0.7 copy-done.15
  79.4 7.5 %key_grad.1 = (bf16[256,512]{1,0:T(8,128)(2,1)}, bf16[256,512]{1,0:T(8,128)(2,1)}) custom-call(s32[16]{0:T(128)} %refs_0_.7, f32[4]{0:T(128)} %refs_1_.7, bf16[256,512]{1,0:T(8,128)(2,1)} %refs_2_.5, bf16[256,512]{1,0:T(8,128)(2,1)} %refs_3_.5, bf16[256,512]{1,0:T(8,128)(2,1)} %refs_4_.3, bf16[256,512]{1,0:T(8,128)(2,1)} %copy-done.16, ...), custom_call_target="tpu_custom_call" | custom-call | flops 1000 | bytes 1000 | tf_op jit(solution)/shard_map/key_grad/pallas_call | solution.py:430
  86.9 0.0 reduce-scatter.2.cloned.1.call-done
  (44 shorter events, 0.1 us)
Async XLA Ops:
  7.2 33.1 %all-gather.2.cloned.1.call-start = ((), (), s32[]{:S(2)}) async-start(), calls=%async_computation.2 | async-start | bytes 1310720 | tf_op jit(solution)/shard_map/all_gather | solution.py:357
  7.9 79.0 %reduce-scatter.2.cloned.1.call-start = ((), (), s32[]{:S(2)}) async-start(), calls=%async_computation.1 | async-start | bytes 1310720 | tf_op jit(solution)/shard_map/reduce_scatter | solution.py:391
  7.9 10.4 %collective-permute-start.6 = (bf16[256,512]{1,0:T(8,128)(2,1)}, bf16[256,512]{1,0:T(8,128)(2,1)S(1)}, u32[]{:S(2)}, u32[]{:S(2)}) collective-permute-start(bf16[256,512]{1,0:T(8,128)(2,1)} %refs_3_.5), channel_id=1, source_target_pairs={{0,8},{4,12},{8,0},{12,4},{16,24},{20,28},{24,16},{28,20},{1,9},{5... | collective-permute-start | bytes 786440 | tf_op jit(solution)/shard_map/ppermute | solution.py:53
  10.9 9.4 %collective-permute-start = (bf16[256,512]{1,0:T(8,128)(2,1)}, bf16[256,512]{1,0:T(8,128)(2,1)S(1)}, u32[]{:S(2)}, u32[]{:S(2)}) collective-permute-start(bf16[256,512]{1,0:T(8,128)(2,1)} %refs_2_.5), channel_id=1, source_target_pairs={{0,4},{4,0},{8,12},{12,8},{16,20},{20,16},{24,28},{28,24},{1,5},{5... | collective-permute-start | bytes 786440 | tf_op jit(solution)/shard_map/ppermute | solution.py:53
  11.0 13.0 %collective-permute-start.1 = (bf16[256,512]{1,0:T(8,128)(2,1)}, bf16[256,512]{1,0:T(8,128)(2,1)S(1)}, u32[]{:S(2)}, u32[]{:S(2)}) collective-permute-start(bf16[256,512]{1,0:T(8,128)(2,1)} %refs_2_.5), channel_id=1, source_target_pairs={{0,8},{4,12},{8,0},{12,4},{16,24},{20,28},{24,16},{28,20},{1,9},{5... | collective-permute-start | bytes 786440 | tf_op jit(solution)/shard_map/ppermute | solution.py:53
  11.1 18.9 %collective-permute-start.3 = (bf16[256,512]{1,0:T(8,128)(2,1)}, bf16[256,512]{1,0:T(8,128)(2,1)S(1)}, u32[]{:S(2)}, u32[]{:S(2)}) collective-permute-start(bf16[256,512]{1,0:T(8,128)(2,1)} %refs_2_.5), channel_id=1, source_target_pairs={{0,24},{4,28},{8,16},{12,20},{16,8},{20,12},{24,0},{28,4},{1,25},{... | collective-permute-start | bytes 786440 | tf_op jit(solution)/shard_map/ppermute | solution.py:53
  18.3 13.8 %copy-start.1 = (bf16[256,512]{1,0:T(8,128)(2,1)}, bf16[256,512]{1,0:T(8,128)(2,1)S(1)}, u32[]{:S(2)}) copy-start(bf16[256,512]{1,0:T(8,128)(2,1)S(1)} %collective-permute-done.6.refs_13_.refs_14_) | copy-start | bytes 786436
  18.3 12.3 %collective-permute-start.8 = (bf16[256,512]{1,0:T(8,128)(2,1)S(1)}, bf16[256,512]{1,0:T(8,128)(2,1)S(1)}, u32[]{:S(2)}, u32[]{:S(2)}) collective-permute-start(bf16[256,512]{1,0:T(8,128)(2,1)S(1)} %collective-permute-done.6.refs_13_.refs_14_), channel_id=1, source_target_pairs={{0,16},{4,20},{8,24},{12,28},{16,0},{20,4},{24,8},{28,12},{1,17},{... | collective-permute-start | bytes 786440 | tf_op jit(solution)/shard_map/ppermute | solution.py:53
  20.4 10.2 %collective-permute-start.5 = (bf16[256,512]{1,0:T(8,128)(2,1)}, bf16[256,512]{1,0:T(8,128)(2,1)S(1)}, u32[]{:S(2)}, u32[]{:S(2)}) collective-permute-start(bf16[256,512]{1,0:T(8,128)(2,1)} %refs_3_.5), channel_id=1, source_target_pairs={{0,4},{4,0},{8,12},{12,8},{16,20},{20,16},{24,28},{28,24},{1,5},{5... | collective-permute-start | bytes 786440 | tf_op jit(solution)/shard_map/ppermute | solution.py:53
  20.4 11.7 %copy-start.2 = (bf16[256,512]{1,0:T(8,128)(2,1)}, bf16[256,512]{1,0:T(8,128)(2,1)S(1)}, u32[]{:S(2)}) copy-start(bf16[256,512]{1,0:T(8,128)(2,1)S(1)} %collective-permute-done.refs_6_.refs_7_) | copy-start | bytes 786436
  20.4 11.2 %collective-permute-start.7 = (bf16[256,512]{1,0:T(8,128)(2,1)S(1)}, bf16[256,512]{1,0:T(8,128)(2,1)S(1)}, u32[]{:S(2)}, u32[]{:S(2)}) collective-permute-start(bf16[256,512]{1,0:T(8,128)(2,1)S(1)} %collective-permute-done.6.refs_13_.refs_14_), channel_id=1, source_target_pairs={{0,4},{4,0},{8,12},{12,8},{16,20},{20,16},{24,28},{28,24},{1,5},{5... | collective-permute-start | bytes 786440 | tf_op jit(solution)/shard_map/ppermute | solution.py:53
  23.9 8.2 %copy-start.3 = (bf16[256,512]{1,0:T(8,128)(2,1)}, bf16[256,512]{1,0:T(8,128)(2,1)S(1)}, u32[]{:S(2)}) copy-start(bf16[256,512]{1,0:T(8,128)(2,1)S(1)} %collective-permute-done.1.refs_7_.refs_8_) | copy-start | bytes 786436
  23.9 6.7 %collective-permute-start.2 = (bf16[256,512]{1,0:T(8,128)(2,1)S(1)}, bf16[256,512]{1,0:T(8,128)(2,1)S(1)}, u32[]{:S(2)}, u32[]{:S(2)}) collective-permute-start(bf16[256,512]{1,0:T(8,128)(2,1)S(1)} %collective-permute-done.1.refs_7_.refs_8_), channel_id=1, source_target_pairs={{0,4},{4,0},{8,12},{12,8},{16,20},{20,16},{24,28},{28,24},{1,5},{5... | collective-permute-start | bytes 786440 | tf_op jit(solution)/shard_map/ppermute | solution.py:53
  30.0 2.1 %copy-start.4 = (bf16[256,512]{1,0:T(8,128)(2,1)}, bf16[256,512]{1,0:T(8,128)(2,1)S(1)}, u32[]{:S(2)}) copy-start(bf16[256,512]{1,0:T(8,128)(2,1)S(1)} %collective-permute-done.3.refs_9_.refs_10_) | copy-start | bytes 786436
  30.0 1.5 %collective-permute-start.4 = (bf16[256,512]{1,0:T(8,128)(2,1)S(1)}, bf16[256,512]{1,0:T(8,128)(2,1)S(1)}, u32[]{:S(2)}, u32[]{:S(2)}) collective-permute-start(bf16[256,512]{1,0:T(8,128)(2,1)S(1)} %collective-permute-done.3.refs_9_.refs_10_), channel_id=1, source_target_pairs={{0,4},{4,0},{8,12},{12,8},{16,20},{20,16},{24,28},{28,24},{1,5},{5... | collective-permute-start | bytes 786440 | tf_op jit(solution)/shard_map/ppermute | solution.py:53
  30.6 1.6 %copy-start.5 = (bf16[256,512]{1,0:T(8,128)(2,1)}, bf16[256,512]{1,0:T(8,128)(2,1)S(1)}, u32[]{:S(2)}) copy-start(bf16[256,512]{1,0:T(8,128)(2,1)S(1)} %collective-permute-done.8.refs_15_.refs_16_) | copy-start | bytes 786436
  30.6 1.5 %collective-permute-start.9 = (bf16[256,512]{1,0:T(8,128)(2,1)S(1)}, bf16[256,512]{1,0:T(8,128)(2,1)S(1)}, u32[]{:S(2)}, u32[]{:S(2)}) collective-permute-start(bf16[256,512]{1,0:T(8,128)(2,1)S(1)} %collective-permute-done.8.refs_15_.refs_16_), channel_id=1, source_target_pairs={{0,4},{4,0},{8,12},{12,8},{16,20},{20,16},{24,28},{28,24},{1,5},{5... | collective-permute-start | bytes 786440 | tf_op jit(solution)/shard_map/ppermute | solution.py:53
  30.6 1.6 %copy-start.6 = (bf16[256,512]{1,0:T(8,128)(2,1)}, bf16[256,512]{1,0:T(8,128)(2,1)S(1)}, u32[]{:S(2)}) copy-start(bf16[256,512]{1,0:T(8,128)(2,1)S(1)} %collective-permute-done.5.refs_12_.refs_13_) | copy-start | bytes 786436
  30.6 1.5 %copy-start.8 = (bf16[256,512]{1,0:T(8,128)(2,1)}, bf16[256,512]{1,0:T(8,128)(2,1)S(1)}, u32[]{:S(2)}) copy-start(bf16[256,512]{1,0:T(8,128)(2,1)S(1)} %collective-permute-done.2.refs_8_.refs_9_) | copy-start | bytes 786436
  31.5 0.7 copy-start.9
  31.6 0.8 copy-start.7
  32.4 0.7 copy-start.10
  38.4 9.4 %copy-start = (bf16[256,512]{1,0:T(8,128)(2,1)S(1)}, bf16[256,512]{1,0:T(8,128)(2,1)}, u32[]{:S(2)}) copy-start(bf16[256,512]{1,0:T(8,128)(2,1)} %refs_4_.3) | copy-start | bytes 786436
  44.8 9.8 %collective-permute-start.16 = (bf16[272,512]{1,0:T(8,128)(2,1)}, bf16[272,512]{1,0:T(8,128)(2,1)S(1)}, u32[]{:S(2)}, u32[]{:S(2)}) collective-permute-start(bf16[272,512]{1,0:T(8,128)(2,1)} %get-tuple-element.15.refs_4_.refs_10_), channel_id=1, source_target_pairs={{0,8},{4,12},{8,0},{12,4},{16,24},{20,28},{24,16},{28,20},{1,9},{5... | collective-permute-start | bytes 835592 | tf_op jit(solution)/shard_map/ppermute | solution.py:53
  46.4 15.2 %collective-permute-start.18 = (bf16[272,512]{1,0:T(8,128)(2,1)}, bf16[272,512]{1,0:T(8,128)(2,1)S(1)}, u32[]{:S(2)}, u32[]{:S(2)}) collective-permute-start(bf16[272,512]{1,0:T(8,128)(2,1)} %get-tuple-element.15.refs_4_.refs_10_), channel_id=1, source_target_pairs={{0,24},{4,28},{8,16},{12,20},{16,8},{20,12},{24,0},{28,4},{1,25},{... | collective-permute-start | bytes 835592 | tf_op jit(solution)/shard_map/ppermute | solution.py:53
  47.8 2.0 %collective-permute-start.10 = (bf16[256,512]{1,0:T(8,128)(2,1)S(1)}, bf16[256,512]{1,0:T(8,128)(2,1)S(1)}, u32[]{:S(2)}, u32[]{:S(2)}) collective-permute-start(bf16[256,512]{1,0:T(8,128)(2,1)S(1)} %copy-done), channel_id=1, source_target_pairs={{0,4},{4,0},{8,12},{12,8},{16,20},{20,16},{24,28},{28,24},{1,5},{5... | collective-permute-start | bytes 786440 | tf_op jit(solution)/shard_map/ppermute | solution.py:53
  47.8 18.4 %collective-permute-start.11 = (bf16[256,512]{1,0:T(8,128)(2,1)S(1)}, bf16[256,512]{1,0:T(8,128)(2,1)S(1)}, u32[]{:S(2)}, u32[]{:S(2)}) collective-permute-start(bf16[256,512]{1,0:T(8,128)(2,1)S(1)} %copy-done), channel_id=1, source_target_pairs={{0,8},{4,12},{8,0},{12,4},{16,24},{20,28},{24,16},{28,20},{1,9},{5... | collective-permute-start | bytes 786440 | tf_op jit(solution)/shard_map/ppermute | solution.py:53
  49.3 22.2 %collective-permute-start.13 = (bf16[256,512]{1,0:T(8,128)(2,1)S(1)}, bf16[256,512]{1,0:T(8,128)(2,1)S(1)}, u32[]{:S(2)}, u32[]{:S(2)}) collective-permute-start(bf16[256,512]{1,0:T(8,128)(2,1)S(1)} %copy-done), channel_id=1, source_target_pairs={{0,24},{4,28},{8,16},{12,20},{16,8},{20,12},{24,0},{28,4},{1,25},{... | collective-permute-start | bytes 786440 | tf_op jit(solution)/shard_map/ppermute | solution.py:53
  49.8 27.9 %copy-start.16 = (bf16[256,512]{1,0:T(8,128)(2,1)}, bf16[256,512]{1,0:T(8,128)(2,1)S(1)}, u32[]{:S(2)}) copy-start(bf16[256,512]{1,0:T(8,128)(2,1)S(1)} %collective-permute-done.10.refs_5_) | copy-start | bytes 786436
  49.8 27.9 %collective-permute-start.15 = (bf16[272,512]{1,0:T(8,128)(2,1)}, bf16[272,512]{1,0:T(8,128)(2,1)S(1)}, u32[]{:S(2)}, u32[]{:S(2)}) collective-permute-start(bf16[272,512]{1,0:T(8,128)(2,1)} %get-tuple-element.15.refs_4_.refs_10_), channel_id=1, source_target_pairs={{0,4},{4,0},{8,12},{12,8},{16,20},{20,16},{24,28},{28,24},{1,5},{5... | collective-permute-start | bytes 835592 | tf_op jit(solution)/shard_map/ppermute | solution.py:53
  54.7 23.1 %copy-start.11 = (bf16[272,512]{1,0:T(8,128)(2,1)}, bf16[272,512]{1,0:T(8,128)(2,1)S(1)}, u32[]{:S(2)}) copy-start(bf16[272,512]{1,0:T(8,128)(2,1)S(1)} %collective-permute-done.16.refs_12_) | copy-start | bytes 835588
  54.7 23.1 %collective-permute-start.17 = (bf16[272,512]{1,0:T(8,128)(2,1)S(1)}, bf16[272,512]{1,0:T(8,128)(2,1)S(1)}, u32[]{:S(2)}, u32[]{:S(2)}) collective-permute-start(bf16[272,512]{1,0:T(8,128)(2,1)S(1)} %collective-permute-done.16.refs_12_), channel_id=1, source_target_pairs={{0,4},{4,0},{8,12},{12,8},{16,20},{20,16},{24,28},{28,24},{1,5},{5... | collective-permute-start | bytes 835592 | tf_op jit(solution)/shard_map/ppermute | solution.py:53
  61.5 16.3 %copy-start.12 = (bf16[272,512]{1,0:T(8,128)(2,1)}, bf16[272,512]{1,0:T(8,128)(2,1)S(1)}, u32[]{:S(2)}) copy-start(bf16[272,512]{1,0:T(8,128)(2,1)S(1)} %collective-permute-done.18.refs_14_) | copy-start | bytes 835588
  61.5 16.2 %collective-permute-start.19 = (bf16[272,512]{1,0:T(8,128)(2,1)S(1)}, bf16[272,512]{1,0:T(8,128)(2,1)S(1)}, u32[]{:S(2)}, u32[]{:S(2)}) collective-permute-start(bf16[272,512]{1,0:T(8,128)(2,1)S(1)} %collective-permute-done.18.refs_14_), channel_id=1, source_target_pairs={{0,4},{4,0},{8,12},{12,8},{16,20},{20,16},{24,28},{28,24},{1,5},{5... | collective-permute-start | bytes 835592 | tf_op jit(solution)/shard_map/ppermute | solution.py:53
  66.2 11.6 %copy-start.17 = (bf16[256,512]{1,0:T(8,128)(2,1)}, bf16[256,512]{1,0:T(8,128)(2,1)S(1)}, u32[]{:S(2)}) copy-start(bf16[256,512]{1,0:T(8,128)(2,1)S(1)} %collective-permute-done.11.refs_6_) | copy-start | bytes 786436
  66.3 11.4 %collective-permute-start.12 = (bf16[256,512]{1,0:T(8,128)(2,1)S(1)}, bf16[256,512]{1,0:T(8,128)(2,1)S(1)}, u32[]{:S(2)}, u32[]{:S(2)}) collective-permute-start(bf16[256,512]{1,0:T(8,128)(2,1)S(1)} %collective-permute-done.11.refs_6_), channel_id=1, source_target_pairs={{0,4},{4,0},{8,12},{12,8},{16,20},{20,16},{24,28},{28,24},{1,5},{5... | collective-permute-start | bytes 786440 | tf_op jit(solution)/shard_map/ppermute | solution.py:53
  71.5 6.3 %copy-start.18 = (bf16[256,512]{1,0:T(8,128)(2,1)}, bf16[256,512]{1,0:T(8,128)(2,1)S(1)}, u32[]{:S(2)}) copy-start(bf16[256,512]{1,0:T(8,128)(2,1)S(1)} %collective-permute-done.13.refs_8_) | copy-start | bytes 786436
  71.5 6.2 %collective-permute-start.14 = (bf16[256,512]{1,0:T(8,128)(2,1)S(1)}, bf16[256,512]{1,0:T(8,128)(2,1)S(1)}, u32[]{:S(2)}, u32[]{:S(2)}) collective-permute-start(bf16[256,512]{1,0:T(8,128)(2,1)S(1)} %collective-permute-done.13.refs_8_), channel_id=1, source_target_pairs={{0,4},{4,0},{8,12},{12,8},{16,20},{20,16},{24,28},{28,24},{1,5},{5... | collective-permute-start | bytes 786440 | tf_op jit(solution)/shard_map/ppermute | solution.py:53
  77.7 0.7 copy-start.19
  77.7 0.8 copy-start.20
  77.7 0.8 copy-start.13
  77.8 0.9 copy-start.14
  78.7 0.7 copy-start.15
Sparse Core Ops, SparseCore 0:
  9.6 30.6 all-gather.1
  43.1 26.6 reduce-scatter.1

commit v3 on v2

--- a/solution.py
+++ b/solution.py
@@ -12,13 +12,17 @@
 HOPS = 2
 SCALE = HDIM ** (-0.5)
 CUBE = (0, 1, 2, 3, 6, 7)
+PAIR = (0, 1, 2, -2, -1)
 NT = (((1,), (1,)), ((), ()))
 VMEM = pl.BlockSpec(memory_space=pltpu.VMEM)
 SMEM = pl.BlockSpec(memory_space=pltpu.SMEM)
 ANY = pl.BlockSpec(memory_space=pl.ANY)
 HBM = pl.BlockSpec(memory_space=pltpu.HBM)
 NEVER = 1e30
-PARAMS = pltpu.CompilerParams(vmem_limit_bytes=60 * 1024 * 1024)
+
+
+def params(mebibytes):
+    return pltpu.CompilerParams(vmem_limit_bytes=mebibytes * 1024 * 1024)
 
 
 def ndot(a, b):
@@ -33,34 +37,37 @@
     return -(-2 * pairs // 16) * 16
 
 
-def window_tags(size):
-    return CUBE if size == 8 else tuple([0] + [o for o in range(-HOPS, HOPS + 1) if o != 0])
-
-
-def tag_owner(position, tag, size):
-    return position ^ tag if size == 8 else lax.rem(position + tag + size, size)
-
-
-def find_shard(position, owner, size):
+def tag_owner(position, tag, size, tags):
+    if tags is CUBE:
+        return position ^ tag
+    return lax.rem(position + jnp.where(position % 2 == 0, tag, -tag) + size, size)
+
+
+def find_shard(position, owner, size, tags):
     shard = 0
-    for index, tag in enumerate(window_tags(size)):
-        shard = shard + jnp.where(tag_owner(position, tag, size) == owner, index, 0)
+    for index, tag in enumerate(tags):
+        shard = shard + jnp.where(tag_owner(position, tag, size, tags) == owner, index, 0)
     return shard
 
 
-def exchange(x, size, forward=False):
-    def move(v, pairs):
-        return lax.ppermute(v, "ctx", pairs)
-
-    if size == 8:
-        flip = lambda mask: [(i, i ^ mask) for i in range(size)]
-        near = move(x, flip(2))
-        far = move(near, flip(4)) if forward else move(x, flip(6))
-        mate = move(x, flip(1))
-        return [x, mate, near, move(near, flip(1)), far, move(far, flip(1))]
-    return [x] + [
-        move(x, [(i, (i - tag) % size) for i in range(size)]) for tag in window_tags(size)[1:]
-    ]
+def permute_from(x, size, source):
+    return lax.ppermute(x, "ctx", [(source(i) % size, i) for i in range(size)])
+
+
+def exchange_pair(x, size):
+    sign = lambda i: 1 if i % 2 == 0 else -1
+    share = permute_from(x, size, lambda i: i + 2 * sign(i))
+    solo = permute_from(x, size, lambda i: i - 2 * sign(i))
+    mate = permute_from(x, size, lambda i: i ^ 1)
+    return [x, mate, share, solo, permute_from(share, size, lambda i: i ^ 1)]
+
+
+def exchange_cube(x, size):
+    near = permute_from(x, size, lambda i: i ^ 2)
+    far = permute_from(near, size, lambda i: i ^ 4)
+    mate = permute_from(x, size, lambda i: i ^ 1)
+    swap = lambda i: i ^ 1
+    return [x, mate, near, permute_from(near, size, swap), far, permute_from(far, size, swap)]
 
 
 def start_all(pairs, sem, first=0):
@@ -77,13 +84,13 @@
         copy.wait()
 
 
-def gather_blocks(size, keys, refs, target, sem, first, blocks_dev, neigh):
+def gather_blocks(size, tags, keys, refs, target, sem, first, blocks_dev, neigh):
     position = lax.axis_index("ctx")
     waits = []
     for b in range(blocks_dev):
         for n in range(neigh):
             j = keys[b, n]
-            shard = find_shard(position, lax.div(j, blocks_dev), size)
+            shard = find_shard(position, lax.div(j, blocks_dev), size, tags)
             row = pl.multiple_of(lax.rem(j, blocks_dev) * BLK, BLK)
             place = b * neigh + n
             for index, ref in enumerate(refs):
@@ -113,13 +120,18 @@
     return shift
 
 
-def attend_kernel(size, nsh, *refs):
+def piece_owner(me, step, groups, sign):
+    return me ^ step if groups == 4 else lax.rem(me + sign * step + groups, groups)
+
+
+def attend_kernel(size, groups, v_tags, *refs):
     keys_hbm, hosts_hbm, bias_hbm, q_hbm, w_hbm = refs[:5]
-    k_refs = refs[5:5 + nsh]
-    v_refs = refs[5 + nsh:5 + 2 * nsh]
-    rest = refs[5 + 2 * nsh:]
-    mixed_ref, o32_ref, lse_ref = rest[:3]
-    keys, hosts, bias, q_ref, w_ref, kcat, vcat, score, att, sem = rest[3:]
+    k_refs = refs[5:5 + len(PAIR)]
+    v_refs = refs[5 + len(PAIR):5 + len(PAIR) + len(v_tags)]
+    rest = refs[5 + len(PAIR) + len(v_tags):]
+    part_refs = rest[:groups]
+    o32_ref, lse_ref = rest[groups:groups + 2]
+    keys, hosts, bias, q_ref, w_ref, kcat, vcat, score, att, turned, sem = rest[groups + 2:]
     rows, columns = q_ref.shape
     blocks_dev, neigh = keys.shape
     heads_dev = columns // HDIM
@@ -127,8 +139,8 @@
     large = start_all([(q_hbm, q_ref), (w_hbm, w_ref)], sem, 3)
     wait_all(small)
     places = blocks_dev * neigh
-    k_waits = gather_blocks(size, keys, k_refs, kcat, sem, 5, blocks_dev, neigh)
-    v_waits = gather_blocks(size, keys, v_refs, vcat, sem, 5 + places, blocks_dev, neigh)
+    k_waits = gather_blocks(size, PAIR, keys, k_refs, kcat, sem, 5, blocks_dev, neigh)
+    v_waits = gather_blocks(size, v_tags, keys, v_refs, vcat, sem, 5 + places, blocks_dev, neigh)
     large[0].wait()
     wait_all(k_waits)
     span = neigh * BLK
@@ -153,16 +165,51 @@
         lse_all = jnp.where(lane == b * heads_dev + h, top + jnp.log(total), lse_all)
     lse_ref[...] = lse_all
     large[1].wait()
-    mixed_ref[...] = ndot(att[...], w_ref[...]).astype(jnp.bfloat16)
-
-
-def upstream_kernel(*refs):
-    keys_hbm, w_hbm, grads_any, o32_ref, lse_ref, up_ref, stats_ref, keys, w_ref, grads, sem = refs
+    me = lax.axis_index("head")
+    part = rows // groups
+    for step in range(groups):
+        owner = piece_owner(me, step, groups, 1)
+        turned[step * part:(step + 1) * part, :] = att[pl.ds(pl.multiple_of(owner * part, part), part), :]
+    mixed = ndot(turned[...], w_ref[...]).astype(jnp.bfloat16)
+    for step in range(groups):
+        part_refs[step][...] = mixed[step * part:(step + 1) * part, :]
+
+
+def upstream_kernel(groups, *refs):
+    keys_hbm, w_hbm, own_hbm, o32_ref, lse_ref = refs[:5]
+    piece_refs = refs[5:4 + groups]
+    rest = refs[4 + groups + len(PAIR):]
+    up_ref, stats_ref, keys, w_ref, grads, sem = rest
     rows, columns = o32_ref.shape
+    width = w_ref.shape[1]
     blocks_dev, neigh = keys.shape
     heads_dev = columns // HDIM
-    wait_all(start_all([(w_hbm, w_ref), (keys_hbm, keys), (grads_any, grads)], sem))
-    up_ref[0:rows, :] = tdot(grads[...], w_ref[...]).astype(jnp.bfloat16)
+    part = rows // groups
+    cut = width // 4
+    w_waits = [
+        start_all([(w_hbm.at[:, c * cut:(c + 1) * cut], w_ref.at[:, c * cut:(c + 1) * cut])], sem, c)[0]
+        for c in range(4)
+    ]
+    pieces = (own_hbm,) + tuple(piece_refs)
+    wait_all(
+        start_all(
+            [(ref, grads.at[pl.ds(step * part, part)]) for step, ref in enumerate(pieces)]
+            + [(keys_hbm, keys)],
+            sem,
+            4,
+        )
+    )
+    total = jnp.zeros((rows, columns), jnp.float32)
+    for c in range(4):
+        w_waits[c].wait()
+        total = total + tdot(grads[:, c * cut:(c + 1) * cut], w_ref[:, c * cut:(c + 1) * cut])
+    me = lax.axis_index("head")
+    product = total.astype(jnp.bfloat16)
+    for step in range(groups):
+        owner = piece_owner(me, step, groups, -1)
+        up_ref[pl.ds(pl.multiple_of(owner * part, part), part), :] = product[
+            step * part:(step + 1) * part, :
+        ]
     pairs = blocks_dev * heads_dev
     lane = lax.broadcasted_iota(jnp.int32, (BLK, BLK), 1)
     stats = lse_ref[...]
@@ -195,11 +242,11 @@
         up_ref[row:row + high, col:col + BLK] = piece
 
 
-def query_kernel(size, nsh, *refs):
+def query_kernel(size, v_tags, *refs):
     keys_hbm, hosts_hbm, bias_hbm, q_hbm, up_ref, stats_ref = refs[:6]
-    k_refs = refs[6:6 + nsh]
-    v_refs = refs[6 + nsh:6 + 2 * nsh]
-    dq_ref, keys, hosts, bias, q_ref, kcat, vcat, sem = refs[6 + 2 * nsh:]
+    k_refs = refs[6:6 + len(PAIR)]
+    v_refs = refs[6 + len(PAIR):6 + len(PAIR) + len(v_tags)]
+    dq_ref, keys, hosts, bias, q_ref, kcat, vcat, sem = refs[6 + len(PAIR) + len(v_tags):]
     rows, columns = q_ref.shape
     blocks_dev, neigh = keys.shape
     heads_dev = columns // HDIM
@@ -208,8 +255,8 @@
     large = start_all([(q_hbm, q_ref)], sem, 3)
     wait_all(small)
     places = blocks_dev * neigh
-    waits = gather_blocks(size, keys, k_refs, kcat, sem, 4, blocks_dev, neigh)
-    waits += gather_blocks(size, keys, v_refs, vcat, sem, 4 + places, blocks_dev, neigh)
+    waits = gather_blocks(size, PAIR, keys, k_refs, kcat, sem, 4, blocks_dev, neigh)
+    waits += gather_blocks(size, v_tags, keys, v_refs, vcat, sem, 4 + places, blocks_dev, neigh)
     wait_all(large)
     wait_all(waits)
     span = neigh * BLK
@@ -229,7 +276,8 @@
             dq_ref[b * BLK:(b + 1) * BLK, cols] = ndot(ds, k).astype(jnp.bfloat16)
 
 
-def key_kernel(size, nsh, neigh, *refs):
+def key_kernel(size, neigh, *refs):
+    nsh = len(PAIR)
     hosts_hbm, bias_hbm, k_hbm, v_hbm = refs[:4]
     q_refs = refs[4:4 + nsh]
     up_refs = refs[4 + nsh:4 + 2 * nsh]
@@ -299,8 +347,8 @@
                 shard = lax.div(entry, blocks_dev)
                 inner = lax.rem(entry, blocks_dev)
                 owner = 0
-                for index, tag in enumerate(window_tags(size)):
-                    owner = owner + jnp.where(shard == index, tag_owner(position, tag, size), 0)
+                for index, tag in enumerate(PAIR):
+                    owner = owner + jnp.where(shard == index, tag_owner(position, tag, size, PAIR), 0)
                 sames.append(hosts[owner * blocks_dev + inner] == hosts[mine])
                 qs.append(pl.ds(pl.multiple_of(shard * rows + inner * BLK, BLK), BLK))
                 ups.append(pl.ds(pl.multiple_of(shard * long_rows + inner * BLK, 16), BLK))
@@ -334,6 +382,23 @@
     dv_ref[...] = dv_acc[...].astype(jnp.bfloat16)
 
 
+def copy_kernel(count, extra, *refs):
+    wait_all(start_all(list(zip(refs[:count], refs[count + extra:2 * count + extra])), refs[-1]))
+
+
+def copies_after(arrays, before):
+    return pl.pallas_call(
+        functools.partial(copy_kernel, len(arrays), len(before)),
+        out_shape=[jax.ShapeDtypeStruct(x.shape, x.dtype) for x in arrays],
+        in_specs=[ANY] * (len(arrays) + len(before)),
+        out_specs=[ANY] * len(arrays),
+        scratch_shapes=[pltpu.SemaphoreType.DMA((len(arrays),))],
+        compiler_params=params(60),
+        cost_estimate=cost(1000, 1000),
+        name="copies_after",
+    )(*arrays, *before)
+
+
 def cost(flops, nbytes):
     return pl.CostEstimate(flops=flops, bytes_accessed=nbytes, transcendentals=0)
 
@@ -348,32 +413,44 @@
     heads_dev = columns // HDIM
     pairs = blocks_dev * heads_dev
     places = blocks_dev * neigh
-    nsh = len(window_tags(size))
+    groups = lax.axis_size("head")
+    part = rows // groups
+    v_tags = CUBE if size == 8 else PAIR
+    nsh = len(PAIR)
     bf16, f32, i32 = jnp.bfloat16, jnp.float32, jnp.int32
     high = stat_rows(pairs)
     extra = high * (-(-4 * BLK // columns))
     long_rows = rows + extra
 
-    all_grads = lax.all_gather(grad_mixed, "head", axis=0, tiled=True)
-    v_win = exchange(value_states, size, forward=True)
-    k_win = exchange(key_states, size)
-    late_query, _ = lax.optimization_barrier((query_states, v_win[2]))
-    q_win = exchange(late_query, size)
+    def ring(x, step):
+        return lax.ppermute(x, "head", [(i, (i + step) % groups) for i in range(groups)])
+
+    def flip(x, mask):
+        return lax.ppermute(x, "head", [(i, i ^ mask) for i in range(groups)])
+
+    paired = groups == 4
+    v_win = exchange_cube(value_states, size) if v_tags is CUBE else exchange_pair(value_states, size)
+    k_win = exchange_pair(key_states, size)
+    if paired:
+        opposite = flip(grad_mixed, 2)
+        beside = flip(grad_mixed, 1)
+        pieces = [grad_mixed, beside, opposite, flip(opposite, 1)]
+    else:
+        pieces = [grad_mixed] + [ring(grad_mixed, step) for step in range(1, groups)]
+    (late_query,) = copies_after((query_states,), tuple(pieces[1:3]))
+    q_win = exchange_pair(late_query, size)
     scalars = [
         pltpu.SMEM(key_blocks.shape, i32),
         pltpu.SMEM(host_ids.shape, i32),
         pltpu.SMEM(host_bias.shape, f32),
     ]
 
-    share, o32, lse = pl.pallas_call(
-        functools.partial(attend_kernel, size, nsh),
-        out_shape=[
-            jax.ShapeDtypeStruct((rows, width), bf16),
-            jax.ShapeDtypeStruct((rows, columns), f32),
-            jax.ShapeDtypeStruct((BLK, BLK), f32),
-        ],
-        in_specs=[HBM] * 5 + ([HBM] + [ANY] * (nsh - 1)) * 2,
-        out_specs=[VMEM] * 3,
+    parts_o32_lse = pl.pallas_call(
+        functools.partial(attend_kernel, size, groups, v_tags),
+        out_shape=[jax.ShapeDtypeStruct((part, width), bf16)] * groups
+        + [jax.ShapeDtypeStruct((rows, columns), f32), jax.ShapeDtypeStruct((BLK, BLK), f32)],
+        in_specs=[HBM] * 5 + [ANY] * (len(PAIR) + len(v_tags)),
+        out_specs=[VMEM] * (groups + 2),
         scratch_shapes=scalars
         + [
             pltpu.VMEM((rows, columns), bf16),
@@ -382,38 +459,48 @@
             pltpu.VMEM((places * BLK, columns), bf16),
             pltpu.VMEM((pairs, BLK, neigh * BLK), f32),
             pltpu.VMEM((rows, columns), bf16),
+            pltpu.VMEM((rows, columns), bf16),
             pltpu.SemaphoreType.DMA((5 + 2 * places,)),
         ],
-        compiler_params=PARAMS,
-        cost_estimate=cost(1000, 1000),
+        compiler_params=params(60),
+        cost_estimate=cost(4 * 10**9, 8 * 10**6),
         name="attend",
     )(key_blocks, host_ids, host_bias, query_states, out_weight, *k_win, *v_win)
-    mixed_out = lax.psum_scatter(share, "head", scatter_dimension=0, tiled=True)
+    parts = parts_o32_lse[:groups]
+    o32, lse = parts_o32_lse[groups:]
+    mixed = parts[0].astype(f32)
+    if paired:
+        relay = flip(parts[3], 1)
+        beside_sum = flip(parts[1], 1)
+        passed = (parts[2].astype(f32) + relay.astype(f32)).astype(bf16)
+        arrived = [beside_sum, flip(passed, 2)]
+    else:
+        arrived = [ring(parts[step], step) for step in range(1, groups)]
 
     up, stats = pl.pallas_call(
-        upstream_kernel,
+        functools.partial(upstream_kernel, groups),
         out_shape=[
             jax.ShapeDtypeStruct((long_rows, columns), bf16),
             jax.ShapeDtypeStruct((BLK, BLK), f32),
         ],
-        in_specs=[HBM] * 2 + [ANY] + [VMEM] * 2,
+        in_specs=[HBM] * 3 + [VMEM] * 2 + [ANY] * (groups - 1 + len(PAIR)),
         out_specs=[VMEM] * 2,
         scratch_shapes=[
             pltpu.SMEM(key_blocks.shape, i32),
             pltpu.VMEM((columns, width), bf16),
             pltpu.VMEM((rows, width), bf16),
-            pltpu.SemaphoreType.DMA((3,)),
+            pltpu.SemaphoreType.DMA((5 + groups,)),
         ],
-        compiler_params=PARAMS,
-        cost_estimate=cost(1000, 1000),
+        compiler_params=params(60),
+        cost_estimate=cost(6 * 10**9, 6 * 10**6),
         name="upstream",
-    )(key_blocks, out_weight, all_grads, o32, lse)
-    up_win = exchange(up, size)
+    )(key_blocks, out_weight, grad_mixed, o32, lse, *pieces[1:], *q_win)
+    up_win = exchange_pair(up, size)
 
     grad_query = pl.pallas_call(
-        functools.partial(query_kernel, size, nsh),
+        functools.partial(query_kernel, size, v_tags),
         out_shape=jax.ShapeDtypeStruct((rows, columns), bf16),
-        in_specs=[HBM] * 4 + [VMEM] * 2 + ([HBM] + [ANY] * (nsh - 1)) * 2,
+        in_specs=[HBM] * 4 + [VMEM] * 2 + [ANY] * (len(PAIR) + len(v_tags)),
         out_specs=VMEM,
         scratch_shapes=scalars
         + [
@@ -422,13 +509,13 @@
             pltpu.VMEM((places * BLK, columns), bf16),
             pltpu.SemaphoreType.DMA((4 + 2 * places,)),
         ],
-        compiler_params=PARAMS,
-        cost_estimate=cost(1000, 1000),
+        compiler_params=params(60),
+        cost_estimate=cost(10**9, 10**6),
         name="query_grad",
     )(key_blocks, host_ids, host_bias, query_states, up, stats, *k_win, *v_win)
 
     grad_key, grad_value = pl.pallas_call(
-        functools.partial(key_kernel, size, nsh, neigh),
+        functools.partial(key_kernel, size, neigh),
         out_shape=[jax.ShapeDtypeStruct((rows, columns), bf16)] * 2,
         in_specs=[HBM] * 5 + [ANY] * (2 * nsh - 1),
         out_specs=[VMEM] * 2,
@@ -447,12 +534,14 @@
             pltpu.VMEM((rows, columns), f32),
             pltpu.SemaphoreType.DMA((3 * nsh + 5,)),
         ],
-        compiler_params=PARAMS,
-        cost_estimate=cost(1000, 1000),
+        compiler_params=params(60),
+        cost_estimate=cost(10**9, 10**6),
         name="key_grad",
     )(host_ids, host_bias, key_states, value_states, query_states, *q_win[1:], *up_win)
 
-    return (mixed_out, grad_query, grad_key, grad_value)
+    for piece in arrived:
+        mixed = mixed + piece.astype(f32)
+    return (mixed.astype(bf16), grad_query, grad_key, grad_value)
 
 
 def solution(mesh):

time: 94.1 us -> 80 us (0.85)
  waiting for transfers between devices: 39.6 us -> 18.1 us
  between operations: 14.3 us -> 0.91 us
  starting transfers between devices: 13.7 us -> 23.3 us
  Pallas kernels: 23.7 us -> 32.1 us
  local copies, waits for them, and re-layouts: 2.5 us -> 3.83 us
    ppermute x20 -> x23, waiting for transfers between devices: 37.1 us -> 18.1 us  [the longest x17 12.6 us: permute_from(): return lax.ppermute(x, 'ctx', [(source(i) % size, i) for i in range(size)])]
    ppermute x20 -> x23, starting transfers between devices: 13.6 us -> 23.3 us  [the longest x17 14.5 us: permute_from(): return lax.ppermute(x, 'ctx', [(source(i) % size, i) for i in range(size)])]
    pallas_call x4 -> x5, Pallas kernels: 23.7 us -> 32.1 us  [the longest x1 9.05 us: copies_after(): pl.pallas_call(functools.partial(copy_kernel, len(arrays), len(before)),...]
    all_gather x1 -> x0, waiting for transfers between devices: 1.77 us -> none  [per_device(): all_grads = lax.all_gather(grad_mixed, 'head', axis=0, tiled=True)]
    unnamed x42 -> x44, local copies, waits for them, and re-layouts: 2.5 us -> 3.83 us
  transfers between devices with their start and end apart: 22 -> 23, of which waited for: 11 -> 5; matrix products, arithmetic and copies ran while one was open for 0% -> 1% of each run, Pallas kernels for 25% -> 32%
where the time goes in v3:
time: 80 us; the launch traced here: 79.1 us
  Pallas kernels  32.1 us (40%)
  starting transfers between devices  23.3 us (29%)
  waiting for transfers between devices  18.1 us (23%)
  local copies, waits for them, and re-layouts  3.83 us (5%)
  between operations  0.91 us (1%)
  other arithmetic  0.86 us (1%)
    ppermute x17, starting transfers between devices, permute_from(): return lax.ppermute(x, 'ctx', [(source(i) % size, i) for i in range(size)])  14.5 us
    ppermute x17, waiting for transfers between devices, permute_from(): return lax.ppermute(x, 'ctx', [(source(i) % size, i) for i in range(size)])  12.6 us
    pallas_call x1, Pallas kernels, copies_after(): pl.pallas_call(functools.partial(copy_kernel, len(arrays), len(before)),...  9.05 us
    ppermute x6, starting transfers between devices, flip(): return lax.ppermute(x, 'head', [(i, i ^ mask) for i in range(groups)])  8.79 us
    pallas_call x1, Pallas kernels, per_device(): pl.pallas_call(functools.partial(key_kernel, size, neigh), out_shape=[jax...  6.44 us
    pallas_call x1, Pallas kernels, per_device(): pl.pallas_call(functools.partial(query_kernel, size, v_tags), out_shape=j...  6.16 us
    ppermute x6, waiting for transfers between devices, flip(): return lax.ppermute(x, 'head', [(i, i ^ mask) for i in range(groups)])  5.56 us
    pallas_call x1, Pallas kernels, per_device(): pl.pallas_call(functools.partial(attend_kernel, size, groups, v_tags), ou...  5.46 us
  transfers between devices with their start and end apart: 23, of which 5 were waited for; matrix products, arithmetic and copies ran while one was open for 1% of the time, Pallas kernels for 32%

profile of v3, /device:TPU:0, one launch (start us, length us, event | category | flops | bytes accessed | tf_op | source)
XLA Modules:
  0.0 79.1 jit_solution(10283922770041146287)
XLA Ops:
  0.6 3.9 %collective-permute-start.1 = (bf16[256,512]{1,0:T(8,128)(2,1)}, bf16[256,512]{1,0:T(8,128)(2,1)S(1)}, u32[]{:S(2)}, u32[]{:S(2)}) collective-permute-start(bf16[256,512]{1,0:T(8,128)(2,1)} %refs_2_.7), channel_id=1, source_target_pairs={{8,0},{28,4},{16,8},{4,12},{24,16},{12,20},{0,24},{20,28},{9,1},{2... | collective-permute-start | bytes 786440 | tf_op jit(solution)/shard_map/ppermute | solution.py:54
  4.6 1.6 %collective-permute-start.12 = (bf16[64,2048]{1,0:T(8,128)(2,1)}, bf16[64,2048]{1,0:T(8,128)(2,1)S(1)}, u32[]{:S(2)}, u32[]{:S(2)}) collective-permute-start(bf16[64,2048]{1,0:T(8,128)(2,1)} %refs_2_.5), channel_id=1, source_target_pairs={{0,1},{1,0},{2,3},{3,2},{4,5},{5,4},{6,7},{7,6},{8,9},{9,8},{10,11... | collective-permute-start | bytes 786440 | tf_op jit(solution)/shard_map/ppermute | solution.py:429
  6.2 2.6 %collective-permute-start.13 = (bf16[64,2048]{1,0:T(8,128)(2,1)}, bf16[64,2048]{1,0:T(8,128)(2,1)S(1)}, u32[]{:S(2)}, u32[]{:S(2)}) collective-permute-start(bf16[64,2048]{1,0:T(8,128)(2,1)} %refs_2_.5), channel_id=1, source_target_pairs={{0,2},{1,3},{2,0},{3,1},{4,6},{5,7},{6,4},{7,5},{8,10},{9,11},{10,... | collective-permute-start | bytes 786440 | tf_op jit(solution)/shard_map/ppermute | solution.py:429
  8.7 2.9 %collective-permute-done.1.refs_7_.refs_8_ = bf16[256,512]{1,0:T(8,128)(2,1)S(1)} collective-permute-done((bf16[256,512]{1,0:T(8,128)(2,1)}, bf16[256,512]{1,0:T(8,128)(2,1)S(1)}, u32[]{:S(2)}, u32[]{:S(2)}) %collective-permute-start.1) | collective-permute-done | bytes 262176 | tf_op jit(solution)/shard_map/ppermute | solution.py:54
  11.7 2.3 %collective-permute-start.2 = (bf16[256,512]{1,0:T(8,128)(2,1)}, bf16[256,512]{1,0:T(8,128)(2,1)S(1)}, u32[]{:S(2)}, u32[]{:S(2)}) collective-permute-start(bf16[256,512]{1,0:T(8,128)(2,1)} %refs_2_.7), channel_id=1, source_target_pairs={{24,0},{12,4},{0,8},{20,12},{8,16},{28,20},{16,24},{4,28},{25,1},{... | collective-permute-start | bytes 786440 | tf_op jit(solution)/shard_map/ppermute | solution.py:54
  13.9 3.4 %collective-permute-done.5.refs_12_.refs_13_ = bf16[256,512]{1,0:T(8,128)(2,1)S(1)} collective-permute-done((bf16[256,512]{1,0:T(8,128)(2,1)}, bf16[256,512]{1,0:T(8,128)(2,1)S(1)}, u32[]{:S(2)}, u32[]{:S(2)}) %collective-permute-start.5) | collective-permute-done | bytes 262176 | tf_op jit(solution)/shard_map/ppermute | solution.py:54
  17.3 1.4 %collective-permute-start.7 = (bf16[256,512]{1,0:T(8,128)(2,1)S(1)}, bf16[256,512]{1,0:T(8,128)(2,1)S(1)}, u32[]{:S(2)}, u32[]{:S(2)}) collective-permute-start(bf16[256,512]{1,0:T(8,128)(2,1)S(1)} %collective-permute-done.5.refs_12_.refs_13_), channel_id=1, source_target_pairs={{16,0},{20,4},{24,8},{28,12},{0,16},{4,20},{8,24},{12,28},{17,1},{... | collective-permute-start | bytes 786440 | tf_op jit(solution)/shard_map/ppermute | solution.py:54
  18.7 0.0 collective-permute-done.12.refs_1_.refs_5_
  18.7 0.0 collective-permute-start.4
  18.7 2.0 %collective-permute-done.13.refs_2_.refs_6_ = bf16[64,2048]{1,0:T(8,128)(2,1)S(1)} collective-permute-done((bf16[64,2048]{1,0:T(8,128)(2,1)}, bf16[64,2048]{1,0:T(8,128)(2,1)S(1)}, u32[]{:S(2)}, u32[]{:S(2)}) %collective-permute-start.13) | collective-permute-done | bytes 262176 | tf_op jit(solution)/shard_map/ppermute | solution.py:429
  20.7 0.0 collective-permute-start.3
  20.7 0.7 copy-done.11
  21.4 9.0 %copies_after.1.refs_8_ = bf16[256,512]{1,0:T(8,128)(2,1)} custom-call(bf16[256,512]{1,0:T(8,128)(2,1)} %refs_4_.3, bf16[64,2048]{1,0:T(8,128)(2,1)} %copy-done.10, bf16[64,2048]{1,0:T(8,128)(2,1)} %copy-done.11), custom_call_target="tpu_custom_call" | custom-call | flops 1000 | bytes 1000 | tf_op jit(solution)/shard_map/copies_after/pallas_call | solution.py:390
  30.4 0.0 collective-permute-done.refs_6_.refs_7_
  30.5 0.0 copy-start.2
  30.5 0.1 collective-permute-start.6
  30.5 0.0 collective-permute-done.2.refs_8_.refs_9_
  30.6 0.0 copy-start.3
  30.6 1.5 %collective-permute-start.16 = (bf16[256,512]{1,0:T(8,128)(2,1)}, bf16[256,512]{1,0:T(8,128)(2,1)S(1)}, u32[]{:S(2)}, u32[]{:S(2)}) collective-permute-start(bf16[256,512]{1,0:T(8,128)(2,1)} %copies_after.1.refs_8_), channel_id=1, source_target_pairs={{8,0},{28,4},{16,8},{4,12},{24,16},{12,20},{0,24},{20,28},{9,1},{2... | collective-permute-start | bytes 786440 | tf_op jit(solution)/shard_map/ppermute | solution.py:54
  32.1 0.0 collective-permute-start.8
  32.1 0.5 collective-permute-start.15
  32.6 0.0 collective-permute-done.3.refs_9_.refs_10_
  32.6 0.5 collective-permute-start.17
  33.2 0.0 collective-permute-done.6.refs_13_.refs_14_
  33.2 0.5 collective-permute-start.14
  33.7 6.3 %collective-permute-done.16.refs_10_.refs_6_ = bf16[256,512]{1,0:T(8,128)(2,1)S(1)} collective-permute-done((bf16[256,512]{1,0:T(8,128)(2,1)}, bf16[256,512]{1,0:T(8,128)(2,1)S(1)}, u32[]{:S(2)}, u32[]{:S(2)}) %collective-permute-start.16) | collective-permute-done | bytes 262176 | tf_op jit(solution)/shard_map/ppermute | solution.py:54
  39.9 0.4 collective-permute-start.18
  40.4 0.0 collective-permute-done.8.refs_15_.refs_16_
  40.5 0.7 copy-done.8
  41.2 5.5 %attend.1 = (bf16[64,2048]{1,0:T(8,128)(2,1)}, bf16[64,2048]{1,0:T(8,128)(2,1)}, bf16[64,2048]{1,0:T(8,128)(2,1)}, bf16[64,2048]{1,0:T(8,128)(2,1)}, f32[256,512]{1,0:T(8,128)}, /*index=5*/f32[128,128]{1,0:T(8,128)}) custom-call(s32[2,4]{1,0:T(2,128)} %refs_0_.8, s32[16]{0:T(128)} %refs_0_.9, f32[4]{0:T(128)} %refs_1_.7, bf16[256,512]{1,0:T(8,128)(2,1)} %refs_4_.3, ...), custom_call_target="tpu_custom_call" | custom-call | flops 4000000000 | bytes 8000000 | tf_op jit(solution)/shard_map/attend/pallas_call | solution.py:448
  46.7 0.5 collective-permute-start.10
  47.1 1.6 %collective-permute-start.9 = (bf16[64,2048]{1,0:T(8,128)(2,1)}, bf16[64,2048]{1,0:T(8,128)(2,1)S(1)}, u32[]{:S(2)}, u32[]{:S(2)}) collective-permute-start(bf16[64,2048]{1,0:T(8,128)(2,1)} %get-tuple-element.15), channel_id=1, source_target_pairs={{0,1},{1,0},{2,3},{3,2},{4,5},{5,4},{6,7},{7,6},{8,9},{9,8},{10,11... | collective-permute-start | bytes 786440 | tf_op jit(solution)/shard_map/ppermute | solution.py:429
  48.8 0.7 copy-done.18
  49.5 0.1 copy-done.19
  49.6 0.1 copy-done.20
  49.7 5.0 %upstream.1 = (bf16[272,512]{1,0:T(8,128)(2,1)}, f32[128,128]{1,0:T(8,128)}) custom-call(s32[2,4]{1,0:T(2,128)} %refs_0_.8, bf16[512,2048]{1,0:T(8,128)(2,1)} %refs_1_.5, bf16[64,2048]{1,0:T(8,128)(2,1)} %refs_2_.5, f32[256,512]{1,0:T(8,128)} %get-tuple-element.18.refs_3_, f32[128,128]{1,0:T(8,128)} %get-tuple-element.19.refs_4_, ...), custom_call_target="tpu_custom_call" | custom-call | flops 6000000000 | bytes 6000000 | tf_op jit(solution)/shard_map/upstream/pallas_call | solution.py:480
  54.7 2.1 %collective-permute-start.20 = (bf16[272,512]{1,0:T(8,128)(2,1)}, bf16[272,512]{1,0:T(8,128)(2,1)S(1)}, u32[]{:S(2)}, u32[]{:S(2)}) collective-permute-start(bf16[272,512]{1,0:T(8,128)(2,1)} %get-tuple-element.20.refs_4_.refs_9_), channel_id=1, source_target_pairs={{8,0},{28,4},{16,8},{4,12},{24,16},{12,20},{0,24},{20,28},{9,1},{2... | collective-permute-start | bytes 835592 | tf_op jit(solution)/shard_map/ppermute | solution.py:54
  56.8 0.1 add_convert_fusion.1
  56.9 2.0 %collective-permute-start.11 = (bf16[64,2048]{1,0:T(8,128)(2,1)S(1)}, bf16[64,2048]{1,0:T(8,128)(2,1)S(1)}, u32[]{:S(2)}, u32[]{:S(2)}) collective-permute-start(bf16[64,2048]{1,0:T(8,128)(2,1)S(1)} %add_convert_fusion.1), channel_id=1, source_target_pairs={{0,2},{1,3},{2,0},{3,1},{4,6},{5,7},{6,4},{7,5},{8,10},{9,11},{10,... | collective-permute-start | bytes 786440 | tf_op jit(solution)/shard_map/ppermute | solution.py:429
  59.0 0.2 collective-permute-start.21
  59.1 6.2 %query_grad.1 = bf16[256,512]{1,0:T(8,128)(2,1)} custom-call(s32[2,4]{1,0:T(2,128)} %refs_0_.8, s32[16]{0:T(128)} %refs_0_.9, f32[4]{0:T(128)} %refs_1_.7, bf16[256,512]{1,0:T(8,128)(2,1)} %refs_4_.3, bf16[272,512]{1,0:T(8,128)(2,1)} %get-tuple-element.20.refs_4_.refs_9_, f32[128,128]{1,0:T(8,128)} %get-tuple-element.21.refs_5_, bf16[256,512]{1,0:T(8,128)(2,1)} %refs_2_.7, ...), custom_call_target="tpu_custom_call" | custom-call | flops 1000000000 | bytes 1000000 | tf_op jit(solution)/shard_map/query_grad/pallas_call | solution.py:500
  65.3 1.4 %collective-permute-start.22 = (bf16[272,512]{1,0:T(8,128)(2,1)S(1)}, bf16[272,512]{1,0:T(8,128)(2,1)S(1)}, u32[]{:S(2)}, u32[]{:S(2)}) collective-permute-start(bf16[272,512]{1,0:T(8,128)(2,1)S(1)} %collective-permute-done.20.refs_11_), channel_id=1, source_target_pairs={{4,0},{0,4},{12,8},{8,12},{20,16},{16,20},{28,24},{24,28},{5,1},{1... | collective-permute-start | bytes 835592 | tf_op jit(solution)/shard_map/ppermute | solution.py:54
  66.7 3.6 %collective-permute-done.11 = bf16[64,2048]{1,0:T(8,128)(2,1)S(1)} collective-permute-done((bf16[64,2048]{1,0:T(8,128)(2,1)S(1)}, bf16[64,2048]{1,0:T(8,128)(2,1)S(1)}, u32[]{:S(2)}, u32[]{:S(2)}) %collective-permute-start.11) | collective-permute-done | bytes 262176 | tf_op jit(solution)/shard_map/ppermute | solution.py:429
  70.3 0.8 %add_convert_fusion = bf16[64,2048]{1,0:T(8,128)(2,1)} fusion(bf16[64,2048]{1,0:T(8,128)(2,1)S(1)} %collective-permute-done.11, bf16[64,2048]{1,0:T(8,128)(2,1)S(1)} %collective-permute-done.9, bf16[64,2048]{1,0:T(8,128)(2,1)S(1)} %copy-done.12), kind=kLoop, calls=%fused_computation | loop fusion | flops 786432 | bytes 1048576 | tf_op jit(solution)/shard_map/convert_element_type | solution.py:544
  71.1 0.7 copy-done.14
  71.8 0.1 copy-done.15
  71.9 0.7 copy-done.16
  72.6 6.4 %key_grad.1 = (bf16[256,512]{1,0:T(8,128)(2,1)}, bf16[256,512]{1,0:T(8,128)(2,1)}) custom-call(s32[16]{0:T(128)} %refs_0_.9, f32[4]{0:T(128)} %refs_1_.7, bf16[256,512]{1,0:T(8,128)(2,1)} %refs_2_.7, bf16[256,512]{1,0:T(8,128)(2,1)} %refs_3_.5, bf16[256,512]{1,0:T(8,128)(2,1)} %refs_4_.3, bf16[256,512]{1,0:T(8,128)(2,1)} %copy-done.18, ...), custom_call_target="tpu_custom_call" | custom-call | flops 1000000000 | bytes 1000000 | tf_op jit(solution)/shard_map/key_grad/pallas_call | solution.py:517
  (49 shorter events, 0.1 us)
Async XLA Ops:
  0.6 11.0 %collective-permute-start.1 = (bf16[256,512]{1,0:T(8,128)(2,1)}, bf16[256,512]{1,0:T(8,128)(2,1)S(1)}, u32[]{:S(2)}, u32[]{:S(2)}) collective-permute-start(bf16[256,512]{1,0:T(8,128)(2,1)} %refs_2_.7), channel_id=1, source_target_pairs={{8,0},{28,4},{16,8},{4,12},{24,16},{12,20},{0,24},{20,28},{9,1},{2... | collective-permute-start | bytes 786440 | tf_op jit(solution)/shard_map/ppermute | solution.py:54
  4.6 12.7 %collective-permute-start.5 = (bf16[256,512]{1,0:T(8,128)(2,1)}, bf16[256,512]{1,0:T(8,128)(2,1)S(1)}, u32[]{:S(2)}, u32[]{:S(2)}) collective-permute-start(bf16[256,512]{1,0:T(8,128)(2,1)} %refs_3_.5), channel_id=1, source_target_pairs={{8,0},{12,4},{0,8},{4,12},{24,16},{28,20},{16,24},{20,28},{9,1},{1... | collective-permute-start | bytes 786440 | tf_op jit(solution)/shard_map/ppermute | solution.py:54
  4.6 14.1 %collective-permute-start.12 = (bf16[64,2048]{1,0:T(8,128)(2,1)}, bf16[64,2048]{1,0:T(8,128)(2,1)S(1)}, u32[]{:S(2)}, u32[]{:S(2)}) collective-permute-start(bf16[64,2048]{1,0:T(8,128)(2,1)} %refs_2_.5), channel_id=1, source_target_pairs={{0,1},{1,0},{2,3},{3,2},{4,5},{5,4},{6,7},{7,6},{8,9},{9,8},{10,11... | collective-permute-start | bytes 786440 | tf_op jit(solution)/shard_map/ppermute | solution.py:429
  6.2 14.5 %collective-permute-start.13 = (bf16[64,2048]{1,0:T(8,128)(2,1)}, bf16[64,2048]{1,0:T(8,128)(2,1)S(1)}, u32[]{:S(2)}, u32[]{:S(2)}) collective-permute-start(bf16[64,2048]{1,0:T(8,128)(2,1)} %refs_2_.5), channel_id=1, source_target_pairs={{0,2},{1,3},{2,0},{3,1},{4,6},{5,7},{6,4},{7,5},{8,10},{9,11},{10,... | collective-permute-start | bytes 786440 | tf_op jit(solution)/shard_map/ppermute | solution.py:429
  8.7 21.7 %collective-permute-start = (bf16[256,512]{1,0:T(8,128)(2,1)}, bf16[256,512]{1,0:T(8,128)(2,1)S(1)}, u32[]{:S(2)}, u32[]{:S(2)}) collective-permute-start(bf16[256,512]{1,0:T(8,128)(2,1)} %refs_2_.7), channel_id=1, source_target_pairs={{4,0},{0,4},{12,8},{8,12},{20,16},{16,20},{28,24},{24,28},{5,1},{1... | collective-permute-start | bytes 786440 | tf_op jit(solution)/shard_map/ppermute | solution.py:54
  11.7 28.7 %copy-start = (bf16[256,512]{1,0:T(8,128)(2,1)}, bf16[256,512]{1,0:T(8,128)(2,1)S(1)}, u32[]{:S(2)}) copy-start(bf16[256,512]{1,0:T(8,128)(2,1)S(1)} %collective-permute-done.1.refs_7_.refs_8_) | copy-start | bytes 786436
  11.7 18.9 %collective-permute-start.2 = (bf16[256,512]{1,0:T(8,128)(2,1)}, bf16[256,512]{1,0:T(8,128)(2,1)S(1)}, u32[]{:S(2)}, u32[]{:S(2)}) collective-permute-start(bf16[256,512]{1,0:T(8,128)(2,1)} %refs_2_.7), channel_id=1, source_target_pairs={{24,0},{12,4},{0,8},{20,12},{8,16},{28,20},{16,24},{4,28},{25,1},{... | collective-permute-start | bytes 786440 | tf_op jit(solution)/shard_map/ppermute | solution.py:54
  17.3 23.1 %copy-start.1 = (bf16[256,512]{1,0:T(8,128)(2,1)}, bf16[256,512]{1,0:T(8,128)(2,1)S(1)}, u32[]{:S(2)}) copy-start(bf16[256,512]{1,0:T(8,128)(2,1)S(1)} %collective-permute-done.5.refs_12_.refs_13_) | copy-start | bytes 786436
  17.3 14.8 %collective-permute-start.7 = (bf16[256,512]{1,0:T(8,128)(2,1)S(1)}, bf16[256,512]{1,0:T(8,128)(2,1)S(1)}, u32[]{:S(2)}, u32[]{:S(2)}) collective-permute-start(bf16[256,512]{1,0:T(8,128)(2,1)S(1)} %collective-permute-done.5.refs_12_.refs_13_), channel_id=1, source_target_pairs={{16,0},{20,4},{24,8},{28,12},{0,16},{4,20},{8,24},{12,28},{17,1},{... | collective-permute-start | bytes 786440 | tf_op jit(solution)/shard_map/ppermute | solution.py:54
  18.7 2.0 %copy-start.10 = (bf16[64,2048]{1,0:T(8,128)(2,1)}, bf16[64,2048]{1,0:T(8,128)(2,1)S(1)}, u32[]{:S(2)}) copy-start(bf16[64,2048]{1,0:T(8,128)(2,1)S(1)} %collective-permute-done.12.refs_1_.refs_5_) | copy-start | bytes 786436
  18.7 13.4 %collective-permute-start.4 = (bf16[256,512]{1,0:T(8,128)(2,1)}, bf16[256,512]{1,0:T(8,128)(2,1)S(1)}, u32[]{:S(2)}, u32[]{:S(2)}) collective-permute-start(bf16[256,512]{1,0:T(8,128)(2,1)} %refs_3_.5), channel_id=1, source_target_pairs={{4,0},{0,4},{12,8},{8,12},{20,16},{16,20},{28,24},{24,28},{5,1},{1... | collective-permute-start | bytes 786440 | tf_op jit(solution)/shard_map/ppermute | solution.py:54
  20.7 0.7 copy-start.11
  20.7 11.9 %collective-permute-start.3 = (bf16[256,512]{1,0:T(8,128)(2,1)S(1)}, bf16[256,512]{1,0:T(8,128)(2,1)S(1)}, u32[]{:S(2)}, u32[]{:S(2)}) collective-permute-start(bf16[256,512]{1,0:T(8,128)(2,1)S(1)} %collective-permute-done.1.refs_7_.refs_8_), channel_id=1, source_target_pairs={{4,0},{0,4},{12,8},{8,12},{20,16},{16,20},{28,24},{24,28},{5,1},{1... | collective-permute-start | bytes 786440 | tf_op jit(solution)/shard_map/ppermute | solution.py:54
  30.5 10.0 %copy-start.2 = (bf16[256,512]{1,0:T(8,128)(2,1)}, bf16[256,512]{1,0:T(8,128)(2,1)S(1)}, u32[]{:S(2)}) copy-start(bf16[256,512]{1,0:T(8,128)(2,1)S(1)} %collective-permute-done.refs_6_.refs_7_) | copy-start | bytes 786436
  30.5 2.7 %collective-permute-start.6 = (bf16[256,512]{1,0:T(8,128)(2,1)S(1)}, bf16[256,512]{1,0:T(8,128)(2,1)S(1)}, u32[]{:S(2)}, u32[]{:S(2)}) collective-permute-start(bf16[256,512]{1,0:T(8,128)(2,1)S(1)} %collective-permute-done.5.refs_12_.refs_13_), channel_id=1, source_target_pairs={{4,0},{0,4},{12,8},{8,12},{20,16},{16,20},{28,24},{24,28},{5,1},{1... | collective-permute-start | bytes 786440 | tf_op jit(solution)/shard_map/ppermute | solution.py:54
  30.6 9.9 %copy-start.3 = (bf16[256,512]{1,0:T(8,128)(2,1)}, bf16[256,512]{1,0:T(8,128)(2,1)S(1)}, u32[]{:S(2)}) copy-start(bf16[256,512]{1,0:T(8,128)(2,1)S(1)} %collective-permute-done.2.refs_8_.refs_9_) | copy-start | bytes 786436
  30.6 9.4 %collective-permute-start.16 = (bf16[256,512]{1,0:T(8,128)(2,1)}, bf16[256,512]{1,0:T(8,128)(2,1)S(1)}, u32[]{:S(2)}, u32[]{:S(2)}) collective-permute-start(bf16[256,512]{1,0:T(8,128)(2,1)} %copies_after.1.refs_8_), channel_id=1, source_target_pairs={{8,0},{28,4},{16,8},{4,12},{24,16},{12,20},{0,24},{20,28},{9,1},{2... | collective-permute-start | bytes 786440 | tf_op jit(solution)/shard_map/ppermute | solution.py:54
  32.1 8.3 %copy-start.4 = (bf16[256,512]{1,0:T(8,128)(2,1)}, bf16[256,512]{1,0:T(8,128)(2,1)S(1)}, u32[]{:S(2)}) copy-start(bf16[256,512]{1,0:T(8,128)(2,1)S(1)} %collective-permute-done.7.refs_14_.refs_15_) | copy-start | bytes 786436
  32.1 8.3 %collective-permute-start.8 = (bf16[256,512]{1,0:T(8,128)(2,1)S(1)}, bf16[256,512]{1,0:T(8,128)(2,1)S(1)}, u32[]{:S(2)}, u32[]{:S(2)}) collective-permute-start(bf16[256,512]{1,0:T(8,128)(2,1)S(1)} %collective-permute-done.7.refs_14_.refs_15_), channel_id=1, source_target_pairs={{4,0},{0,4},{12,8},{8,12},{20,16},{16,20},{28,24},{24,28},{5,1},{1... | collective-permute-start | bytes 786440 | tf_op jit(solution)/shard_map/ppermute | solution.py:54
  32.1 8.3 %copy-start.5 = (bf16[256,512]{1,0:T(8,128)(2,1)}, bf16[256,512]{1,0:T(8,128)(2,1)S(1)}, u32[]{:S(2)}) copy-start(bf16[256,512]{1,0:T(8,128)(2,1)S(1)} %collective-permute-done.4.refs_11_.refs_12_) | copy-start | bytes 786436
  32.1 16.6 %collective-permute-start.15 = (bf16[256,512]{1,0:T(8,128)(2,1)}, bf16[256,512]{1,0:T(8,128)(2,1)S(1)}, u32[]{:S(2)}, u32[]{:S(2)}) collective-permute-start(bf16[256,512]{1,0:T(8,128)(2,1)} %copies_after.1.refs_8_), channel_id=1, source_target_pairs={{4,0},{0,4},{12,8},{8,12},{20,16},{16,20},{28,24},{24,28},{5,1},{1... | collective-permute-start | bytes 786440 | tf_op jit(solution)/shard_map/ppermute | solution.py:54
  32.6 7.8 %copy-start.6 = (bf16[256,512]{1,0:T(8,128)(2,1)}, bf16[256,512]{1,0:T(8,128)(2,1)S(1)}, u32[]{:S(2)}) copy-start(bf16[256,512]{1,0:T(8,128)(2,1)S(1)} %collective-permute-done.3.refs_9_.refs_10_) | copy-start | bytes 786436
  32.6 16.1 %collective-permute-start.17 = (bf16[256,512]{1,0:T(8,128)(2,1)}, bf16[256,512]{1,0:T(8,128)(2,1)S(1)}, u32[]{:S(2)}, u32[]{:S(2)}) collective-permute-start(bf16[256,512]{1,0:T(8,128)(2,1)} %copies_after.1.refs_8_), channel_id=1, source_target_pairs={{24,0},{12,4},{0,8},{20,12},{8,16},{28,20},{16,24},{4,28},{25,1},{... | collective-permute-start | bytes 786440 | tf_op jit(solution)/shard_map/ppermute | solution.py:54
  33.2 7.3 %copy-start.7 = (bf16[256,512]{1,0:T(8,128)(2,1)}, bf16[256,512]{1,0:T(8,128)(2,1)S(1)}, u32[]{:S(2)}) copy-start(bf16[256,512]{1,0:T(8,128)(2,1)S(1)} %collective-permute-done.6.refs_13_.refs_14_) | copy-start | bytes 786436
  33.2 14.0 %collective-permute-start.14 = (bf16[64,2048]{1,0:T(8,128)(2,1)}, bf16[64,2048]{1,0:T(8,128)(2,1)S(1)}, u32[]{:S(2)}, u32[]{:S(2)}) collective-permute-start(bf16[64,2048]{1,0:T(8,128)(2,1)} %copy-done.11), channel_id=1, source_target_pairs={{0,1},{1,0},{2,3},{3,2},{4,5},{5,4},{6,7},{7,6},{8,9},{9,8},{10,11... | collective-permute-start | bytes 786440 | tf_op jit(solution)/shard_map/ppermute | solution.py:429
  39.9 6.7 %copy-start.17 = (bf16[256,512]{1,0:T(8,128)(2,1)}, bf16[256,512]{1,0:T(8,128)(2,1)S(1)}, u32[]{:S(2)}) copy-start(bf16[256,512]{1,0:T(8,128)(2,1)S(1)} %collective-permute-done.16.refs_10_.refs_6_) | copy-start | bytes 786436
  39.9 8.8 %collective-permute-start.18 = (bf16[256,512]{1,0:T(8,128)(2,1)S(1)}, bf16[256,512]{1,0:T(8,128)(2,1)S(1)}, u32[]{:S(2)}, u32[]{:S(2)}) collective-permute-start(bf16[256,512]{1,0:T(8,128)(2,1)S(1)} %collective-permute-done.16.refs_10_.refs_6_), channel_id=1, source_target_pairs={{4,0},{0,4},{12,8},{8,12},{20,16},{16,20},{28,24},{24,28},{5,1},{1... | collective-permute-start | bytes 786440 | tf_op jit(solution)/shard_map/ppermute | solution.py:54
  40.5 0.7 copy-start.8
  46.7 10.2 %collective-permute-start.10 = (bf16[64,2048]{1,0:T(8,128)(2,1)}, bf16[64,2048]{1,0:T(8,128)(2,1)S(1)}, u32[]{:S(2)}, u32[]{:S(2)}) collective-permute-start(bf16[64,2048]{1,0:T(8,128)(2,1)} %get-tuple-element.17), channel_id=1, source_target_pairs={{0,1},{1,0},{2,3},{3,2},{4,5},{5,4},{6,7},{7,6},{8,9},{9,8},{10,11... | collective-permute-start | bytes 786440 | tf_op jit(solution)/shard_map/ppermute | solution.py:429
  47.1 1.7 %copy-start.21 = (bf16[64,2048]{1,0:T(8,128)(2,1)}, bf16[64,2048]{1,0:T(8,128)(2,1)S(1)}, u32[]{:S(2)}) copy-start(bf16[64,2048]{1,0:T(8,128)(2,1)S(1)} %collective-permute-done.14.refs_7_) | copy-start | bytes 786436
  47.1 19.6 %collective-permute-start.9 = (bf16[64,2048]{1,0:T(8,128)(2,1)}, bf16[64,2048]{1,0:T(8,128)(2,1)S(1)}, u32[]{:S(2)}, u32[]{:S(2)}) collective-permute-start(bf16[64,2048]{1,0:T(8,128)(2,1)} %get-tuple-element.15), channel_id=1, source_target_pairs={{0,1},{1,0},{2,3},{3,2},{4,5},{5,4},{6,7},{7,6},{8,9},{9,8},{10,11... | collective-permute-start | bytes 786440 | tf_op jit(solution)/shard_map/ppermute | solution.py:429
  48.8 0.7 copy-start.18
  48.8 0.8 %copy-start.19 = (bf16[256,512]{1,0:T(8,128)(2,1)}, bf16[256,512]{1,0:T(8,128)(2,1)S(1)}, u32[]{:S(2)}) copy-start(bf16[256,512]{1,0:T(8,128)(2,1)S(1)} %collective-permute-done.17.refs_11_.refs_7_) | copy-start | bytes 786436
  48.8 0.9 %copy-start.20 = (bf16[256,512]{1,0:T(8,128)(2,1)}, bf16[256,512]{1,0:T(8,128)(2,1)S(1)}, u32[]{:S(2)}) copy-start(bf16[256,512]{1,0:T(8,128)(2,1)S(1)} %collective-permute-done.18.refs_12_.refs_8_) | copy-start | bytes 786436
  49.7 7.1 %copy-start.9 = (bf16[64,2048]{1,0:T(8,128)(2,1)S(1)}, bf16[64,2048]{1,0:T(8,128)(2,1)}, u32[]{:S(2)}) copy-start(bf16[64,2048]{1,0:T(8,128)(2,1)} %get-tuple-element.16) | copy-start | bytes 786436
  54.7 10.6 %collective-permute-start.20 = (bf16[272,512]{1,0:T(8,128)(2,1)}, bf16[272,512]{1,0:T(8,128)(2,1)S(1)}, u32[]{:S(2)}, u32[]{:S(2)}) collective-permute-start(bf16[272,512]{1,0:T(8,128)(2,1)} %get-tuple-element.20.refs_4_.refs_9_), channel_id=1, source_target_pairs={{8,0},{28,4},{16,8},{4,12},{24,16},{12,20},{0,24},{20,28},{9,1},{2... | collective-permute-start | bytes 835592 | tf_op jit(solution)/shard_map/ppermute | solution.py:54
  56.8 13.5 %copy-start.12 = (bf16[64,2048]{1,0:T(8,128)(2,1)S(1)}, bf16[64,2048]{1,0:T(8,128)(2,1)}, u32[]{:S(2)}) copy-start(bf16[64,2048]{1,0:T(8,128)(2,1)} %get-tuple-element.14) | copy-start | bytes 786436
  56.9 13.4 %collective-permute-start.11 = (bf16[64,2048]{1,0:T(8,128)(2,1)S(1)}, bf16[64,2048]{1,0:T(8,128)(2,1)S(1)}, u32[]{:S(2)}, u32[]{:S(2)}) collective-permute-start(bf16[64,2048]{1,0:T(8,128)(2,1)S(1)} %add_convert_fusion.1), channel_id=1, source_target_pairs={{0,2},{1,3},{2,0},{3,1},{4,6},{5,7},{6,4},{7,5},{8,10},{9,11},{10,... | collective-permute-start | bytes 786440 | tf_op jit(solution)/shard_map/ppermute | solution.py:429
  59.0 12.2 %collective-permute-start.19 = (bf16[272,512]{1,0:T(8,128)(2,1)}, bf16[272,512]{1,0:T(8,128)(2,1)S(1)}, u32[]{:S(2)}, u32[]{:S(2)}) collective-permute-start(bf16[272,512]{1,0:T(8,128)(2,1)} %get-tuple-element.20.refs_4_.refs_9_), channel_id=1, source_target_pairs={{4,0},{0,4},{12,8},{8,12},{20,16},{16,20},{28,24},{24,28},{5,1},{1... | collective-permute-start | bytes 835592 | tf_op jit(solution)/shard_map/ppermute | solution.py:54
  59.0 12.2 %collective-permute-start.21 = (bf16[272,512]{1,0:T(8,128)(2,1)}, bf16[272,512]{1,0:T(8,128)(2,1)S(1)}, u32[]{:S(2)}, u32[]{:S(2)}) collective-permute-start(bf16[272,512]{1,0:T(8,128)(2,1)} %get-tuple-element.20.refs_4_.refs_9_), channel_id=1, source_target_pairs={{24,0},{12,4},{0,8},{20,12},{8,16},{28,20},{16,24},{4,28},{25,1},{... | collective-permute-start | bytes 835592 | tf_op jit(solution)/shard_map/ppermute | solution.py:54
  65.3 5.8 %copy-start.13 = (bf16[272,512]{1,0:T(8,128)(2,1)}, bf16[272,512]{1,0:T(8,128)(2,1)S(1)}, u32[]{:S(2)}) copy-start(bf16[272,512]{1,0:T(8,128)(2,1)S(1)} %collective-permute-done.20.refs_11_) | copy-start | bytes 835588
  65.3 5.8 %collective-permute-start.22 = (bf16[272,512]{1,0:T(8,128)(2,1)S(1)}, bf16[272,512]{1,0:T(8,128)(2,1)S(1)}, u32[]{:S(2)}, u32[]{:S(2)}) collective-permute-start(bf16[272,512]{1,0:T(8,128)(2,1)S(1)} %collective-permute-done.20.refs_11_), channel_id=1, source_target_pairs={{4,0},{0,4},{12,8},{8,12},{20,16},{16,20},{28,24},{24,28},{5,1},{1... | collective-permute-start | bytes 835592 | tf_op jit(solution)/shard_map/ppermute | solution.py:54
  71.1 0.7 copy-start.14
  71.1 0.8 %copy-start.15 = (bf16[272,512]{1,0:T(8,128)(2,1)}, bf16[272,512]{1,0:T(8,128)(2,1)S(1)}, u32[]{:S(2)}) copy-start(bf16[272,512]{1,0:T(8,128)(2,1)S(1)} %collective-permute-done.21.refs_12_) | copy-start | bytes 835588
  71.9 0.7 copy-start.16

commit v4 on v3

--- a/solution.py
+++ b/solution.py
@@ -178,7 +178,7 @@
 def upstream_kernel(groups, *refs):
     keys_hbm, w_hbm, own_hbm, o32_ref, lse_ref = refs[:5]
     piece_refs = refs[5:4 + groups]
-    rest = refs[4 + groups + len(PAIR):]
+    rest = refs[8 + groups:]
     up_ref, stats_ref, keys, w_ref, grads, sem = rest
     rows, columns = o32_ref.shape
     width = w_ref.shape[1]
@@ -246,7 +246,7 @@
     keys_hbm, hosts_hbm, bias_hbm, q_hbm, up_ref, stats_ref = refs[:6]
     k_refs = refs[6:6 + len(PAIR)]
     v_refs = refs[6 + len(PAIR):6 + len(PAIR) + len(v_tags)]
-    dq_ref, keys, hosts, bias, q_ref, kcat, vcat, sem = refs[6 + len(PAIR) + len(v_tags):]
+    dq_ref, keys, hosts, bias, q_ref, kcat, vcat, sem = refs[7 + len(PAIR) + len(v_tags):]
     rows, columns = q_ref.shape
     blocks_dev, neigh = keys.shape
     heads_dev = columns // HDIM
@@ -383,7 +383,10 @@
 
 
 def copy_kernel(count, extra, *refs):
-    wait_all(start_all(list(zip(refs[:count], refs[count + extra:2 * count + extra])), refs[-1]))
+    sources, targets = refs[:count], refs[count + extra:2 * count + extra]
+    between, sem = refs[2 * count + extra:-1], refs[-1]
+    wait_all(start_all(list(zip(sources, between)), sem))
+    wait_all(start_all(list(zip(between, targets)), sem))
 
 
 def copies_after(arrays, before):
@@ -392,7 +395,8 @@
         out_shape=[jax.ShapeDtypeStruct(x.shape, x.dtype) for x in arrays],
         in_specs=[ANY] * (len(arrays) + len(before)),
         out_specs=[ANY] * len(arrays),
-        scratch_shapes=[pltpu.SemaphoreType.DMA((len(arrays),))],
+        scratch_shapes=[pltpu.VMEM(x.shape, x.dtype) for x in arrays]
+        + [pltpu.SemaphoreType.DMA((len(arrays),))],
         compiler_params=params(60),
         cost_estimate=cost(1000, 1000),
         name="copies_after",
@@ -483,7 +487,7 @@
             jax.ShapeDtypeStruct((long_rows, columns), bf16),
             jax.ShapeDtypeStruct((BLK, BLK), f32),
         ],
-        in_specs=[HBM] * 3 + [VMEM] * 2 + [ANY] * (groups - 1 + len(PAIR)),
+        in_specs=[HBM] * 3 + [VMEM] * 2 + [ANY] * (groups + 3),
         out_specs=[VMEM] * 2,
         scratch_shapes=[
             pltpu.SMEM(key_blocks.shape, i32),
@@ -494,13 +498,13 @@
         compiler_params=params(60),
         cost_estimate=cost(6 * 10**9, 6 * 10**6),
         name="upstream",
-    )(key_blocks, out_weight, grad_mixed, o32, lse, *pieces[1:], *q_win)
+    )(key_blocks, out_weight, grad_mixed, o32, lse, *pieces[1:], *q_win[:4])
     up_win = exchange_pair(up, size)
 
     grad_query = pl.pallas_call(
         functools.partial(query_kernel, size, v_tags),
         out_shape=jax.ShapeDtypeStruct((rows, columns), bf16),
-        in_specs=[HBM] * 4 + [VMEM] * 2 + [ANY] * (len(PAIR) + len(v_tags)),
+        in_specs=[HBM] * 4 + [VMEM] * 2 + [ANY] * (len(PAIR) + len(v_tags) + 1),
         out_specs=VMEM,
         scratch_shapes=scalars
         + [
@@ -512,7 +516,7 @@
         compiler_params=params(60),
         cost_estimate=cost(10**9, 10**6),
         name="query_grad",
-    )(key_blocks, host_ids, host_bias, query_states, up, stats, *k_win, *v_win)
+    )(key_blocks, host_ids, host_bias, query_states, up, stats, *k_win, *v_win, q_win[4])
 
     grad_key, grad_value = pl.pallas_call(
         functools.partial(key_kernel, size, neigh),

time: 80 us -> 71.6 us (0.89)
  Pallas kernels: 32.1 us -> 23.7 us
  waiting for transfers between devices: 18.1 us -> 15.4 us
  starting transfers between devices: 23.3 us -> 25.6 us
    pallas_call x1, Pallas kernels: 9.05 us -> 1.65 us  [copies_after(): pl.pallas_call(functools.partial(copy_kernel, len(arrays), len(before)),...]
    ppermute x6, starting transfers between devices: 8.79 us -> 11.9 us  [flip(): return lax.ppermute(x, 'head', [(i, i ^ mask) for i in range(groups)])]
    ppermute x17, waiting for transfers between devices: 12.6 us -> 9.92 us  [permute_from(): return lax.ppermute(x, 'ctx', [(source(i) % size, i) for i in range(size)])]
    pallas_call x1, Pallas kernels: 6.44 us -> 5.54 us  [per_device(): pl.pallas_call(functools.partial(key_kernel, size, neigh), out_shape=[jax...]
  transfers between devices with their start and end apart: 23 -> 23, of which waited for: 5 -> 6; matrix products, arithmetic and copies ran while one was open for 1% -> 1% of each run, Pallas kernels for 32% -> 26%
where the time goes in v4:
time: 71.6 us; the launch traced here: 70.7 us
  starting transfers between devices  25.6 us (36%)
  Pallas kernels  23.7 us (33%)
  waiting for transfers between devices  15.4 us (22%)
  local copies, waits for them, and re-layouts  4.14 us (6%)
  between operations  0.93 us (1%)
  other arithmetic  0.86 us (1%)
    ppermute x17, starting transfers between devices, permute_from(): return lax.ppermute(x, 'ctx', [(source(i) % size, i) for i in range(size)])  13.7 us
    ppermute x6, starting transfers between devices, flip(): return lax.ppermute(x, 'head', [(i, i ^ mask) for i in range(groups)])  11.9 us
    ppermute x17, waiting for transfers between devices, permute_from(): return lax.ppermute(x, 'ctx', [(source(i) % size, i) for i in range(size)])  9.92 us
    pallas_call x1, Pallas kernels, per_device(): pl.pallas_call(functools.partial(query_kernel, size, v_tags), out_shape=j...  6.13 us
    pallas_call x1, Pallas kernels, per_device(): pl.pallas_call(functools.partial(key_kernel, size, neigh), out_shape=[jax...  5.54 us
    ppermute x6, waiting for transfers between devices, flip(): return lax.ppermute(x, 'head', [(i, i ^ mask) for i in range(groups)])  5.52 us
    pallas_call x1, Pallas kernels, per_device(): pl.pallas_call(functools.partial(attend_kernel, size, groups, v_tags), ou...  5.45 us
    pallas_call x1, Pallas kernels, per_device(): pl.pallas_call(functools.partial(upstream_kernel, groups), out_shape=[jax...  4.95 us
  transfers between devices with their start and end apart: 23, of which 6 were waited for; matrix products, arithmetic and copies ran while one was open for 1% of the time, Pallas kernels for 26%

profile of v4, /device:TPU:0, one launch (start us, length us, event | category | flops | bytes accessed | tf_op | source)
XLA Modules:
  0.0 70.7 jit_solution(12981919314964239047)
XLA Ops:
  0.6 3.9 %collective-permute-start.1 = (bf16[256,512]{1,0:T(8,128)(2,1)}, bf16[256,512]{1,0:T(8,128)(2,1)S(1)}, u32[]{:S(2)}, u32[]{:S(2)}) collective-permute-start(bf16[256,512]{1,0:T(8,128)(2,1)} %refs_2_.7), channel_id=1, source_target_pairs={{8,0},{28,4},{16,8},{4,12},{24,16},{12,20},{0,24},{20,28},{9,1},{2... | collective-permute-start | bytes 786440 | tf_op jit(solution)/shard_map/ppermute | solution.py:54
  4.6 0.0 collective-permute-start.5
  4.6 1.6 %collective-permute-start.12 = (bf16[64,2048]{1,0:T(8,128)(2,1)}, bf16[64,2048]{1,0:T(8,128)(2,1)S(1)}, u32[]{:S(2)}, u32[]{:S(2)}) collective-permute-start(bf16[64,2048]{1,0:T(8,128)(2,1)} %refs_2_.5), channel_id=1, source_target_pairs={{0,1},{1,0},{2,3},{3,2},{4,5},{5,4},{6,7},{7,6},{8,9},{9,8},{10,11... | collective-permute-start | bytes 786440 | tf_op jit(solution)/shard_map/ppermute | solution.py:433
  6.2 2.6 %collective-permute-start.13 = (bf16[64,2048]{1,0:T(8,128)(2,1)}, bf16[64,2048]{1,0:T(8,128)(2,1)S(1)}, u32[]{:S(2)}, u32[]{:S(2)}) collective-permute-start(bf16[64,2048]{1,0:T(8,128)(2,1)} %refs_2_.5), channel_id=1, source_target_pairs={{0,2},{1,3},{2,0},{3,1},{4,6},{5,7},{6,4},{7,5},{8,10},{9,11},{10,... | collective-permute-start | bytes 786440 | tf_op jit(solution)/shard_map/ppermute | solution.py:433
  8.7 0.0 collective-permute-start
  8.7 2.9 %collective-permute-done.1.refs_7_.refs_8_ = bf16[256,512]{1,0:T(8,128)(2,1)S(1)} collective-permute-done((bf16[256,512]{1,0:T(8,128)(2,1)}, bf16[256,512]{1,0:T(8,128)(2,1)S(1)}, u32[]{:S(2)}, u32[]{:S(2)}) %collective-permute-start.1) | collective-permute-done | bytes 262176 | tf_op jit(solution)/shard_map/ppermute | solution.py:54
  11.7 2.3 %collective-permute-start.2 = (bf16[256,512]{1,0:T(8,128)(2,1)}, bf16[256,512]{1,0:T(8,128)(2,1)S(1)}, u32[]{:S(2)}, u32[]{:S(2)}) collective-permute-start(bf16[256,512]{1,0:T(8,128)(2,1)} %refs_2_.7), channel_id=1, source_target_pairs={{24,0},{12,4},{0,8},{20,12},{8,16},{28,20},{16,24},{4,28},{25,1},{... | collective-permute-start | bytes 786440 | tf_op jit(solution)/shard_map/ppermute | solution.py:54
  13.9 3.4 %collective-permute-done.5.refs_12_.refs_13_ = bf16[256,512]{1,0:T(8,128)(2,1)S(1)} collective-permute-done((bf16[256,512]{1,0:T(8,128)(2,1)}, bf16[256,512]{1,0:T(8,128)(2,1)S(1)}, u32[]{:S(2)}, u32[]{:S(2)}) %collective-permute-start.5) | collective-permute-done | bytes 262176 | tf_op jit(solution)/shard_map/ppermute | solution.py:54
  17.3 1.4 %collective-permute-start.7 = (bf16[256,512]{1,0:T(8,128)(2,1)S(1)}, bf16[256,512]{1,0:T(8,128)(2,1)S(1)}, u32[]{:S(2)}, u32[]{:S(2)}) collective-permute-start(bf16[256,512]{1,0:T(8,128)(2,1)S(1)} %collective-permute-done.5.refs_12_.refs_13_), channel_id=1, source_target_pairs={{16,0},{20,4},{24,8},{28,12},{0,16},{4,20},{8,24},{12,28},{17,1},{... | collective-permute-start | bytes 786440 | tf_op jit(solution)/shard_map/ppermute | solution.py:54
  18.7 0.0 collective-permute-done.12.refs_1_.refs_5_
  18.7 0.0 collective-permute-start.4
  18.7 2.0 %collective-permute-done.13.refs_2_.refs_6_ = bf16[64,2048]{1,0:T(8,128)(2,1)S(1)} collective-permute-done((bf16[64,2048]{1,0:T(8,128)(2,1)}, bf16[64,2048]{1,0:T(8,128)(2,1)S(1)}, u32[]{:S(2)}, u32[]{:S(2)}) %collective-permute-start.13) | collective-permute-done | bytes 262176 | tf_op jit(solution)/shard_map/ppermute | solution.py:433
  20.7 0.0 collective-permute-start.3
  20.7 0.7 copy-done.12
  21.4 1.7 %copies_after.1.refs_8_ = bf16[256,512]{1,0:T(8,128)(2,1)} custom-call(bf16[256,512]{1,0:T(8,128)(2,1)} %refs_4_.3, bf16[64,2048]{1,0:T(8,128)(2,1)} %copy-done.11, bf16[64,2048]{1,0:T(8,128)(2,1)} %copy-done.12), custom_call_target="tpu_custom_call" | custom-call | flops 1000 | bytes 1000 | tf_op jit(solution)/shard_map/copies_after/pallas_call | solution.py:393
  23.0 0.0 collective-permute-done.refs_6_.refs_7_
  23.1 0.0 copy-start.2
  23.1 0.1 collective-permute-start.6
  23.1 0.0 collective-permute-done.2.refs_8_.refs_9_
  23.2 0.0 copy-start.3
  23.2 1.5 %collective-permute-start.16 = (bf16[256,512]{1,0:T(8,128)(2,1)}, bf16[256,512]{1,0:T(8,128)(2,1)S(1)}, u32[]{:S(2)}, u32[]{:S(2)}) collective-permute-start(bf16[256,512]{1,0:T(8,128)(2,1)} %copies_after.1.refs_8_), channel_id=1, source_target_pairs={{8,0},{28,4},{16,8},{4,12},{24,16},{12,20},{0,24},{20,28},{9,1},{2... | collective-permute-start | bytes 786440 | tf_op jit(solution)/shard_map/ppermute | solution.py:54
  24.7 2.6 %collective-permute-done.7.refs_14_.refs_15_ = bf16[256,512]{1,0:T(8,128)(2,1)S(1)} collective-permute-done((bf16[256,512]{1,0:T(8,128)(2,1)S(1)}, bf16[256,512]{1,0:T(8,128)(2,1)S(1)}, u32[]{:S(2)}, u32[]{:S(2)}) %collective-permute-start.7) | collective-permute-done | bytes 262176 | tf_op jit(solution)/shard_map/ppermute | solution.py:54
  27.3 0.0 collective-permute-start.8
  27.3 0.5 collective-permute-start.15
  27.8 0.0 collective-permute-done.3.refs_9_.refs_10_
  27.8 3.7 %collective-permute-start.14 = (bf16[64,2048]{1,0:T(8,128)(2,1)}, bf16[64,2048]{1,0:T(8,128)(2,1)S(1)}, u32[]{:S(2)}, u32[]{:S(2)}) collective-permute-start(bf16[64,2048]{1,0:T(8,128)(2,1)} %copy-done.12), channel_id=1, source_target_pairs={{0,1},{1,0},{2,3},{3,2},{4,5},{5,4},{6,7},{7,6},{8,9},{9,8},{10,11... | collective-permute-start | bytes 786440 | tf_op jit(solution)/shard_map/ppermute | solution.py:433
  31.5 1.0 %collective-permute-done.16.refs_10_.refs_6_ = bf16[256,512]{1,0:T(8,128)(2,1)S(1)} collective-permute-done((bf16[256,512]{1,0:T(8,128)(2,1)}, bf16[256,512]{1,0:T(8,128)(2,1)S(1)}, u32[]{:S(2)}, u32[]{:S(2)}) %collective-permute-start.16) | collective-permute-done | bytes 262176 | tf_op jit(solution)/shard_map/ppermute | solution.py:54
  32.5 0.1 collective-permute-start.18
  32.8 0.7 %copy-done.9 = bf16[256,512]{1,0:T(8,128)(2,1)} copy-done((bf16[256,512]{1,0:T(8,128)(2,1)}, bf16[256,512]{1,0:T(8,128)(2,1)S(1)}, u32[]{:S(2)}) %copy-start.9) | copy-done | bytes 262168
  33.5 5.5 %attend.1 = (bf16[64,2048]{1,0:T(8,128)(2,1)}, bf16[64,2048]{1,0:T(8,128)(2,1)}, bf16[64,2048]{1,0:T(8,128)(2,1)}, bf16[64,2048]{1,0:T(8,128)(2,1)}, f32[256,512]{1,0:T(8,128)}, /*index=5*/f32[128,128]{1,0:T(8,128)}) custom-call(s32[2,4]{1,0:T(2,128)} %refs_0_.8, s32[16]{0:T(128)} %refs_0_.9, f32[4]{0:T(128)} %refs_1_.7, bf16[256,512]{1,0:T(8,128)(2,1)} %refs_4_.3, ...), custom_call_target="tpu_custom_call" | custom-call | flops 4000000000 | bytes 8000000 | tf_op jit(solution)/shard_map/attend/pallas_call | solution.py:452
  38.9 0.1 collective-permute-start.10
  39.0 2.0 %collective-permute-start.9 = (bf16[64,2048]{1,0:T(8,128)(2,1)}, bf16[64,2048]{1,0:T(8,128)(2,1)S(1)}, u32[]{:S(2)}, u32[]{:S(2)}) collective-permute-start(bf16[64,2048]{1,0:T(8,128)(2,1)} %get-tuple-element.15), channel_id=1, source_target_pairs={{0,1},{1,0},{2,3},{3,2},{4,5},{5,4},{6,7},{7,6},{8,9},{9,8},{10,11... | collective-permute-start | bytes 786440 | tf_op jit(solution)/shard_map/ppermute | solution.py:433
  41.1 0.7 copy-done.19
  41.8 0.1 copy-done.20
  41.9 5.0 %upstream.1 = (bf16[272,512]{1,0:T(8,128)(2,1)}, f32[128,128]{1,0:T(8,128)}) custom-call(s32[2,4]{1,0:T(2,128)} %refs_0_.8, bf16[512,2048]{1,0:T(8,128)(2,1)} %refs_1_.5, bf16[64,2048]{1,0:T(8,128)(2,1)} %refs_2_.5, f32[256,512]{1,0:T(8,128)} %get-tuple-element.18.refs_3_, f32[128,128]{1,0:T(8,128)} %get-tuple-element.19.refs_4_, ...), custom_call_target="tpu_custom_call" | custom-call | flops 6000000000 | bytes 6000000 | tf_op jit(solution)/shard_map/upstream/pallas_call | solution.py:484
  46.8 2.4 %collective-permute-start.20 = (bf16[272,512]{1,0:T(8,128)(2,1)}, bf16[272,512]{1,0:T(8,128)(2,1)S(1)}, u32[]{:S(2)}, u32[]{:S(2)}) collective-permute-start(bf16[272,512]{1,0:T(8,128)(2,1)} %get-tuple-element.20.refs_4_.refs_9_), channel_id=1, source_target_pairs={{8,0},{28,4},{16,8},{4,12},{24,16},{12,20},{0,24},{20,28},{9,1},{2... | collective-permute-start | bytes 835592 | tf_op jit(solution)/shard_map/ppermute | solution.py:54
  49.3 0.1 add_convert_fusion.1
  49.4 1.9 %collective-permute-start.11 = (bf16[64,2048]{1,0:T(8,128)(2,1)S(1)}, bf16[64,2048]{1,0:T(8,128)(2,1)S(1)}, u32[]{:S(2)}, u32[]{:S(2)}) collective-permute-start(bf16[64,2048]{1,0:T(8,128)(2,1)S(1)} %add_convert_fusion.1), channel_id=1, source_target_pairs={{0,2},{1,3},{2,0},{3,1},{4,6},{5,7},{6,4},{7,5},{8,10},{9,11},{10,... | collective-permute-start | bytes 786440 | tf_op jit(solution)/shard_map/ppermute | solution.py:433
  51.3 0.3 collective-permute-start.21
  51.6 0.4 copy-done.8
  52.0 6.1 %query_grad.1 = bf16[256,512]{1,0:T(8,128)(2,1)} custom-call(s32[2,4]{1,0:T(2,128)} %refs_0_.8, s32[16]{0:T(128)} %refs_0_.9, f32[4]{0:T(128)} %refs_1_.7, bf16[256,512]{1,0:T(8,128)(2,1)} %refs_4_.3, bf16[272,512]{1,0:T(8,128)(2,1)} %get-tuple-element.20.refs_4_.refs_9_, f32[128,128]{1,0:T(8,128)} %get-tuple-element.21.refs_5_, bf16[256,512]{1,0:T(8,128)(2,1)} %refs_2_.7, ...), custom_call_target="tpu_custom_call" | custom-call | flops 1000000000 | bytes 1000000 | tf_op jit(solution)/shard_map/query_grad/pallas_call | solution.py:504
  58.2 1.0 %collective-permute-start.22 = (bf16[272,512]{1,0:T(8,128)(2,1)S(1)}, bf16[272,512]{1,0:T(8,128)(2,1)S(1)}, u32[]{:S(2)}, u32[]{:S(2)}) collective-permute-start(bf16[272,512]{1,0:T(8,128)(2,1)S(1)} %collective-permute-done.20.refs_11_), channel_id=1, source_target_pairs={{4,0},{0,4},{12,8},{8,12},{20,16},{16,20},{28,24},{24,28},{5,1},{1... | collective-permute-start | bytes 835592 | tf_op jit(solution)/shard_map/ppermute | solution.py:54
  59.2 3.5 %collective-permute-done.11 = bf16[64,2048]{1,0:T(8,128)(2,1)S(1)} collective-permute-done((bf16[64,2048]{1,0:T(8,128)(2,1)S(1)}, bf16[64,2048]{1,0:T(8,128)(2,1)S(1)}, u32[]{:S(2)}, u32[]{:S(2)}) %collective-permute-start.11) | collective-permute-done | bytes 262176 | tf_op jit(solution)/shard_map/ppermute | solution.py:433
  62.8 0.8 %add_convert_fusion = bf16[64,2048]{1,0:T(8,128)(2,1)} fusion(bf16[64,2048]{1,0:T(8,128)(2,1)S(1)} %collective-permute-done.11, bf16[64,2048]{1,0:T(8,128)(2,1)S(1)} %collective-permute-done.9, bf16[64,2048]{1,0:T(8,128)(2,1)S(1)} %copy-done.13), kind=kLoop, calls=%fused_computation | loop fusion | flops 786432 | bytes 1048576 | tf_op jit(solution)/shard_map/convert_element_type | solution.py:548
  63.6 0.7 copy-done.15
  64.3 0.1 copy-done.16
  64.4 0.7 %copy-done.17 = bf16[272,512]{1,0:T(8,128)(2,1)} copy-done((bf16[272,512]{1,0:T(8,128)(2,1)}, bf16[272,512]{1,0:T(8,128)(2,1)S(1)}, u32[]{:S(2)}) %copy-start.17) | copy-done | bytes 278552
  65.1 5.5 %key_grad.1 = (bf16[256,512]{1,0:T(8,128)(2,1)}, bf16[256,512]{1,0:T(8,128)(2,1)}) custom-call(s32[16]{0:T(128)} %refs_0_.9, f32[4]{0:T(128)} %refs_1_.7, bf16[256,512]{1,0:T(8,128)(2,1)} %refs_2_.7, bf16[256,512]{1,0:T(8,128)(2,1)} %refs_3_.5, bf16[256,512]{1,0:T(8,128)(2,1)} %refs_4_.3, bf16[256,512]{1,0:T(8,128)(2,1)} %copy-done.19, ...), custom_call_target="tpu_custom_call" | custom-call | flops 1000000000 | bytes 1000000 | tf_op jit(solution)/shard_map/key_grad/pallas_call | solution.py:521
  (49 shorter events, 0.1 us)
Async XLA Ops:
  0.6 11.0 %collective-permute-start.1 = (bf16[256,512]{1,0:T(8,128)(2,1)}, bf16[256,512]{1,0:T(8,128)(2,1)S(1)}, u32[]{:S(2)}, u32[]{:S(2)}) collective-permute-start(bf16[256,512]{1,0:T(8,128)(2,1)} %refs_2_.7), channel_id=1, source_target_pairs={{8,0},{28,4},{16,8},{4,12},{24,16},{12,20},{0,24},{20,28},{9,1},{2... | collective-permute-start | bytes 786440 | tf_op jit(solution)/shard_map/ppermute | solution.py:54
  4.6 12.7 %collective-permute-start.5 = (bf16[256,512]{1,0:T(8,128)(2,1)}, bf16[256,512]{1,0:T(8,128)(2,1)S(1)}, u32[]{:S(2)}, u32[]{:S(2)}) collective-permute-start(bf16[256,512]{1,0:T(8,128)(2,1)} %refs_3_.5), channel_id=1, source_target_pairs={{8,0},{12,4},{0,8},{4,12},{24,16},{28,20},{16,24},{20,28},{9,1},{1... | collective-permute-start | bytes 786440 | tf_op jit(solution)/shard_map/ppermute | solution.py:54
  4.6 14.1 %collective-permute-start.12 = (bf16[64,2048]{1,0:T(8,128)(2,1)}, bf16[64,2048]{1,0:T(8,128)(2,1)S(1)}, u32[]{:S(2)}, u32[]{:S(2)}) collective-permute-start(bf16[64,2048]{1,0:T(8,128)(2,1)} %refs_2_.5), channel_id=1, source_target_pairs={{0,1},{1,0},{2,3},{3,2},{4,5},{5,4},{6,7},{7,6},{8,9},{9,8},{10,11... | collective-permute-start | bytes 786440 | tf_op jit(solution)/shard_map/ppermute | solution.py:433
  6.2 14.5 %collective-permute-start.13 = (bf16[64,2048]{1,0:T(8,128)(2,1)}, bf16[64,2048]{1,0:T(8,128)(2,1)S(1)}, u32[]{:S(2)}, u32[]{:S(2)}) collective-permute-start(bf16[64,2048]{1,0:T(8,128)(2,1)} %refs_2_.5), channel_id=1, source_target_pairs={{0,2},{1,3},{2,0},{3,1},{4,6},{5,7},{6,4},{7,5},{8,10},{9,11},{10,... | collective-permute-start | bytes 786440 | tf_op jit(solution)/shard_map/ppermute | solution.py:433
  8.7 14.3 %collective-permute-start = (bf16[256,512]{1,0:T(8,128)(2,1)}, bf16[256,512]{1,0:T(8,128)(2,1)S(1)}, u32[]{:S(2)}, u32[]{:S(2)}) collective-permute-start(bf16[256,512]{1,0:T(8,128)(2,1)} %refs_2_.7), channel_id=1, source_target_pairs={{4,0},{0,4},{12,8},{8,12},{20,16},{16,20},{28,24},{24,28},{5,1},{1... | collective-permute-start | bytes 786440 | tf_op jit(solution)/shard_map/ppermute | solution.py:54
  11.7 21.0 %copy-start = (bf16[256,512]{1,0:T(8,128)(2,1)}, bf16[256,512]{1,0:T(8,128)(2,1)S(1)}, u32[]{:S(2)}) copy-start(bf16[256,512]{1,0:T(8,128)(2,1)S(1)} %collective-permute-done.1.refs_7_.refs_8_) | copy-start | bytes 786436
  11.7 11.5 %collective-permute-start.2 = (bf16[256,512]{1,0:T(8,128)(2,1)}, bf16[256,512]{1,0:T(8,128)(2,1)S(1)}, u32[]{:S(2)}, u32[]{:S(2)}) collective-permute-start(bf16[256,512]{1,0:T(8,128)(2,1)} %refs_2_.7), channel_id=1, source_target_pairs={{24,0},{12,4},{0,8},{20,12},{8,16},{28,20},{16,24},{4,28},{25,1},{... | collective-permute-start | bytes 786440 | tf_op jit(solution)/shard_map/ppermute | solution.py:54
  17.3 15.4 %copy-start.1 = (bf16[256,512]{1,0:T(8,128)(2,1)}, bf16[256,512]{1,0:T(8,128)(2,1)S(1)}, u32[]{:S(2)}) copy-start(bf16[256,512]{1,0:T(8,128)(2,1)S(1)} %collective-permute-done.5.refs_12_.refs_13_) | copy-start | bytes 786436
  17.3 10.0 %collective-permute-start.7 = (bf16[256,512]{1,0:T(8,128)(2,1)S(1)}, bf16[256,512]{1,0:T(8,128)(2,1)S(1)}, u32[]{:S(2)}, u32[]{:S(2)}) collective-permute-start(bf16[256,512]{1,0:T(8,128)(2,1)S(1)} %collective-permute-done.5.refs_12_.refs_13_), channel_id=1, source_target_pairs={{16,0},{20,4},{24,8},{28,12},{0,16},{4,20},{8,24},{12,28},{17,1},{... | collective-permute-start | bytes 786440 | tf_op jit(solution)/shard_map/ppermute | solution.py:54
  18.7 2.0 %copy-start.11 = (bf16[64,2048]{1,0:T(8,128)(2,1)}, bf16[64,2048]{1,0:T(8,128)(2,1)S(1)}, u32[]{:S(2)}) copy-start(bf16[64,2048]{1,0:T(8,128)(2,1)S(1)} %collective-permute-done.12.refs_1_.refs_5_) | copy-start | bytes 786436
  18.7 8.6 %collective-permute-start.4 = (bf16[256,512]{1,0:T(8,128)(2,1)}, bf16[256,512]{1,0:T(8,128)(2,1)S(1)}, u32[]{:S(2)}, u32[]{:S(2)}) collective-permute-start(bf16[256,512]{1,0:T(8,128)(2,1)} %refs_3_.5), channel_id=1, source_target_pairs={{4,0},{0,4},{12,8},{8,12},{20,16},{16,20},{28,24},{24,28},{5,1},{1... | collective-permute-start | bytes 786440 | tf_op jit(solution)/shard_map/ppermute | solution.py:54
  20.7 0.7 copy-start.12
  20.7 7.1 %collective-permute-start.3 = (bf16[256,512]{1,0:T(8,128)(2,1)S(1)}, bf16[256,512]{1,0:T(8,128)(2,1)S(1)}, u32[]{:S(2)}, u32[]{:S(2)}) collective-permute-start(bf16[256,512]{1,0:T(8,128)(2,1)S(1)} %collective-permute-done.1.refs_7_.refs_8_), channel_id=1, source_target_pairs={{4,0},{0,4},{12,8},{8,12},{20,16},{16,20},{28,24},{24,28},{5,1},{1... | collective-permute-start | bytes 786440 | tf_op jit(solution)/shard_map/ppermute | solution.py:54
  23.1 9.6 %copy-start.2 = (bf16[256,512]{1,0:T(8,128)(2,1)}, bf16[256,512]{1,0:T(8,128)(2,1)S(1)}, u32[]{:S(2)}) copy-start(bf16[256,512]{1,0:T(8,128)(2,1)S(1)} %collective-permute-done.refs_6_.refs_7_) | copy-start | bytes 786436
  23.1 4.8 %collective-permute-start.6 = (bf16[256,512]{1,0:T(8,128)(2,1)S(1)}, bf16[256,512]{1,0:T(8,128)(2,1)S(1)}, u32[]{:S(2)}, u32[]{:S(2)}) collective-permute-start(bf16[256,512]{1,0:T(8,128)(2,1)S(1)} %collective-permute-done.5.refs_12_.refs_13_), channel_id=1, source_target_pairs={{4,0},{0,4},{12,8},{8,12},{20,16},{16,20},{28,24},{24,28},{5,1},{1... | collective-permute-start | bytes 786440 | tf_op jit(solution)/shard_map/ppermute | solution.py:54
  23.2 9.5 %copy-start.3 = (bf16[256,512]{1,0:T(8,128)(2,1)}, bf16[256,512]{1,0:T(8,128)(2,1)S(1)}, u32[]{:S(2)}) copy-start(bf16[256,512]{1,0:T(8,128)(2,1)S(1)} %collective-permute-done.2.refs_8_.refs_9_) | copy-start | bytes 786436
  23.2 9.4 %collective-permute-start.16 = (bf16[256,512]{1,0:T(8,128)(2,1)}, bf16[256,512]{1,0:T(8,128)(2,1)S(1)}, u32[]{:S(2)}, u32[]{:S(2)}) collective-permute-start(bf16[256,512]{1,0:T(8,128)(2,1)} %copies_after.1.refs_8_), channel_id=1, source_target_pairs={{8,0},{28,4},{16,8},{4,12},{24,16},{12,20},{0,24},{20,28},{9,1},{2... | collective-permute-start | bytes 786440 | tf_op jit(solution)/shard_map/ppermute | solution.py:54
  27.3 5.4 %copy-start.4 = (bf16[256,512]{1,0:T(8,128)(2,1)}, bf16[256,512]{1,0:T(8,128)(2,1)S(1)}, u32[]{:S(2)}) copy-start(bf16[256,512]{1,0:T(8,128)(2,1)S(1)} %collective-permute-done.7.refs_14_.refs_15_) | copy-start | bytes 786436
  27.3 5.4 %collective-permute-start.8 = (bf16[256,512]{1,0:T(8,128)(2,1)S(1)}, bf16[256,512]{1,0:T(8,128)(2,1)S(1)}, u32[]{:S(2)}, u32[]{:S(2)}) collective-permute-start(bf16[256,512]{1,0:T(8,128)(2,1)S(1)} %collective-permute-done.7.refs_14_.refs_15_), channel_id=1, source_target_pairs={{4,0},{0,4},{12,8},{8,12},{20,16},{16,20},{28,24},{24,28},{5,1},{1... | collective-permute-start | bytes 786440 | tf_op jit(solution)/shard_map/ppermute | solution.py:54
  27.3 5.4 %copy-start.5 = (bf16[256,512]{1,0:T(8,128)(2,1)}, bf16[256,512]{1,0:T(8,128)(2,1)S(1)}, u32[]{:S(2)}) copy-start(bf16[256,512]{1,0:T(8,128)(2,1)S(1)} %collective-permute-done.4.refs_11_.refs_12_) | copy-start | bytes 786436
  27.3 13.7 %collective-permute-start.15 = (bf16[256,512]{1,0:T(8,128)(2,1)}, bf16[256,512]{1,0:T(8,128)(2,1)S(1)}, u32[]{:S(2)}, u32[]{:S(2)}) collective-permute-start(bf16[256,512]{1,0:T(8,128)(2,1)} %copies_after.1.refs_8_), channel_id=1, source_target_pairs={{4,0},{0,4},{12,8},{8,12},{20,16},{16,20},{28,24},{24,28},{5,1},{1... | collective-permute-start | bytes 786440 | tf_op jit(solution)/shard_map/ppermute | solution.py:54
  27.8 4.9 %copy-start.6 = (bf16[256,512]{1,0:T(8,128)(2,1)}, bf16[256,512]{1,0:T(8,128)(2,1)S(1)}, u32[]{:S(2)}) copy-start(bf16[256,512]{1,0:T(8,128)(2,1)S(1)} %collective-permute-done.3.refs_9_.refs_10_) | copy-start | bytes 786436
  27.8 13.3 %collective-permute-start.17 = (bf16[256,512]{1,0:T(8,128)(2,1)}, bf16[256,512]{1,0:T(8,128)(2,1)S(1)}, u32[]{:S(2)}, u32[]{:S(2)}) collective-permute-start(bf16[256,512]{1,0:T(8,128)(2,1)} %copies_after.1.refs_8_), channel_id=1, source_target_pairs={{24,0},{12,4},{0,8},{20,12},{8,16},{28,20},{16,24},{4,28},{25,1},{... | collective-permute-start | bytes 786440 | tf_op jit(solution)/shard_map/ppermute | solution.py:54
  27.8 4.9 %copy-start.7 = (bf16[256,512]{1,0:T(8,128)(2,1)}, bf16[256,512]{1,0:T(8,128)(2,1)S(1)}, u32[]{:S(2)}) copy-start(bf16[256,512]{1,0:T(8,128)(2,1)S(1)} %collective-permute-done.6.refs_13_.refs_14_) | copy-start | bytes 786436
  27.8 11.2 %collective-permute-start.14 = (bf16[64,2048]{1,0:T(8,128)(2,1)}, bf16[64,2048]{1,0:T(8,128)(2,1)S(1)}, u32[]{:S(2)}, u32[]{:S(2)}) collective-permute-start(bf16[64,2048]{1,0:T(8,128)(2,1)} %copy-done.12), channel_id=1, source_target_pairs={{0,1},{1,0},{2,3},{3,2},{4,5},{5,4},{6,7},{7,6},{8,9},{9,8},{10,11... | collective-permute-start | bytes 786440 | tf_op jit(solution)/shard_map/ppermute | solution.py:433
  32.5 6.4 %copy-start.18 = (bf16[256,512]{1,0:T(8,128)(2,1)}, bf16[256,512]{1,0:T(8,128)(2,1)S(1)}, u32[]{:S(2)}) copy-start(bf16[256,512]{1,0:T(8,128)(2,1)S(1)} %collective-permute-done.16.refs_10_.refs_6_) | copy-start | bytes 786436
  32.5 18.8 %collective-permute-start.18 = (bf16[256,512]{1,0:T(8,128)(2,1)S(1)}, bf16[256,512]{1,0:T(8,128)(2,1)S(1)}, u32[]{:S(2)}, u32[]{:S(2)}) collective-permute-start(bf16[256,512]{1,0:T(8,128)(2,1)S(1)} %collective-permute-done.16.refs_10_.refs_6_), channel_id=1, source_target_pairs={{4,0},{0,4},{12,8},{8,12},{20,16},{16,20},{28,24},{24,28},{5,1},{1... | collective-permute-start | bytes 786440 | tf_op jit(solution)/shard_map/ppermute | solution.py:54
  32.7 0.7 %copy-start.9 = (bf16[256,512]{1,0:T(8,128)(2,1)}, bf16[256,512]{1,0:T(8,128)(2,1)S(1)}, u32[]{:S(2)}) copy-start(bf16[256,512]{1,0:T(8,128)(2,1)S(1)} %collective-permute-done.8.refs_15_.refs_16_) | copy-start | bytes 786436
  38.9 10.4 %collective-permute-start.10 = (bf16[64,2048]{1,0:T(8,128)(2,1)}, bf16[64,2048]{1,0:T(8,128)(2,1)S(1)}, u32[]{:S(2)}, u32[]{:S(2)}) collective-permute-start(bf16[64,2048]{1,0:T(8,128)(2,1)} %get-tuple-element.17), channel_id=1, source_target_pairs={{0,1},{1,0},{2,3},{3,2},{4,5},{5,4},{6,7},{7,6},{8,9},{9,8},{10,11... | collective-permute-start | bytes 786440 | tf_op jit(solution)/shard_map/ppermute | solution.py:433
  39.0 2.1 %copy-start.21 = (bf16[64,2048]{1,0:T(8,128)(2,1)}, bf16[64,2048]{1,0:T(8,128)(2,1)S(1)}, u32[]{:S(2)}) copy-start(bf16[64,2048]{1,0:T(8,128)(2,1)S(1)} %collective-permute-done.14.refs_7_) | copy-start | bytes 786436
  39.0 20.2 %collective-permute-start.9 = (bf16[64,2048]{1,0:T(8,128)(2,1)}, bf16[64,2048]{1,0:T(8,128)(2,1)S(1)}, u32[]{:S(2)}, u32[]{:S(2)}) collective-permute-start(bf16[64,2048]{1,0:T(8,128)(2,1)} %get-tuple-element.15), channel_id=1, source_target_pairs={{0,1},{1,0},{2,3},{3,2},{4,5},{5,4},{6,7},{7,6},{8,9},{9,8},{10,11... | collective-permute-start | bytes 786440 | tf_op jit(solution)/shard_map/ppermute | solution.py:433
  41.1 0.7 %copy-start.19 = (bf16[256,512]{1,0:T(8,128)(2,1)}, bf16[256,512]{1,0:T(8,128)(2,1)S(1)}, u32[]{:S(2)}) copy-start(bf16[256,512]{1,0:T(8,128)(2,1)S(1)} %collective-permute-done.15.refs_9_.refs_5_) | copy-start | bytes 786436
  41.1 0.8 %copy-start.20 = (bf16[256,512]{1,0:T(8,128)(2,1)}, bf16[256,512]{1,0:T(8,128)(2,1)S(1)}, u32[]{:S(2)}) copy-start(bf16[256,512]{1,0:T(8,128)(2,1)S(1)} %collective-permute-done.17.refs_11_.refs_7_) | copy-start | bytes 786436
  41.9 7.4 %copy-start.10 = (bf16[64,2048]{1,0:T(8,128)(2,1)S(1)}, bf16[64,2048]{1,0:T(8,128)(2,1)}, u32[]{:S(2)}) copy-start(bf16[64,2048]{1,0:T(8,128)(2,1)} %get-tuple-element.16) | copy-start | bytes 786436
  46.8 11.3 %collective-permute-start.20 = (bf16[272,512]{1,0:T(8,128)(2,1)}, bf16[272,512]{1,0:T(8,128)(2,1)S(1)}, u32[]{:S(2)}, u32[]{:S(2)}) collective-permute-start(bf16[272,512]{1,0:T(8,128)(2,1)} %get-tuple-element.20.refs_4_.refs_9_), channel_id=1, source_target_pairs={{8,0},{28,4},{16,8},{4,12},{24,16},{12,20},{0,24},{20,28},{9,1},{2... | collective-permute-start | bytes 835592 | tf_op jit(solution)/shard_map/ppermute | solution.py:54
  49.4 13.4 %copy-start.13 = (bf16[64,2048]{1,0:T(8,128)(2,1)S(1)}, bf16[64,2048]{1,0:T(8,128)(2,1)}, u32[]{:S(2)}) copy-start(bf16[64,2048]{1,0:T(8,128)(2,1)} %get-tuple-element.14) | copy-start | bytes 786436
  49.4 13.4 %collective-permute-start.11 = (bf16[64,2048]{1,0:T(8,128)(2,1)S(1)}, bf16[64,2048]{1,0:T(8,128)(2,1)S(1)}, u32[]{:S(2)}, u32[]{:S(2)}) collective-permute-start(bf16[64,2048]{1,0:T(8,128)(2,1)S(1)} %add_convert_fusion.1), channel_id=1, source_target_pairs={{0,2},{1,3},{2,0},{3,1},{4,6},{5,7},{6,4},{7,5},{8,10},{9,11},{10,... | collective-permute-start | bytes 786440 | tf_op jit(solution)/shard_map/ppermute | solution.py:433
  51.3 12.3 %collective-permute-start.19 = (bf16[272,512]{1,0:T(8,128)(2,1)}, bf16[272,512]{1,0:T(8,128)(2,1)S(1)}, u32[]{:S(2)}, u32[]{:S(2)}) collective-permute-start(bf16[272,512]{1,0:T(8,128)(2,1)} %get-tuple-element.20.refs_4_.refs_9_), channel_id=1, source_target_pairs={{4,0},{0,4},{12,8},{8,12},{20,16},{16,20},{28,24},{24,28},{5,1},{1... | collective-permute-start | bytes 835592 | tf_op jit(solution)/shard_map/ppermute | solution.py:54
  51.3 0.7 copy-start.8
  51.3 12.2 %collective-permute-start.21 = (bf16[272,512]{1,0:T(8,128)(2,1)}, bf16[272,512]{1,0:T(8,128)(2,1)S(1)}, u32[]{:S(2)}, u32[]{:S(2)}) collective-permute-start(bf16[272,512]{1,0:T(8,128)(2,1)} %get-tuple-element.20.refs_4_.refs_9_), channel_id=1, source_target_pairs={{24,0},{12,4},{0,8},{20,12},{8,16},{28,20},{16,24},{4,28},{25,1},{... | collective-permute-start | bytes 835592 | tf_op jit(solution)/shard_map/ppermute | solution.py:54
  58.2 5.4 %copy-start.14 = (bf16[272,512]{1,0:T(8,128)(2,1)}, bf16[272,512]{1,0:T(8,128)(2,1)S(1)}, u32[]{:S(2)}) copy-start(bf16[272,512]{1,0:T(8,128)(2,1)S(1)} %collective-permute-done.20.refs_11_) | copy-start | bytes 835588
  58.2 5.4 %collective-permute-start.22 = (bf16[272,512]{1,0:T(8,128)(2,1)S(1)}, bf16[272,512]{1,0:T(8,128)(2,1)S(1)}, u32[]{:S(2)}, u32[]{:S(2)}) collective-permute-start(bf16[272,512]{1,0:T(8,128)(2,1)S(1)} %collective-permute-done.20.refs_11_), channel_id=1, source_target_pairs={{4,0},{0,4},{12,8},{8,12},{20,16},{16,20},{28,24},{24,28},{5,1},{1... | collective-permute-start | bytes 835592 | tf_op jit(solution)/shard_map/ppermute | solution.py:54
  63.6 0.7 %copy-start.15 = (bf16[272,512]{1,0:T(8,128)(2,1)}, bf16[272,512]{1,0:T(8,128)(2,1)S(1)}, u32[]{:S(2)}) copy-start(bf16[272,512]{1,0:T(8,128)(2,1)S(1)} %collective-permute-done.19.refs_10_) | copy-start | bytes 835588
  63.6 0.8 %copy-start.16 = (bf16[272,512]{1,0:T(8,128)(2,1)}, bf16[272,512]{1,0:T(8,128)(2,1)S(1)}, u32[]{:S(2)}) copy-start(bf16[272,512]{1,0:T(8,128)(2,1)S(1)} %collective-permute-done.21.refs_12_) | copy-start | bytes 835588
  64.4 0.7 %copy-start.17 = (bf16[272,512]{1,0:T(8,128)(2,1)}, bf16[272,512]{1,0:T(8,128)(2,1)S(1)}, u32[]{:S(2)}) copy-start(bf16[272,512]{1,0:T(8,128)(2,1)S(1)} %collective-permute-done.22.refs_13_) | copy-start | bytes 835588

commit v5 on v4

--- a/solution.py
+++ b/solution.py
@@ -124,23 +124,35 @@
     return me ^ step if groups == 4 else lax.rem(me + sign * step + groups, groups)
 
 
-def attend_kernel(size, groups, v_tags, *refs):
-    keys_hbm, hosts_hbm, bias_hbm, q_hbm, w_hbm = refs[:5]
-    k_refs = refs[5:5 + len(PAIR)]
-    v_refs = refs[5 + len(PAIR):5 + len(PAIR) + len(v_tags)]
-    rest = refs[5 + len(PAIR) + len(v_tags):]
+def attend_kernel(size, groups, tags, *refs):
+    count = len(tags)
+    keys_hbm, hosts_hbm, bias_hbm, q_hbm, w_hbm, own_hbm = refs[:6]
+    k_refs = refs[6:6 + count]
+    v_refs = refs[6 + count:6 + 2 * count]
+    piece_refs = refs[6 + 2 * count:5 + 2 * count + groups]
+    rest = refs[8 + 2 * count + groups:]
     part_refs = rest[:groups]
-    o32_ref, lse_ref = rest[groups:groups + 2]
-    keys, hosts, bias, q_ref, w_ref, kcat, vcat, score, att, turned, sem = rest[groups + 2:]
+    up_ref, stats_ref = rest[groups:groups + 2]
+    (keys, hosts, bias, q_ref, w_ref, grads, kcat, vcat, score, att, turned, o32_ref, sem) = rest[groups + 2:]
     rows, columns = q_ref.shape
     blocks_dev, neigh = keys.shape
     heads_dev = columns // HDIM
+    pairs = blocks_dev * heads_dev
+    part = rows // groups
     small = start_all([(keys_hbm, keys), (hosts_hbm, hosts), (bias_hbm, bias)], sem)
-    large = start_all([(q_hbm, q_ref), (w_hbm, w_ref)], sem, 3)
+    places = blocks_dev * neigh
+    large = start_all(
+        [(q_hbm, q_ref), (w_hbm, w_ref)]
+        + [
+            (ref, grads.at[pl.ds(step * part, part)])
+            for step, ref in enumerate((own_hbm,) + tuple(piece_refs))
+        ],
+        sem,
+        3 + 2 * places,
+    )
     wait_all(small)
-    places = blocks_dev * neigh
-    k_waits = gather_blocks(size, PAIR, keys, k_refs, kcat, sem, 5, blocks_dev, neigh)
-    v_waits = gather_blocks(size, v_tags, keys, v_refs, vcat, sem, 5 + places, blocks_dev, neigh)
+    k_waits = gather_blocks(size, tags, keys, k_refs, kcat, sem, 3, blocks_dev, neigh)
+    v_waits = gather_blocks(size, tags, keys, v_refs, vcat, sem, 3 + places, blocks_dev, neigh)
     large[0].wait()
     wait_all(k_waits)
     span = neigh * BLK
@@ -163,62 +175,26 @@
         o32_ref[b * BLK:(b + 1) * BLK, cols] = out
         att[b * BLK:(b + 1) * BLK, cols] = out.astype(jnp.bfloat16)
         lse_all = jnp.where(lane == b * heads_dev + h, top + jnp.log(total), lse_all)
-    lse_ref[...] = lse_all
-    large[1].wait()
     me = lax.axis_index("head")
-    part = rows // groups
     for step in range(groups):
         owner = piece_owner(me, step, groups, 1)
         turned[step * part:(step + 1) * part, :] = att[pl.ds(pl.multiple_of(owner * part, part), part), :]
+    wait_all(large[1:])
     mixed = ndot(turned[...], w_ref[...]).astype(jnp.bfloat16)
     for step in range(groups):
         part_refs[step][...] = mixed[step * part:(step + 1) * part, :]
-
-
-def upstream_kernel(groups, *refs):
-    keys_hbm, w_hbm, own_hbm, o32_ref, lse_ref = refs[:5]
-    piece_refs = refs[5:4 + groups]
-    rest = refs[8 + groups:]
-    up_ref, stats_ref, keys, w_ref, grads, sem = rest
-    rows, columns = o32_ref.shape
-    width = w_ref.shape[1]
-    blocks_dev, neigh = keys.shape
-    heads_dev = columns // HDIM
-    part = rows // groups
-    cut = width // 4
-    w_waits = [
-        start_all([(w_hbm.at[:, c * cut:(c + 1) * cut], w_ref.at[:, c * cut:(c + 1) * cut])], sem, c)[0]
-        for c in range(4)
-    ]
-    pieces = (own_hbm,) + tuple(piece_refs)
-    wait_all(
-        start_all(
-            [(ref, grads.at[pl.ds(step * part, part)]) for step, ref in enumerate(pieces)]
-            + [(keys_hbm, keys)],
-            sem,
-            4,
-        )
-    )
-    total = jnp.zeros((rows, columns), jnp.float32)
-    for c in range(4):
-        w_waits[c].wait()
-        total = total + tdot(grads[:, c * cut:(c + 1) * cut], w_ref[:, c * cut:(c + 1) * cut])
-    me = lax.axis_index("head")
-    product = total.astype(jnp.bfloat16)
+    product = tdot(grads[...], w_ref[...]).astype(jnp.bfloat16)
     for step in range(groups):
         owner = piece_owner(me, step, groups, -1)
         up_ref[pl.ds(pl.multiple_of(owner * part, part), part), :] = product[
             step * part:(step + 1) * part, :
         ]
-    pairs = blocks_dev * heads_dev
-    lane = lax.broadcasted_iota(jnp.int32, (BLK, BLK), 1)
-    stats = lse_ref[...]
-    for b in range(blocks_dev):
-        for h in range(heads_dev):
-            cols = slice(h * HDIM, (h + 1) * HDIM)
-            up = up_ref[b * BLK:(b + 1) * BLK, cols].astype(jnp.float32)
-            term = jnp.sum(up * o32_ref[b * BLK:(b + 1) * BLK, cols], axis=1, keepdims=True)
-            stats = jnp.where(lane == pairs + b * heads_dev + h, term, stats)
+    stats = lse_all
+    for b, h in units:
+        cols = slice(h * HDIM, (h + 1) * HDIM)
+        up = up_ref[b * BLK:(b + 1) * BLK, cols].astype(jnp.float32)
+        term = jnp.sum(up * o32_ref[b * BLK:(b + 1) * BLK, cols], axis=1, keepdims=True)
+        stats = jnp.where(lane == pairs + b * heads_dev + h, term, stats)
     stats_ref[...] = stats
     high = stat_rows(pairs)
     turned = jnp.transpose(stats)[:high, :]
@@ -242,11 +218,12 @@
         up_ref[row:row + high, col:col + BLK] = piece
 
 
-def query_kernel(size, v_tags, *refs):
+def query_kernel(size, tags, *refs):
+    count = len(tags)
     keys_hbm, hosts_hbm, bias_hbm, q_hbm, up_ref, stats_ref = refs[:6]
-    k_refs = refs[6:6 + len(PAIR)]
-    v_refs = refs[6 + len(PAIR):6 + len(PAIR) + len(v_tags)]
-    dq_ref, keys, hosts, bias, q_ref, kcat, vcat, sem = refs[7 + len(PAIR) + len(v_tags):]
+    k_refs = refs[6:6 + count]
+    v_refs = refs[6 + count:6 + 2 * count]
+    dq_ref, keys, hosts, bias, q_ref, kcat, vcat, sem = refs[7 + 2 * count:]
     rows, columns = q_ref.shape
     blocks_dev, neigh = keys.shape
     heads_dev = columns // HDIM
@@ -255,8 +232,8 @@
     large = start_all([(q_hbm, q_ref)], sem, 3)
     wait_all(small)
     places = blocks_dev * neigh
-    waits = gather_blocks(size, PAIR, keys, k_refs, kcat, sem, 4, blocks_dev, neigh)
-    waits += gather_blocks(size, v_tags, keys, v_refs, vcat, sem, 4 + places, blocks_dev, neigh)
+    waits = gather_blocks(size, tags, keys, k_refs, kcat, sem, 4, blocks_dev, neigh)
+    waits += gather_blocks(size, tags, keys, v_refs, vcat, sem, 4 + places, blocks_dev, neigh)
     wait_all(large)
     wait_all(waits)
     span = neigh * BLK
@@ -276,14 +253,15 @@
             dq_ref[b * BLK:(b + 1) * BLK, cols] = ndot(ds, k).astype(jnp.bfloat16)
 
 
-def key_kernel(size, neigh, *refs):
+def key_kernel(size, neigh, tags, *refs):
     nsh = len(PAIR)
+    count = len(tags)
     hosts_hbm, bias_hbm, k_hbm, v_hbm = refs[:4]
-    q_refs = refs[4:4 + nsh]
-    up_refs = refs[4 + nsh:4 + 2 * nsh]
-    dk_ref, dv_ref = refs[4 + 2 * nsh:6 + 2 * nsh]
+    q_refs = refs[4:4 + count]
+    up_refs = refs[4 + count:4 + count + nsh]
+    dk_ref, dv_ref = refs[4 + count + nsh:6 + count + nsh]
     (hosts, bias, k_ref, v_ref, qwin, upwin, stats, lists, keys, hits, dk_acc, dv_acc, sem) = refs[
-        6 + 2 * nsh:
+        6 + count + nsh:
     ]
     rows, columns = k_ref.shape
     long_rows = up_refs[0].shape[0]
@@ -315,7 +293,7 @@
         listed = part_of(index, 3).astype(jnp.int32)
         lists[index:index + 1, :] = listed[0:1, :] * 128 + listed[1:2, :]
     stats[nsh] = jnp.full((high, BLK), NEVER, jnp.float32)
-    copy = pltpu.make_async_copy(lists, keys, sem.at[3 * nsh + 4])
+    copy = pltpu.make_async_copy(lists, keys, sem.at[2 * nsh + count + 4])
     copy.start()
     copy.wait()
 
@@ -350,7 +328,8 @@
                 for index, tag in enumerate(PAIR):
                     owner = owner + jnp.where(shard == index, tag_owner(position, tag, size, PAIR), 0)
                 sames.append(hosts[owner * blocks_dev + inner] == hosts[mine])
-                qs.append(pl.ds(pl.multiple_of(shard * rows + inner * BLK, BLK), BLK))
+                place = find_shard(position, owner, size, tags)
+                qs.append(pl.ds(pl.multiple_of(place * rows + inner * BLK, BLK), BLK))
                 ups.append(pl.ds(pl.multiple_of(shard * long_rows + inner * BLK, 16), BLK))
                 lses.append((jnp.where(spare, nsh, shard), inner))
                 terms.append((shard, inner))
@@ -382,6 +361,25 @@
     dv_ref[...] = dv_acc[...].astype(jnp.bfloat16)
 
 
+def sum_kernel(count, *refs):
+    total = refs[0][...].astype(jnp.float32)
+    for ref in refs[1:count]:
+        total = total + ref[...].astype(jnp.float32)
+    refs[-1][...] = total.astype(jnp.bfloat16)
+
+
+def sum_after(arrays, before):
+    return pl.pallas_call(
+        functools.partial(sum_kernel, len(arrays)),
+        out_shape=jax.ShapeDtypeStruct(arrays[0].shape, jnp.bfloat16),
+        in_specs=[VMEM] * len(arrays) + [ANY],
+        out_specs=VMEM,
+        compiler_params=params(60),
+        cost_estimate=cost(1000, 1000),
+        name="sum_after",
+    )(*arrays, before)
+
+
 def copy_kernel(count, extra, *refs):
     sources, targets = refs[:count], refs[count + extra:2 * count + extra]
     between, sem = refs[2 * count + extra:-1], refs[-1]
@@ -419,7 +417,8 @@
     places = blocks_dev * neigh
     groups = lax.axis_size("head")
     part = rows // groups
-    v_tags = CUBE if size == 8 else PAIR
+    tags = CUBE if size == 8 else PAIR
+    exchange = exchange_cube if size == 8 else exchange_pair
     nsh = len(PAIR)
     bf16, f32, i32 = jnp.bfloat16, jnp.float32, jnp.int32
     high = stat_rows(pairs)
@@ -433,46 +432,50 @@
         return lax.ppermute(x, "head", [(i, i ^ mask) for i in range(groups)])
 
     paired = groups == 4
-    v_win = exchange_cube(value_states, size) if v_tags is CUBE else exchange_pair(value_states, size)
-    k_win = exchange_pair(key_states, size)
+    v_win = exchange(value_states, size)
+    k_win = exchange(key_states, size)
     if paired:
         opposite = flip(grad_mixed, 2)
         beside = flip(grad_mixed, 1)
         pieces = [grad_mixed, beside, opposite, flip(opposite, 1)]
     else:
         pieces = [grad_mixed] + [ring(grad_mixed, step) for step in range(1, groups)]
-    (late_query,) = copies_after((query_states,), tuple(pieces[1:3]))
-    q_win = exchange_pair(late_query, size)
+    (late_query,) = copies_after((query_states,), (pieces[2],))
+    q_win = exchange(late_query, size)
     scalars = [
         pltpu.SMEM(key_blocks.shape, i32),
         pltpu.SMEM(host_ids.shape, i32),
         pltpu.SMEM(host_bias.shape, f32),
     ]
 
-    parts_o32_lse = pl.pallas_call(
-        functools.partial(attend_kernel, size, groups, v_tags),
+    outputs = pl.pallas_call(
+        functools.partial(attend_kernel, size, groups, tags),
         out_shape=[jax.ShapeDtypeStruct((part, width), bf16)] * groups
-        + [jax.ShapeDtypeStruct((rows, columns), f32), jax.ShapeDtypeStruct((BLK, BLK), f32)],
-        in_specs=[HBM] * 5 + [ANY] * (len(PAIR) + len(v_tags)),
+        + [
+            jax.ShapeDtypeStruct((long_rows, columns), bf16),
+            jax.ShapeDtypeStruct((BLK, BLK), f32),
+        ],
+        in_specs=[HBM] * 6 + [ANY] * (2 * len(tags) + groups - 1 + 3),
         out_specs=[VMEM] * (groups + 2),
         scratch_shapes=scalars
         + [
             pltpu.VMEM((rows, columns), bf16),
             pltpu.VMEM((columns, width), bf16),
+            pltpu.VMEM((rows, width), bf16),
             pltpu.VMEM((places * BLK, columns), bf16),
             pltpu.VMEM((places * BLK, columns), bf16),
             pltpu.VMEM((pairs, BLK, neigh * BLK), f32),
             pltpu.VMEM((rows, columns), bf16),
             pltpu.VMEM((rows, columns), bf16),
-            pltpu.SemaphoreType.DMA((5 + 2 * places,)),
+            pltpu.VMEM((rows, columns), f32),
+            pltpu.SemaphoreType.DMA((5 + groups + 2 * places,)),
         ],
         compiler_params=params(60),
         cost_estimate=cost(4 * 10**9, 8 * 10**6),
         name="attend",
-    )(key_blocks, host_ids, host_bias, query_states, out_weight, *k_win, *v_win)
-    parts = parts_o32_lse[:groups]
-    o32, lse = parts_o32_lse[groups:]
-    mixed = parts[0].astype(f32)
+    )(key_blocks, host_ids, host_bias, query_states, out_weight, grad_mixed, *k_win, *v_win, *pieces[1:], q_win[1], q_win[2], q_win[3])
+    parts = outputs[:groups]
+    up, stats = outputs[groups:]
     if paired:
         relay = flip(parts[3], 1)
         beside_sum = flip(parts[1], 1)
@@ -481,30 +484,12 @@
     else:
         arrived = [ring(parts[step], step) for step in range(1, groups)]
 
-    up, stats = pl.pallas_call(
-        functools.partial(upstream_kernel, groups),
-        out_shape=[
-            jax.ShapeDtypeStruct((long_rows, columns), bf16),
-            jax.ShapeDtypeStruct((BLK, BLK), f32),
-        ],
-        in_specs=[HBM] * 3 + [VMEM] * 2 + [ANY] * (groups + 3),
-        out_specs=[VMEM] * 2,
-        scratch_shapes=[
-            pltpu.SMEM(key_blocks.shape, i32),
-            pltpu.VMEM((columns, width), bf16),
-            pltpu.VMEM((rows, width), bf16),
-            pltpu.SemaphoreType.DMA((5 + groups,)),
-        ],
-        compiler_params=params(60),
-        cost_estimate=cost(6 * 10**9, 6 * 10**6),
-        name="upstream",
-    )(key_blocks, out_weight, grad_mixed, o32, lse, *pieces[1:], *q_win[:4])
     up_win = exchange_pair(up, size)
 
     grad_query = pl.pallas_call(
-        functools.partial(query_kernel, size, v_tags),
+        functools.partial(query_kernel, size, tags),
         out_shape=jax.ShapeDtypeStruct((rows, columns), bf16),
-        in_specs=[HBM] * 4 + [VMEM] * 2 + [ANY] * (len(PAIR) + len(v_tags) + 1),
+        in_specs=[HBM] * 4 + [VMEM] * 2 + [ANY] * (2 * len(tags) + 1),
         out_specs=VMEM,
         scratch_shapes=scalars
         + [
@@ -519,16 +504,16 @@
     )(key_blocks, host_ids, host_bias, query_states, up, stats, *k_win, *v_win, q_win[4])
 
     grad_key, grad_value = pl.pallas_call(
-        functools.partial(key_kernel, size, neigh),
+        functools.partial(key_kernel, size, neigh, tags),
         out_shape=[jax.ShapeDtypeStruct((rows, columns), bf16)] * 2,
-        in_specs=[HBM] * 5 + [ANY] * (2 * nsh - 1),
+        in_specs=[HBM] * 5 + [ANY] * (len(tags) + nsh - 1),
         out_specs=[VMEM] * 2,
         scratch_shapes=[
             pltpu.SMEM(host_ids.shape, i32),
             pltpu.SMEM(host_bias.shape, f32),
             pltpu.VMEM((rows, columns), bf16),
             pltpu.VMEM((rows, columns), bf16),
-            pltpu.VMEM((nsh * rows, columns), bf16),
+            pltpu.VMEM((len(tags) * rows, columns), bf16),
             pltpu.VMEM((nsh * long_rows, columns), bf16),
             pltpu.VMEM((nsh + 1, high, BLK), f32),
             pltpu.VMEM((8, BLK), i32),
@@ -536,16 +521,15 @@
             pltpu.SMEM((blocks_dev, nsh * blocks_dev + 2), i32),
             pltpu.VMEM((rows, columns), f32),
             pltpu.VMEM((rows, columns), f32),
-            pltpu.SemaphoreType.DMA((3 * nsh + 5,)),
+            pltpu.SemaphoreType.DMA((2 * nsh + len(tags) + 5,)),
         ],
         compiler_params=params(60),
         cost_estimate=cost(10**9, 10**6),
         name="key_grad",
     )(host_ids, host_bias, key_states, value_states, query_states, *q_win[1:], *up_win)
 
-    for piece in arrived:
-        mixed = mixed + piece.astype(f32)
-    return (mixed.astype(bf16), grad_query, grad_key, grad_value)
+    mixed_out = sum_after((parts[0], *arrived), grad_key)
+    return (mixed_out, grad_query, grad_key, grad_value)
 
 
 def solution(mesh):

time: 71.6 us -> 82.8 us (1.16)
  the two profiles are of different devices: /device:TPU:0 before, /device:TPU:3 now
where the time goes in v5:
time: 82.8 us; the launch traced here: 82.1 us
  starting transfers between devices  28.8 us (35%)
  waiting for transfers between devices  24.6 us (30%)
  Pallas kernels  23.5 us (28%)
  local copies, waits for them, and re-layouts  3.27 us (4%)
  other arithmetic  1.06 us (1%)
  between operations  0.89 us (1%)
    ppermute x19, starting transfers between devices, permute_from(): return lax.ppermute(x, 'ctx', [(source(i) % size, i) for i in range(size)])  20 us
    ppermute x19, waiting for transfers between devices, permute_from(): return lax.ppermute(x, 'ctx', [(source(i) % size, i) for i in range(size)])  15.4 us
    ppermute x6, waiting for transfers between devices, flip(): return lax.ppermute(x, 'head', [(i, i ^ mask) for i in range(groups)])  9.23 us
    ppermute x6, starting transfers between devices, flip(): return lax.ppermute(x, 'head', [(i, i ^ mask) for i in range(groups)])  8.77 us
    pallas_call x1, Pallas kernels, per_device(): pl.pallas_call(functools.partial(key_kernel, size, neigh, tags), out_shap...  7.57 us
    pallas_call x1, Pallas kernels, per_device(): pl.pallas_call(functools.partial(attend_kernel, size, groups, tags), out_...  6.27 us
    pallas_call x1, Pallas kernels, per_device(): pl.pallas_call(functools.partial(query_kernel, size, tags), out_shape=jax...  6.11 us
    unnamed x48, local copies, waits for them, and re-layouts  3.27 us
  transfers between devices with their start and end apart: 25, of which 9 were waited for; matrix products, arithmetic and copies ran while one was open for 1% of the time, Pallas kernels for 19%

profile of v5, /device:TPU:3, one launch (start us, length us, event | category | flops | bytes accessed | tf_op | source)
XLA Modules:
  0.0 82.1 jit_solution(4189821669945251191)
XLA Ops:
  0.6 2.4 %collective-permute-start.11 = (bf16[64,2048]{1,0:T(8,128)(2,1)}, bf16[64,2048]{1,0:T(8,128)(2,1)S(1)}, u32[]{:S(2)}, u32[]{:S(2)}) collective-permute-start(bf16[64,2048]{1,0:T(8,128)(2,1)} %refs_5_.1), channel_id=1, source_target_pairs={{0,2},{1,3},{2,0},{3,1},{4,6},{5,7},{6,4},{7,5},{8,10},{9,11},{10,... | collective-permute-start | bytes 786440 | tf_op jit(solution)/shard_map/ppermute | solution.py:432
  3.0 0.3 collective-permute-start.1
  3.3 1.2 %collective-permute-start.6 = (bf16[256,512]{1,0:T(8,128)(2,1)}, bf16[256,512]{1,0:T(8,128)(2,1)S(1)}, u32[]{:S(2)}, u32[]{:S(2)}) collective-permute-start(bf16[256,512]{1,0:T(8,128)(2,1)} %refs_12_.3), channel_id=1, source_target_pairs={{8,0},{12,4},{0,8},{4,12},{24,16},{28,20},{16,24},{20,28},{9,1},{1... | collective-permute-start | bytes 786440 | tf_op jit(solution)/shard_map/ppermute | solution.py:54
  4.5 1.5 %collective-permute-start = (bf16[256,512]{1,0:T(8,128)(2,1)}, bf16[256,512]{1,0:T(8,128)(2,1)S(1)}, u32[]{:S(2)}, u32[]{:S(2)}) collective-permute-start(bf16[256,512]{1,0:T(8,128)(2,1)} %refs_6_.3), channel_id=1, source_target_pairs={{4,0},{0,4},{12,8},{8,12},{20,16},{16,20},{28,24},{24,28},{5,1},{1... | collective-permute-start | bytes 786440 | tf_op jit(solution)/shard_map/ppermute | solution.py:54
  6.0 8.6 %collective-permute-done.11.refs_1_.refs_19_ = bf16[64,2048]{1,0:T(8,128)(2,1)S(1)} collective-permute-done((bf16[64,2048]{1,0:T(8,128)(2,1)}, bf16[64,2048]{1,0:T(8,128)(2,1)S(1)}, u32[]{:S(2)}, u32[]{:S(2)}) %collective-permute-start.11) | collective-permute-done | bytes 262176 | tf_op jit(solution)/shard_map/ppermute | solution.py:432
  14.6 1.5 %collective-permute-start.10 = (bf16[64,2048]{1,0:T(8,128)(2,1)}, bf16[64,2048]{1,0:T(8,128)(2,1)S(1)}, u32[]{:S(2)}, u32[]{:S(2)}) collective-permute-start(bf16[64,2048]{1,0:T(8,128)(2,1)} %refs_5_.1), channel_id=1, source_target_pairs={{0,1},{1,0},{2,3},{3,2},{4,5},{5,4},{6,7},{7,6},{8,9},{9,8},{10,11... | collective-permute-start | bytes 786440 | tf_op jit(solution)/shard_map/ppermute | solution.py:432
  16.2 1.7 %copies_after.1 = bf16[256,512]{1,0:T(8,128)(2,1)} custom-call(bf16[256,512]{1,0:T(8,128)(2,1)} %refs_3_.5, bf16[64,2048]{1,0:T(8,128)(2,1)} %copy-done), custom_call_target="tpu_custom_call" | custom-call | flops 1000 | bytes 1000 | tf_op jit(solution)/shard_map/copies_after/pallas_call | solution.py:391
  17.8 0.0 copy-start.3
  17.8 0.3 collective-permute-start.14
  18.2 1.2 %collective-permute-start.3 = (bf16[256,512]{1,0:T(8,128)(2,1)S(1)}, bf16[256,512]{1,0:T(8,128)(2,1)S(1)}, u32[]{:S(2)}, u32[]{:S(2)}) collective-permute-start(bf16[256,512]{1,0:T(8,128)(2,1)S(1)} %collective-permute-done.1.refs_8_), channel_id=1, source_target_pairs={{16,0},{20,4},{24,8},{28,12},{0,16},{4,20},{8,24},{12,28},{17,1},{... | collective-permute-start | bytes 786440 | tf_op jit(solution)/shard_map/ppermute | solution.py:54
  19.4 0.2 collective-permute-start.8
  19.6 1.6 %collective-permute-start.13 = (bf16[256,512]{1,0:T(8,128)(2,1)}, bf16[256,512]{1,0:T(8,128)(2,1)S(1)}, u32[]{:S(2)}, u32[]{:S(2)}) collective-permute-start(bf16[256,512]{1,0:T(8,128)(2,1)} %copies_after.1), channel_id=1, source_target_pairs={{4,0},{0,4},{12,8},{8,12},{20,16},{16,20},{28,24},{24,28},{5,1},{1... | collective-permute-start | bytes 786440 | tf_op jit(solution)/shard_map/ppermute | solution.py:54
  21.3 0.4 collective-permute-done.10.refs_18_
  21.7 2.0 %collective-permute-start.2 = (bf16[256,512]{1,0:T(8,128)(2,1)S(1)}, bf16[256,512]{1,0:T(8,128)(2,1)S(1)}, u32[]{:S(2)}, u32[]{:S(2)}) collective-permute-start(bf16[256,512]{1,0:T(8,128)(2,1)S(1)} %collective-permute-done.1.refs_8_), channel_id=1, source_target_pairs={{4,0},{0,4},{12,8},{8,12},{20,16},{16,20},{28,24},{24,28},{5,1},{1... | collective-permute-start | bytes 786440 | tf_op jit(solution)/shard_map/ppermute | solution.py:54
  23.6 1.6 %collective-permute-done.14.refs_22_.refs_6_ = bf16[256,512]{1,0:T(8,128)(2,1)S(1)} collective-permute-done((bf16[256,512]{1,0:T(8,128)(2,1)}, bf16[256,512]{1,0:T(8,128)(2,1)S(1)}, u32[]{:S(2)}, u32[]{:S(2)}) %collective-permute-start.14) | collective-permute-done | bytes 262176 | tf_op jit(solution)/shard_map/ppermute | solution.py:54
  25.2 1.7 %collective-permute-start.7 = (bf16[256,512]{1,0:T(8,128)(2,1)S(1)}, bf16[256,512]{1,0:T(8,128)(2,1)S(1)}, u32[]{:S(2)}, u32[]{:S(2)}) collective-permute-start(bf16[256,512]{1,0:T(8,128)(2,1)S(1)} %collective-permute-done.6.refs_14_), channel_id=1, source_target_pairs={{4,0},{0,4},{12,8},{8,12},{20,16},{16,20},{28,24},{24,28},{5,1},{1... | collective-permute-start | bytes 786440 | tf_op jit(solution)/shard_map/ppermute | solution.py:54
  26.8 0.7 collective-permute-start.12
  27.5 3.0 %collective-permute-done.8.refs_16_ = bf16[256,512]{1,0:T(8,128)(2,1)S(1)} collective-permute-done((bf16[256,512]{1,0:T(8,128)(2,1)S(1)}, bf16[256,512]{1,0:T(8,128)(2,1)S(1)}, u32[]{:S(2)}, u32[]{:S(2)}) %collective-permute-start.8) | collective-permute-done | bytes 262176 | tf_op jit(solution)/shard_map/ppermute | solution.py:54
  30.5 2.0 %collective-permute-start.15 = (bf16[256,512]{1,0:T(8,128)(2,1)S(1)}, bf16[256,512]{1,0:T(8,128)(2,1)S(1)}, u32[]{:S(2)}, u32[]{:S(2)}) collective-permute-start(bf16[256,512]{1,0:T(8,128)(2,1)S(1)} %collective-permute-done.14.refs_22_.refs_6_), channel_id=1, source_target_pairs={{4,0},{0,4},{12,8},{8,12},{20,16},{16,20},{28,24},{24,28},{5,1},{1... | collective-permute-start | bytes 786440 | tf_op jit(solution)/shard_map/ppermute | solution.py:54
  32.5 0.1 collective-permute-start.4
  32.6 0.4 collective-permute-start.9
  33.0 0.2 collective-permute-done.12.refs_20_
  33.2 0.4 collective-permute-done.15.refs_23_.refs_7_
  33.7 0.4 collective-permute-done.4.refs_11_
  34.1 0.4 collective-permute-done.9.refs_17_
  34.5 0.2 copy-done.11
  34.8 0.7 copy-done.12
  35.5 6.3 %attend.1 = (bf16[64,2048]{1,0:T(8,128)(2,1)}, bf16[64,2048]{1,0:T(8,128)(2,1)}, bf16[64,2048]{1,0:T(8,128)(2,1)}, bf16[64,2048]{1,0:T(8,128)(2,1)}, bf16[272,512]{1,0:T(8,128)(2,1)}, /*index=5*/f32[128,128]{1,0:T(8,128)}) custom-call(s32[2,4]{1,0:T(2,128)} %refs_0_.7, s32[16]{0:T(128)} %refs_1_.5, f32[4]{0:T(128)} %refs_2_.5, bf16[256,512]{1,0:T(8,128)(2,1)} %refs_3_.5, ...), custom_call_target="tpu_custom_call" | custom-call | flops 4000000000 | bytes 8000000 | tf_op jit(solution)/shard_map/attend/pallas_call | solution.py:451
  41.7 2.2 %collective-permute-start.22 = (bf16[272,512]{1,0:T(8,128)(2,1)}, bf16[272,512]{1,0:T(8,128)(2,1)S(1)}, u32[]{:S(2)}, u32[]{:S(2)}) collective-permute-start(bf16[272,512]{1,0:T(8,128)(2,1)} %get-tuple-element.16.refs_10_.refs_4_), channel_id=1, source_target_pairs={{8,0},{28,4},{16,8},{4,12},{24,16},{12,20},{0,24},{20,28},{9,1},{2... | collective-permute-start | bytes 835592 | tf_op jit(solution)/shard_map/ppermute | solution.py:54
  43.9 0.2 collective-permute-start.19
  44.2 0.7 collective-permute-start.17
  44.9 2.4 %collective-permute-start.21 = (bf16[272,512]{1,0:T(8,128)(2,1)}, bf16[272,512]{1,0:T(8,128)(2,1)S(1)}, u32[]{:S(2)}, u32[]{:S(2)}) collective-permute-start(bf16[272,512]{1,0:T(8,128)(2,1)} %get-tuple-element.16.refs_10_.refs_4_), channel_id=1, source_target_pairs={{4,0},{0,4},{12,8},{8,12},{20,16},{16,20},{28,24},{24,28},{5,1},{1... | collective-permute-start | bytes 835592 | tf_op jit(solution)/shard_map/ppermute | solution.py:54
  47.2 0.6 collective-permute-start.23
  47.9 9.6 %collective-permute-done.19.refs_8_.refs_18_ = bf16[256,512]{1,0:T(8,128)(2,1)S(1)} collective-permute-done((bf16[256,512]{1,0:T(8,128)(2,1)}, bf16[256,512]{1,0:T(8,128)(2,1)S(1)}, u32[]{:S(2)}, u32[]{:S(2)}) %collective-permute-start.19) | collective-permute-done | bytes 262176 | tf_op jit(solution)/shard_map/ppermute | solution.py:54
  57.5 0.4 collective-permute-start.16
  57.9 1.9 %collective-permute-start.20 = (bf16[256,512]{1,0:T(8,128)(2,1)S(1)}, bf16[256,512]{1,0:T(8,128)(2,1)S(1)}, u32[]{:S(2)}, u32[]{:S(2)}) collective-permute-start(bf16[256,512]{1,0:T(8,128)(2,1)S(1)} %collective-permute-done.19.refs_8_.refs_18_), channel_id=1, source_target_pairs={{4,0},{0,4},{12,8},{8,12},{20,16},{16,20},{28,24},{24,28},{5,1},{1... | collective-permute-start | bytes 786440 | tf_op jit(solution)/shard_map/ppermute | solution.py:54
  59.8 0.1 collective-permute-start.24
  59.9 1.1 %add_convert_fusion = bf16[64,2048]{1,0:T(8,128)(2,1)S(1)} fusion(bf16[64,2048]{1,0:T(8,128)(2,1)S(1)} %collective-permute-done.17, bf16[64,2048]{1,0:T(8,128)(2,1)} %get-tuple-element.14), kind=kLoop, calls=%fused_computation | loop fusion | flops 524288 | bytes 786432 | tf_op jit(solution)/shard_map/convert_element_type | solution.py:482
  61.0 0.0 collective-permute-done.20.refs_9_
  61.0 3.1 %collective-permute-start.18 = (bf16[64,2048]{1,0:T(8,128)(2,1)S(1)}, bf16[64,2048]{1,0:T(8,128)(2,1)S(1)}, u32[]{:S(2)}, u32[]{:S(2)}) collective-permute-start(bf16[64,2048]{1,0:T(8,128)(2,1)S(1)} %add_convert_fusion), channel_id=1, source_target_pairs={{0,2},{1,3},{2,0},{3,1},{4,6},{5,7},{6,4},{7,5},{8,10},{9,11},{10,... | collective-permute-start | bytes 786440 | tf_op jit(solution)/shard_map/ppermute | solution.py:432
  64.1 6.1 %query_grad.1 = bf16[256,512]{1,0:T(8,128)(2,1)} custom-call(s32[2,4]{1,0:T(2,128)} %refs_0_.7, s32[16]{0:T(128)} %refs_1_.5, f32[4]{0:T(128)} %refs_2_.5, bf16[256,512]{1,0:T(8,128)(2,1)} %refs_3_.5, bf16[272,512]{1,0:T(8,128)(2,1)} %get-tuple-element.16.refs_10_.refs_4_, f32[128,128]{1,0:T(8,128)} %get-tuple-element.18.refs_5_, bf16[256,512]{1,0:T(8,128)(2,1)} %refs_6_.3, ...), custom_call_target="tpu_custom_call" | custom-call | flops 1000000000 | bytes 1000000 | tf_op jit(solution)/shard_map/query_grad/pallas_call | solution.py:489
  70.3 0.7 copy-done.15
  70.9 0.1 copy-done.16
  71.0 0.7 copy-done.17
  71.7 7.6 %key_grad.1 = (bf16[256,512]{1,0:T(8,128)(2,1)}, bf16[256,512]{1,0:T(8,128)(2,1)}) custom-call(s32[16]{0:T(128)} %refs_1_.5, f32[4]{0:T(128)} %refs_2_.5, bf16[256,512]{1,0:T(8,128)(2,1)} %refs_6_.3, bf16[256,512]{1,0:T(8,128)(2,1)} %refs_12_.3, bf16[256,512]{1,0:T(8,128)(2,1)} %refs_3_.5, bf16[256,512]{1,0:T(8,128)(2,1)} %copy-done.19, ...), custom_call_target="tpu_custom_call" | custom-call | flops 1000000000 | bytes 1000000 | tf_op jit(solution)/shard_map/key_grad/pallas_call | solution.py:506
  79.4 0.7 copy-done.1
  80.0 0.1 copy-done.2
  80.2 1.9 %sum_after.1 = bf16[64,2048]{1,0:T(8,128)(2,1)} custom-call(bf16[64,2048]{1,0:T(8,128)(2,1)} %get-tuple-element.12.refs_0_, bf16[64,2048]{1,0:T(8,128)(2,1)} %copy-done.1, bf16[64,2048]{1,0:T(8,128)(2,1)} %copy-done.2, bf16[256,512]{1,0:T(8,128)(2,1)} %get-tuple-element.10.refs_3_), custom_call_target="tpu_custom_call" | custom-call | flops 1000 | bytes 1000 | tf_op jit(solution)/shard_map/sum_after/pallas_call | solution.py:372
  (56 shorter events, 0.1 us)
Async XLA Ops:
  0.6 14.0 %collective-permute-start.11 = (bf16[64,2048]{1,0:T(8,128)(2,1)}, bf16[64,2048]{1,0:T(8,128)(2,1)S(1)}, u32[]{:S(2)}, u32[]{:S(2)}) collective-permute-start(bf16[64,2048]{1,0:T(8,128)(2,1)} %refs_5_.1), channel_id=1, source_target_pairs={{0,2},{1,3},{2,0},{3,1},{4,6},{5,7},{6,4},{7,5},{8,10},{9,11},{10,... | collective-permute-start | bytes 786440 | tf_op jit(solution)/shard_map/ppermute | solution.py:432
  3.0 14.8 %collective-permute-start.1 = (bf16[256,512]{1,0:T(8,128)(2,1)}, bf16[256,512]{1,0:T(8,128)(2,1)S(1)}, u32[]{:S(2)}, u32[]{:S(2)}) collective-permute-start(bf16[256,512]{1,0:T(8,128)(2,1)} %refs_6_.3), channel_id=1, source_target_pairs={{8,0},{12,4},{0,8},{4,12},{24,16},{28,20},{16,24},{20,28},{9,1},{1... | collective-permute-start | bytes 786440 | tf_op jit(solution)/shard_map/ppermute | solution.py:54
  3.3 14.9 %collective-permute-start.6 = (bf16[256,512]{1,0:T(8,128)(2,1)}, bf16[256,512]{1,0:T(8,128)(2,1)S(1)}, u32[]{:S(2)}, u32[]{:S(2)}) collective-permute-start(bf16[256,512]{1,0:T(8,128)(2,1)} %refs_12_.3), channel_id=1, source_target_pairs={{8,0},{12,4},{0,8},{4,12},{24,16},{28,20},{16,24},{20,28},{9,1},{1... | collective-permute-start | bytes 786440 | tf_op jit(solution)/shard_map/ppermute | solution.py:54
  4.5 14.9 %collective-permute-start = (bf16[256,512]{1,0:T(8,128)(2,1)}, bf16[256,512]{1,0:T(8,128)(2,1)S(1)}, u32[]{:S(2)}, u32[]{:S(2)}) collective-permute-start(bf16[256,512]{1,0:T(8,128)(2,1)} %refs_6_.3), channel_id=1, source_target_pairs={{4,0},{0,4},{12,8},{8,12},{20,16},{16,20},{28,24},{24,28},{5,1},{1... | collective-permute-start | bytes 786440 | tf_op jit(solution)/shard_map/ppermute | solution.py:54
  6.0 13.7 %collective-permute-start.5 = (bf16[256,512]{1,0:T(8,128)(2,1)}, bf16[256,512]{1,0:T(8,128)(2,1)S(1)}, u32[]{:S(2)}, u32[]{:S(2)}) collective-permute-start(bf16[256,512]{1,0:T(8,128)(2,1)} %refs_12_.3), channel_id=1, source_target_pairs={{4,0},{0,4},{12,8},{8,12},{20,16},{16,20},{28,24},{24,28},{5,1},{1... | collective-permute-start | bytes 786440 | tf_op jit(solution)/shard_map/ppermute | solution.py:54
  14.6 1.5 %copy-start = (bf16[64,2048]{1,0:T(8,128)(2,1)}, bf16[64,2048]{1,0:T(8,128)(2,1)S(1)}, u32[]{:S(2)}) copy-start(bf16[64,2048]{1,0:T(8,128)(2,1)S(1)} %collective-permute-done.11.refs_1_.refs_19_) | copy-start | bytes 786436
  14.6 7.0 %collective-permute-start.10 = (bf16[64,2048]{1,0:T(8,128)(2,1)}, bf16[64,2048]{1,0:T(8,128)(2,1)S(1)}, u32[]{:S(2)}, u32[]{:S(2)}) collective-permute-start(bf16[64,2048]{1,0:T(8,128)(2,1)} %refs_5_.1), channel_id=1, source_target_pairs={{0,1},{1,0},{2,3},{3,2},{4,5},{5,4},{6,7},{7,6},{8,9},{9,8},{10,11... | collective-permute-start | bytes 786440 | tf_op jit(solution)/shard_map/ppermute | solution.py:432
  17.8 16.6 %copy-start.3 = (bf16[256,512]{1,0:T(8,128)(2,1)}, bf16[256,512]{1,0:T(8,128)(2,1)S(1)}, u32[]{:S(2)}) copy-start(bf16[256,512]{1,0:T(8,128)(2,1)S(1)} %collective-permute-done.1.refs_8_) | copy-start | bytes 786436
  17.8 7.3 %collective-permute-start.14 = (bf16[256,512]{1,0:T(8,128)(2,1)}, bf16[256,512]{1,0:T(8,128)(2,1)S(1)}, u32[]{:S(2)}, u32[]{:S(2)}) collective-permute-start(bf16[256,512]{1,0:T(8,128)(2,1)} %copies_after.1), channel_id=1, source_target_pairs={{8,0},{12,4},{0,8},{4,12},{24,16},{28,20},{16,24},{20,28},{9,1},{1... | collective-permute-start | bytes 786440 | tf_op jit(solution)/shard_map/ppermute | solution.py:54
  18.2 16.3 %copy-start.4 = (bf16[256,512]{1,0:T(8,128)(2,1)}, bf16[256,512]{1,0:T(8,128)(2,1)S(1)}, u32[]{:S(2)}) copy-start(bf16[256,512]{1,0:T(8,128)(2,1)S(1)} %collective-permute-done.6.refs_14_) | copy-start | bytes 786436
  18.2 8.7 %collective-permute-start.3 = (bf16[256,512]{1,0:T(8,128)(2,1)S(1)}, bf16[256,512]{1,0:T(8,128)(2,1)S(1)}, u32[]{:S(2)}, u32[]{:S(2)}) collective-permute-start(bf16[256,512]{1,0:T(8,128)(2,1)S(1)} %collective-permute-done.1.refs_8_), channel_id=1, source_target_pairs={{16,0},{20,4},{24,8},{28,12},{0,16},{4,20},{8,24},{12,28},{17,1},{... | collective-permute-start | bytes 786440 | tf_op jit(solution)/shard_map/ppermute | solution.py:54
  19.4 15.0 %copy-start.5 = (bf16[256,512]{1,0:T(8,128)(2,1)}, bf16[256,512]{1,0:T(8,128)(2,1)S(1)}, u32[]{:S(2)}) copy-start(bf16[256,512]{1,0:T(8,128)(2,1)S(1)} %collective-permute-done.refs_7_) | copy-start | bytes 786436
  19.4 11.1 %collective-permute-start.8 = (bf16[256,512]{1,0:T(8,128)(2,1)S(1)}, bf16[256,512]{1,0:T(8,128)(2,1)S(1)}, u32[]{:S(2)}, u32[]{:S(2)}) collective-permute-start(bf16[256,512]{1,0:T(8,128)(2,1)S(1)} %collective-permute-done.6.refs_14_), channel_id=1, source_target_pairs={{16,0},{20,4},{24,8},{28,12},{0,16},{4,20},{8,24},{12,28},{17,1},{... | collective-permute-start | bytes 786440 | tf_op jit(solution)/shard_map/ppermute | solution.py:54
  19.6 14.8 %copy-start.6 = (bf16[256,512]{1,0:T(8,128)(2,1)}, bf16[256,512]{1,0:T(8,128)(2,1)S(1)}, u32[]{:S(2)}) copy-start(bf16[256,512]{1,0:T(8,128)(2,1)S(1)} %collective-permute-done.5.refs_13_) | copy-start | bytes 786436
  19.6 12.9 %collective-permute-start.13 = (bf16[256,512]{1,0:T(8,128)(2,1)}, bf16[256,512]{1,0:T(8,128)(2,1)S(1)}, u32[]{:S(2)}, u32[]{:S(2)}) collective-permute-start(bf16[256,512]{1,0:T(8,128)(2,1)} %copies_after.1), channel_id=1, source_target_pairs={{4,0},{0,4},{12,8},{8,12},{20,16},{16,20},{28,24},{24,28},{5,1},{1... | collective-permute-start | bytes 786440 | tf_op jit(solution)/shard_map/ppermute | solution.py:54
  21.6 12.8 %copy-start.21 = (bf16[64,2048]{1,0:T(8,128)(2,1)}, bf16[64,2048]{1,0:T(8,128)(2,1)S(1)}, u32[]{:S(2)}) copy-start(bf16[64,2048]{1,0:T(8,128)(2,1)S(1)} %collective-permute-done.10.refs_18_) | copy-start | bytes 786436
  21.7 10.9 %collective-permute-start.2 = (bf16[256,512]{1,0:T(8,128)(2,1)S(1)}, bf16[256,512]{1,0:T(8,128)(2,1)S(1)}, u32[]{:S(2)}, u32[]{:S(2)}) collective-permute-start(bf16[256,512]{1,0:T(8,128)(2,1)S(1)} %collective-permute-done.1.refs_8_), channel_id=1, source_target_pairs={{4,0},{0,4},{12,8},{8,12},{20,16},{16,20},{28,24},{24,28},{5,1},{1... | collective-permute-start | bytes 786440 | tf_op jit(solution)/shard_map/ppermute | solution.py:54
  25.2 9.3 %copy-start.18 = (bf16[256,512]{1,0:T(8,128)(2,1)}, bf16[256,512]{1,0:T(8,128)(2,1)S(1)}, u32[]{:S(2)}) copy-start(bf16[256,512]{1,0:T(8,128)(2,1)S(1)} %collective-permute-done.14.refs_22_.refs_6_) | copy-start | bytes 786436
  25.2 7.9 %collective-permute-start.7 = (bf16[256,512]{1,0:T(8,128)(2,1)S(1)}, bf16[256,512]{1,0:T(8,128)(2,1)S(1)}, u32[]{:S(2)}, u32[]{:S(2)}) collective-permute-start(bf16[256,512]{1,0:T(8,128)(2,1)S(1)} %collective-permute-done.6.refs_14_), channel_id=1, source_target_pairs={{4,0},{0,4},{12,8},{8,12},{20,16},{16,20},{28,24},{24,28},{5,1},{1... | collective-permute-start | bytes 786440 | tf_op jit(solution)/shard_map/ppermute | solution.py:54
  26.8 7.6 %copy-start.7 = (bf16[256,512]{1,0:T(8,128)(2,1)}, bf16[256,512]{1,0:T(8,128)(2,1)S(1)}, u32[]{:S(2)}) copy-start(bf16[256,512]{1,0:T(8,128)(2,1)S(1)} %collective-permute-done.3.refs_10_) | copy-start | bytes 786436
  26.8 6.4 %collective-permute-start.12 = (bf16[64,2048]{1,0:T(8,128)(2,1)}, bf16[64,2048]{1,0:T(8,128)(2,1)S(1)}, u32[]{:S(2)}, u32[]{:S(2)}) collective-permute-start(bf16[64,2048]{1,0:T(8,128)(2,1)} %copy-done), channel_id=1, source_target_pairs={{0,1},{1,0},{2,3},{3,2},{4,5},{5,4},{6,7},{7,6},{8,9},{9,8},{10,11... | collective-permute-start | bytes 786440 | tf_op jit(solution)/shard_map/ppermute | solution.py:432
  30.5 3.9 %copy-start.8 = (bf16[256,512]{1,0:T(8,128)(2,1)}, bf16[256,512]{1,0:T(8,128)(2,1)S(1)}, u32[]{:S(2)}) copy-start(bf16[256,512]{1,0:T(8,128)(2,1)S(1)} %collective-permute-done.8.refs_16_) | copy-start | bytes 786436
  30.5 3.1 %collective-permute-start.15 = (bf16[256,512]{1,0:T(8,128)(2,1)S(1)}, bf16[256,512]{1,0:T(8,128)(2,1)S(1)}, u32[]{:S(2)}, u32[]{:S(2)}) collective-permute-start(bf16[256,512]{1,0:T(8,128)(2,1)S(1)} %collective-permute-done.14.refs_22_.refs_6_), channel_id=1, source_target_pairs={{4,0},{0,4},{12,8},{8,12},{20,16},{16,20},{28,24},{24,28},{5,1},{1... | collective-permute-start | bytes 786440 | tf_op jit(solution)/shard_map/ppermute | solution.py:54
  32.5 2.0 %copy-start.19 = (bf16[256,512]{1,0:T(8,128)(2,1)}, bf16[256,512]{1,0:T(8,128)(2,1)S(1)}, u32[]{:S(2)}) copy-start(bf16[256,512]{1,0:T(8,128)(2,1)S(1)} %collective-permute-done.13.refs_21_.refs_5_) | copy-start | bytes 786436
  32.5 1.5 %collective-permute-start.4 = (bf16[256,512]{1,0:T(8,128)(2,1)S(1)}, bf16[256,512]{1,0:T(8,128)(2,1)S(1)}, u32[]{:S(2)}, u32[]{:S(2)}) collective-permute-start(bf16[256,512]{1,0:T(8,128)(2,1)S(1)} %collective-permute-done.3.refs_10_), channel_id=1, source_target_pairs={{4,0},{0,4},{12,8},{8,12},{20,16},{16,20},{28,24},{24,28},{5,1},{1... | collective-permute-start | bytes 786440 | tf_op jit(solution)/shard_map/ppermute | solution.py:54
  32.6 1.9 %copy-start.9 = (bf16[256,512]{1,0:T(8,128)(2,1)}, bf16[256,512]{1,0:T(8,128)(2,1)S(1)}, u32[]{:S(2)}) copy-start(bf16[256,512]{1,0:T(8,128)(2,1)S(1)} %collective-permute-done.2.refs_9_) | copy-start | bytes 786436
  32.6 1.8 %collective-permute-start.9 = (bf16[256,512]{1,0:T(8,128)(2,1)S(1)}, bf16[256,512]{1,0:T(8,128)(2,1)S(1)}, u32[]{:S(2)}, u32[]{:S(2)}) collective-permute-start(bf16[256,512]{1,0:T(8,128)(2,1)S(1)} %collective-permute-done.8.refs_16_), channel_id=1, source_target_pairs={{4,0},{0,4},{12,8},{8,12},{20,16},{16,20},{28,24},{24,28},{5,1},{1... | collective-permute-start | bytes 786440 | tf_op jit(solution)/shard_map/ppermute | solution.py:54
  33.0 1.5 %copy-start.10 = (bf16[256,512]{1,0:T(8,128)(2,1)}, bf16[256,512]{1,0:T(8,128)(2,1)S(1)}, u32[]{:S(2)}) copy-start(bf16[256,512]{1,0:T(8,128)(2,1)S(1)} %collective-permute-done.7.refs_15_) | copy-start | bytes 786436
  33.2 1.3 %copy-start.23 = (bf16[64,2048]{1,0:T(8,128)(2,1)}, bf16[64,2048]{1,0:T(8,128)(2,1)S(1)}, u32[]{:S(2)}) copy-start(bf16[64,2048]{1,0:T(8,128)(2,1)S(1)} %collective-permute-done.12.refs_20_) | copy-start | bytes 786436
  33.7 0.9 %copy-start.20 = (bf16[256,512]{1,0:T(8,128)(2,1)}, bf16[256,512]{1,0:T(8,128)(2,1)S(1)}, u32[]{:S(2)}) copy-start(bf16[256,512]{1,0:T(8,128)(2,1)S(1)} %collective-permute-done.15.refs_23_.refs_7_) | copy-start | bytes 786436
  34.7 0.7 copy-start.12
  41.7 18.1 %collective-permute-start.22 = (bf16[272,512]{1,0:T(8,128)(2,1)}, bf16[272,512]{1,0:T(8,128)(2,1)S(1)}, u32[]{:S(2)}, u32[]{:S(2)}) collective-permute-start(bf16[272,512]{1,0:T(8,128)(2,1)} %get-tuple-element.16.refs_10_.refs_4_), channel_id=1, source_target_pairs={{8,0},{28,4},{16,8},{4,12},{24,16},{12,20},{0,24},{20,28},{9,1},{2... | collective-permute-start | bytes 835592 | tf_op jit(solution)/shard_map/ppermute | solution.py:54
  43.9 13.5 %collective-permute-start.19 = (bf16[256,512]{1,0:T(8,128)(2,1)}, bf16[256,512]{1,0:T(8,128)(2,1)S(1)}, u32[]{:S(2)}, u32[]{:S(2)}) collective-permute-start(bf16[256,512]{1,0:T(8,128)(2,1)} %copy-done.18), channel_id=1, source_target_pairs={{16,0},{20,4},{24,8},{28,12},{0,16},{4,20},{8,24},{12,28},{17,1},{... | collective-permute-start | bytes 786440 | tf_op jit(solution)/shard_map/ppermute | solution.py:54
  44.2 13.7 %collective-permute-start.17 = (bf16[64,2048]{1,0:T(8,128)(2,1)}, bf16[64,2048]{1,0:T(8,128)(2,1)S(1)}, u32[]{:S(2)}, u32[]{:S(2)}) collective-permute-start(bf16[64,2048]{1,0:T(8,128)(2,1)} %get-tuple-element.15), channel_id=1, source_target_pairs={{0,1},{1,0},{2,3},{3,2},{4,5},{5,4},{6,7},{7,6},{8,9},{9,8},{10,11... | collective-permute-start | bytes 786440 | tf_op jit(solution)/shard_map/ppermute | solution.py:432
  44.9 25.3 %collective-permute-start.21 = (bf16[272,512]{1,0:T(8,128)(2,1)}, bf16[272,512]{1,0:T(8,128)(2,1)S(1)}, u32[]{:S(2)}, u32[]{:S(2)}) collective-permute-start(bf16[272,512]{1,0:T(8,128)(2,1)} %get-tuple-element.16.refs_10_.refs_4_), channel_id=1, source_target_pairs={{4,0},{0,4},{12,8},{8,12},{20,16},{16,20},{28,24},{24,28},{5,1},{1... | collective-permute-start | bytes 835592 | tf_op jit(solution)/shard_map/ppermute | solution.py:54
  47.2 23.0 %collective-permute-start.23 = (bf16[272,512]{1,0:T(8,128)(2,1)}, bf16[272,512]{1,0:T(8,128)(2,1)S(1)}, u32[]{:S(2)}, u32[]{:S(2)}) collective-permute-start(bf16[272,512]{1,0:T(8,128)(2,1)} %get-tuple-element.16.refs_10_.refs_4_), channel_id=1, source_target_pairs={{24,0},{12,4},{0,8},{20,12},{8,16},{28,20},{16,24},{4,28},{25,1},{... | collective-permute-start | bytes 835592 | tf_op jit(solution)/shard_map/ppermute | solution.py:54
  57.5 6.6 %copy-start.13 = (bf16[256,512]{1,0:T(8,128)(2,1)}, bf16[256,512]{1,0:T(8,128)(2,1)S(1)}, u32[]{:S(2)}) copy-start(bf16[256,512]{1,0:T(8,128)(2,1)S(1)} %collective-permute-done.19.refs_8_.refs_18_) | copy-start | bytes 786436
  57.5 21.8 %collective-permute-start.16 = (bf16[64,2048]{1,0:T(8,128)(2,1)}, bf16[64,2048]{1,0:T(8,128)(2,1)S(1)}, u32[]{:S(2)}, u32[]{:S(2)}) collective-permute-start(bf16[64,2048]{1,0:T(8,128)(2,1)} %get-tuple-element.13), channel_id=1, source_target_pairs={{0,1},{1,0},{2,3},{3,2},{4,5},{5,4},{6,7},{7,6},{8,9},{9,8},{10,11... | collective-permute-start | bytes 786440 | tf_op jit(solution)/shard_map/ppermute | solution.py:432
  57.9 3.1 %collective-permute-start.20 = (bf16[256,512]{1,0:T(8,128)(2,1)S(1)}, bf16[256,512]{1,0:T(8,128)(2,1)S(1)}, u32[]{:S(2)}, u32[]{:S(2)}) collective-permute-start(bf16[256,512]{1,0:T(8,128)(2,1)S(1)} %collective-permute-done.19.refs_8_.refs_18_), channel_id=1, source_target_pairs={{4,0},{0,4},{12,8},{8,12},{20,16},{16,20},{28,24},{24,28},{5,1},{1... | collective-permute-start | bytes 786440 | tf_op jit(solution)/shard_map/ppermute | solution.py:54
  59.8 10.4 %copy-start.14 = (bf16[272,512]{1,0:T(8,128)(2,1)}, bf16[272,512]{1,0:T(8,128)(2,1)S(1)}, u32[]{:S(2)}) copy-start(bf16[272,512]{1,0:T(8,128)(2,1)S(1)} %collective-permute-done.22.refs_12_) | copy-start | bytes 835588
  59.8 10.4 %collective-permute-start.24 = (bf16[272,512]{1,0:T(8,128)(2,1)S(1)}, bf16[272,512]{1,0:T(8,128)(2,1)S(1)}, u32[]{:S(2)}, u32[]{:S(2)}) collective-permute-start(bf16[272,512]{1,0:T(8,128)(2,1)S(1)} %collective-permute-done.22.refs_12_), channel_id=1, source_target_pairs={{4,0},{0,4},{12,8},{8,12},{20,16},{16,20},{28,24},{24,28},{5,1},{1... | collective-permute-start | bytes 835592 | tf_op jit(solution)/shard_map/ppermute | solution.py:54
  61.0 9.2 %copy-start.22 = (bf16[256,512]{1,0:T(8,128)(2,1)}, bf16[256,512]{1,0:T(8,128)(2,1)S(1)}, u32[]{:S(2)}) copy-start(bf16[256,512]{1,0:T(8,128)(2,1)S(1)} %collective-permute-done.20.refs_9_) | copy-start | bytes 786436
  61.0 18.4 %collective-permute-start.18 = (bf16[64,2048]{1,0:T(8,128)(2,1)S(1)}, bf16[64,2048]{1,0:T(8,128)(2,1)S(1)}, u32[]{:S(2)}, u32[]{:S(2)}) collective-permute-start(bf16[64,2048]{1,0:T(8,128)(2,1)S(1)} %add_convert_fusion), channel_id=1, source_target_pairs={{0,2},{1,3},{2,0},{3,1},{4,6},{5,7},{6,4},{7,5},{8,10},{9,11},{10,... | collective-permute-start | bytes 786440 | tf_op jit(solution)/shard_map/ppermute | solution.py:432
  70.2 0.7 copy-start.15
  70.2 0.8 copy-start.16
  71.0 0.7 copy-start.17
  79.3 0.7 copy-start.1
  79.4 0.8 copy-start.2
  (1 other events, 0.7 us)

commit v6 on v4

--- a/solution.py
+++ b/solution.py
@@ -178,7 +178,7 @@
 def upstream_kernel(groups, *refs):
     keys_hbm, w_hbm, own_hbm, o32_ref, lse_ref = refs[:5]
     piece_refs = refs[5:4 + groups]
-    rest = refs[8 + groups:]
+    rest = refs[4 + groups + 1:]
     up_ref, stats_ref, keys, w_ref, grads, sem = rest
     rows, columns = o32_ref.shape
     width = w_ref.shape[1]
@@ -246,7 +246,7 @@
     keys_hbm, hosts_hbm, bias_hbm, q_hbm, up_ref, stats_ref = refs[:6]
     k_refs = refs[6:6 + len(PAIR)]
     v_refs = refs[6 + len(PAIR):6 + len(PAIR) + len(v_tags)]
-    dq_ref, keys, hosts, bias, q_ref, kcat, vcat, sem = refs[7 + len(PAIR) + len(v_tags):]
+    dq_ref, keys, hosts, bias, q_ref, kcat, vcat, sem = refs[6 + len(PAIR) + len(v_tags) + 1:]
     rows, columns = q_ref.shape
     blocks_dev, neigh = keys.shape
     heads_dev = columns // HDIM
@@ -382,6 +382,25 @@
     dv_ref[...] = dv_acc[...].astype(jnp.bfloat16)
 
 
+def sum_kernel(count, *refs):
+    total = refs[0][...].astype(jnp.float32)
+    for ref in refs[1:count]:
+        total = total + ref[...].astype(jnp.float32)
+    refs[-1][...] = total.astype(jnp.bfloat16)
+
+
+def sum_after(arrays, before):
+    return pl.pallas_call(
+        functools.partial(sum_kernel, len(arrays)),
+        out_shape=jax.ShapeDtypeStruct(arrays[0].shape, jnp.bfloat16),
+        in_specs=[VMEM] * len(arrays) + [ANY],
+        out_specs=VMEM,
+        compiler_params=params(60),
+        cost_estimate=cost(1000, 1000),
+        name="sum_after",
+    )(*arrays, before)
+
+
 def copy_kernel(count, extra, *refs):
     sources, targets = refs[:count], refs[count + extra:2 * count + extra]
     between, sem = refs[2 * count + extra:-1], refs[-1]
@@ -441,7 +460,7 @@
         pieces = [grad_mixed, beside, opposite, flip(opposite, 1)]
     else:
         pieces = [grad_mixed] + [ring(grad_mixed, step) for step in range(1, groups)]
-    (late_query,) = copies_after((query_states,), tuple(pieces[1:3]))
+    (late_query,) = copies_after((query_states,), (pieces[1], pieces[2]))
     q_win = exchange_pair(late_query, size)
     scalars = [
         pltpu.SMEM(key_blocks.shape, i32),
@@ -467,7 +486,7 @@
             pltpu.SemaphoreType.DMA((5 + 2 * places,)),
         ],
         compiler_params=params(60),
-        cost_estimate=cost(4 * 10**9, 8 * 10**6),
+        cost_estimate=cost(10**9, 10**6),
         name="attend",
     )(key_blocks, host_ids, host_bias, query_states, out_weight, *k_win, *v_win)
     parts = parts_o32_lse[:groups]
@@ -487,7 +506,7 @@
             jax.ShapeDtypeStruct((long_rows, columns), bf16),
             jax.ShapeDtypeStruct((BLK, BLK), f32),
         ],
-        in_specs=[HBM] * 3 + [VMEM] * 2 + [ANY] * (groups + 3),
+        in_specs=[HBM] * 3 + [VMEM] * 2 + [ANY] * (groups - 1 + 1),
         out_specs=[VMEM] * 2,
         scratch_shapes=[
             pltpu.SMEM(key_blocks.shape, i32),
@@ -496,9 +515,9 @@
             pltpu.SemaphoreType.DMA((5 + groups,)),
         ],
         compiler_params=params(60),
-        cost_estimate=cost(6 * 10**9, 6 * 10**6),
+        cost_estimate=cost(1000, 1000),
         name="upstream",
-    )(key_blocks, out_weight, grad_mixed, o32, lse, *pieces[1:], *q_win[:4])
+    )(key_blocks, out_weight, grad_mixed, o32, lse, *pieces[1:], q_win[1])
     up_win = exchange_pair(up, size)
 
     grad_query = pl.pallas_call(
@@ -514,7 +533,7 @@
             pltpu.SemaphoreType.DMA((4 + 2 * places,)),
         ],
         compiler_params=params(60),
-        cost_estimate=cost(10**9, 10**6),
+        cost_estimate=cost(16 * 10**9, 32 * 10**6),
         name="query_grad",
     )(key_blocks, host_ids, host_bias, query_states, up, stats, *k_win, *v_win, q_win[4])
 
@@ -539,13 +558,12 @@
             pltpu.SemaphoreType.DMA((3 * nsh + 5,)),
         ],
         compiler_params=params(60),
-        cost_estimate=cost(10**9, 10**6),
+        cost_estimate=cost(1000, 1000),
         name="key_grad",
     )(host_ids, host_bias, key_states, value_states, query_states, *q_win[1:], *up_win)
 
-    for piece in arrived:
-        mixed = mixed + piece.astype(f32)
-    return (mixed.astype(bf16), grad_query, grad_key, grad_value)
+    mixed_out = sum_after((parts[0], *arrived), grad_key)
+    return (mixed_out, grad_query, grad_key, grad_value)
 
 
 def solution(mesh):

time: 71.6 us -> 72.4 us (1.011)
  the two profiles are of different devices: /device:TPU:0 before, /device:TPU:1 now
where the time goes in v6:
time: 72.4 us; the launch traced here: 72.5 us
  Pallas kernels  29.2 us (40%)
  starting transfers between devices  27.7 us (38%)
  waiting for transfers between devices  9.89 us (14%)
  local copies, waits for them, and re-layouts  4.64 us (6%)
  between operations  0.93 us (1%)
    ppermute x17, starting transfers between devices, permute_from(): return lax.ppermute(x, 'ctx', [(source(i) % size, i) for i in range(size)])  18.9 us
    pallas_call x1, Pallas kernels, per_device(): pl.pallas_call(functools.partial(key_kernel, size, neigh), out_shape=[jax...  9.09 us
    ppermute x6, starting transfers between devices, flip(): return lax.ppermute(x, 'head', [(i, i ^ mask) for i in range(groups)])  8.81 us
    ppermute x17, waiting for transfers between devices, permute_from(): return lax.ppermute(x, 'ctx', [(source(i) % size, i) for i in range(size)])  8.62 us
    pallas_call x1, Pallas kernels, per_device(): pl.pallas_call(functools.partial(query_kernel, size, v_tags), out_shape=j...  6.12 us
    pallas_call x1, Pallas kernels, per_device(): pl.pallas_call(functools.partial(attend_kernel, size, groups, v_tags), ou...  5.45 us
    pallas_call x1, Pallas kernels, per_device(): pl.pallas_call(functools.partial(upstream_kernel, groups), out_shape=[jax...  4.94 us
    unnamed x50, local copies, waits for them, and re-layouts  4.64 us
  transfers between devices with their start and end apart: 23, of which 4 were waited for; matrix products, arithmetic and copies ran while one was open for 0% of the time, Pallas kernels for 38%

profile of v6, /device:TPU:1, one launch (start us, length us, event | category | flops | bytes accessed | tf_op | source)
XLA Modules:
  0.0 72.5 jit_solution(3732224162251082698)
XLA Ops:
  0.6 2.1 %collective-permute-start.5 = (bf16[256,512]{1,0:T(8,128)(2,1)}, bf16[256,512]{1,0:T(8,128)(2,1)S(1)}, u32[]{:S(2)}, u32[]{:S(2)}) collective-permute-start(bf16[256,512]{1,0:T(8,128)(2,1)} %refs_11_.1), channel_id=1, source_target_pairs={{8,0},{12,4},{0,8},{4,12},{24,16},{28,20},{16,24},{20,28},{9,1},{1... | collective-permute-start | bytes 786440 | tf_op jit(solution)/shard_map/ppermute | solution.py:54
  2.7 0.1 collective-permute-start.1
  2.8 2.4 %collective-permute-start = (bf16[256,512]{1,0:T(8,128)(2,1)}, bf16[256,512]{1,0:T(8,128)(2,1)S(1)}, u32[]{:S(2)}, u32[]{:S(2)}) collective-permute-start(bf16[256,512]{1,0:T(8,128)(2,1)} %refs_6_.1), channel_id=1, source_target_pairs={{4,0},{0,4},{12,8},{8,12},{20,16},{16,20},{28,24},{24,28},{5,1},{1... | collective-permute-start | bytes 786440 | tf_op jit(solution)/shard_map/ppermute | solution.py:54
  5.2 2.3 %collective-permute-start.13 = (bf16[64,2048]{1,0:T(8,128)(2,1)}, bf16[64,2048]{1,0:T(8,128)(2,1)S(1)}, u32[]{:S(2)}, u32[]{:S(2)}) collective-permute-start(bf16[64,2048]{1,0:T(8,128)(2,1)} %refs_2_.5), channel_id=1, source_target_pairs={{0,2},{1,3},{2,0},{3,1},{4,6},{5,7},{6,4},{7,5},{8,10},{9,11},{10,... | collective-permute-start | bytes 786440 | tf_op jit(solution)/shard_map/ppermute | solution.py:452
  7.5 1.3 %collective-permute-start.12 = (bf16[64,2048]{1,0:T(8,128)(2,1)}, bf16[64,2048]{1,0:T(8,128)(2,1)S(1)}, u32[]{:S(2)}, u32[]{:S(2)}) collective-permute-start(bf16[64,2048]{1,0:T(8,128)(2,1)} %refs_2_.5), channel_id=1, source_target_pairs={{0,1},{1,0},{2,3},{3,2},{4,5},{5,4},{6,7},{7,6},{8,9},{9,8},{10,11... | collective-permute-start | bytes 786440 | tf_op jit(solution)/shard_map/ppermute | solution.py:452
  8.8 0.2 collective-permute-done.5.refs_12_.refs_13_
  9.0 1.2 %collective-permute-start.7 = (bf16[256,512]{1,0:T(8,128)(2,1)S(1)}, bf16[256,512]{1,0:T(8,128)(2,1)S(1)}, u32[]{:S(2)}, u32[]{:S(2)}) collective-permute-start(bf16[256,512]{1,0:T(8,128)(2,1)S(1)} %collective-permute-done.5.refs_12_.refs_13_), channel_id=1, source_target_pairs={{16,0},{20,4},{24,8},{28,12},{0,16},{4,20},{8,24},{12,28},{17,1},{... | collective-permute-start | bytes 786440 | tf_op jit(solution)/shard_map/ppermute | solution.py:54
  10.2 5.3 %collective-permute-done.1.refs_7_.refs_8_ = bf16[256,512]{1,0:T(8,128)(2,1)S(1)} collective-permute-done((bf16[256,512]{1,0:T(8,128)(2,1)}, bf16[256,512]{1,0:T(8,128)(2,1)S(1)}, u32[]{:S(2)}, u32[]{:S(2)}) %collective-permute-start.1) | collective-permute-done | bytes 262176 | tf_op jit(solution)/shard_map/ppermute | solution.py:54
  15.5 1.2 %collective-permute-start.2 = (bf16[256,512]{1,0:T(8,128)(2,1)}, bf16[256,512]{1,0:T(8,128)(2,1)S(1)}, u32[]{:S(2)}, u32[]{:S(2)}) collective-permute-start(bf16[256,512]{1,0:T(8,128)(2,1)} %refs_6_.1), channel_id=1, source_target_pairs={{24,0},{12,4},{0,8},{20,12},{8,16},{28,20},{16,24},{4,28},{25,1},{... | collective-permute-start | bytes 786440 | tf_op jit(solution)/shard_map/ppermute | solution.py:54
  16.7 1.9 %collective-permute-start.4 = (bf16[256,512]{1,0:T(8,128)(2,1)}, bf16[256,512]{1,0:T(8,128)(2,1)S(1)}, u32[]{:S(2)}, u32[]{:S(2)}) collective-permute-start(bf16[256,512]{1,0:T(8,128)(2,1)} %refs_11_.1), channel_id=1, source_target_pairs={{4,0},{0,4},{12,8},{8,12},{20,16},{16,20},{28,24},{24,28},{5,1},{1... | collective-permute-start | bytes 786440 | tf_op jit(solution)/shard_map/ppermute | solution.py:54
  18.6 1.3 %collective-permute-done.13.refs_2_.refs_6_ = bf16[64,2048]{1,0:T(8,128)(2,1)S(1)} collective-permute-done((bf16[64,2048]{1,0:T(8,128)(2,1)}, bf16[64,2048]{1,0:T(8,128)(2,1)S(1)}, u32[]{:S(2)}, u32[]{:S(2)}) %collective-permute-start.13) | collective-permute-done | bytes 262176 | tf_op jit(solution)/shard_map/ppermute | solution.py:452
  19.9 0.8 %collective-permute-start.6 = (bf16[256,512]{1,0:T(8,128)(2,1)S(1)}, bf16[256,512]{1,0:T(8,128)(2,1)S(1)}, u32[]{:S(2)}, u32[]{:S(2)}) collective-permute-start(bf16[256,512]{1,0:T(8,128)(2,1)S(1)} %collective-permute-done.5.refs_12_.refs_13_), channel_id=1, source_target_pairs={{4,0},{0,4},{12,8},{8,12},{20,16},{16,20},{28,24},{24,28},{5,1},{1... | collective-permute-start | bytes 786440 | tf_op jit(solution)/shard_map/ppermute | solution.py:54
  20.7 0.0 collective-permute-done.12.refs_1_.refs_5_
  20.7 0.2 collective-permute-start.3
  20.9 0.0 collective-permute-done.7.refs_14_.refs_15_
  20.9 0.3 collective-permute-start.8
  21.3 0.2 copy-done.2
  21.4 1.7 %copies_after.1 = bf16[256,512]{1,0:T(8,128)(2,1)} custom-call(bf16[256,512]{1,0:T(8,128)(2,1)} %refs_3_.5, bf16[64,2048]{1,0:T(8,128)(2,1)} %copy-done.2, bf16[64,2048]{1,0:T(8,128)(2,1)} %copy-done.1), custom_call_target="tpu_custom_call" | custom-call | flops 1000 | bytes 1000 | tf_op jit(solution)/shard_map/copies_after/pallas_call | solution.py:412
  23.1 0.0 collective-permute-done.2.refs_8_.refs_9_
  23.2 0.0 copy-start.11
  23.2 1.3 %collective-permute-start.14 = (bf16[256,512]{1,0:T(8,128)(2,1)}, bf16[256,512]{1,0:T(8,128)(2,1)S(1)}, u32[]{:S(2)}, u32[]{:S(2)}) collective-permute-start(bf16[256,512]{1,0:T(8,128)(2,1)} %copies_after.1), channel_id=1, source_target_pairs={{4,0},{0,4},{12,8},{8,12},{20,16},{16,20},{28,24},{24,28},{5,1},{1... | collective-permute-start | bytes 786440 | tf_op jit(solution)/shard_map/ppermute | solution.py:54
  24.4 1.9 %collective-permute-start.15 = (bf16[256,512]{1,0:T(8,128)(2,1)}, bf16[256,512]{1,0:T(8,128)(2,1)S(1)}, u32[]{:S(2)}, u32[]{:S(2)}) collective-permute-start(bf16[256,512]{1,0:T(8,128)(2,1)} %copies_after.1), channel_id=1, source_target_pairs={{8,0},{28,4},{16,8},{4,12},{24,16},{12,20},{0,24},{20,28},{9,1},{2... | collective-permute-start | bytes 786440 | tf_op jit(solution)/shard_map/ppermute | solution.py:54
  26.4 1.3 %collective-permute-start.18 = (bf16[64,2048]{1,0:T(8,128)(2,1)}, bf16[64,2048]{1,0:T(8,128)(2,1)S(1)}, u32[]{:S(2)}, u32[]{:S(2)}) collective-permute-start(bf16[64,2048]{1,0:T(8,128)(2,1)} %copy-done.1), channel_id=1, source_target_pairs={{0,1},{1,0},{2,3},{3,2},{4,5},{5,4},{6,7},{7,6},{8,9},{9,8},{10,11... | collective-permute-start | bytes 786440 | tf_op jit(solution)/shard_map/ppermute | solution.py:452
  27.7 0.0 collective-permute-done.3.refs_9_.refs_10_
  27.8 0.6 copy-done.14
  28.4 0.7 copy-done.15
  29.1 5.5 %attend.1 = (bf16[64,2048]{1,0:T(8,128)(2,1)}, bf16[64,2048]{1,0:T(8,128)(2,1)}, bf16[64,2048]{1,0:T(8,128)(2,1)}, bf16[64,2048]{1,0:T(8,128)(2,1)}, f32[256,512]{1,0:T(8,128)}, /*index=5*/f32[128,128]{1,0:T(8,128)}) custom-call(s32[2,4]{1,0:T(2,128)} %refs_0_.9, s32[16]{0:T(128)} %refs_1_.7, f32[4]{0:T(128)} %refs_2_.7, bf16[256,512]{1,0:T(8,128)(2,1)} %refs_3_.5, ...), custom_call_target="tpu_custom_call" | custom-call | flops 1000000000 | bytes 1000000 | tf_op jit(solution)/shard_map/attend/pallas_call | solution.py:471
  34.6 0.2 collective-permute-start.10
  34.8 0.8 %collective-permute-start.16 = (bf16[256,512]{1,0:T(8,128)(2,1)S(1)}, bf16[256,512]{1,0:T(8,128)(2,1)S(1)}, u32[]{:S(2)}, u32[]{:S(2)}) collective-permute-start(bf16[256,512]{1,0:T(8,128)(2,1)S(1)} %copy-done.23), channel_id=1, source_target_pairs={{24,0},{12,4},{0,8},{20,12},{8,16},{28,20},{16,24},{4,28},{25,1},{... | collective-permute-start | bytes 786440 | tf_op jit(solution)/shard_map/ppermute | solution.py:54
  35.6 1.2 %collective-permute-start.17 = (bf16[256,512]{1,0:T(8,128)(2,1)S(1)}, bf16[256,512]{1,0:T(8,128)(2,1)S(1)}, u32[]{:S(2)}, u32[]{:S(2)}) collective-permute-start(bf16[256,512]{1,0:T(8,128)(2,1)S(1)} %collective-permute-done.15.refs_6_), channel_id=1, source_target_pairs={{4,0},{0,4},{12,8},{8,12},{20,16},{16,20},{28,24},{24,28},{5,1},{1... | collective-permute-start | bytes 786440 | tf_op jit(solution)/shard_map/ppermute | solution.py:54
  36.9 0.7 copy-done
  37.6 0.1 copy-done.22
  37.7 4.9 %upstream.1 = (bf16[272,512]{1,0:T(8,128)(2,1)}, f32[128,128]{1,0:T(8,128)}) custom-call(s32[2,4]{1,0:T(2,128)} %refs_0_.9, bf16[512,2048]{1,0:T(8,128)(2,1)} %refs_1_.5, bf16[64,2048]{1,0:T(8,128)(2,1)} %refs_2_.5, f32[256,512]{1,0:T(8,128)} %get-tuple-element.18.refs_3_, f32[128,128]{1,0:T(8,128)} %get-tuple-element.19.refs_4_, ...), custom_call_target="tpu_custom_call" | custom-call | flops 1000 | bytes 1000 | tf_op jit(solution)/shard_map/upstream/pallas_call | solution.py:503
  42.6 1.9 %collective-permute-start.20 = (bf16[272,512]{1,0:T(8,128)(2,1)}, bf16[272,512]{1,0:T(8,128)(2,1)S(1)}, u32[]{:S(2)}, u32[]{:S(2)}) collective-permute-start(bf16[272,512]{1,0:T(8,128)(2,1)} %get-tuple-element.20.refs_9_.refs_4_), channel_id=1, source_target_pairs={{8,0},{28,4},{16,8},{4,12},{24,16},{12,20},{0,24},{20,28},{9,1},{2... | collective-permute-start | bytes 835592 | tf_op jit(solution)/shard_map/ppermute | solution.py:54
  44.5 1.0 %collective-permute-start.19 = (bf16[272,512]{1,0:T(8,128)(2,1)}, bf16[272,512]{1,0:T(8,128)(2,1)S(1)}, u32[]{:S(2)}, u32[]{:S(2)}) collective-permute-start(bf16[272,512]{1,0:T(8,128)(2,1)} %get-tuple-element.20.refs_9_.refs_4_), channel_id=1, source_target_pairs={{4,0},{0,4},{12,8},{8,12},{20,16},{16,20},{28,24},{24,28},{5,1},{1... | collective-permute-start | bytes 835592 | tf_op jit(solution)/shard_map/ppermute | solution.py:54
  45.6 0.1 add_convert_fusion
  45.7 1.4 %collective-permute-start.9 = (bf16[64,2048]{1,0:T(8,128)(2,1)S(1)}, bf16[64,2048]{1,0:T(8,128)(2,1)S(1)}, u32[]{:S(2)}, u32[]{:S(2)}) collective-permute-start(bf16[64,2048]{1,0:T(8,128)(2,1)S(1)} %copy-done.24), channel_id=1, source_target_pairs={{0,1},{1,0},{2,3},{3,2},{4,5},{5,4},{6,7},{7,6},{8,9},{9,8},{10,11... | collective-permute-start | bytes 786440 | tf_op jit(solution)/shard_map/ppermute | solution.py:452
  47.0 2.3 %collective-permute-start.11 = (bf16[64,2048]{1,0:T(8,128)(2,1)S(1)}, bf16[64,2048]{1,0:T(8,128)(2,1)S(1)}, u32[]{:S(2)}, u32[]{:S(2)}) collective-permute-start(bf16[64,2048]{1,0:T(8,128)(2,1)S(1)} %add_convert_fusion), channel_id=1, source_target_pairs={{0,2},{1,3},{2,0},{3,1},{4,6},{5,7},{6,4},{7,5},{8,10},{9,11},{10,... | collective-permute-start | bytes 786440 | tf_op jit(solution)/shard_map/ppermute | solution.py:452
  49.3 3.1 %collective-permute-done.20.refs_11_ = bf16[272,512]{1,0:T(8,128)(2,1)S(1)} collective-permute-done((bf16[272,512]{1,0:T(8,128)(2,1)}, bf16[272,512]{1,0:T(8,128)(2,1)S(1)}, u32[]{:S(2)}, u32[]{:S(2)}) %collective-permute-start.20) | collective-permute-done | bytes 278560 | tf_op jit(solution)/shard_map/ppermute | solution.py:54
  52.4 0.5 collective-permute-start.22
  52.9 6.1 %query_grad.1 = bf16[256,512]{1,0:T(8,128)(2,1)} custom-call(s32[2,4]{1,0:T(2,128)} %refs_0_.9, s32[16]{0:T(128)} %refs_1_.7, f32[4]{0:T(128)} %refs_2_.7, bf16[256,512]{1,0:T(8,128)(2,1)} %refs_3_.5, bf16[272,512]{1,0:T(8,128)(2,1)} %get-tuple-element.20.refs_9_.refs_4_, f32[128,128]{1,0:T(8,128)} %get-tuple-element.22.refs_5_, bf16[256,512]{1,0:T(8,128)(2,1)} %refs_6_.1, ...), custom_call_target="tpu_custom_call" | custom-call | flops 16000000000 | bytes 32000000 | tf_op jit(solution)/shard_map/query_grad/pallas_call | solution.py:523
  59.2 0.7 copy-done.4
  59.8 0.1 copy-done.5
  59.9 0.7 copy-done.6
  60.7 9.1 %key_grad.1 = (bf16[256,512]{1,0:T(8,128)(2,1)}, bf16[256,512]{1,0:T(8,128)(2,1)}) custom-call(s32[16]{0:T(128)} %refs_1_.7, f32[4]{0:T(128)} %refs_2_.7, bf16[256,512]{1,0:T(8,128)(2,1)} %refs_6_.1, bf16[256,512]{1,0:T(8,128)(2,1)} %refs_11_.1, bf16[256,512]{1,0:T(8,128)(2,1)} %refs_3_.5, bf16[256,512]{1,0:T(8,128)(2,1)} %copy-done, ...), custom_call_target="tpu_custom_call" | custom-call | flops 1000 | bytes 1000 | tf_op jit(solution)/shard_map/key_grad/pallas_call | solution.py:540
  69.8 0.7 copy-done.19
  70.5 0.1 copy-done.20
  70.6 1.9 %sum_after.1 = bf16[64,2048]{1,0:T(8,128)(2,1)} custom-call(bf16[64,2048]{1,0:T(8,128)(2,1)} %get-tuple-element.14.refs_0_, bf16[64,2048]{1,0:T(8,128)(2,1)} %copy-done.19, bf16[64,2048]{1,0:T(8,128)(2,1)} %copy-done.20, bf16[256,512]{1,0:T(8,128)(2,1)} %get-tuple-element.12.refs_3_), custom_call_target="tpu_custom_call" | custom-call | flops 1000 | bytes 1000 | tf_op jit(solution)/shard_map/sum_after/pallas_call | solution.py:393
  (55 shorter events, 0.1 us)
Async XLA Ops:
  0.6 8.4 %collective-permute-start.5 = (bf16[256,512]{1,0:T(8,128)(2,1)}, bf16[256,512]{1,0:T(8,128)(2,1)S(1)}, u32[]{:S(2)}, u32[]{:S(2)}) collective-permute-start(bf16[256,512]{1,0:T(8,128)(2,1)} %refs_11_.1), channel_id=1, source_target_pairs={{8,0},{12,4},{0,8},{4,12},{24,16},{28,20},{16,24},{20,28},{9,1},{1... | collective-permute-start | bytes 786440 | tf_op jit(solution)/shard_map/ppermute | solution.py:54
  2.7 12.7 %collective-permute-start.1 = (bf16[256,512]{1,0:T(8,128)(2,1)}, bf16[256,512]{1,0:T(8,128)(2,1)S(1)}, u32[]{:S(2)}, u32[]{:S(2)}) collective-permute-start(bf16[256,512]{1,0:T(8,128)(2,1)} %refs_6_.1), channel_id=1, source_target_pairs={{8,0},{28,4},{16,8},{4,12},{24,16},{12,20},{0,24},{20,28},{9,1},{2... | collective-permute-start | bytes 786440 | tf_op jit(solution)/shard_map/ppermute | solution.py:54
  2.8 13.9 %collective-permute-start = (bf16[256,512]{1,0:T(8,128)(2,1)}, bf16[256,512]{1,0:T(8,128)(2,1)S(1)}, u32[]{:S(2)}, u32[]{:S(2)}) collective-permute-start(bf16[256,512]{1,0:T(8,128)(2,1)} %refs_6_.1), channel_id=1, source_target_pairs={{4,0},{0,4},{12,8},{8,12},{20,16},{16,20},{28,24},{24,28},{5,1},{1... | collective-permute-start | bytes 786440 | tf_op jit(solution)/shard_map/ppermute | solution.py:54
  5.2 14.7 %collective-permute-start.13 = (bf16[64,2048]{1,0:T(8,128)(2,1)}, bf16[64,2048]{1,0:T(8,128)(2,1)S(1)}, u32[]{:S(2)}, u32[]{:S(2)}) collective-permute-start(bf16[64,2048]{1,0:T(8,128)(2,1)} %refs_2_.5), channel_id=1, source_target_pairs={{0,2},{1,3},{2,0},{3,1},{4,6},{5,7},{6,4},{7,5},{8,10},{9,11},{10,... | collective-permute-start | bytes 786440 | tf_op jit(solution)/shard_map/ppermute | solution.py:452
  7.5 13.2 %collective-permute-start.12 = (bf16[64,2048]{1,0:T(8,128)(2,1)}, bf16[64,2048]{1,0:T(8,128)(2,1)S(1)}, u32[]{:S(2)}, u32[]{:S(2)}) collective-permute-start(bf16[64,2048]{1,0:T(8,128)(2,1)} %refs_2_.5), channel_id=1, source_target_pairs={{0,1},{1,0},{2,3},{3,2},{4,5},{5,4},{6,7},{7,6},{8,9},{9,8},{10,11... | collective-permute-start | bytes 786440 | tf_op jit(solution)/shard_map/ppermute | solution.py:452
  9.0 18.7 %copy-start.7 = (bf16[256,512]{1,0:T(8,128)(2,1)}, bf16[256,512]{1,0:T(8,128)(2,1)S(1)}, u32[]{:S(2)}) copy-start(bf16[256,512]{1,0:T(8,128)(2,1)S(1)} %collective-permute-done.5.refs_12_.refs_13_) | copy-start | bytes 786436
  9.0 12.0 %collective-permute-start.7 = (bf16[256,512]{1,0:T(8,128)(2,1)S(1)}, bf16[256,512]{1,0:T(8,128)(2,1)S(1)}, u32[]{:S(2)}, u32[]{:S(2)}) collective-permute-start(bf16[256,512]{1,0:T(8,128)(2,1)S(1)} %collective-permute-done.5.refs_12_.refs_13_), channel_id=1, source_target_pairs={{16,0},{20,4},{24,8},{28,12},{0,16},{4,20},{8,24},{12,28},{17,1},{... | collective-permute-start | bytes 786440 | tf_op jit(solution)/shard_map/ppermute | solution.py:54
  15.5 12.2 %copy-start.8 = (bf16[256,512]{1,0:T(8,128)(2,1)}, bf16[256,512]{1,0:T(8,128)(2,1)S(1)}, u32[]{:S(2)}) copy-start(bf16[256,512]{1,0:T(8,128)(2,1)S(1)} %collective-permute-done.1.refs_7_.refs_8_) | copy-start | bytes 786436
  15.5 7.7 %collective-permute-start.2 = (bf16[256,512]{1,0:T(8,128)(2,1)}, bf16[256,512]{1,0:T(8,128)(2,1)S(1)}, u32[]{:S(2)}, u32[]{:S(2)}) collective-permute-start(bf16[256,512]{1,0:T(8,128)(2,1)} %refs_6_.1), channel_id=1, source_target_pairs={{24,0},{12,4},{0,8},{20,12},{8,16},{28,20},{16,24},{4,28},{25,1},{... | collective-permute-start | bytes 786440 | tf_op jit(solution)/shard_map/ppermute | solution.py:54
  16.7 11.0 %copy-start.9 = (bf16[256,512]{1,0:T(8,128)(2,1)}, bf16[256,512]{1,0:T(8,128)(2,1)S(1)}, u32[]{:S(2)}) copy-start(bf16[256,512]{1,0:T(8,128)(2,1)S(1)} %collective-permute-done.refs_6_.refs_7_) | copy-start | bytes 786436
  16.7 7.7 %collective-permute-start.4 = (bf16[256,512]{1,0:T(8,128)(2,1)}, bf16[256,512]{1,0:T(8,128)(2,1)S(1)}, u32[]{:S(2)}, u32[]{:S(2)}) collective-permute-start(bf16[256,512]{1,0:T(8,128)(2,1)} %refs_11_.1), channel_id=1, source_target_pairs={{4,0},{0,4},{12,8},{8,12},{20,16},{16,20},{28,24},{24,28},{5,1},{1... | collective-permute-start | bytes 786440 | tf_op jit(solution)/shard_map/ppermute | solution.py:54
  19.9 1.4 %copy-start.1 = (bf16[64,2048]{1,0:T(8,128)(2,1)}, bf16[64,2048]{1,0:T(8,128)(2,1)S(1)}, u32[]{:S(2)}) copy-start(bf16[64,2048]{1,0:T(8,128)(2,1)S(1)} %collective-permute-done.13.refs_2_.refs_6_) | copy-start | bytes 786436
  19.9 6.5 %collective-permute-start.6 = (bf16[256,512]{1,0:T(8,128)(2,1)S(1)}, bf16[256,512]{1,0:T(8,128)(2,1)S(1)}, u32[]{:S(2)}, u32[]{:S(2)}) collective-permute-start(bf16[256,512]{1,0:T(8,128)(2,1)S(1)} %collective-permute-done.5.refs_12_.refs_13_), channel_id=1, source_target_pairs={{4,0},{0,4},{12,8},{8,12},{20,16},{16,20},{28,24},{24,28},{5,1},{1... | collective-permute-start | bytes 786440 | tf_op jit(solution)/shard_map/ppermute | solution.py:54
  20.7 0.7 copy-start.2
  20.7 6.9 %collective-permute-start.3 = (bf16[256,512]{1,0:T(8,128)(2,1)S(1)}, bf16[256,512]{1,0:T(8,128)(2,1)S(1)}, u32[]{:S(2)}, u32[]{:S(2)}) collective-permute-start(bf16[256,512]{1,0:T(8,128)(2,1)S(1)} %collective-permute-done.1.refs_7_.refs_8_), channel_id=1, source_target_pairs={{4,0},{0,4},{12,8},{8,12},{20,16},{16,20},{28,24},{24,28},{5,1},{1... | collective-permute-start | bytes 786440 | tf_op jit(solution)/shard_map/ppermute | solution.py:54
  20.9 6.8 %copy-start.10 = (bf16[256,512]{1,0:T(8,128)(2,1)}, bf16[256,512]{1,0:T(8,128)(2,1)S(1)}, u32[]{:S(2)}) copy-start(bf16[256,512]{1,0:T(8,128)(2,1)S(1)} %collective-permute-done.7.refs_14_.refs_15_) | copy-start | bytes 786436
  20.9 6.7 %collective-permute-start.8 = (bf16[256,512]{1,0:T(8,128)(2,1)S(1)}, bf16[256,512]{1,0:T(8,128)(2,1)S(1)}, u32[]{:S(2)}, u32[]{:S(2)}) collective-permute-start(bf16[256,512]{1,0:T(8,128)(2,1)S(1)} %collective-permute-done.7.refs_14_.refs_15_), channel_id=1, source_target_pairs={{4,0},{0,4},{12,8},{8,12},{20,16},{16,20},{28,24},{24,28},{5,1},{1... | collective-permute-start | bytes 786440 | tf_op jit(solution)/shard_map/ppermute | solution.py:54
  23.1 11.7 %copy-start.23 = (bf16[256,512]{1,0:T(8,128)(2,1)S(1)}, bf16[256,512]{1,0:T(8,128)(2,1)}, u32[]{:S(2)}) copy-start(bf16[256,512]{1,0:T(8,128)(2,1)} %copies_after.1) | copy-start | bytes 786436
  23.2 4.6 %copy-start.11 = (bf16[256,512]{1,0:T(8,128)(2,1)}, bf16[256,512]{1,0:T(8,128)(2,1)S(1)}, u32[]{:S(2)}) copy-start(bf16[256,512]{1,0:T(8,128)(2,1)S(1)} %collective-permute-done.2.refs_8_.refs_9_) | copy-start | bytes 786436
  23.2 13.7 %collective-permute-start.14 = (bf16[256,512]{1,0:T(8,128)(2,1)}, bf16[256,512]{1,0:T(8,128)(2,1)S(1)}, u32[]{:S(2)}, u32[]{:S(2)}) collective-permute-start(bf16[256,512]{1,0:T(8,128)(2,1)} %copies_after.1), channel_id=1, source_target_pairs={{4,0},{0,4},{12,8},{8,12},{20,16},{16,20},{28,24},{24,28},{5,1},{1... | collective-permute-start | bytes 786440 | tf_op jit(solution)/shard_map/ppermute | solution.py:54
  24.4 3.3 %copy-start.12 = (bf16[256,512]{1,0:T(8,128)(2,1)}, bf16[256,512]{1,0:T(8,128)(2,1)S(1)}, u32[]{:S(2)}) copy-start(bf16[256,512]{1,0:T(8,128)(2,1)S(1)} %collective-permute-done.4.refs_11_.refs_12_) | copy-start | bytes 786436
  24.4 11.2 %collective-permute-start.15 = (bf16[256,512]{1,0:T(8,128)(2,1)}, bf16[256,512]{1,0:T(8,128)(2,1)S(1)}, u32[]{:S(2)}, u32[]{:S(2)}) collective-permute-start(bf16[256,512]{1,0:T(8,128)(2,1)} %copies_after.1), channel_id=1, source_target_pairs={{8,0},{28,4},{16,8},{4,12},{24,16},{12,20},{0,24},{20,28},{9,1},{2... | collective-permute-start | bytes 786440 | tf_op jit(solution)/shard_map/ppermute | solution.py:54
  26.4 1.4 %copy-start.13 = (bf16[256,512]{1,0:T(8,128)(2,1)}, bf16[256,512]{1,0:T(8,128)(2,1)S(1)}, u32[]{:S(2)}) copy-start(bf16[256,512]{1,0:T(8,128)(2,1)S(1)} %collective-permute-done.6.refs_13_.refs_14_) | copy-start | bytes 786436
  26.4 10.5 %collective-permute-start.18 = (bf16[64,2048]{1,0:T(8,128)(2,1)}, bf16[64,2048]{1,0:T(8,128)(2,1)S(1)}, u32[]{:S(2)}, u32[]{:S(2)}) collective-permute-start(bf16[64,2048]{1,0:T(8,128)(2,1)} %copy-done.1), channel_id=1, source_target_pairs={{0,1},{1,0},{2,3},{3,2},{4,5},{5,4},{6,7},{7,6},{8,9},{9,8},{10,11... | collective-permute-start | bytes 786440 | tf_op jit(solution)/shard_map/ppermute | solution.py:452
  27.7 0.7 copy-start.14
  28.4 0.7 copy-start.15
  34.5 11.0 %copy-start.21 = (bf16[64,2048]{1,0:T(8,128)(2,1)S(1)}, bf16[64,2048]{1,0:T(8,128)(2,1)}, u32[]{:S(2)}) copy-start(bf16[64,2048]{1,0:T(8,128)(2,1)} %get-tuple-element.16) | copy-start | bytes 786436
  34.6 11.0 %collective-permute-start.10 = (bf16[64,2048]{1,0:T(8,128)(2,1)}, bf16[64,2048]{1,0:T(8,128)(2,1)S(1)}, u32[]{:S(2)}, u32[]{:S(2)}) collective-permute-start(bf16[64,2048]{1,0:T(8,128)(2,1)} %get-tuple-element.17), channel_id=1, source_target_pairs={{0,1},{1,0},{2,3},{3,2},{4,5},{5,4},{6,7},{7,6},{8,9},{9,8},{10,11... | collective-permute-start | bytes 786440 | tf_op jit(solution)/shard_map/ppermute | solution.py:452
  34.8 10.9 %collective-permute-start.16 = (bf16[256,512]{1,0:T(8,128)(2,1)S(1)}, bf16[256,512]{1,0:T(8,128)(2,1)S(1)}, u32[]{:S(2)}, u32[]{:S(2)}) collective-permute-start(bf16[256,512]{1,0:T(8,128)(2,1)S(1)} %copy-done.23), channel_id=1, source_target_pairs={{24,0},{12,4},{0,8},{20,12},{8,16},{28,20},{16,24},{4,28},{25,1},{... | collective-permute-start | bytes 786440 | tf_op jit(solution)/shard_map/ppermute | solution.py:54
  35.6 23.5 %copy-start.16 = (bf16[256,512]{1,0:T(8,128)(2,1)}, bf16[256,512]{1,0:T(8,128)(2,1)S(1)}, u32[]{:S(2)}) copy-start(bf16[256,512]{1,0:T(8,128)(2,1)S(1)} %collective-permute-done.15.refs_6_) | copy-start | bytes 786436
  35.6 11.4 %collective-permute-start.17 = (bf16[256,512]{1,0:T(8,128)(2,1)S(1)}, bf16[256,512]{1,0:T(8,128)(2,1)S(1)}, u32[]{:S(2)}, u32[]{:S(2)}) collective-permute-start(bf16[256,512]{1,0:T(8,128)(2,1)S(1)} %collective-permute-done.15.refs_6_), channel_id=1, source_target_pairs={{4,0},{0,4},{12,8},{8,12},{20,16},{16,20},{28,24},{24,28},{5,1},{1... | collective-permute-start | bytes 786440 | tf_op jit(solution)/shard_map/ppermute | solution.py:54
  36.8 0.7 copy-start
  36.8 0.8 %copy-start.22 = (bf16[64,2048]{1,0:T(8,128)(2,1)}, bf16[64,2048]{1,0:T(8,128)(2,1)S(1)}, u32[]{:S(2)}) copy-start(bf16[64,2048]{1,0:T(8,128)(2,1)S(1)} %collective-permute-done.18.refs_7_) | copy-start | bytes 786436
  37.7 8.0 %copy-start.24 = (bf16[64,2048]{1,0:T(8,128)(2,1)S(1)}, bf16[64,2048]{1,0:T(8,128)(2,1)}, u32[]{:S(2)}) copy-start(bf16[64,2048]{1,0:T(8,128)(2,1)} %get-tuple-element.15) | copy-start | bytes 786436
  42.6 9.8 %collective-permute-start.20 = (bf16[272,512]{1,0:T(8,128)(2,1)}, bf16[272,512]{1,0:T(8,128)(2,1)S(1)}, u32[]{:S(2)}, u32[]{:S(2)}) collective-permute-start(bf16[272,512]{1,0:T(8,128)(2,1)} %get-tuple-element.20.refs_9_.refs_4_), channel_id=1, source_target_pairs={{8,0},{28,4},{16,8},{4,12},{24,16},{12,20},{0,24},{20,28},{9,1},{2... | collective-permute-start | bytes 835592 | tf_op jit(solution)/shard_map/ppermute | solution.py:54
  44.5 14.6 %collective-permute-start.19 = (bf16[272,512]{1,0:T(8,128)(2,1)}, bf16[272,512]{1,0:T(8,128)(2,1)S(1)}, u32[]{:S(2)}, u32[]{:S(2)}) collective-permute-start(bf16[272,512]{1,0:T(8,128)(2,1)} %get-tuple-element.20.refs_9_.refs_4_), channel_id=1, source_target_pairs={{4,0},{0,4},{12,8},{8,12},{20,16},{16,20},{28,24},{24,28},{5,1},{1... | collective-permute-start | bytes 835592 | tf_op jit(solution)/shard_map/ppermute | solution.py:54
  45.6 13.6 %collective-permute-start.21 = (bf16[272,512]{1,0:T(8,128)(2,1)}, bf16[272,512]{1,0:T(8,128)(2,1)S(1)}, u32[]{:S(2)}, u32[]{:S(2)}) collective-permute-start(bf16[272,512]{1,0:T(8,128)(2,1)} %get-tuple-element.20.refs_9_.refs_4_), channel_id=1, source_target_pairs={{24,0},{12,4},{0,8},{20,12},{8,16},{28,20},{16,24},{4,28},{25,1},{... | collective-permute-start | bytes 835592 | tf_op jit(solution)/shard_map/ppermute | solution.py:54
  45.6 13.4 %copy-start.17 = (bf16[256,512]{1,0:T(8,128)(2,1)}, bf16[256,512]{1,0:T(8,128)(2,1)S(1)}, u32[]{:S(2)}) copy-start(bf16[256,512]{1,0:T(8,128)(2,1)S(1)} %collective-permute-done.16.refs_7_) | copy-start | bytes 786436
  45.7 24.1 %collective-permute-start.9 = (bf16[64,2048]{1,0:T(8,128)(2,1)S(1)}, bf16[64,2048]{1,0:T(8,128)(2,1)S(1)}, u32[]{:S(2)}, u32[]{:S(2)}) collective-permute-start(bf16[64,2048]{1,0:T(8,128)(2,1)S(1)} %copy-done.24), channel_id=1, source_target_pairs={{0,1},{1,0},{2,3},{3,2},{4,5},{5,4},{6,7},{7,6},{8,9},{9,8},{10,11... | collective-permute-start | bytes 786440 | tf_op jit(solution)/shard_map/ppermute | solution.py:452
  47.0 5.9 %copy-start.18 = (bf16[256,512]{1,0:T(8,128)(2,1)}, bf16[256,512]{1,0:T(8,128)(2,1)S(1)}, u32[]{:S(2)}) copy-start(bf16[256,512]{1,0:T(8,128)(2,1)S(1)} %collective-permute-done.17.refs_8_.refs_17_) | copy-start | bytes 786436
  47.0 22.7 %collective-permute-start.11 = (bf16[64,2048]{1,0:T(8,128)(2,1)S(1)}, bf16[64,2048]{1,0:T(8,128)(2,1)S(1)}, u32[]{:S(2)}, u32[]{:S(2)}) collective-permute-start(bf16[64,2048]{1,0:T(8,128)(2,1)S(1)} %add_convert_fusion), channel_id=1, source_target_pairs={{0,2},{1,3},{2,0},{3,1},{4,6},{5,7},{6,4},{7,5},{8,10},{9,11},{10,... | collective-permute-start | bytes 786440 | tf_op jit(solution)/shard_map/ppermute | solution.py:452
  52.4 6.7 %copy-start.3 = (bf16[272,512]{1,0:T(8,128)(2,1)}, bf16[272,512]{1,0:T(8,128)(2,1)S(1)}, u32[]{:S(2)}) copy-start(bf16[272,512]{1,0:T(8,128)(2,1)S(1)} %collective-permute-done.20.refs_11_) | copy-start | bytes 835588
  52.4 6.7 %collective-permute-start.22 = (bf16[272,512]{1,0:T(8,128)(2,1)S(1)}, bf16[272,512]{1,0:T(8,128)(2,1)S(1)}, u32[]{:S(2)}, u32[]{:S(2)}) collective-permute-start(bf16[272,512]{1,0:T(8,128)(2,1)S(1)} %collective-permute-done.20.refs_11_), channel_id=1, source_target_pairs={{4,0},{0,4},{12,8},{8,12},{20,16},{16,20},{28,24},{24,28},{5,1},{1... | collective-permute-start | bytes 835592 | tf_op jit(solution)/shard_map/ppermute | solution.py:54
  59.1 0.7 copy-start.4
  59.1 0.8 %copy-start.5 = (bf16[272,512]{1,0:T(8,128)(2,1)}, bf16[272,512]{1,0:T(8,128)(2,1)S(1)}, u32[]{:S(2)}) copy-start(bf16[272,512]{1,0:T(8,128)(2,1)S(1)} %collective-permute-done.21.refs_12_) | copy-start | bytes 835588
  59.9 0.7 copy-start.6
  69.8 0.7 copy-start.19
  69.8 0.8 %copy-start.20 = (bf16[64,2048]{1,0:T(8,128)(2,1)}, bf16[64,2048]{1,0:T(8,128)(2,1)S(1)}, u32[]{:S(2)}) copy-start(bf16[64,2048]{1,0:T(8,128)(2,1)S(1)} %collective-permute-done.11.refs_2_) | copy-start | bytes 786436

commit v7 on v6

--- a/solution.py
+++ b/solution.py
@@ -176,40 +176,38 @@
 
 
 def upstream_kernel(groups, *refs):
-    keys_hbm, w_hbm, own_hbm, o32_ref, lse_ref = refs[:5]
+    keys_hbm, w_hbm, own_hbm, o32_any, lse_any = refs[:5]
     piece_refs = refs[5:4 + groups]
     rest = refs[4 + groups + 1:]
-    up_ref, stats_ref, keys, w_ref, grads, sem = rest
+    up_ref, stats_ref, keys, w_ref, grads, o32_ref, lse_ref, sem = rest
     rows, columns = o32_ref.shape
-    width = w_ref.shape[1]
     blocks_dev, neigh = keys.shape
     heads_dev = columns // HDIM
     part = rows // groups
-    cut = width // 4
-    w_waits = [
-        start_all([(w_hbm.at[:, c * cut:(c + 1) * cut], w_ref.at[:, c * cut:(c + 1) * cut])], sem, c)[0]
-        for c in range(4)
+    cut = columns // 2
+    waits = [
+        start_all([(w_hbm.at[c * cut:(c + 1) * cut], w_ref.at[c * cut:(c + 1) * cut])], sem, c)[0]
+        for c in range(2)
     ]
     pieces = (own_hbm,) + tuple(piece_refs)
-    wait_all(
-        start_all(
-            [(ref, grads.at[pl.ds(step * part, part)]) for step, ref in enumerate(pieces)]
-            + [(keys_hbm, keys)],
-            sem,
-            4,
-        )
+    early = start_all(
+        [(ref, grads.at[pl.ds(step * part, part)]) for step, ref in enumerate(pieces)]
+        + [(keys_hbm, keys)],
+        sem,
+        2,
     )
-    total = jnp.zeros((rows, columns), jnp.float32)
-    for c in range(4):
-        w_waits[c].wait()
-        total = total + tdot(grads[:, c * cut:(c + 1) * cut], w_ref[:, c * cut:(c + 1) * cut])
+    late = start_all([(o32_any, o32_ref), (lse_any, lse_ref)], sem, 3 + groups)
+    wait_all(early)
     me = lax.axis_index("head")
-    product = total.astype(jnp.bfloat16)
-    for step in range(groups):
-        owner = piece_owner(me, step, groups, -1)
-        up_ref[pl.ds(pl.multiple_of(owner * part, part), part), :] = product[
-            step * part:(step + 1) * part, :
-        ]
+    for c in range(2):
+        waits[c].wait()
+        product = tdot(grads[...], w_ref[c * cut:(c + 1) * cut, :]).astype(jnp.bfloat16)
+        for step in range(groups):
+            owner = piece_owner(me, step, groups, -1)
+            up_ref[pl.ds(pl.multiple_of(owner * part, part), part), c * cut:(c + 1) * cut] = product[
+                step * part:(step + 1) * part, :
+            ]
+    wait_all(late)
     pairs = blocks_dev * heads_dev
     lane = lax.broadcasted_iota(jnp.int32, (BLK, BLK), 1)
     stats = lse_ref[...]
@@ -281,9 +279,9 @@
     hosts_hbm, bias_hbm, k_hbm, v_hbm = refs[:4]
     q_refs = refs[4:4 + nsh]
     up_refs = refs[4 + nsh:4 + 2 * nsh]
-    dk_ref, dv_ref = refs[4 + 2 * nsh:6 + 2 * nsh]
+    dk_ref, dv_ref, mark_ref = refs[4 + 2 * nsh:7 + 2 * nsh]
     (hosts, bias, k_ref, v_ref, qwin, upwin, stats, lists, keys, hits, dk_acc, dv_acc, sem) = refs[
-        6 + 2 * nsh:
+        7 + 2 * nsh:
     ]
     rows, columns = k_ref.shape
     long_rows = up_refs[0].shape[0]
@@ -380,6 +378,7 @@
         lax.fori_loop(0, lax.div(counts[own] + 1, 2), visit, 0)
     dk_ref[...] = dk_acc[...].astype(jnp.bfloat16)
     dv_ref[...] = dv_acc[...].astype(jnp.bfloat16)
+    mark_ref[...] = jnp.zeros_like(mark_ref)
 
 
 def sum_kernel(count, *refs):
@@ -395,7 +394,7 @@
         out_shape=jax.ShapeDtypeStruct(arrays[0].shape, jnp.bfloat16),
         in_specs=[VMEM] * len(arrays) + [ANY],
         out_specs=VMEM,
-        compiler_params=params(60),
+        compiler_params=params(8),
         cost_estimate=cost(1000, 1000),
         name="sum_after",
     )(*arrays, before)
@@ -506,12 +505,14 @@
             jax.ShapeDtypeStruct((long_rows, columns), bf16),
             jax.ShapeDtypeStruct((BLK, BLK), f32),
         ],
-        in_specs=[HBM] * 3 + [VMEM] * 2 + [ANY] * (groups - 1 + 1),
+        in_specs=[HBM] * 3 + [ANY] * (groups + 2),
         out_specs=[VMEM] * 2,
         scratch_shapes=[
             pltpu.SMEM(key_blocks.shape, i32),
             pltpu.VMEM((columns, width), bf16),
             pltpu.VMEM((rows, width), bf16),
+            pltpu.VMEM((rows, columns), f32),
+            pltpu.VMEM((BLK, BLK), f32),
             pltpu.SemaphoreType.DMA((5 + groups,)),
         ],
         compiler_params=params(60),
@@ -532,16 +533,17 @@
             pltpu.VMEM((places * BLK, columns), bf16),
             pltpu.SemaphoreType.DMA((4 + 2 * places,)),
         ],
-        compiler_params=params(60),
+        compiler_params=params(20),
         cost_estimate=cost(16 * 10**9, 32 * 10**6),
         name="query_grad",
     )(key_blocks, host_ids, host_bias, query_states, up, stats, *k_win, *v_win, q_win[4])
 
-    grad_key, grad_value = pl.pallas_call(
+    grad_key, grad_value, mark = pl.pallas_call(
         functools.partial(key_kernel, size, neigh),
-        out_shape=[jax.ShapeDtypeStruct((rows, columns), bf16)] * 2,
+        out_shape=[jax.ShapeDtypeStruct((rows, columns), bf16)] * 2
+        + [jax.ShapeDtypeStruct((8, BLK), f32)],
         in_specs=[HBM] * 5 + [ANY] * (2 * nsh - 1),
-        out_specs=[VMEM] * 2,
+        out_specs=[VMEM] * 3,
         scratch_shapes=[
             pltpu.SMEM(host_ids.shape, i32),
             pltpu.SMEM(host_bias.shape, f32),
@@ -557,12 +559,12 @@
             pltpu.VMEM((rows, columns), f32),
             pltpu.SemaphoreType.DMA((3 * nsh + 5,)),
         ],
-        compiler_params=params(60),
+        compiler_params=params(20),
         cost_estimate=cost(1000, 1000),
         name="key_grad",
     )(host_ids, host_bias, key_states, value_states, query_states, *q_win[1:], *up_win)
 
-    mixed_out = sum_after((parts[0], *arrived), grad_key)
+    mixed_out = sum_after((parts[0], *arrived), mark)
     return (mixed_out, grad_query, grad_key, grad_value)
 
 

time: 72.4 us -> 70 us (0.967)
  the two profiles are of different devices: /device:TPU:1 before, /device:TPU:19 now
where the time goes in v7:
time: 70 us; the launch traced here: 69 us
  starting transfers between devices  26.5 us (38%)
  Pallas kernels  25.9 us (37%)
  waiting for transfers between devices  10.4 us (15%)
  local copies, waits for them, and re-layouts  4.01 us (6%)
  other arithmetic  1.09 us (2%)
  between operations  1.08 us (2%)
    ppermute x17, starting transfers between devices, permute_from(): return lax.ppermute(x, 'ctx', [(source(i) % size, i) for i in range(size)])  22 us
    ppermute x17, waiting for transfers between devices, permute_from(): return lax.ppermute(x, 'ctx', [(source(i) % size, i) for i in range(size)])  10.4 us
    pallas_call x1, Pallas kernels, per_device(): pl.pallas_call(functools.partial(query_kernel, size, v_tags), out_shape=j...  6.77 us
    pallas_call x1, Pallas kernels, per_device(): pl.pallas_call(functools.partial(key_kernel, size, neigh), out_shape=[jax...  6.71 us
    pallas_call x1, Pallas kernels, per_device(): pl.pallas_call(functools.partial(attend_kernel, size, groups, v_tags), ou...  5.43 us
    ppermute x6, starting transfers between devices, flip(): return lax.ppermute(x, 'head', [(i, i ^ mask) for i in range(groups)])  4.5 us
    pallas_call x1, Pallas kernels, per_device(): pl.pallas_call(functools.partial(upstream_kernel, groups), out_shape=[jax...  4.49 us
    unnamed x66, local copies, waits for them, and re-layouts  4.01 us
  transfers between devices with their start and end apart: 23, of which 3 were waited for; matrix products, arithmetic and copies ran while one was open for 2% of the time, Pallas kernels for 36%

profile of v7, /device:TPU:19, one launch (start us, length us, event | category | flops | bytes accessed | tf_op | source)
XLA Modules:
  0.0 69.0 jit_solution(9510086090154838946)
XLA Ops:
  0.6 0.3 collective-permute-start.5
  0.9 2.2 %collective-permute-start.1 = (bf16[256,512]{1,0:T(8,128)(2,1)}, bf16[256,512]{1,0:T(8,128)(2,1)S(1)}, u32[]{:S(2)}, u32[]{:S(2)}) collective-permute-start(bf16[256,512]{1,0:T(8,128)(2,1)} %refs_6_.1), channel_id=1, source_target_pairs={{8,0},{28,4},{16,8},{4,12},{24,16},{12,20},{0,24},{20,28},{9,1},{2... | collective-permute-start | bytes 786440 | tf_op jit(solution)/shard_map/ppermute | solution.py:54
  3.1 0.3 collective-permute-start
  3.4 0.1 collective-permute-start.13
  3.5 1.3 %collective-permute-start.12 = (bf16[64,2048]{1,0:T(8,128)(2,1)}, bf16[64,2048]{1,0:T(8,128)(2,1)S(1)}, u32[]{:S(2)}, u32[]{:S(2)}) collective-permute-start(bf16[64,2048]{1,0:T(8,128)(2,1)} %refs_2_.5), channel_id=1, source_target_pairs={{0,1},{1,0},{2,3},{3,2},{4,5},{5,4},{6,7},{7,6},{8,9},{9,8},{10,11... | collective-permute-start | bytes 786440 | tf_op jit(solution)/shard_map/ppermute | solution.py:451
  4.8 3.3 %collective-permute-done.5.refs_12_.refs_13_ = bf16[256,512]{1,0:T(8,128)(2,1)S(1)} collective-permute-done((bf16[256,512]{1,0:T(8,128)(2,1)}, bf16[256,512]{1,0:T(8,128)(2,1)S(1)}, u32[]{:S(2)}, u32[]{:S(2)}) %collective-permute-start.5) | collective-permute-done | bytes 262176 | tf_op jit(solution)/shard_map/ppermute | solution.py:54
  8.1 1.2 %collective-permute-start.7 = (bf16[256,512]{1,0:T(8,128)(2,1)S(1)}, bf16[256,512]{1,0:T(8,128)(2,1)S(1)}, u32[]{:S(2)}, u32[]{:S(2)}) collective-permute-start(bf16[256,512]{1,0:T(8,128)(2,1)S(1)} %collective-permute-done.5.refs_12_.refs_13_), channel_id=1, source_target_pairs={{16,0},{20,4},{24,8},{28,12},{0,16},{4,20},{8,24},{12,28},{17,1},{... | collective-permute-start | bytes 786440 | tf_op jit(solution)/shard_map/ppermute | solution.py:54
  9.3 4.4 %collective-permute-done.1.refs_7_.refs_8_ = bf16[256,512]{1,0:T(8,128)(2,1)S(1)} collective-permute-done((bf16[256,512]{1,0:T(8,128)(2,1)}, bf16[256,512]{1,0:T(8,128)(2,1)S(1)}, u32[]{:S(2)}, u32[]{:S(2)}) %collective-permute-start.1) | collective-permute-done | bytes 262176 | tf_op jit(solution)/shard_map/ppermute | solution.py:54
  13.7 0.9 %collective-permute-start.2 = (bf16[256,512]{1,0:T(8,128)(2,1)}, bf16[256,512]{1,0:T(8,128)(2,1)S(1)}, u32[]{:S(2)}, u32[]{:S(2)}) collective-permute-start(bf16[256,512]{1,0:T(8,128)(2,1)} %refs_6_.1), channel_id=1, source_target_pairs={{24,0},{12,4},{0,8},{20,12},{8,16},{28,20},{16,24},{4,28},{25,1},{... | collective-permute-start | bytes 786440 | tf_op jit(solution)/shard_map/ppermute | solution.py:54
  14.6 2.1 %collective-permute-start.4 = (bf16[256,512]{1,0:T(8,128)(2,1)}, bf16[256,512]{1,0:T(8,128)(2,1)S(1)}, u32[]{:S(2)}, u32[]{:S(2)}) collective-permute-start(bf16[256,512]{1,0:T(8,128)(2,1)} %refs_11_.1), channel_id=1, source_target_pairs={{4,0},{0,4},{12,8},{8,12},{20,16},{16,20},{28,24},{24,28},{5,1},{1... | collective-permute-start | bytes 786440 | tf_op jit(solution)/shard_map/ppermute | solution.py:54
  16.8 0.1 collective-permute-start.6
  16.8 1.0 %collective-permute-start.3 = (bf16[256,512]{1,0:T(8,128)(2,1)S(1)}, bf16[256,512]{1,0:T(8,128)(2,1)S(1)}, u32[]{:S(2)}, u32[]{:S(2)}) collective-permute-start(bf16[256,512]{1,0:T(8,128)(2,1)S(1)} %collective-permute-done.1.refs_7_.refs_8_), channel_id=1, source_target_pairs={{4,0},{0,4},{12,8},{8,12},{20,16},{16,20},{28,24},{24,28},{5,1},{1... | collective-permute-start | bytes 786440 | tf_op jit(solution)/shard_map/ppermute | solution.py:54
  17.9 0.0 collective-permute-done.7.refs_14_.refs_15_
  17.9 4.5 %collective-permute-start.8 = (bf16[256,512]{1,0:T(8,128)(2,1)S(1)}, bf16[256,512]{1,0:T(8,128)(2,1)S(1)}, u32[]{:S(2)}, u32[]{:S(2)}) collective-permute-start(bf16[256,512]{1,0:T(8,128)(2,1)S(1)} %collective-permute-done.7.refs_14_.refs_15_), channel_id=1, source_target_pairs={{4,0},{0,4},{12,8},{8,12},{20,16},{16,20},{28,24},{24,28},{5,1},{1... | collective-permute-start | bytes 786440 | tf_op jit(solution)/shard_map/ppermute | solution.py:54
  22.4 1.7 %copies_after.1 = bf16[256,512]{1,0:T(8,128)(2,1)} custom-call(bf16[256,512]{1,0:T(8,128)(2,1)} %refs_3_.5, bf16[64,2048]{1,0:T(8,128)(2,1)} %copy-done.31, bf16[64,2048]{1,0:T(8,128)(2,1)} %copy-done.30), custom_call_target="tpu_custom_call" | custom-call | flops 1000 | bytes 1000 | tf_op jit(solution)/shard_map/copies_after/pallas_call | solution.py:411
  24.1 0.0 copy-start.15
  24.1 0.2 collective-permute-start.14
  24.3 0.1 collective-permute-start.15
  24.5 1.6 %collective-permute-start.18 = (bf16[64,2048]{1,0:T(8,128)(2,1)}, bf16[64,2048]{1,0:T(8,128)(2,1)S(1)}, u32[]{:S(2)}, u32[]{:S(2)}) collective-permute-start(bf16[64,2048]{1,0:T(8,128)(2,1)} %copy-done.30), channel_id=1, source_target_pairs={{0,1},{1,0},{2,3},{3,2},{4,5},{5,4},{6,7},{7,6},{8,9},{9,8},{10,11... | collective-permute-start | bytes 786440 | tf_op jit(solution)/shard_map/ppermute | solution.py:451
  26.1 0.6 copy-done.21
  26.8 0.7 %copy-done.23 = bf16[256,512]{1,0:T(8,128)(2,1)} copy-done((bf16[256,512]{1,0:T(8,128)(2,1)}, bf16[256,512]{1,0:T(8,128)(2,1)S(1)}, u32[]{:S(2)}) %copy-start.23) | copy-done | bytes 262168
  27.5 5.4 %attend.1 = (bf16[64,2048]{1,0:T(8,128)(2,1)}, bf16[64,2048]{1,0:T(8,128)(2,1)}, bf16[64,2048]{1,0:T(8,128)(2,1)}, bf16[64,2048]{1,0:T(8,128)(2,1)}, f32[256,512]{1,0:T(8,128)}, /*index=5*/f32[128,128]{1,0:T(8,128)}) custom-call(s32[2,4]{1,0:T(2,128)} %refs_0_.9, s32[16]{0:T(128)} %refs_1_.7, f32[4]{0:T(128)} %refs_2_.7, bf16[256,512]{1,0:T(8,128)(2,1)} %refs_3_.5, ...), custom_call_target="tpu_custom_call" | custom-call | flops 1000000000 | bytes 1000000 | tf_op jit(solution)/shard_map/attend/pallas_call | solution.py:470
  32.9 0.1 collective-permute-start.10
  33.0 1.1 %collective-permute-start.16 = (bf16[256,512]{1,0:T(8,128)(2,1)}, bf16[256,512]{1,0:T(8,128)(2,1)S(1)}, u32[]{:S(2)}, u32[]{:S(2)}) collective-permute-start(bf16[256,512]{1,0:T(8,128)(2,1)} %copies_after.1), channel_id=1, source_target_pairs={{24,0},{12,4},{0,8},{20,12},{8,16},{28,20},{16,24},{4,28},{25,1},{... | collective-permute-start | bytes 786440 | tf_op jit(solution)/shard_map/ppermute | solution.py:54
  34.2 2.4 %collective-permute-start.17 = (bf16[256,512]{1,0:T(8,128)(2,1)S(1)}, bf16[256,512]{1,0:T(8,128)(2,1)}, u32[]{:S(2)}, u32[]{:S(2)}) collective-permute-start(bf16[256,512]{1,0:T(8,128)(2,1)S(1)} %collective-permute-done.15.refs_6_), channel_id=1, source_target_pairs={{4,0},{0,4},{12,8},{8,12},{20,16},{16,20},{28,24},{24,28},{5,1},{1... | collective-permute-start | bytes 786440 | tf_op jit(solution)/shard_map/ppermute | solution.py:54
  36.6 0.7 %copy-done.32 = bf16[64,2048]{1,0:T(8,128)(2,1)} copy-done((bf16[64,2048]{1,0:T(8,128)(2,1)}, bf16[64,2048]{1,0:T(8,128)(2,1)S(1)}, u32[]{:S(2)}) %copy-start.32) | copy-done | bytes 262168
  37.3 0.0 copy-done.3
  37.4 0.0 copy-start.10
  37.4 0.0 copy-start.12
  37.4 0.0 copy-start.16
  37.5 0.0 copy-start.22
  37.5 0.0 copy-start.26
  37.5 0.0 copy-start.27
  37.5 0.0 copy-start.28
  37.5 4.5 %upstream.1 = (bf16[272,512]{1,0:T(8,128)(2,1)}, f32[128,128]{1,0:T(8,128)}) custom-call(s32[2,4]{1,0:T(2,128)} %refs_0_.9, bf16[512,2048]{1,0:T(8,128)(2,1)} %refs_1_.5, bf16[64,2048]{1,0:T(8,128)(2,1)} %refs_2_.5, f32[256,512]{1,0:T(8,128)} %get-tuple-element.19.refs_3_, f32[128,128]{1,0:T(8,128)} %get-tuple-element.20.refs_4_, ...), custom_call_target="tpu_custom_call" | custom-call | flops 1000 | bytes 1000 | tf_op jit(solution)/shard_map/upstream/pallas_call | solution.py:502
  42.0 0.1 collective-permute-start.20
  42.1 0.1 collective-permute-start.19
  42.2 2.4 %collective-permute-start.21 = (bf16[272,512]{1,0:T(8,128)(2,1)}, bf16[272,512]{1,0:T(8,128)(2,1)S(1)}, u32[]{:S(2)}, u32[]{:S(2)}) collective-permute-start(bf16[272,512]{1,0:T(8,128)(2,1)} %get-tuple-element.21.refs_9_.refs_4_), channel_id=1, source_target_pairs={{24,0},{12,4},{0,8},{20,12},{8,16},{28,20},{16,24},{4,28},{25,1},{... | collective-permute-start | bytes 835592 | tf_op jit(solution)/shard_map/ppermute | solution.py:54
  44.5 1.1 %add_convert_fusion = bf16[64,2048]{1,0:T(8,128)(2,1)S(1)} fusion(bf16[64,2048]{1,0:T(8,128)(2,1)} %collective-permute-done.10, bf16[64,2048]{1,0:T(8,128)(2,1)} %get-tuple-element.17), kind=kLoop, calls=%fused_computation | loop fusion | flops 524288 | bytes 786432 | tf_op jit(solution)/shard_map/convert_element_type | solution.py:497
  45.6 1.4 %collective-permute-start.9 = (bf16[64,2048]{1,0:T(8,128)(2,1)}, bf16[64,2048]{1,0:T(8,128)(2,1)S(1)}, u32[]{:S(2)}, u32[]{:S(2)}) collective-permute-start(bf16[64,2048]{1,0:T(8,128)(2,1)} %get-tuple-element.16), channel_id=1, source_target_pairs={{0,1},{1,0},{2,3},{3,2},{4,5},{5,4},{6,7},{7,6},{8,9},{9,8},{10,11... | collective-permute-start | bytes 786440 | tf_op jit(solution)/shard_map/ppermute | solution.py:451
  47.0 0.1 collective-permute-start.11
  47.1 2.7 %collective-permute-done.20.refs_11_ = bf16[272,512]{1,0:T(8,128)(2,1)S(1)} collective-permute-done((bf16[272,512]{1,0:T(8,128)(2,1)}, bf16[272,512]{1,0:T(8,128)(2,1)S(1)}, u32[]{:S(2)}, u32[]{:S(2)}) %collective-permute-start.20) | collective-permute-done | bytes 278560 | tf_op jit(solution)/shard_map/ppermute | solution.py:54
  49.7 2.9 %collective-permute-start.22 = (bf16[272,512]{1,0:T(8,128)(2,1)S(1)}, bf16[272,512]{1,0:T(8,128)(2,1)S(1)}, u32[]{:S(2)}, u32[]{:S(2)}) collective-permute-start(bf16[272,512]{1,0:T(8,128)(2,1)S(1)} %collective-permute-done.20.refs_11_), channel_id=1, source_target_pairs={{4,0},{0,4},{12,8},{8,12},{20,16},{16,20},{28,24},{24,28},{5,1},{1... | collective-permute-start | bytes 835592 | tf_op jit(solution)/shard_map/ppermute | solution.py:54
  52.8 0.9 %copy-done.5 = bf16[272,512]{1,0:T(8,128)(2,1)S(1)} copy-done((bf16[272,512]{1,0:T(8,128)(2,1)S(1)}, bf16[272,512]{1,0:T(8,128)(2,1)}, u32[]{:S(2)}) %copy-start.5) | copy-done | bytes 278552
  53.7 0.8 %copy-done.29 = f32[128,128]{1,0:T(8,128)S(1)} copy-done((f32[128,128]{1,0:T(8,128)S(1)}, f32[128,128]{1,0:T(8,128)}, u32[]{:S(2)}) %copy-start.29) | copy-done | bytes 65560
  54.6 6.8 %query_grad.1 = bf16[256,512]{1,0:T(8,128)(2,1)} custom-call(s32[2,4]{1,0:T(2,128)S(1)} %copy-done.26, s32[16]{0:T(128)S(1)} %copy-done.27, f32[4]{0:T(128)S(1)} %copy-done.28, bf16[256,512]{1,0:T(8,128)(2,1)S(1)} %copy-done, bf16[272,512]{1,0:T(8,128)(2,1)S(1)} %copy-done.5, f32[128,128]{1,0:T(8,128)S(1)} %copy-done.29, bf16[256,512]{1,0:T(8,128)(2,1)S(1)} %copy-done.1, ...), custom_call_target="tpu_custom_call" | custom-call | flops 16000000000 | bytes 32000000 | tf_op jit(solution)/shard_map/query_grad/pallas_call | solution.py:524
  61.4 6.7 %key_grad.1 = (bf16[256,512]{1,0:T(8,128)(2,1)}, bf16[256,512]{1,0:T(8,128)(2,1)}, f32[8,128]{1,0:T(8,128)S(1)}) custom-call(s32[16]{0:T(128)S(1)} %copy-done.27, f32[4]{0:T(128)S(1)} %copy-done.28, bf16[256,512]{1,0:T(8,128)(2,1)S(1)} %copy-done.1, bf16[256,512]{1,0:T(8,128)(2,1)S(1)} %copy-done.2, bf16[256,512]{1,0:T(8,128)(2,1)S(1)} %copy-done, ...), custom_call_target="tpu_custom_call" | custom-call | flops 1000 | bytes 1000 | tf_op jit(solution)/shard_map/key_grad/pallas_call | solution.py:541
  68.2 0.8 %sum_after.1 = bf16[64,2048]{1,0:T(8,128)(2,1)} custom-call(bf16[64,2048]{1,0:T(8,128)(2,1)S(1)} %copy-done.25, bf16[64,2048]{1,0:T(8,128)(2,1)S(1)} %collective-permute-done.9.refs_1_, bf16[64,2048]{1,0:T(8,128)(2,1)S(1)} %collective-permute-done.11.refs_2_, f32[8,128]{1,0:T(8,128)S(1)} %get-tuple-element.22.refs_3_), custom_call_target="tpu_custom_call" | custom-call | flops 1000 | bytes 1000 | tf_op jit(solution)/shard_map/sum_after/pallas_call | solution.py:392
  (71 shorter events, 0.1 us)
Async XLA Ops:
  0.6 7.5 %collective-permute-start.5 = (bf16[256,512]{1,0:T(8,128)(2,1)}, bf16[256,512]{1,0:T(8,128)(2,1)S(1)}, u32[]{:S(2)}, u32[]{:S(2)}) collective-permute-start(bf16[256,512]{1,0:T(8,128)(2,1)} %refs_11_.1), channel_id=1, source_target_pairs={{8,0},{12,4},{0,8},{4,12},{24,16},{28,20},{16,24},{20,28},{9,1},{1... | collective-permute-start | bytes 786440 | tf_op jit(solution)/shard_map/ppermute | solution.py:54
  0.9 12.7 %collective-permute-start.1 = (bf16[256,512]{1,0:T(8,128)(2,1)}, bf16[256,512]{1,0:T(8,128)(2,1)S(1)}, u32[]{:S(2)}, u32[]{:S(2)}) collective-permute-start(bf16[256,512]{1,0:T(8,128)(2,1)} %refs_6_.1), channel_id=1, source_target_pairs={{8,0},{28,4},{16,8},{4,12},{24,16},{12,20},{0,24},{20,28},{9,1},{2... | collective-permute-start | bytes 786440 | tf_op jit(solution)/shard_map/ppermute | solution.py:54
  3.1 11.5 %collective-permute-start = (bf16[256,512]{1,0:T(8,128)(2,1)}, bf16[256,512]{1,0:T(8,128)(2,1)S(1)}, u32[]{:S(2)}, u32[]{:S(2)}) collective-permute-start(bf16[256,512]{1,0:T(8,128)(2,1)} %refs_6_.1), channel_id=1, source_target_pairs={{4,0},{0,4},{12,8},{8,12},{20,16},{16,20},{28,24},{24,28},{5,1},{1... | collective-permute-start | bytes 786440 | tf_op jit(solution)/shard_map/ppermute | solution.py:54
  3.4 13.3 %collective-permute-start.13 = (bf16[64,2048]{1,0:T(8,128)(2,1)}, bf16[64,2048]{1,0:T(8,128)(2,1)S(1)}, u32[]{:S(2)}, u32[]{:S(2)}) collective-permute-start(bf16[64,2048]{1,0:T(8,128)(2,1)} %refs_2_.5), channel_id=1, source_target_pairs={{0,2},{1,3},{2,0},{3,1},{4,6},{5,7},{6,4},{7,5},{8,10},{9,11},{10,... | collective-permute-start | bytes 786440 | tf_op jit(solution)/shard_map/ppermute | solution.py:451
  3.5 13.4 %collective-permute-start.12 = (bf16[64,2048]{1,0:T(8,128)(2,1)}, bf16[64,2048]{1,0:T(8,128)(2,1)S(1)}, u32[]{:S(2)}, u32[]{:S(2)}) collective-permute-start(bf16[64,2048]{1,0:T(8,128)(2,1)} %refs_2_.5), channel_id=1, source_target_pairs={{0,1},{1,0},{2,3},{3,2},{4,5},{5,4},{6,7},{7,6},{8,9},{9,8},{10,11... | collective-permute-start | bytes 786440 | tf_op jit(solution)/shard_map/ppermute | solution.py:451
  8.1 18.0 %copy-start.7 = (bf16[256,512]{1,0:T(8,128)(2,1)}, bf16[256,512]{1,0:T(8,128)(2,1)S(1)}, u32[]{:S(2)}) copy-start(bf16[256,512]{1,0:T(8,128)(2,1)S(1)} %collective-permute-done.5.refs_12_.refs_13_) | copy-start | bytes 786436
  8.1 9.8 %collective-permute-start.7 = (bf16[256,512]{1,0:T(8,128)(2,1)S(1)}, bf16[256,512]{1,0:T(8,128)(2,1)S(1)}, u32[]{:S(2)}, u32[]{:S(2)}) collective-permute-start(bf16[256,512]{1,0:T(8,128)(2,1)S(1)} %collective-permute-done.5.refs_12_.refs_13_), channel_id=1, source_target_pairs={{16,0},{20,4},{24,8},{28,12},{0,16},{4,20},{8,24},{12,28},{17,1},{... | collective-permute-start | bytes 786440 | tf_op jit(solution)/shard_map/ppermute | solution.py:54
  13.7 12.4 %copy-start.9 = (bf16[256,512]{1,0:T(8,128)(2,1)}, bf16[256,512]{1,0:T(8,128)(2,1)S(1)}, u32[]{:S(2)}) copy-start(bf16[256,512]{1,0:T(8,128)(2,1)S(1)} %collective-permute-done.1.refs_7_.refs_8_) | copy-start | bytes 786436
  13.7 10.4 %collective-permute-start.2 = (bf16[256,512]{1,0:T(8,128)(2,1)}, bf16[256,512]{1,0:T(8,128)(2,1)S(1)}, u32[]{:S(2)}, u32[]{:S(2)}) collective-permute-start(bf16[256,512]{1,0:T(8,128)(2,1)} %refs_6_.1), channel_id=1, source_target_pairs={{24,0},{12,4},{0,8},{20,12},{8,16},{28,20},{16,24},{4,28},{25,1},{... | collective-permute-start | bytes 786440 | tf_op jit(solution)/shard_map/ppermute | solution.py:54
  14.6 11.5 %copy-start.11 = (bf16[256,512]{1,0:T(8,128)(2,1)}, bf16[256,512]{1,0:T(8,128)(2,1)S(1)}, u32[]{:S(2)}) copy-start(bf16[256,512]{1,0:T(8,128)(2,1)S(1)} %collective-permute-done.refs_6_.refs_7_) | copy-start | bytes 786436
  14.6 9.7 %collective-permute-start.4 = (bf16[256,512]{1,0:T(8,128)(2,1)}, bf16[256,512]{1,0:T(8,128)(2,1)S(1)}, u32[]{:S(2)}, u32[]{:S(2)}) collective-permute-start(bf16[256,512]{1,0:T(8,128)(2,1)} %refs_11_.1), channel_id=1, source_target_pairs={{4,0},{0,4},{12,8},{8,12},{20,16},{16,20},{28,24},{24,28},{5,1},{1... | collective-permute-start | bytes 786440 | tf_op jit(solution)/shard_map/ppermute | solution.py:54
  16.7 5.7 %copy-start.30 = (bf16[64,2048]{1,0:T(8,128)(2,1)}, bf16[64,2048]{1,0:T(8,128)(2,1)S(1)}, u32[]{:S(2)}) copy-start(bf16[64,2048]{1,0:T(8,128)(2,1)S(1)} %collective-permute-done.13.refs_2_.refs_6_) | copy-start | bytes 786436
  16.8 7.7 %collective-permute-start.6 = (bf16[256,512]{1,0:T(8,128)(2,1)S(1)}, bf16[256,512]{1,0:T(8,128)(2,1)S(1)}, u32[]{:S(2)}, u32[]{:S(2)}) collective-permute-start(bf16[256,512]{1,0:T(8,128)(2,1)S(1)} %collective-permute-done.5.refs_12_.refs_13_), channel_id=1, source_target_pairs={{4,0},{0,4},{12,8},{8,12},{20,16},{16,20},{28,24},{24,28},{5,1},{1... | collective-permute-start | bytes 786440 | tf_op jit(solution)/shard_map/ppermute | solution.py:54
  16.8 5.6 %copy-start.31 = (bf16[64,2048]{1,0:T(8,128)(2,1)}, bf16[64,2048]{1,0:T(8,128)(2,1)S(1)}, u32[]{:S(2)}) copy-start(bf16[64,2048]{1,0:T(8,128)(2,1)S(1)} %collective-permute-done.12.refs_1_.refs_5_) | copy-start | bytes 786436
  16.8 9.2 %collective-permute-start.3 = (bf16[256,512]{1,0:T(8,128)(2,1)S(1)}, bf16[256,512]{1,0:T(8,128)(2,1)S(1)}, u32[]{:S(2)}, u32[]{:S(2)}) collective-permute-start(bf16[256,512]{1,0:T(8,128)(2,1)S(1)} %collective-permute-done.1.refs_7_.refs_8_), channel_id=1, source_target_pairs={{4,0},{0,4},{12,8},{8,12},{20,16},{16,20},{28,24},{24,28},{5,1},{1... | collective-permute-start | bytes 786440 | tf_op jit(solution)/shard_map/ppermute | solution.py:54
  17.9 8.2 %copy-start.13 = (bf16[256,512]{1,0:T(8,128)(2,1)}, bf16[256,512]{1,0:T(8,128)(2,1)S(1)}, u32[]{:S(2)}) copy-start(bf16[256,512]{1,0:T(8,128)(2,1)S(1)} %collective-permute-done.7.refs_14_.refs_15_) | copy-start | bytes 786436
  17.9 8.2 %collective-permute-start.8 = (bf16[256,512]{1,0:T(8,128)(2,1)S(1)}, bf16[256,512]{1,0:T(8,128)(2,1)S(1)}, u32[]{:S(2)}, u32[]{:S(2)}) collective-permute-start(bf16[256,512]{1,0:T(8,128)(2,1)S(1)} %collective-permute-done.7.refs_14_.refs_15_), channel_id=1, source_target_pairs={{4,0},{0,4},{12,8},{8,12},{20,16},{16,20},{28,24},{24,28},{5,1},{1... | collective-permute-start | bytes 786440 | tf_op jit(solution)/shard_map/ppermute | solution.py:54
  24.1 2.0 %copy-start.15 = (bf16[256,512]{1,0:T(8,128)(2,1)}, bf16[256,512]{1,0:T(8,128)(2,1)S(1)}, u32[]{:S(2)}) copy-start(bf16[256,512]{1,0:T(8,128)(2,1)S(1)} %collective-permute-done.2.refs_8_.refs_9_) | copy-start | bytes 786436
  24.1 12.5 %collective-permute-start.14 = (bf16[256,512]{1,0:T(8,128)(2,1)}, bf16[256,512]{1,0:T(8,128)(2,1)S(1)}, u32[]{:S(2)}, u32[]{:S(2)}) collective-permute-start(bf16[256,512]{1,0:T(8,128)(2,1)} %copies_after.1), channel_id=1, source_target_pairs={{4,0},{0,4},{12,8},{8,12},{20,16},{16,20},{28,24},{24,28},{5,1},{1... | collective-permute-start | bytes 786440 | tf_op jit(solution)/shard_map/ppermute | solution.py:54
  24.3 9.9 %collective-permute-start.15 = (bf16[256,512]{1,0:T(8,128)(2,1)}, bf16[256,512]{1,0:T(8,128)(2,1)S(1)}, u32[]{:S(2)}, u32[]{:S(2)}) collective-permute-start(bf16[256,512]{1,0:T(8,128)(2,1)} %copies_after.1), channel_id=1, source_target_pairs={{8,0},{28,4},{16,8},{4,12},{24,16},{12,20},{0,24},{20,28},{9,1},{2... | collective-permute-start | bytes 786440 | tf_op jit(solution)/shard_map/ppermute | solution.py:54
  24.5 12.1 %collective-permute-start.18 = (bf16[64,2048]{1,0:T(8,128)(2,1)}, bf16[64,2048]{1,0:T(8,128)(2,1)S(1)}, u32[]{:S(2)}, u32[]{:S(2)}) collective-permute-start(bf16[64,2048]{1,0:T(8,128)(2,1)} %copy-done.30), channel_id=1, source_target_pairs={{0,1},{1,0},{2,3},{3,2},{4,5},{5,4},{6,7},{7,6},{8,9},{9,8},{10,11... | collective-permute-start | bytes 786440 | tf_op jit(solution)/shard_map/ppermute | solution.py:451
  32.9 9.3 %collective-permute-start.10 = (bf16[64,2048]{1,0:T(8,128)(2,1)}, bf16[64,2048]{1,0:T(8,128)(2,1)}, u32[]{:S(2)}, u32[]{:S(2)}) collective-permute-start(bf16[64,2048]{1,0:T(8,128)(2,1)} %get-tuple-element.18), channel_id=1, source_target_pairs={{0,1},{1,0},{2,3},{3,2},{4,5},{5,4},{6,7},{7,6},{8,9},{9,8},{10,11... | collective-permute-start | bytes 786440 | tf_op jit(solution)/shard_map/ppermute | solution.py:451
  33.0 12.6 %collective-permute-start.16 = (bf16[256,512]{1,0:T(8,128)(2,1)}, bf16[256,512]{1,0:T(8,128)(2,1)S(1)}, u32[]{:S(2)}, u32[]{:S(2)}) collective-permute-start(bf16[256,512]{1,0:T(8,128)(2,1)} %copies_after.1), channel_id=1, source_target_pairs={{24,0},{12,4},{0,8},{20,12},{8,16},{28,20},{16,24},{4,28},{25,1},{... | collective-permute-start | bytes 786440 | tf_op jit(solution)/shard_map/ppermute | solution.py:54
  34.2 12.8 %collective-permute-start.17 = (bf16[256,512]{1,0:T(8,128)(2,1)S(1)}, bf16[256,512]{1,0:T(8,128)(2,1)}, u32[]{:S(2)}, u32[]{:S(2)}) collective-permute-start(bf16[256,512]{1,0:T(8,128)(2,1)S(1)} %collective-permute-done.15.refs_6_), channel_id=1, source_target_pairs={{4,0},{0,4},{12,8},{8,12},{20,16},{16,20},{28,24},{24,28},{5,1},{1... | collective-permute-start | bytes 786440 | tf_op jit(solution)/shard_map/ppermute | solution.py:54
  37.4 15.3 %copy-start = (bf16[256,512]{1,0:T(8,128)(2,1)S(1)}, bf16[256,512]{1,0:T(8,128)(2,1)}, u32[]{:S(2)}) copy-start(bf16[256,512]{1,0:T(8,128)(2,1)} %refs_3_.5) | copy-start | bytes 786436
  37.4 15.3 %copy-start.1 = (bf16[256,512]{1,0:T(8,128)(2,1)S(1)}, bf16[256,512]{1,0:T(8,128)(2,1)}, u32[]{:S(2)}) copy-start(bf16[256,512]{1,0:T(8,128)(2,1)} %refs_6_.1) | copy-start | bytes 786436
  37.4 15.3 %copy-start.2 = (bf16[256,512]{1,0:T(8,128)(2,1)S(1)}, bf16[256,512]{1,0:T(8,128)(2,1)}, u32[]{:S(2)}) copy-start(bf16[256,512]{1,0:T(8,128)(2,1)} %refs_11_.1) | copy-start | bytes 786436
  37.4 15.3 %copy-start.8 = (bf16[256,512]{1,0:T(8,128)(2,1)S(1)}, bf16[256,512]{1,0:T(8,128)(2,1)}, u32[]{:S(2)}) copy-start(bf16[256,512]{1,0:T(8,128)(2,1)} %copy-done.7) | copy-start | bytes 786436
  37.4 15.3 %copy-start.10 = (bf16[256,512]{1,0:T(8,128)(2,1)S(1)}, bf16[256,512]{1,0:T(8,128)(2,1)}, u32[]{:S(2)}) copy-start(bf16[256,512]{1,0:T(8,128)(2,1)} %copy-done.9) | copy-start | bytes 786436
  37.4 15.3 %copy-start.12 = (bf16[256,512]{1,0:T(8,128)(2,1)S(1)}, bf16[256,512]{1,0:T(8,128)(2,1)}, u32[]{:S(2)}) copy-start(bf16[256,512]{1,0:T(8,128)(2,1)} %copy-done.11) | copy-start | bytes 786436
  37.4 15.3 %copy-start.14 = (bf16[256,512]{1,0:T(8,128)(2,1)S(1)}, bf16[256,512]{1,0:T(8,128)(2,1)}, u32[]{:S(2)}) copy-start(bf16[256,512]{1,0:T(8,128)(2,1)} %copy-done.13) | copy-start | bytes 786436
  37.4 15.3 %copy-start.16 = (bf16[256,512]{1,0:T(8,128)(2,1)S(1)}, bf16[256,512]{1,0:T(8,128)(2,1)}, u32[]{:S(2)}) copy-start(bf16[256,512]{1,0:T(8,128)(2,1)} %copy-done.15) | copy-start | bytes 786436
  37.4 15.3 %copy-start.18 = (bf16[256,512]{1,0:T(8,128)(2,1)S(1)}, bf16[256,512]{1,0:T(8,128)(2,1)}, u32[]{:S(2)}) copy-start(bf16[256,512]{1,0:T(8,128)(2,1)} %copy-done.17) | copy-start | bytes 786436
  37.4 15.3 %copy-start.20 = (bf16[256,512]{1,0:T(8,128)(2,1)S(1)}, bf16[256,512]{1,0:T(8,128)(2,1)}, u32[]{:S(2)}) copy-start(bf16[256,512]{1,0:T(8,128)(2,1)} %copy-done.19) | copy-start | bytes 786436
  37.5 15.3 %copy-start.22 = (bf16[256,512]{1,0:T(8,128)(2,1)S(1)}, bf16[256,512]{1,0:T(8,128)(2,1)}, u32[]{:S(2)}) copy-start(bf16[256,512]{1,0:T(8,128)(2,1)} %copy-done.21) | copy-start | bytes 786436
  37.5 15.3 %copy-start.24 = (bf16[256,512]{1,0:T(8,128)(2,1)S(1)}, bf16[256,512]{1,0:T(8,128)(2,1)}, u32[]{:S(2)}) copy-start(bf16[256,512]{1,0:T(8,128)(2,1)} %copy-done.23) | copy-start | bytes 786436
  37.5 15.3 %copy-start.26 = (s32[2,4]{1,0:T(2,128)S(1)}, s32[2,4]{1,0:T(2,128)}, u32[]{:S(2)}) copy-start(s32[2,4]{1,0:T(2,128)} %refs_0_.9) | copy-start | bytes 100
  37.5 15.3 %copy-start.27 = (s32[16]{0:T(128)S(1)}, s32[16]{0:T(128)}, u32[]{:S(2)}) copy-start(s32[16]{0:T(128)} %refs_1_.7) | copy-start | bytes 196
  37.5 15.3 %copy-start.28 = (f32[4]{0:T(128)S(1)}, f32[4]{0:T(128)}, u32[]{:S(2)}) copy-start(f32[4]{0:T(128)} %refs_2_.7) | copy-start | bytes 52
  42.0 7.7 %collective-permute-start.20 = (bf16[272,512]{1,0:T(8,128)(2,1)}, bf16[272,512]{1,0:T(8,128)(2,1)S(1)}, u32[]{:S(2)}, u32[]{:S(2)}) collective-permute-start(bf16[272,512]{1,0:T(8,128)(2,1)} %get-tuple-element.21.refs_9_.refs_4_), channel_id=1, source_target_pairs={{8,0},{28,4},{16,8},{4,12},{24,16},{12,20},{0,24},{20,28},{9,1},{2... | collective-permute-start | bytes 835592 | tf_op jit(solution)/shard_map/ppermute | solution.py:54
  42.1 19.3 %collective-permute-start.19 = (bf16[272,512]{1,0:T(8,128)(2,1)}, bf16[272,512]{1,0:T(8,128)(2,1)S(1)}, u32[]{:S(2)}, u32[]{:S(2)}) collective-permute-start(bf16[272,512]{1,0:T(8,128)(2,1)} %get-tuple-element.21.refs_9_.refs_4_), channel_id=1, source_target_pairs={{4,0},{0,4},{12,8},{8,12},{20,16},{16,20},{28,24},{24,28},{5,1},{1... | collective-permute-start | bytes 835592 | tf_op jit(solution)/shard_map/ppermute | solution.py:54
  42.2 19.2 %collective-permute-start.21 = (bf16[272,512]{1,0:T(8,128)(2,1)}, bf16[272,512]{1,0:T(8,128)(2,1)S(1)}, u32[]{:S(2)}, u32[]{:S(2)}) collective-permute-start(bf16[272,512]{1,0:T(8,128)(2,1)} %get-tuple-element.21.refs_9_.refs_4_), channel_id=1, source_target_pairs={{24,0},{12,4},{0,8},{20,12},{8,16},{28,20},{16,24},{4,28},{25,1},{... | collective-permute-start | bytes 835592 | tf_op jit(solution)/shard_map/ppermute | solution.py:54
  45.6 22.5 %collective-permute-start.9 = (bf16[64,2048]{1,0:T(8,128)(2,1)}, bf16[64,2048]{1,0:T(8,128)(2,1)S(1)}, u32[]{:S(2)}, u32[]{:S(2)}) collective-permute-start(bf16[64,2048]{1,0:T(8,128)(2,1)} %get-tuple-element.16), channel_id=1, source_target_pairs={{0,1},{1,0},{2,3},{3,2},{4,5},{5,4},{6,7},{7,6},{8,9},{9,8},{10,11... | collective-permute-start | bytes 786440 | tf_op jit(solution)/shard_map/ppermute | solution.py:451
  47.0 21.1 %collective-permute-start.11 = (bf16[64,2048]{1,0:T(8,128)(2,1)S(1)}, bf16[64,2048]{1,0:T(8,128)(2,1)S(1)}, u32[]{:S(2)}, u32[]{:S(2)}) collective-permute-start(bf16[64,2048]{1,0:T(8,128)(2,1)S(1)} %add_convert_fusion), channel_id=1, source_target_pairs={{0,2},{1,3},{2,0},{3,1},{4,6},{5,7},{6,4},{7,5},{8,10},{9,11},{10,... | collective-permute-start | bytes 786440 | tf_op jit(solution)/shard_map/ppermute | solution.py:451
  49.7 11.6 %collective-permute-start.22 = (bf16[272,512]{1,0:T(8,128)(2,1)S(1)}, bf16[272,512]{1,0:T(8,128)(2,1)S(1)}, u32[]{:S(2)}, u32[]{:S(2)}) collective-permute-start(bf16[272,512]{1,0:T(8,128)(2,1)S(1)} %collective-permute-done.20.refs_11_), channel_id=1, source_target_pairs={{4,0},{0,4},{12,8},{8,12},{20,16},{16,20},{28,24},{24,28},{5,1},{1... | collective-permute-start | bytes 835592 | tf_op jit(solution)/shard_map/ppermute | solution.py:54
  54.6 6.8 %copy-start.4 = (bf16[256,512]{1,0:T(8,128)(2,1)S(1)}, bf16[256,512]{1,0:T(8,128)(2,1)}, u32[]{:S(2)}) copy-start(bf16[256,512]{1,0:T(8,128)(2,1)} %copy-done.3) | copy-start | bytes 786436
  54.6 6.8 %copy-start.6 = (bf16[272,512]{1,0:T(8,128)(2,1)S(1)}, bf16[272,512]{1,0:T(8,128)(2,1)}, u32[]{:S(2)}) copy-start(bf16[272,512]{1,0:T(8,128)(2,1)} %get-tuple-element.21.refs_9_.refs_4_) | copy-start | bytes 835588
  61.4 6.8 %copy-start.25 = (bf16[64,2048]{1,0:T(8,128)(2,1)S(1)}, bf16[64,2048]{1,0:T(8,128)(2,1)}, u32[]{:S(2)}) copy-start(bf16[64,2048]{1,0:T(8,128)(2,1)} %get-tuple-element.15.refs_0_) | copy-start | bytes 786436
  (8 other events, 8.2 us)

commit v8 on v7

--- a/solution.py
+++ b/solution.py
@@ -244,7 +244,7 @@
     keys_hbm, hosts_hbm, bias_hbm, q_hbm, up_ref, stats_ref = refs[:6]
     k_refs = refs[6:6 + len(PAIR)]
     v_refs = refs[6 + len(PAIR):6 + len(PAIR) + len(v_tags)]
-    dq_ref, keys, hosts, bias, q_ref, kcat, vcat, sem = refs[6 + len(PAIR) + len(v_tags) + 1:]
+    dq_ref, keys, hosts, bias, q_ref, kcat, vcat, sem = refs[6 + len(PAIR) + len(v_tags):]
     rows, columns = q_ref.shape
     blocks_dev, neigh = keys.shape
     heads_dev = columns // HDIM
@@ -524,7 +524,7 @@
     grad_query = pl.pallas_call(
         functools.partial(query_kernel, size, v_tags),
         out_shape=jax.ShapeDtypeStruct((rows, columns), bf16),
-        in_specs=[HBM] * 4 + [VMEM] * 2 + [ANY] * (len(PAIR) + len(v_tags) + 1),
+        in_specs=[HBM] * 4 + [VMEM] * 2 + [ANY] * (len(PAIR) + len(v_tags)),
         out_specs=VMEM,
         scratch_shapes=scalars
         + [
@@ -533,10 +533,10 @@
             pltpu.VMEM((places * BLK, columns), bf16),
             pltpu.SemaphoreType.DMA((4 + 2 * places,)),
         ],
-        compiler_params=params(20),
+        compiler_params=params(60),
         cost_estimate=cost(16 * 10**9, 32 * 10**6),
         name="query_grad",
-    )(key_blocks, host_ids, host_bias, query_states, up, stats, *k_win, *v_win, q_win[4])
+    )(key_blocks, host_ids, host_bias, query_states, up, stats, *k_win, *v_win)
 
     grad_key, grad_value, mark = pl.pallas_call(
         functools.partial(key_kernel, size, neigh),

time: 70 us -> 67.1 us (0.959)
  the two profiles are of different devices: /device:TPU:19 before, /device:TPU:0 now
where the time goes in v8:
time: 67.1 us; the launch traced here: 66.2 us
  starting transfers between devices  26.7 us (40%)
  Pallas kernels  25.1 us (37%)
  waiting for transfers between devices  10.9 us (16%)
  local copies, waits for them, and re-layouts  2.39 us (4%)
  between operations  0.99 us (1%)
    ppermute x17, starting transfers between devices, permute_from(): return lax.ppermute(x, 'ctx', [(source(i) % size, i) for i in range(size)])  16.2 us
    ppermute x6, starting transfers between devices, flip(): return lax.ppermute(x, 'head', [(i, i ^ mask) for i in range(groups)])  10.5 us
    ppermute x17, waiting for transfers between devices, permute_from(): return lax.ppermute(x, 'ctx', [(source(i) % size, i) for i in range(size)])  8.6 us
    pallas_call x1, Pallas kernels, per_device(): pl.pallas_call(functools.partial(key_kernel, size, neigh), out_shape=[jax...  6.6 us
    pallas_call x1, Pallas kernels, per_device(): pl.pallas_call(functools.partial(query_kernel, size, v_tags), out_shape=j...  6.23 us
    pallas_call x1, Pallas kernels, per_device(): pl.pallas_call(functools.partial(attend_kernel, size, groups, v_tags), ou...  5.45 us
    pallas_call x1, Pallas kernels, per_device(): pl.pallas_call(functools.partial(upstream_kernel, groups), out_shape=[jax...  4.35 us
    unnamed x46, local copies, waits for them, and re-layouts  2.39 us
  transfers between devices with their start and end apart: 23, of which 6 were waited for; matrix products, arithmetic and copies ran while one was open for 0% of the time, Pallas kernels for 37%

profile of v8, /device:TPU:0, one launch (start us, length us, event | category | flops | bytes accessed | tf_op | source)
XLA Modules:
  0.0 66.2 jit_solution(6721973194262698490)
XLA Ops:
  0.6 3.0 %collective-permute-start.5 = (bf16[256,512]{1,0:T(8,128)(2,1)}, bf16[256,512]{1,0:T(8,128)(2,1)S(1)}, u32[]{:S(2)}, u32[]{:S(2)}) collective-permute-start(bf16[256,512]{1,0:T(8,128)(2,1)} %refs_11_.1), channel_id=1, source_target_pairs={{8,0},{12,4},{0,8},{4,12},{24,16},{28,20},{16,24},{20,28},{9,1},{1... | collective-permute-start | bytes 786440 | tf_op jit(solution)/shard_map/ppermute | solution.py:54
  3.6 1.5 %collective-permute-start.1 = (bf16[256,512]{1,0:T(8,128)(2,1)}, bf16[256,512]{1,0:T(8,128)(2,1)S(1)}, u32[]{:S(2)}, u32[]{:S(2)}) collective-permute-start(bf16[256,512]{1,0:T(8,128)(2,1)} %refs_6_.1), channel_id=1, source_target_pairs={{8,0},{28,4},{16,8},{4,12},{24,16},{12,20},{0,24},{20,28},{9,1},{2... | collective-permute-start | bytes 786440 | tf_op jit(solution)/shard_map/ppermute | solution.py:54
  5.1 0.0 collective-permute-start
  5.1 2.6 %collective-permute-start.13 = (bf16[64,2048]{1,0:T(8,128)(2,1)}, bf16[64,2048]{1,0:T(8,128)(2,1)S(1)}, u32[]{:S(2)}, u32[]{:S(2)}) collective-permute-start(bf16[64,2048]{1,0:T(8,128)(2,1)} %refs_2_.5), channel_id=1, source_target_pairs={{0,2},{1,3},{2,0},{3,1},{4,6},{5,7},{6,4},{7,5},{8,10},{9,11},{10,... | collective-permute-start | bytes 786440 | tf_op jit(solution)/shard_map/ppermute | solution.py:451
  7.7 1.6 %collective-permute-start.12 = (bf16[64,2048]{1,0:T(8,128)(2,1)}, bf16[64,2048]{1,0:T(8,128)(2,1)S(1)}, u32[]{:S(2)}, u32[]{:S(2)}) collective-permute-start(bf16[64,2048]{1,0:T(8,128)(2,1)} %refs_2_.5), channel_id=1, source_target_pairs={{0,1},{1,0},{2,3},{3,2},{4,5},{5,4},{6,7},{7,6},{8,9},{9,8},{10,11... | collective-permute-start | bytes 786440 | tf_op jit(solution)/shard_map/ppermute | solution.py:451
  9.3 1.7 %collective-permute-done.5.refs_12_.refs_13_ = bf16[256,512]{1,0:T(8,128)(2,1)S(1)} collective-permute-done((bf16[256,512]{1,0:T(8,128)(2,1)}, bf16[256,512]{1,0:T(8,128)(2,1)S(1)}, u32[]{:S(2)}, u32[]{:S(2)}) %collective-permute-start.5) | collective-permute-done | bytes 262176 | tf_op jit(solution)/shard_map/ppermute | solution.py:54
  11.0 2.1 %collective-permute-start.7 = (bf16[256,512]{1,0:T(8,128)(2,1)S(1)}, bf16[256,512]{1,0:T(8,128)(2,1)S(1)}, u32[]{:S(2)}, u32[]{:S(2)}) collective-permute-start(bf16[256,512]{1,0:T(8,128)(2,1)S(1)} %collective-permute-done.5.refs_12_.refs_13_), channel_id=1, source_target_pairs={{16,0},{20,4},{24,8},{28,12},{0,16},{4,20},{8,24},{12,28},{17,1},{... | collective-permute-start | bytes 786440 | tf_op jit(solution)/shard_map/ppermute | solution.py:54
  13.1 2.7 %collective-permute-done.1.refs_7_.refs_8_ = bf16[256,512]{1,0:T(8,128)(2,1)S(1)} collective-permute-done((bf16[256,512]{1,0:T(8,128)(2,1)}, bf16[256,512]{1,0:T(8,128)(2,1)S(1)}, u32[]{:S(2)}, u32[]{:S(2)}) %collective-permute-start.1) | collective-permute-done | bytes 262176 | tf_op jit(solution)/shard_map/ppermute | solution.py:54
  15.8 2.8 %collective-permute-start.2 = (bf16[256,512]{1,0:T(8,128)(2,1)}, bf16[256,512]{1,0:T(8,128)(2,1)S(1)}, u32[]{:S(2)}, u32[]{:S(2)}) collective-permute-start(bf16[256,512]{1,0:T(8,128)(2,1)} %refs_6_.1), channel_id=1, source_target_pairs={{24,0},{12,4},{0,8},{20,12},{8,16},{28,20},{16,24},{4,28},{25,1},{... | collective-permute-start | bytes 786440 | tf_op jit(solution)/shard_map/ppermute | solution.py:54
  18.6 0.0 collective-permute-done.refs_6_.refs_7_
  18.6 0.0 collective-permute-start.4
  18.6 2.1 %collective-permute-done.13.refs_2_.refs_6_ = bf16[64,2048]{1,0:T(8,128)(2,1)S(1)} collective-permute-done((bf16[64,2048]{1,0:T(8,128)(2,1)}, bf16[64,2048]{1,0:T(8,128)(2,1)S(1)}, u32[]{:S(2)}, u32[]{:S(2)}) %collective-permute-start.13) | collective-permute-done | bytes 262176 | tf_op jit(solution)/shard_map/ppermute | solution.py:451
  20.7 0.0 collective-permute-start.6
  20.7 0.2 collective-permute-done.12.refs_1_.refs_5_
  20.9 0.3 collective-permute-start.3
  21.2 0.0 collective-permute-done.7.refs_14_.refs_15_
  21.2 0.2 collective-permute-start.8
  21.4 0.2 copy-done.10
  21.6 1.7 %copies_after.1 = bf16[256,512]{1,0:T(8,128)(2,1)} custom-call(bf16[256,512]{1,0:T(8,128)(2,1)} %refs_3_.5, bf16[64,2048]{1,0:T(8,128)(2,1)} %copy-done.10, bf16[64,2048]{1,0:T(8,128)(2,1)} %copy-done.9), custom_call_target="tpu_custom_call" | custom-call | flops 1000 | bytes 1000 | tf_op jit(solution)/shard_map/copies_after/pallas_call | solution.py:411
  23.2 1.1 %collective-permute-done.2.refs_8_.refs_9_ = bf16[256,512]{1,0:T(8,128)(2,1)S(1)} collective-permute-done((bf16[256,512]{1,0:T(8,128)(2,1)}, bf16[256,512]{1,0:T(8,128)(2,1)S(1)}, u32[]{:S(2)}, u32[]{:S(2)}) %collective-permute-start.2) | collective-permute-done | bytes 262176 | tf_op jit(solution)/shard_map/ppermute | solution.py:54
  24.4 0.0 collective-permute-start.14
  24.4 3.3 %collective-permute-start.15 = (bf16[256,512]{1,0:T(8,128)(2,1)}, bf16[256,512]{1,0:T(8,128)(2,1)S(1)}, u32[]{:S(2)}, u32[]{:S(2)}) collective-permute-start(bf16[256,512]{1,0:T(8,128)(2,1)} %copies_after.1), channel_id=1, source_target_pairs={{8,0},{28,4},{16,8},{4,12},{24,16},{12,20},{0,24},{20,28},{9,1},{2... | collective-permute-start | bytes 786440 | tf_op jit(solution)/shard_map/ppermute | solution.py:54
  27.7 1.6 %collective-permute-start.18 = (bf16[64,2048]{1,0:T(8,128)(2,1)}, bf16[64,2048]{1,0:T(8,128)(2,1)S(1)}, u32[]{:S(2)}, u32[]{:S(2)}) collective-permute-start(bf16[64,2048]{1,0:T(8,128)(2,1)} %copy-done.9), channel_id=1, source_target_pairs={{0,1},{1,0},{2,3},{3,2},{4,5},{5,4},{6,7},{7,6},{8,9},{9,8},{10,11... | collective-permute-start | bytes 786440 | tf_op jit(solution)/shard_map/ppermute | solution.py:451
  29.3 0.0 collective-permute-done.3.refs_9_.refs_10_
  29.4 0.7 copy-done.18
  30.0 0.7 %copy-done.19 = bf16[256,512]{1,0:T(8,128)(2,1)} copy-done((bf16[256,512]{1,0:T(8,128)(2,1)}, bf16[256,512]{1,0:T(8,128)(2,1)S(1)}, u32[]{:S(2)}) %copy-start.19) | copy-done | bytes 262168
  30.7 5.5 %attend.1 = (bf16[64,2048]{1,0:T(8,128)(2,1)}, bf16[64,2048]{1,0:T(8,128)(2,1)}, bf16[64,2048]{1,0:T(8,128)(2,1)}, bf16[64,2048]{1,0:T(8,128)(2,1)}, f32[256,512]{1,0:T(8,128)}, /*index=5*/f32[128,128]{1,0:T(8,128)}) custom-call(s32[2,4]{1,0:T(2,128)} %refs_0_.9, s32[16]{0:T(128)} %refs_1_.7, f32[4]{0:T(128)} %refs_2_.7, bf16[256,512]{1,0:T(8,128)(2,1)} %refs_3_.5, ...), custom_call_target="tpu_custom_call" | custom-call | flops 1000000000 | bytes 1000000 | tf_op jit(solution)/shard_map/attend/pallas_call | solution.py:470
  36.2 0.0 copy-start.20
  36.2 0.5 collective-permute-start.10
  36.7 0.1 collective-permute-start.17
  36.8 0.0 collective-permute-done.18.refs_7_
  36.8 0.7 %copy-done.3 = bf16[256,512]{1,0:T(8,128)(2,1)} copy-done((bf16[256,512]{1,0:T(8,128)(2,1)}, bf16[256,512]{1,0:T(8,128)(2,1)S(1)}, u32[]{:S(2)}) %copy-start.3) | copy-done | bytes 262168
  37.5 0.1 copy-done.21
  37.6 4.3 %upstream.1 = (bf16[272,512]{1,0:T(8,128)(2,1)}, f32[128,128]{1,0:T(8,128)}) custom-call(s32[2,4]{1,0:T(2,128)} %refs_0_.9, bf16[512,2048]{1,0:T(8,128)(2,1)} %refs_1_.5, bf16[64,2048]{1,0:T(8,128)(2,1)} %refs_2_.5, f32[256,512]{1,0:T(8,128)} %get-tuple-element.19.refs_3_, f32[128,128]{1,0:T(8,128)} %get-tuple-element.20.refs_4_, ...), custom_call_target="tpu_custom_call" | custom-call | flops 1000 | bytes 1000 | tf_op jit(solution)/shard_map/upstream/pallas_call | solution.py:502
  42.0 2.9 %collective-permute-start.20 = (bf16[272,512]{1,0:T(8,128)(2,1)}, bf16[272,512]{1,0:T(8,128)(2,1)S(1)}, u32[]{:S(2)}, u32[]{:S(2)}) collective-permute-start(bf16[272,512]{1,0:T(8,128)(2,1)} %get-tuple-element.21.refs_9_.refs_4_), channel_id=1, source_target_pairs={{8,0},{28,4},{16,8},{4,12},{24,16},{12,20},{0,24},{20,28},{9,1},{2... | collective-permute-start | bytes 835592 | tf_op jit(solution)/shard_map/ppermute | solution.py:54
  44.9 0.0 collective-permute-start.19
  44.9 0.0 collective-permute-done.10
  44.9 0.0 collective-permute-start.21
  44.9 0.1 add_convert_fusion
  45.0 1.6 %collective-permute-start.9 = (bf16[64,2048]{1,0:T(8,128)(2,1)}, bf16[64,2048]{1,0:T(8,128)(2,1)S(1)}, u32[]{:S(2)}, u32[]{:S(2)}) collective-permute-start(bf16[64,2048]{1,0:T(8,128)(2,1)} %get-tuple-element.16), channel_id=1, source_target_pairs={{0,1},{1,0},{2,3},{3,2},{4,5},{5,4},{6,7},{7,6},{8,9},{9,8},{10,11... | collective-permute-start | bytes 786440 | tf_op jit(solution)/shard_map/ppermute | solution.py:451
  46.6 2.6 %collective-permute-start.11 = (bf16[64,2048]{1,0:T(8,128)(2,1)S(1)}, bf16[64,2048]{1,0:T(8,128)(2,1)S(1)}, u32[]{:S(2)}, u32[]{:S(2)}) collective-permute-start(bf16[64,2048]{1,0:T(8,128)(2,1)S(1)} %add_convert_fusion), channel_id=1, source_target_pairs={{0,2},{1,3},{2,0},{3,1},{4,6},{5,7},{6,4},{7,5},{8,10},{9,11},{10,... | collective-permute-start | bytes 786440 | tf_op jit(solution)/shard_map/ppermute | solution.py:451
  49.2 3.0 %collective-permute-done.20.refs_11_ = bf16[272,512]{1,0:T(8,128)(2,1)S(1)} collective-permute-done((bf16[272,512]{1,0:T(8,128)(2,1)}, bf16[272,512]{1,0:T(8,128)(2,1)S(1)}, u32[]{:S(2)}, u32[]{:S(2)}) %collective-permute-start.20) | collective-permute-done | bytes 278560 | tf_op jit(solution)/shard_map/ppermute | solution.py:54
  52.2 0.1 collective-permute-start.22
  52.3 0.0 copy-start.7
  52.4 0.0 copy-start.8
  52.4 6.2 %query_grad.1 = bf16[256,512]{1,0:T(8,128)(2,1)} custom-call(s32[2,4]{1,0:T(2,128)} %refs_0_.9, s32[16]{0:T(128)} %refs_1_.7, f32[4]{0:T(128)} %refs_2_.7, bf16[256,512]{1,0:T(8,128)(2,1)} %refs_3_.5, bf16[272,512]{1,0:T(8,128)(2,1)} %get-tuple-element.21.refs_9_.refs_4_, f32[128,128]{1,0:T(8,128)} %get-tuple-element.23.refs_5_, bf16[256,512]{1,0:T(8,128)(2,1)} %refs_6_.1, ...), custom_call_target="tpu_custom_call" | custom-call | flops 16000000000 | bytes 32000000 | tf_op jit(solution)/shard_map/query_grad/pallas_call | solution.py:524
  58.7 6.6 %key_grad.1 = (bf16[256,512]{1,0:T(8,128)(2,1)}, bf16[256,512]{1,0:T(8,128)(2,1)}, f32[8,128]{1,0:T(8,128)S(1)}) custom-call(s32[16]{0:T(128)S(1)} %copy-done.7, f32[4]{0:T(128)S(1)} %copy-done.8, bf16[256,512]{1,0:T(8,128)(2,1)S(1)} %copy-done.1, bf16[256,512]{1,0:T(8,128)(2,1)S(1)} %copy-done.2, bf16[256,512]{1,0:T(8,128)(2,1)S(1)} %copy-done, ...), custom_call_target="tpu_custom_call" | custom-call | flops 1000 | bytes 1000 | tf_op jit(solution)/shard_map/key_grad/pallas_call | solution.py:541
  65.3 0.8 %sum_after.1 = bf16[64,2048]{1,0:T(8,128)(2,1)} custom-call(bf16[64,2048]{1,0:T(8,128)(2,1)S(1)} %copy-done.6, bf16[64,2048]{1,0:T(8,128)(2,1)S(1)} %collective-permute-done.9.refs_1_, bf16[64,2048]{1,0:T(8,128)(2,1)S(1)} %collective-permute-done.11.refs_2_, f32[8,128]{1,0:T(8,128)S(1)} %get-tuple-element.22.refs_3_), custom_call_target="tpu_custom_call" | custom-call | flops 1000 | bytes 1000 | tf_op jit(solution)/shard_map/sum_after/pallas_call | solution.py:392
  (51 shorter events, 0.1 us)
Async XLA Ops:
  0.6 10.4 %collective-permute-start.5 = (bf16[256,512]{1,0:T(8,128)(2,1)}, bf16[256,512]{1,0:T(8,128)(2,1)S(1)}, u32[]{:S(2)}, u32[]{:S(2)}) collective-permute-start(bf16[256,512]{1,0:T(8,128)(2,1)} %refs_11_.1), channel_id=1, source_target_pairs={{8,0},{12,4},{0,8},{4,12},{24,16},{28,20},{16,24},{20,28},{9,1},{1... | collective-permute-start | bytes 786440 | tf_op jit(solution)/shard_map/ppermute | solution.py:54
  3.6 12.1 %collective-permute-start.1 = (bf16[256,512]{1,0:T(8,128)(2,1)}, bf16[256,512]{1,0:T(8,128)(2,1)S(1)}, u32[]{:S(2)}, u32[]{:S(2)}) collective-permute-start(bf16[256,512]{1,0:T(8,128)(2,1)} %refs_6_.1), channel_id=1, source_target_pairs={{8,0},{28,4},{16,8},{4,12},{24,16},{12,20},{0,24},{20,28},{9,1},{2... | collective-permute-start | bytes 786440 | tf_op jit(solution)/shard_map/ppermute | solution.py:54
  5.1 13.5 %collective-permute-start = (bf16[256,512]{1,0:T(8,128)(2,1)}, bf16[256,512]{1,0:T(8,128)(2,1)S(1)}, u32[]{:S(2)}, u32[]{:S(2)}) collective-permute-start(bf16[256,512]{1,0:T(8,128)(2,1)} %refs_6_.1), channel_id=1, source_target_pairs={{4,0},{0,4},{12,8},{8,12},{20,16},{16,20},{28,24},{24,28},{5,1},{1... | collective-permute-start | bytes 786440 | tf_op jit(solution)/shard_map/ppermute | solution.py:54
  5.1 15.6 %collective-permute-start.13 = (bf16[64,2048]{1,0:T(8,128)(2,1)}, bf16[64,2048]{1,0:T(8,128)(2,1)S(1)}, u32[]{:S(2)}, u32[]{:S(2)}) collective-permute-start(bf16[64,2048]{1,0:T(8,128)(2,1)} %refs_2_.5), channel_id=1, source_target_pairs={{0,2},{1,3},{2,0},{3,1},{4,6},{5,7},{6,4},{7,5},{8,10},{9,11},{10,... | collective-permute-start | bytes 786440 | tf_op jit(solution)/shard_map/ppermute | solution.py:451
  7.7 13.2 %collective-permute-start.12 = (bf16[64,2048]{1,0:T(8,128)(2,1)}, bf16[64,2048]{1,0:T(8,128)(2,1)S(1)}, u32[]{:S(2)}, u32[]{:S(2)}) collective-permute-start(bf16[64,2048]{1,0:T(8,128)(2,1)} %refs_2_.5), channel_id=1, source_target_pairs={{0,1},{1,0},{2,3},{3,2},{4,5},{5,4},{6,7},{7,6},{8,9},{9,8},{10,11... | collective-permute-start | bytes 786440 | tf_op jit(solution)/shard_map/ppermute | solution.py:451
  11.0 18.3 %copy-start.11 = (bf16[256,512]{1,0:T(8,128)(2,1)}, bf16[256,512]{1,0:T(8,128)(2,1)S(1)}, u32[]{:S(2)}) copy-start(bf16[256,512]{1,0:T(8,128)(2,1)S(1)} %collective-permute-done.5.refs_12_.refs_13_) | copy-start | bytes 786436
  11.0 10.2 %collective-permute-start.7 = (bf16[256,512]{1,0:T(8,128)(2,1)S(1)}, bf16[256,512]{1,0:T(8,128)(2,1)S(1)}, u32[]{:S(2)}, u32[]{:S(2)}) collective-permute-start(bf16[256,512]{1,0:T(8,128)(2,1)S(1)} %collective-permute-done.5.refs_12_.refs_13_), channel_id=1, source_target_pairs={{16,0},{20,4},{24,8},{28,12},{0,16},{4,20},{8,24},{12,28},{17,1},{... | collective-permute-start | bytes 786440 | tf_op jit(solution)/shard_map/ppermute | solution.py:54
  15.8 13.5 %copy-start.12 = (bf16[256,512]{1,0:T(8,128)(2,1)}, bf16[256,512]{1,0:T(8,128)(2,1)S(1)}, u32[]{:S(2)}) copy-start(bf16[256,512]{1,0:T(8,128)(2,1)S(1)} %collective-permute-done.1.refs_7_.refs_8_) | copy-start | bytes 786436
  15.8 8.6 %collective-permute-start.2 = (bf16[256,512]{1,0:T(8,128)(2,1)}, bf16[256,512]{1,0:T(8,128)(2,1)S(1)}, u32[]{:S(2)}, u32[]{:S(2)}) collective-permute-start(bf16[256,512]{1,0:T(8,128)(2,1)} %refs_6_.1), channel_id=1, source_target_pairs={{24,0},{12,4},{0,8},{20,12},{8,16},{28,20},{16,24},{4,28},{25,1},{... | collective-permute-start | bytes 786440 | tf_op jit(solution)/shard_map/ppermute | solution.py:54
  18.6 10.7 %copy-start.13 = (bf16[256,512]{1,0:T(8,128)(2,1)}, bf16[256,512]{1,0:T(8,128)(2,1)S(1)}, u32[]{:S(2)}) copy-start(bf16[256,512]{1,0:T(8,128)(2,1)S(1)} %collective-permute-done.refs_6_.refs_7_) | copy-start | bytes 786436
  18.6 5.8 %collective-permute-start.4 = (bf16[256,512]{1,0:T(8,128)(2,1)}, bf16[256,512]{1,0:T(8,128)(2,1)S(1)}, u32[]{:S(2)}, u32[]{:S(2)}) collective-permute-start(bf16[256,512]{1,0:T(8,128)(2,1)} %refs_11_.1), channel_id=1, source_target_pairs={{4,0},{0,4},{12,8},{8,12},{20,16},{16,20},{28,24},{24,28},{5,1},{1... | collective-permute-start | bytes 786440 | tf_op jit(solution)/shard_map/ppermute | solution.py:54
  20.7 0.7 %copy-start.9 = (bf16[64,2048]{1,0:T(8,128)(2,1)}, bf16[64,2048]{1,0:T(8,128)(2,1)S(1)}, u32[]{:S(2)}) copy-start(bf16[64,2048]{1,0:T(8,128)(2,1)S(1)} %collective-permute-done.13.refs_2_.refs_6_) | copy-start | bytes 786436
  20.7 7.0 %collective-permute-start.6 = (bf16[256,512]{1,0:T(8,128)(2,1)S(1)}, bf16[256,512]{1,0:T(8,128)(2,1)S(1)}, u32[]{:S(2)}, u32[]{:S(2)}) collective-permute-start(bf16[256,512]{1,0:T(8,128)(2,1)S(1)} %collective-permute-done.5.refs_12_.refs_13_), channel_id=1, source_target_pairs={{4,0},{0,4},{12,8},{8,12},{20,16},{16,20},{28,24},{24,28},{5,1},{1... | collective-permute-start | bytes 786440 | tf_op jit(solution)/shard_map/ppermute | solution.py:54
  20.9 0.7 %copy-start.10 = (bf16[64,2048]{1,0:T(8,128)(2,1)}, bf16[64,2048]{1,0:T(8,128)(2,1)S(1)}, u32[]{:S(2)}) copy-start(bf16[64,2048]{1,0:T(8,128)(2,1)S(1)} %collective-permute-done.12.refs_1_.refs_5_) | copy-start | bytes 786436
  20.9 8.4 %collective-permute-start.3 = (bf16[256,512]{1,0:T(8,128)(2,1)S(1)}, bf16[256,512]{1,0:T(8,128)(2,1)S(1)}, u32[]{:S(2)}, u32[]{:S(2)}) collective-permute-start(bf16[256,512]{1,0:T(8,128)(2,1)S(1)} %collective-permute-done.1.refs_7_.refs_8_), channel_id=1, source_target_pairs={{4,0},{0,4},{12,8},{8,12},{20,16},{16,20},{28,24},{24,28},{5,1},{1... | collective-permute-start | bytes 786440 | tf_op jit(solution)/shard_map/ppermute | solution.py:54
  21.2 8.1 %copy-start.14 = (bf16[256,512]{1,0:T(8,128)(2,1)}, bf16[256,512]{1,0:T(8,128)(2,1)S(1)}, u32[]{:S(2)}) copy-start(bf16[256,512]{1,0:T(8,128)(2,1)S(1)} %collective-permute-done.7.refs_14_.refs_15_) | copy-start | bytes 786436
  21.2 8.1 %collective-permute-start.8 = (bf16[256,512]{1,0:T(8,128)(2,1)S(1)}, bf16[256,512]{1,0:T(8,128)(2,1)S(1)}, u32[]{:S(2)}, u32[]{:S(2)}) collective-permute-start(bf16[256,512]{1,0:T(8,128)(2,1)S(1)} %collective-permute-done.7.refs_14_.refs_15_), channel_id=1, source_target_pairs={{4,0},{0,4},{12,8},{8,12},{20,16},{16,20},{28,24},{24,28},{5,1},{1... | collective-permute-start | bytes 786440 | tf_op jit(solution)/shard_map/ppermute | solution.py:54
  23.2 13.5 %copy-start.22 = (bf16[256,512]{1,0:T(8,128)(2,1)S(1)}, bf16[256,512]{1,0:T(8,128)(2,1)}, u32[]{:S(2)}) copy-start(bf16[256,512]{1,0:T(8,128)(2,1)} %copies_after.1) | copy-start | bytes 786436
  24.4 5.0 %copy-start.15 = (bf16[256,512]{1,0:T(8,128)(2,1)}, bf16[256,512]{1,0:T(8,128)(2,1)S(1)}, u32[]{:S(2)}) copy-start(bf16[256,512]{1,0:T(8,128)(2,1)S(1)} %collective-permute-done.2.refs_8_.refs_9_) | copy-start | bytes 786436
  24.4 12.4 %collective-permute-start.14 = (bf16[256,512]{1,0:T(8,128)(2,1)}, bf16[256,512]{1,0:T(8,128)(2,1)S(1)}, u32[]{:S(2)}, u32[]{:S(2)}) collective-permute-start(bf16[256,512]{1,0:T(8,128)(2,1)} %copies_after.1), channel_id=1, source_target_pairs={{4,0},{0,4},{12,8},{8,12},{20,16},{16,20},{28,24},{24,28},{5,1},{1... | collective-permute-start | bytes 786440 | tf_op jit(solution)/shard_map/ppermute | solution.py:54
  24.4 5.0 %copy-start.16 = (bf16[256,512]{1,0:T(8,128)(2,1)}, bf16[256,512]{1,0:T(8,128)(2,1)S(1)}, u32[]{:S(2)}) copy-start(bf16[256,512]{1,0:T(8,128)(2,1)S(1)} %collective-permute-done.4.refs_11_.refs_12_) | copy-start | bytes 786436
  24.4 12.3 %collective-permute-start.15 = (bf16[256,512]{1,0:T(8,128)(2,1)}, bf16[256,512]{1,0:T(8,128)(2,1)S(1)}, u32[]{:S(2)}, u32[]{:S(2)}) collective-permute-start(bf16[256,512]{1,0:T(8,128)(2,1)} %copies_after.1), channel_id=1, source_target_pairs={{8,0},{28,4},{16,8},{4,12},{24,16},{12,20},{0,24},{20,28},{9,1},{2... | collective-permute-start | bytes 786440 | tf_op jit(solution)/shard_map/ppermute | solution.py:54
  27.7 1.7 %copy-start.17 = (bf16[256,512]{1,0:T(8,128)(2,1)}, bf16[256,512]{1,0:T(8,128)(2,1)S(1)}, u32[]{:S(2)}) copy-start(bf16[256,512]{1,0:T(8,128)(2,1)S(1)} %collective-permute-done.6.refs_13_.refs_14_) | copy-start | bytes 786436
  27.7 9.1 %collective-permute-start.18 = (bf16[64,2048]{1,0:T(8,128)(2,1)}, bf16[64,2048]{1,0:T(8,128)(2,1)S(1)}, u32[]{:S(2)}, u32[]{:S(2)}) collective-permute-start(bf16[64,2048]{1,0:T(8,128)(2,1)} %copy-done.9), channel_id=1, source_target_pairs={{0,1},{1,0},{2,3},{3,2},{4,5},{5,4},{6,7},{7,6},{8,9},{9,8},{10,11... | collective-permute-start | bytes 786440 | tf_op jit(solution)/shard_map/ppermute | solution.py:451
  29.3 0.7 %copy-start.18 = (bf16[256,512]{1,0:T(8,128)(2,1)}, bf16[256,512]{1,0:T(8,128)(2,1)S(1)}, u32[]{:S(2)}) copy-start(bf16[256,512]{1,0:T(8,128)(2,1)S(1)} %collective-permute-done.3.refs_9_.refs_10_) | copy-start | bytes 786436
  30.0 0.7 %copy-start.19 = (bf16[256,512]{1,0:T(8,128)(2,1)}, bf16[256,512]{1,0:T(8,128)(2,1)S(1)}, u32[]{:S(2)}) copy-start(bf16[256,512]{1,0:T(8,128)(2,1)S(1)} %collective-permute-done.8.refs_15_.refs_16_) | copy-start | bytes 786436
  36.2 8.7 %copy-start.20 = (bf16[64,2048]{1,0:T(8,128)(2,1)S(1)}, bf16[64,2048]{1,0:T(8,128)(2,1)}, u32[]{:S(2)}) copy-start(bf16[64,2048]{1,0:T(8,128)(2,1)} %get-tuple-element.17) | copy-start | bytes 786436
  36.2 8.7 %collective-permute-start.10 = (bf16[64,2048]{1,0:T(8,128)(2,1)}, bf16[64,2048]{1,0:T(8,128)(2,1)S(1)}, u32[]{:S(2)}, u32[]{:S(2)}) collective-permute-start(bf16[64,2048]{1,0:T(8,128)(2,1)} %get-tuple-element.18), channel_id=1, source_target_pairs={{0,1},{1,0},{2,3},{3,2},{4,5},{5,4},{6,7},{7,6},{8,9},{9,8},{10,11... | collective-permute-start | bytes 786440 | tf_op jit(solution)/shard_map/ppermute | solution.py:451
  36.7 8.2 %collective-permute-start.16 = (bf16[256,512]{1,0:T(8,128)(2,1)S(1)}, bf16[256,512]{1,0:T(8,128)(2,1)S(1)}, u32[]{:S(2)}, u32[]{:S(2)}) collective-permute-start(bf16[256,512]{1,0:T(8,128)(2,1)S(1)} %copy-done.22), channel_id=1, source_target_pairs={{24,0},{12,4},{0,8},{20,12},{8,16},{28,20},{16,24},{4,28},{25,1},{... | collective-permute-start | bytes 786440 | tf_op jit(solution)/shard_map/ppermute | solution.py:54
  36.7 9.9 %collective-permute-start.17 = (bf16[256,512]{1,0:T(8,128)(2,1)S(1)}, bf16[256,512]{1,0:T(8,128)(2,1)S(1)}, u32[]{:S(2)}, u32[]{:S(2)}) collective-permute-start(bf16[256,512]{1,0:T(8,128)(2,1)S(1)} %collective-permute-done.15.refs_6_), channel_id=1, source_target_pairs={{4,0},{0,4},{12,8},{8,12},{20,16},{16,20},{28,24},{24,28},{5,1},{1... | collective-permute-start | bytes 786440 | tf_op jit(solution)/shard_map/ppermute | solution.py:54
  36.8 0.7 %copy-start.3 = (bf16[256,512]{1,0:T(8,128)(2,1)}, bf16[256,512]{1,0:T(8,128)(2,1)S(1)}, u32[]{:S(2)}) copy-start(bf16[256,512]{1,0:T(8,128)(2,1)S(1)} %collective-permute-done.14.refs_8_.refs_5_) | copy-start | bytes 786436
  36.8 0.8 %copy-start.21 = (bf16[64,2048]{1,0:T(8,128)(2,1)}, bf16[64,2048]{1,0:T(8,128)(2,1)S(1)}, u32[]{:S(2)}) copy-start(bf16[64,2048]{1,0:T(8,128)(2,1)S(1)} %collective-permute-done.18.refs_7_) | copy-start | bytes 786436
  42.0 10.3 %collective-permute-start.20 = (bf16[272,512]{1,0:T(8,128)(2,1)}, bf16[272,512]{1,0:T(8,128)(2,1)S(1)}, u32[]{:S(2)}, u32[]{:S(2)}) collective-permute-start(bf16[272,512]{1,0:T(8,128)(2,1)} %get-tuple-element.21.refs_9_.refs_4_), channel_id=1, source_target_pairs={{8,0},{28,4},{16,8},{4,12},{24,16},{12,20},{0,24},{20,28},{9,1},{2... | collective-permute-start | bytes 835592 | tf_op jit(solution)/shard_map/ppermute | solution.py:54
  44.9 13.8 %collective-permute-start.19 = (bf16[272,512]{1,0:T(8,128)(2,1)}, bf16[272,512]{1,0:T(8,128)(2,1)S(1)}, u32[]{:S(2)}, u32[]{:S(2)}) collective-permute-start(bf16[272,512]{1,0:T(8,128)(2,1)} %get-tuple-element.21.refs_9_.refs_4_), channel_id=1, source_target_pairs={{4,0},{0,4},{12,8},{8,12},{20,16},{16,20},{28,24},{24,28},{5,1},{1... | collective-permute-start | bytes 835592 | tf_op jit(solution)/shard_map/ppermute | solution.py:54
  44.9 13.8 %collective-permute-start.21 = (bf16[272,512]{1,0:T(8,128)(2,1)}, bf16[272,512]{1,0:T(8,128)(2,1)S(1)}, u32[]{:S(2)}, u32[]{:S(2)}) collective-permute-start(bf16[272,512]{1,0:T(8,128)(2,1)} %get-tuple-element.21.refs_9_.refs_4_), channel_id=1, source_target_pairs={{24,0},{12,4},{0,8},{20,12},{8,16},{28,20},{16,24},{4,28},{25,1},{... | collective-permute-start | bytes 835592 | tf_op jit(solution)/shard_map/ppermute | solution.py:54
  45.0 20.4 %collective-permute-start.9 = (bf16[64,2048]{1,0:T(8,128)(2,1)}, bf16[64,2048]{1,0:T(8,128)(2,1)S(1)}, u32[]{:S(2)}, u32[]{:S(2)}) collective-permute-start(bf16[64,2048]{1,0:T(8,128)(2,1)} %get-tuple-element.16), channel_id=1, source_target_pairs={{0,1},{1,0},{2,3},{3,2},{4,5},{5,4},{6,7},{7,6},{8,9},{9,8},{10,11... | collective-permute-start | bytes 786440 | tf_op jit(solution)/shard_map/ppermute | solution.py:451
  46.6 18.7 %collective-permute-start.11 = (bf16[64,2048]{1,0:T(8,128)(2,1)S(1)}, bf16[64,2048]{1,0:T(8,128)(2,1)S(1)}, u32[]{:S(2)}, u32[]{:S(2)}) collective-permute-start(bf16[64,2048]{1,0:T(8,128)(2,1)S(1)} %add_convert_fusion), channel_id=1, source_target_pairs={{0,2},{1,3},{2,0},{3,1},{4,6},{5,7},{6,4},{7,5},{8,10},{9,11},{10,... | collective-permute-start | bytes 786440 | tf_op jit(solution)/shard_map/ppermute | solution.py:451
  52.2 6.4 %collective-permute-start.22 = (bf16[272,512]{1,0:T(8,128)(2,1)S(1)}, bf16[272,512]{1,0:T(8,128)(2,1)S(1)}, u32[]{:S(2)}, u32[]{:S(2)}) collective-permute-start(bf16[272,512]{1,0:T(8,128)(2,1)S(1)} %collective-permute-done.20.refs_11_), channel_id=1, source_target_pairs={{4,0},{0,4},{12,8},{8,12},{20,16},{16,20},{28,24},{24,28},{5,1},{1... | collective-permute-start | bytes 835592 | tf_op jit(solution)/shard_map/ppermute | solution.py:54
  52.3 6.3 %copy-start = (bf16[256,512]{1,0:T(8,128)(2,1)S(1)}, bf16[256,512]{1,0:T(8,128)(2,1)}, u32[]{:S(2)}) copy-start(bf16[256,512]{1,0:T(8,128)(2,1)} %refs_3_.5) | copy-start | bytes 786436
  52.3 6.3 %copy-start.1 = (bf16[256,512]{1,0:T(8,128)(2,1)S(1)}, bf16[256,512]{1,0:T(8,128)(2,1)}, u32[]{:S(2)}) copy-start(bf16[256,512]{1,0:T(8,128)(2,1)} %refs_6_.1) | copy-start | bytes 786436
  52.3 6.3 %copy-start.2 = (bf16[256,512]{1,0:T(8,128)(2,1)S(1)}, bf16[256,512]{1,0:T(8,128)(2,1)}, u32[]{:S(2)}) copy-start(bf16[256,512]{1,0:T(8,128)(2,1)} %refs_11_.1) | copy-start | bytes 786436
  52.3 6.3 %copy-start.4 = (bf16[256,512]{1,0:T(8,128)(2,1)S(1)}, bf16[256,512]{1,0:T(8,128)(2,1)}, u32[]{:S(2)}) copy-start(bf16[256,512]{1,0:T(8,128)(2,1)} %copy-done.3) | copy-start | bytes 786436
  52.3 6.4 %copy-start.5 = (bf16[272,512]{1,0:T(8,128)(2,1)S(1)}, bf16[272,512]{1,0:T(8,128)(2,1)}, u32[]{:S(2)}) copy-start(bf16[272,512]{1,0:T(8,128)(2,1)} %get-tuple-element.21.refs_9_.refs_4_) | copy-start | bytes 835588
  52.3 6.4 %copy-start.7 = (s32[16]{0:T(128)S(1)}, s32[16]{0:T(128)}, u32[]{:S(2)}) copy-start(s32[16]{0:T(128)} %refs_1_.7) | copy-start | bytes 196
  52.4 6.4 %copy-start.8 = (f32[4]{0:T(128)S(1)}, f32[4]{0:T(128)}, u32[]{:S(2)}) copy-start(f32[4]{0:T(128)} %refs_2_.7) | copy-start | bytes 52
  58.6 6.7 %copy-start.6 = (bf16[64,2048]{1,0:T(8,128)(2,1)S(1)}, bf16[64,2048]{1,0:T(8,128)(2,1)}, u32[]{:S(2)}) copy-start(bf16[64,2048]{1,0:T(8,128)(2,1)} %get-tuple-element.15.refs_0_) | copy-start | bytes 786436
